TPU v7x, 32 devices: a whole 2x2x4 slice. The times are simulated.
32 devices in a mesh: dp: 8 (over y, x, core), fsdp: 4 (over z).
Axes of the slice: x: 2, y: 2, z: 4, core: 2. Of those that a mesh axis runs over, the one named last changes fastest.
Arguments:
- owner_ids: int32 [16384, 8], P(('dp', 'fsdp')), may hold values from 0 to 31, all different within a row; in each aligned block of 512 rows (0 to 511, 512 to 1023, ...) at most 256 rows name the same one
- row_ids: int32 [16384, 8], P(('dp', 'fsdp')), may hold values from 0 to 4095
- embed_table: bfloat16 [131072, 64], P(('dp', 'fsdp')), may hold values from -6 to 6
- expandone: bfloat16 [3072, 256], P(('dp', 'fsdp')), may hold values from -0.25 to 0.25
- expbiasone: bfloat16 [1536], P(('dp', 'fsdp')), may hold values from -4 to 4
- reduceone: bfloat16 [1536, 256], P(('dp', 'fsdp')), may hold values from -0.375 to 0.375
- redbiasone: bfloat16 [1536], P(('dp', 'fsdp')), may hold values from -6 to 6
- normgainone: bfloat16 [1536], P(('dp', 'fsdp')), may hold values from 0.25 to 1.75
- taskgateone: bfloat16 [1024, 4], P(('dp', 'fsdp')), may hold values from -0.4375 to 0.4375
- sharegateone: bfloat16 [512, 6], P(('dp', 'fsdp')), may hold values from -0.4375 to 0.4375
- expandtwo: bfloat16 [1536, 256], P(('dp', 'fsdp')), may hold values from -0.375 to 0.375
- expbiastwo: bfloat16 [1536], P(('dp', 'fsdp')), may hold values from -4 to 4
- reducetwo: bfloat16 [1536, 256], P(('dp', 'fsdp')), may hold values from -0.375 to 0.375
- redbiastwo: bfloat16 [1536], P(('dp', 'fsdp')), may hold values from -6 to 6
- normgaintwo: bfloat16 [1536], P(('dp', 'fsdp')), may hold values from 0.25 to 1.75
- taskgatetwo: bfloat16 [512, 4], P(('dp', 'fsdp')), may hold values from -1 to 1
- towerinner: bfloat16 [512, 128], P(('dp', 'fsdp')), may hold values from -0.375 to 0.375
- towerbias: bfloat16 [256], P(('dp', 'fsdp')), may hold values from -4 to 4
- towermiddle: bfloat16 [256, 64], P(('dp', 'fsdp')), may hold values from -0.5 to 0.5
- towertail: bfloat16 [256], P(('dp', 'fsdp')), may hold values from -4 to 4
- logit_cot: float32 [2, 16384], P(None, ('dp', 'fsdp')), may hold values from -6 to 6
Outputs:
- logits: float32 [2, 16384], P(None, ('dp', 'fsdp'))
- x_grad: float32 [16384, 512], P(('dp', 'fsdp'))
- embed_table_grad: float32 [131072, 64], P(('dp', 'fsdp'))
- expandone_grad: float32 [3072, 256], replicated
- expbiasone_grad: float32 [1536], replicated
- reduceone_grad: float32 [1536, 256], replicated
- redbiasone_grad: float32 [1536], replicated
- normgainone_grad: float32 [1536], replicated
- taskgateone_grad: float32 [1024, 4], replicated
- sharegateone_grad: float32 [512, 6], replicated
- expandtwo_grad: float32 [1536, 256], replicated
- expbiastwo_grad: float32 [1536], replicated
- reducetwo_grad: float32 [1536, 256], replicated
- redbiastwo_grad: float32 [1536], replicated
- normgaintwo_grad: float32 [1536], replicated
- taskgatetwo_grad: float32 [512, 4], replicated
- towerinner_grad: float32 [512, 128], replicated
- towerbias_grad: float32 [256], replicated
- towermiddle_grad: float32 [256, 64], replicated
- towertail_grad: float32 [256], replicated
Inputs may be any that keep to these rules, and one draw needn't show every extreme that they name: `owner_ids`: an event's 8 owners are different. Among the lookups of one device's events, no owner is named more than 256 times, a bound that some block reaches.
All inputs are finite; a program needn't handle non-finite values.
Results may differ from a plain program's by a relative error of at most 0.017.
Values may be sent and summed in bfloat16 or wider, within the bound.
No kernel may reach another device: no remote copies, remote signals or barrier semaphores. Data moves between devices by JAX's collectives and lax.ppermute only.
A program may use at most 128 MiB of HBM per device.

v0:
```python
import jax
import jax.numpy as jnp
from jax import lax
from jax.experimental import pallas as pl
from jax.experimental.pallas import tpu as pltpu
from jax.sharding import PartitionSpec as P

EPS = 1e-05
VMEM_LIMIT = 56 * 1024 * 1024
ROW_BLOCKS = 8


def local_kernel(body, out_shape, flops, moved, scratch=()):
    return pl.pallas_call(
        body,
        out_shape=out_shape,
        scratch_shapes=list(scratch),
        compiler_params=pltpu.CompilerParams(vmem_limit_bytes=VMEM_LIMIT),
        cost_estimate=pl.CostEstimate(flops=flops, bytes_accessed=moved, transcendentals=0),
    )


def one_hot(hit):
    return jnp.where(hit, 1.0, 0.0).astype(jnp.bfloat16)


def iota(shape, axis):
    return lax.broadcasted_iota(jnp.int32, shape, axis)


def slot_body(owner_ref, row_ref, request_ref, rank_ref):
    fields, events = owner_ref.shape
    devices, capacity = request_ref.shape
    place = iota((devices, events), 0)
    asked = jnp.zeros((devices, events), jnp.float32)
    for field in range(fields):
        asked = asked + jnp.where(owner_ref[field : field + 1, :] == place, 1.0, 0.0)
    earlier = one_hot(iota((events, events), 0) < iota((events, events), 1))
    rank = jnp.dot(asked.astype(jnp.bfloat16), earlier, preferred_element_type=jnp.float32)
    rank = jnp.where(asked > 0.5, rank.astype(jnp.int32), -1)
    rank_ref[...] = rank
    slots = iota((capacity, events), 0)
    total = jnp.zeros((2 * devices, capacity), jnp.float32)
    for field in range(fields):
        mine = owner_ref[field : field + 1, :] == place
        field_rank = jnp.max(jnp.where(mine, rank, -1).astype(jnp.float32), axis=0, keepdims=True)
        rows = row_ref[field : field + 1, :]
        high = jnp.where(mine, (rows >> 6).astype(jnp.float32), 0.0)
        low = jnp.where(mine, (rows & 63).astype(jnp.float32), 0.0)
        value = jnp.concatenate([high, low], axis=0).astype(jnp.bfloat16)
        total = total + lax.dot_general(
            value,
            one_hot(field_rank.astype(jnp.int32) == slots),
            (((1,), (1,)), ((), ())),
            preferred_element_type=jnp.float32,
        )
    request_ref[...] = (total[:devices] * 64.0 + total[devices:]).astype(jnp.int32)


def assign_slots(owner_rows, row_rows, devices, capacity):
    fields, events = owner_rows.shape
    return local_kernel(
        slot_body,
        (
            jax.ShapeDtypeStruct((devices, capacity), jnp.int32),
            jax.ShapeDtypeStruct((devices, events), jnp.int32),
        ),
        2 * devices * events * (events + 2 * fields * capacity),
        4 * events * (2 * fields + devices),
    )(owner_rows, row_rows)


def find_body(request_ref, table_ref, found_ref):
    devices, capacity = request_ref.shape
    depth, span = table_ref.shape
    width = depth // ROW_BLOCKS
    places = iota((span, capacity), 0)

    def step(source, carry):
        rows = request_ref[pl.ds(source, 1), :]
        block = rows // span
        hits = one_hot(rows - block * span == places)
        rows_all = jnp.dot(table_ref[...], hits, preferred_element_type=jnp.float32)
        picked = jnp.zeros((width, capacity), jnp.float32)
        for index in range(ROW_BLOCKS):
            picked = jnp.where(
                block == index, rows_all[index * width : (index + 1) * width, :], picked
            )
        found_ref[source] = picked.astype(jnp.bfloat16)
        return carry

    lax.fori_loop(0, devices, step, 0, unroll=2)


def find_rows(request, table_wide):
    devices, capacity = request.shape
    depth, span = table_wide.shape
    return local_kernel(
        find_body,
        jax.ShapeDtypeStruct((devices, depth // ROW_BLOCKS, capacity), jnp.bfloat16),
        2 * devices * capacity * depth * span,
        2 * (depth * span + devices * capacity * depth // ROW_BLOCKS),
    )(request, table_wide)


def place_body(found_ref, rank_ref, owner_ref, flipped_ref, total_ref):
    devices, width, capacity = found_ref.shape
    fields, events = owner_ref.shape
    slots = iota((capacity, events), 0)
    group = 4
    total_ref[...] = jnp.zeros_like(total_ref)

    def step(start, carry):
        pieces = []
        for index in range(group):
            owner = start * group + index
            hits = one_hot(rank_ref[pl.ds(owner, 1), :] == slots)
            pieces.append(jnp.dot(found_ref[owner], hits, preferred_element_type=jnp.float32))
        for field in range(fields):
            rows = slice(field * width, (field + 1) * width)
            owners = owner_ref[field : field + 1, :]
            value = total_ref[rows, :]
            for index in range(group):
                value = jnp.where(owners == start * group + index, pieces[index], value)
            total_ref[rows, :] = value
        return carry

    lax.fori_loop(0, devices // group, step, 0)
    flipped_ref[...] = total_ref[...].astype(jnp.bfloat16)


def place_rows(found, rank, owner_rows):
    devices, width, capacity = found.shape
    fields, events = owner_rows.shape
    return local_kernel(
        place_body,
        jax.ShapeDtypeStruct((fields * width, events), jnp.bfloat16),
        2 * devices * width * capacity * events,
        2 * (devices * width * capacity + fields * width * events),
        [pltpu.VMEM((fields * width, events), jnp.float32)],
    )(found, rank, owner_rows)


def send_body(grad_ref, rank_ref, owner_ref, sent_ref, low_ref):
    devices, width, capacity = sent_ref.shape
    fields, events = owner_ref.shape
    slots = iota((capacity, events), 0)
    low_ref[...] = grad_ref[...].astype(jnp.bfloat16).astype(jnp.float32)

    def step(owner, carry):
        chosen = jnp.zeros((width, events), jnp.float32)
        for field in range(fields):
            rows = slice(field * width, (field + 1) * width)
            chosen = jnp.where(owner_ref[field : field + 1, :] == owner, low_ref[rows, :], chosen)
        hits = one_hot(rank_ref[pl.ds(owner, 1), :] == slots)
        sent_ref[owner] = lax.dot_general(
            chosen.astype(jnp.bfloat16),
            hits,
            (((1,), (1,)), ((), ())),
            preferred_element_type=jnp.float32,
        ).astype(jnp.bfloat16)
        return carry

    lax.fori_loop(0, devices, step, 0, unroll=2)


def send_rows(grad, rank, owner_rows, capacity):
    devices = rank.shape[0]
    fields, events = owner_rows.shape
    width = grad.shape[0] // fields
    return local_kernel(
        send_body,
        jax.ShapeDtypeStruct((devices, width, capacity), jnp.bfloat16),
        2 * devices * width * capacity * events,
        2 * (devices * width * capacity + 2 * fields * width * events),
        [pltpu.VMEM((fields * width, events), jnp.float32)],
    )(grad, rank, owner_rows)


def add_body(came_ref, request_ref, out_ref, total_ref):
    devices, width, capacity = came_ref.shape
    span = total_ref.shape[0]
    group = 4
    places = iota((span, capacity), 0)
    total_ref[...] = jnp.zeros_like(total_ref)

    def step(start, carry):
        hits = []
        spread = []
        for index in range(group):
            source = start * group + index
            rows = request_ref[pl.ds(source, 1), :]
            block = rows // span
            hits.append(one_hot(rows - block * span == places))
            came = came_ref[source].astype(jnp.float32)
            spread.append(
                jnp.concatenate(
                    [jnp.where(block == place, came, 0.0) for place in range(ROW_BLOCKS)], axis=0
                ).astype(jnp.bfloat16)
            )
        total_ref[...] += lax.dot_general(
            jnp.concatenate(hits, axis=1),
            jnp.concatenate(spread, axis=1),
            (((1,), (1,)), ((), ())),
            preferred_element_type=jnp.float32,
        )
        return carry

    lax.fori_loop(0, devices // group, step, 0)
    for index in range(ROW_BLOCKS):
        out_ref[index * span : (index + 1) * span, :] = total_ref[
            :, index * width : (index + 1) * width
        ]


def add_rows(came, request, rows):
    devices, width, capacity = came.shape
    span = rows // ROW_BLOCKS
    return local_kernel(
        add_body,
        jax.ShapeDtypeStruct((rows, width), jnp.float32),
        2 * devices * capacity * rows * width,
        2 * devices * width * capacity + 4 * rows * width,
        [pltpu.VMEM((span, ROW_BLOCKS * width), jnp.float32)],
    )(came, request)


SPAN = 256
ONES = 16


def over_events(left, right):
    return lax.dot_general(left, right, (((1,), (1,)), ((), ())), preferred_element_type=jnp.float32)


def times(left, right):
    return jnp.dot(left, right, preferred_element_type=jnp.float32)


def sum_rows(values):
    return jnp.sum(values, axis=0, keepdims=True)


def sigmoid_of(values):
    return 0.5 * jnp.tanh(0.5 * values) + 0.5


def silu_parts(values):
    sig = sigmoid_of(values)
    active = values * sig
    return active, sig + active * (1.0 - sig)


def expert_up(inputs, expand, expbias, shrink, shrinkbias):
    active, slope = silu_parts(times(expand, inputs) + expbias)
    active = active.astype(jnp.bfloat16)
    output = times(shrink, active) + shrinkbias
    scale = 1.0 / output.shape[0]
    centered = output - sum_rows(output) * scale
    inverse = lax.rsqrt(sum_rows(centered * centered) * scale + EPS)
    return active, slope, centered * inverse, inverse


def soft(scores, count):
    valid = iota(scores.shape, 0) < count
    scores = jnp.where(valid, scores, -1e30)
    shifted = jnp.exp(scores - jnp.max(scores, axis=0, keepdims=True))
    shifted = jnp.where(valid, shifted, 0.0)
    return shifted / sum_rows(shifted)


def soft_back(probs, rows):
    tall = jnp.concatenate(rows + [jnp.zeros_like(rows[0])] * (probs.shape[0] - len(rows)), axis=0)
    return probs * (tall - sum_rows(probs * tall))


def dense_body(
    flipped_ref,
    expand_one_ref,
    expand_one_back_ref,
    shrink_one_ref,
    shrink_one_back_ref,
    expand_two_ref,
    expand_two_back_ref,
    shrink_two_ref,
    shrink_two_back_ref,
    gate_one_ref,
    gate_one_back_ref,
    gate_two_ref,
    gate_two_back_ref,
    inner_ref,
    inner_back_ref,
    middle_ref,
    middle_back_ref,
    columns_ref,
    cot_ref,
    logits_ref,
    flipped_grad_ref,
    grads_ref,
    input_keep,
    active_one,
    out_one,
    pre_one,
    score_one,
    carried_keep,
    active_two,
    out_two,
    pre_two,
    score_two,
    tower_keep,
    tower_act_keep,
    first_keep,
    top_keep,
    tail_keep,
    gain_keep,
):
    width, events = flipped_ref.shape
    hidden = shrink_one_ref.shape[1]
    inner = inner_ref.shape[0] // 2
    narrow = middle_ref.shape[0] // 2
    tall = hidden + ONES
    span = min(SPAN, events)
    unit = jnp.ones((ONES, events), jnp.bfloat16)

    input_keep[:width, :] = flipped_ref[...]
    input_keep[width:, :] = unit
    for expert in range(6):
        active_one[expert * tall + hidden : (expert + 1) * tall, :] = unit
        active_two[expert * tall + hidden : (expert + 1) * tall, :] = unit
    for group in range(3):
        carried_keep[group * tall + hidden : (group + 1) * tall, :] = unit
    for task in range(2):
        tower_keep[task * tall + hidden : (task + 1) * tall, :] = unit
    gain_keep[...] = jnp.zeros_like(gain_keep)

    def column(index, rows=hidden, start=0):
        return columns_ref[start : start + rows, index : index + 1]

    def experts_rows(expert):
        return slice(expert * hidden, (expert + 1) * hidden)

    def span_step(step, carry):
        lanes = pl.ds(pl.multiple_of(step * span, span), span)
        inputs = flipped_ref[:, lanes]

        def up(level, inputs_of, expand_ref, shrink_ref, active_keep):
            kept = []
            for expert in range(6):
                active, slope, normed, inverse = expert_up(
                    inputs_of(expert),
                    expand_ref[experts_rows(expert), :],
                    column(level + expert),
                    shrink_ref[experts_rows(expert), :],
                    column(level + 6 + expert),
                )
                active_keep[expert * tall : expert * tall + hidden, lanes] = active
                kept.append((slope, normed, inverse, normed * column(level + 12 + expert)))
            return kept

        kept_one = up(0, lambda expert: inputs, expand_one_ref, shrink_one_ref, active_one)
        scores = times(gate_one_ref[...], inputs)
        probs_one = [soft(scores[0:8], 4), soft(scores[8:16], 4), soft(scores[16:24], 6)]
        carried = []
        for group in range(3):
            members = [2 * group, 2 * group + 1, 4, 5] if group < 2 else range(6)
            mixed = 0.0
            for place, expert in enumerate(members):
                mixed = mixed + probs_one[group][place : place + 1, :] * kept_one[expert][3]
            carried.append(mixed.astype(jnp.bfloat16))
            carried_keep[group * tall : group * tall + hidden, lanes] = carried[group]

        kept_two = up(
            18, lambda expert: carried[expert // 2], expand_two_ref, shrink_two_ref, active_two
        )
        probs_two = []
        tower_grads = []
        dq_two = []
        for task in range(2):
            probs = soft(times(gate_two_ref[task * 8 : task * 8 + 8, :], carried[task]), 4)
            probs_two.append(probs)
            members = [2 * task, 2 * task + 1, 4, 5]
            mixed = 0.0
            for place, expert in enumerate(members):
                mixed = mixed + probs[place : place + 1, :] * kept_two[expert][3]
            mixed = mixed.astype(jnp.bfloat16)
            tower_keep[task * tall : task * tall + hidden, lanes] = mixed
            first, first_slope = silu_parts(
                times(inner_ref[task * inner : (task + 1) * inner, :], mixed)
                + column(36, inner, task * inner)
            )
            first = first.astype(jnp.bfloat16)
            tower_act_keep[task * inner : (task + 1) * inner, lanes] = first
            top, top_slope = silu_parts(
                times(middle_ref[task * narrow : (task + 1) * narrow, :], first)
                + column(37, narrow, 2 * task * narrow)
            )
            weight = column(37, narrow, (2 * task + 1) * narrow)
            logits_ref[task : task + 1, lanes] = sum_rows(top * weight)
            cot = cot_ref[task : task + 1, lanes]
            top_grad = (cot * weight * top_slope).astype(jnp.bfloat16)
            top_keep[task * narrow : (task + 1) * narrow, lanes] = top_grad
            seen = cot * top
            high = seen.astype(jnp.bfloat16)
            tail_keep[2 * task * narrow : (2 * task + 1) * narrow, lanes] = high
            tail_keep[(2 * task + 1) * narrow : (2 * task + 2) * narrow, lanes] = (
                seen - high.astype(jnp.float32)
            ).astype(jnp.bfloat16)
            first_grad = (
                times(middle_back_ref[task * inner : (task + 1) * inner, :], top_grad) * first_slope
            ).astype(jnp.bfloat16)
            first_keep[task * inner : (task + 1) * inner, lanes] = first_grad
            grad = times(inner_back_ref[task * hidden : (task + 1) * hidden, :], first_grad)
            tower_grads.append(grad)
            dq_two.append([sum_rows(kept_two[expert][3] * grad) for expert in members])

        def expert_down(level, expert, kept, upstream, slant, shrink_back_ref, out_keep, pre_keep):
            slope, normed, inverse, _ = kept
            gained = upstream * normed
            part = gained[:, :128]
            for start in range(128, span, 128):
                part = part + gained[:, start : start + 128]
            gain_rows = slice((level + expert) * hidden, (level + expert + 1) * hidden)
            gain_keep[gain_rows, :] += part
            scaled = upstream * column(3 * level + 12 + expert)
            scale = 1.0 / hidden
            out_low = (
                inverse * (scaled - sum_rows(scaled) * scale - normed * (slant * scale))
            ).astype(jnp.bfloat16)
            out_keep[experts_rows(expert), lanes] = out_low
            pre_low = (times(shrink_back_ref[experts_rows(expert), :], out_low) * slope).astype(
                jnp.bfloat16
            )
            pre_keep[experts_rows(expert), lanes] = pre_low
            return pre_low

        pre_lows = []
        for expert in range(6):
            if expert < 4:
                task, place = expert // 2, expert % 2
                prob = probs_two[task][place : place + 1, :]
                upstream = prob * tower_grads[task]
                slant = prob * dq_two[task][place]
            else:
                place = expert - 2
                prob = [probs_two[task][place : place + 1, :] for task in range(2)]
                upstream = prob[0] * tower_grads[0] + prob[1] * tower_grads[1]
                slant = prob[0] * dq_two[0][place] + prob[1] * dq_two[1][place]
            pre_lows.append(
                expert_down(
                    6, expert, kept_two[expert], upstream, slant, shrink_two_back_ref, out_two, pre_two
                )
            )
        carried_grads = []
        for group in range(3):
            grad = 0.0
            for expert in (2 * group, 2 * group + 1):
                grad = grad + times(expand_two_back_ref[experts_rows(expert), :], pre_lows[expert])
            if group < 2:
                score = soft_back(probs_two[group], dq_two[group])
                score = jnp.concatenate([score, jnp.zeros_like(score)], axis=0).astype(jnp.bfloat16)
                score_two[group * 16 : group * 16 + 16, lanes] = score
                grad = grad + times(gate_two_back_ref[experts_rows(group), :], score)
            carried_grads.append(grad)

        dq_one = []
        for group in range(3):
            members = [2 * group, 2 * group + 1, 4, 5] if group < 2 else range(6)
            dq_one.append([sum_rows(kept_one[expert][3] * carried_grads[group]) for expert in members])
        pre_lows = []
        for expert in range(6):
            prob = probs_one[2][expert : expert + 1, :]
            upstream = prob * carried_grads[2]
            slant = prob * dq_one[2][expert]
            for task in range(2):
                if expert // 2 in (task, 2):
                    place = expert % 2 if expert < 4 else expert - 2
                    prob = probs_one[task][place : place + 1, :]
                    upstream = upstream + prob * carried_grads[task]
                    slant = slant + prob * dq_one[task][place]
            pre_lows.append(
                expert_down(
                    0, expert, kept_one[expert], upstream, slant, shrink_one_back_ref, out_one, pre_one
                )
            )
        scores_low = [soft_back(probs_one[group], dq_one[group]) for group in range(3)]
        score = jnp.concatenate(scores_low + [jnp.zeros_like(scores_low[0])], axis=0).astype(
            jnp.bfloat16
        )
        score_one[:, lanes] = score
        grad = times(gate_one_back_ref[...], score)
        for expert in range(6):
            grad = grad + times(
                expand_one_back_ref[expert * width : (expert + 1) * width, :], pre_lows[expert]
            )
        flipped_grad_ref[:, lanes] = grad
        return carry

    lax.fori_loop(0, events // span, span_step, 0)

    def put(row, value):
        grads_ref[row : row + value.shape[0], :] = value.astype(jnp.bfloat16)

    rows = 0
    biases = []
    for expert in range(6):
        both = over_events(input_keep[...], pre_one[experts_rows(expert), :])
        put(rows + expert * width, both[:width])
        biases.append(both[width : width + 1])
    rows += 6 * width
    for expert in range(6):
        both = over_events(active_one[expert * tall : (expert + 1) * tall, :], out_one[experts_rows(expert), :])
        put(rows + expert * hidden, both[:hidden])
        biases.append(both[hidden : hidden + 1])
    rows += 6 * hidden
    for expert in range(6):
        group = expert // 2
        both = over_events(carried_keep[group * tall : (group + 1) * tall, :], pre_two[experts_rows(expert), :])
        put(rows + expert * hidden, both[:hidden])
        biases.append(both[hidden : hidden + 1])
    rows += 6 * hidden
    for expert in range(6):
        both = over_events(active_two[expert * tall : (expert + 1) * tall, :], out_two[experts_rows(expert), :])
        put(rows + expert * hidden, both[:hidden])
        biases.append(both[hidden : hidden + 1])
    rows += 6 * hidden
    tower = []
    for task in range(2):
        tower.append(
            over_events(tower_keep[task * tall : (task + 1) * tall, :], first_keep[task * inner : (task + 1) * inner, :])
        )
    tower = jnp.concatenate(tower, axis=1)
    put(rows, tower[:hidden])
    biases.append(tower[hidden : hidden + 1])
    rows += hidden
    put(
        rows,
        jnp.concatenate(
            [
                over_events(
                    top_keep[task * narrow : (task + 1) * narrow, :],
                    tower_act_keep[task * inner : (task + 1) * inner, :],
                )
                for task in range(2)
            ],
            axis=1,
        ),
    )
    rows += narrow
    gates = over_events(score_one[...], flipped_ref[...])
    for start in range(0, width, hidden):
        put(rows, gates[:, start : start + hidden])
        rows += gates.shape[0]
    for task in range(2):
        put(
            rows,
            over_events(
                score_two[task * 16 : task * 16 + 16, :],
                carried_keep[task * tall : task * tall + hidden, :],
            ),
        )
        rows += 16
    tops = over_events(unit, top_keep[...])[:1]
    seen = over_events(unit, tail_keep[...])[:1]
    pieces = []
    for task in range(2):
        pieces.append(tops[:, task * narrow : (task + 1) * narrow])
        pieces.append(
            seen[:, 2 * task * narrow : (2 * task + 1) * narrow]
            + seen[:, (2 * task + 1) * narrow : (2 * task + 2) * narrow]
        )
    biases.append(jnp.concatenate(pieces, axis=1))
    gains = gain_keep[...]
    high = gains.astype(jnp.bfloat16)
    low = (gains - high.astype(jnp.float32)).astype(jnp.bfloat16)
    gains = (over_events(unit[:, :128], high) + over_events(unit[:, :128], low))[:1]
    for expert in range(12):
        biases.append(gains[:, experts_rows(expert)])
    biases = jnp.concatenate(biases, axis=0)
    extra = grads_ref.shape[0] - rows - biases.shape[0]
    put(rows, jnp.concatenate([biases, jnp.zeros((extra, hidden), jnp.float32)], axis=0))


def dense(flipped, weights, columns, cot, grad_rows):
    width, events = flipped.shape
    hidden = columns.shape[0]
    inner, narrow = 128, 64
    tall = hidden + ONES
    return pl.pallas_call(
        dense_body,
        out_shape=(
            jax.ShapeDtypeStruct((2, events), jnp.float32),
            jax.ShapeDtypeStruct((width, events), jnp.float32),
            jax.ShapeDtypeStruct((grad_rows, hidden), jnp.bfloat16),
        ),
        scratch_shapes=[
            pltpu.VMEM((rows, events), jnp.bfloat16)
            for rows in (
                width + ONES,
                6 * tall,
                6 * hidden,
                6 * hidden,
                32,
                3 * tall,
                6 * tall,
                6 * hidden,
                6 * hidden,
                32,
                2 * tall,
                2 * inner,
                2 * inner,
                2 * narrow,
                4 * narrow,
            )
        ]
        + [pltpu.VMEM((12 * hidden, 128), jnp.float32)],
        compiler_params=pltpu.CompilerParams(vmem_limit_bytes=VMEM_LIMIT),
        cost_estimate=pl.CostEstimate(
            flops=6 * events * hidden * (6 * (width + 3 * hidden) + 2 * inner),
            bytes_accessed=24 * 1024 * 1024,
            transcendentals=12 * events * hidden,
        ),
    )(flipped, *weights, columns, cot)


def pack_rows(parts, row_tile):
    width = 256
    wide = [part for part in parts if part.ndim == 2 and part.shape[1] == width]
    thin = [part.reshape(-1) for part in parts if part.ndim != 2 or part.shape[1] != width]
    rest = jnp.concatenate(thin)
    rest = jnp.pad(rest, (0, -rest.size % (row_tile * width))).reshape(-1, width)
    return jnp.concatenate(wide + [rest], axis=0)


def unpack_rows(whole, parts):
    devices, rows, width = whole.shape
    wide_rows = sum(part.shape[0] for part in parts if part.ndim == 2 and part.shape[1] == width)
    rest = whole[:, wide_rows:].reshape(devices, -1)
    out = []
    row = 0
    place = 0
    for part in parts:
        if part.ndim == 2 and part.shape[1] == width:
            piece = whole[:, row : row + part.shape[0]]
            row += part.shape[0]
        else:
            piece = rest[:, place : place + part.size]
            place += part.size
        out.append(piece.reshape((devices * part.shape[0],) + part.shape[1:]))
    return out


def split_grads(total, width, hidden):
    place = 0

    def take(rows):
        nonlocal place
        place += rows
        return total[place - rows : place].astype(jnp.float32)

    low_expand = take(6 * width)
    low_shrink = take(6 * hidden)
    up_expand = take(6 * hidden)
    up_shrink = take(6 * hidden)
    inner = take(hidden).reshape(hidden, 2, -1).transpose(1, 0, 2).reshape(2 * hidden, -1)
    middle = take(64).reshape(64, 2, -1).transpose(1, 2, 0).reshape(-1, 64)
    gates = take(32 * (width // hidden)).reshape(-1, 32, hidden).transpose(0, 2, 1).reshape(width, 32)
    taskgate = jnp.concatenate([gates[:, 0:4], gates[:, 8:12]], axis=0)
    sharegate = gates[:, 16:22]
    upper = take(32).reshape(2, 16, hidden)[:, :4].transpose(0, 2, 1).reshape(2 * hidden, 4)
    rows = take(48)
    low_inbias, low_outbias, up_inbias, up_outbias = (
        rows[6 * index : 6 * index + 6].reshape(-1) for index in range(4)
    )
    low_gain, up_gain = (rows[26 + 6 * index : 32 + 6 * index].reshape(-1) for index in range(2))
    return (
        low_expand,
        low_inbias,
        low_shrink,
        low_outbias,
        low_gain,
        taskgate,
        sharegate,
        up_expand,
        up_inbias,
        up_shrink,
        up_outbias,
        up_gain,
        upper,
        inner,
        rows[24],
        middle,
        rows[25],
    )


def on_device(
    owner_ids,
    row_ids,
    embed_table,
    expandone,
    expbiasone,
    reduceone,
    redbiasone,
    normgainone,
    taskgateone,
    sharegateone,
    expandtwo,
    expbiastwo,
    reducetwo,
    redbiastwo,
    normgaintwo,
    taskgatetwo,
    towerinner,
    towerbias,
    towermiddle,
    towertail,
    logit_cot,
):
    devices = lax.axis_size(("dp", "fsdp"))
    events, fields = owner_ids.shape
    emb_width = embed_table.shape[1]
    capacity = 2 * events * fields // devices
    owner_rows = owner_ids.T
    request, rank = assign_slots(owner_rows, row_ids.T, devices, capacity)
    asked_rows = lax.all_to_all(request, ("dp", "fsdp"), split_axis=0, concat_axis=0, tiled=True)
    table_wide = (
        embed_table.reshape(ROW_BLOCKS, -1, emb_width).transpose(0, 2, 1).reshape(ROW_BLOCKS * emb_width, -1)
    )
    found = find_rows(asked_rows, table_wide)
    returned = lax.all_to_all(found, ("dp", "fsdp"), split_axis=0, concat_axis=0, tiled=True)
    flipped = place_rows(returned, rank, owner_rows)
    packed = pack_rows(
        (
            expandone,
            reduceone,
            expandtwo,
            reducetwo,
            expbiasone,
            redbiasone,
            normgainone,
            expbiastwo,
            redbiastwo,
            normgaintwo,
            taskgateone,
            sharegateone,
            taskgatetwo,
            towerinner,
            towerbias,
            towermiddle,
            towertail,
        ),
        16,
    )
    whole = lax.all_gather(packed, "fsdp", axis=0, tiled=False)
    whole = lax.all_gather(whole, "dp", axis=0, tiled=False)
    whole = whole.reshape((devices,) + packed.shape)
    (
        one_expand,
        one_shrink,
        two_expand,
        two_shrink,
        one_inbias,
        one_outbias,
        one_gain,
        two_inbias,
        two_outbias,
        two_gain,
        one_taskgate,
        one_sharegate,
        two_taskgate,
        inner_full,
        tbias_full,
        middle_full,
        tail_full,
    ) = unpack_rows(
        whole,
        (
            expandone,
            reduceone,
            expandtwo,
            reducetwo,
            expbiasone,
            redbiasone,
            normgainone,
            expbiastwo,
            redbiastwo,
            normgaintwo,
            taskgateone,
            sharegateone,
            taskgatetwo,
            towerinner,
            towerbias,
            towermiddle,
            towertail,
        ),
    )
    hidden = expandone.shape[1]
    width = fields * emb_width
    gates = jnp.concatenate(
        [
            jnp.pad(one_taskgate.reshape(2, width, 4), ((0, 0), (0, 0), (0, 4)))[0],
            jnp.pad(one_taskgate.reshape(2, width, 4), ((0, 0), (0, 0), (0, 4)))[1],
            jnp.pad(one_sharegate, ((0, 0), (0, 10))),
        ],
        axis=1,
    )
    upper = jnp.pad(two_taskgate.reshape(2, hidden, 4), ((0, 0), (0, 0), (0, 12)))

    def swap(weight, blocks):
        return weight.reshape(blocks, -1, weight.shape[1]).transpose(0, 2, 1).reshape(
            blocks * weight.shape[1], -1
        )

    weights = (
        swap(one_expand, 6),
        one_expand,
        swap(one_shrink, 6),
        one_shrink,
        swap(two_expand, 6),
        two_expand,
        swap(two_shrink, 6),
        two_shrink,
        gates[:, :24].T,
        gates,
        upper[:, :, :8].transpose(0, 2, 1).reshape(16, hidden),
        upper.reshape(2 * hidden, 16),
        swap(inner_full, 2),
        inner_full,
        swap(middle_full, 2),
        middle_full,
    )
    columns = (
        jnp.concatenate(
            [
                one_inbias,
                one_outbias,
                one_gain,
                two_inbias,
                two_outbias,
                two_gain,
                tbias_full,
                tail_full,
            ]
        )
        .reshape(-1, hidden)
        .astype(jnp.float32)
        .T
    )
    chunk = 16 * devices
    grad_rows = -(-(12 * (width + 3 * hidden) // 2 + 2 * hidden) // chunk) * chunk
    logits, flipped_grad, grads = dense(flipped, weights, columns, logit_cot, grad_rows)
    x_grad = flipped_grad.T
    outgoing = send_rows(flipped_grad, rank, owner_rows, capacity)
    incoming = lax.all_to_all(
        outgoing, ("dp", "fsdp"), split_axis=0, concat_axis=0, tiled=True
    )
    table_grad = add_rows(incoming, asked_rows, embed_table.shape[0])
    part = lax.psum_scatter(grads, "dp", scatter_dimension=0, tiled=True)
    part = lax.psum_scatter(part, "fsdp", scatter_dimension=0, tiled=True)
    total = lax.all_gather(part, "fsdp", axis=0, tiled=True)
    total = lax.all_gather(total, "dp", axis=0, tiled=True)
    return (logits, x_grad, table_grad, *split_grads(total, width, hidden))


def solution(mesh):
    return jax.shard_map(
        on_device,
        mesh=mesh,
        in_specs=(
            P(("dp", "fsdp"), None),
            P(("dp", "fsdp"), None),
            P(("dp", "fsdp"), None),
            P(("dp", "fsdp"), None),
            P(("dp", "fsdp")),
            P(("dp", "fsdp"), None),
            P(("dp", "fsdp")),
            P(("dp", "fsdp")),
            P(("dp", "fsdp"), None),
            P(("dp", "fsdp"), None),
            P(("dp", "fsdp"), None),
            P(("dp", "fsdp")),
            P(("dp", "fsdp"), None),
            P(("dp", "fsdp")),
            P(("dp", "fsdp")),
            P(("dp", "fsdp"), None),
            P(("dp", "fsdp"), None),
            P(("dp", "fsdp")),
            P(("dp", "fsdp"), None),
            P(("dp", "fsdp")),
            P(None, ("dp", "fsdp")),
        ),
        out_specs=(
            P(None, ("dp", "fsdp")),
            P(("dp", "fsdp"), None),
            P(("dp", "fsdp"), None),
            P(),
            P(),
            P(),
            P(),
            P(),
            P(),
            P(),
            P(),
            P(),
            P(),
            P(),
            P(),
            P(),
            P(),
            P(),
            P(),
            P(),
        ),
        check_vma=False,
    )
```

profile of v0, /device:TPU:0, one launch (start us, length us, event | category | flops | bytes accessed | tf_op | source)
XLA Modules:
  0.0 310.9 jit_solution(10097324585768111122)
XLA Ops:
  7.2 0.8 reshape.208
  8.0 0.8 copy.101
  8.9 0.8 copy.102
  9.7 0.8 copy.100
  10.6 6.1 %concatenate.15 = bf16[3152]{0:T(1024)(128)(2,1)S(1)} concatenate(bf16[48]{0:T(256)(128)(2,1)} %param.25, bf16[48]{0:T(256)(128)(2,1)} %param.27, bf16[48]{0:T(256)(128)(2,1)} %param.28, bf16[48]{0:T(256)(128)(2,1)} %param.32, bf16[48]{0:T(256)(128)(2,1)} %param.34, bf16[48]{0:T(256)(128)(2,1)} %param.35, bf16[128]{0:T(256)(128)(2,1)S(1)} %reshape.204, ...), dimensions={0} | concatenate | bytes 12608 | tf_op jit(solution)/shard_map/concatenate | solution.py:629
  16.8 0.8 constant_dynamic-update-slice_fusion.4
  17.6 0.7 constant_dynamic-update-slice_fusion.3
  18.3 0.7 constant_dynamic-update-slice_fusion.2
  19.1 0.7 constant_dynamic-update-slice_fusion.1
  19.8 18.0 %all-gather = bf16[1024,256]{1,0:T(8,128)(2,1)} all-gather(bf16[256,256]{1,0:T(8,128)(2,1)S(1)} %constant_dynamic-update-slice_fusion), channel_id=2, replica_groups=mesh['dp'=8,'fsdp'=4] {'fsdp'}, dimensions={0}, use_global_device_ids=true | all-gather | bytes 655360 | tf_op jit(solution)/shard_map/all_gather | solution.py:754
  37.8 2.4 shard_map.356
  40.2 1.4 copy.98
  41.6 6.5 %all-to-all-start = ((s32[32,1,256]{2,1,0:T(1,128)}), s32[32,1,256]{2,1,0:T(1,128)S(1)}, u32[]{:S(2)}, u32[]{:S(2)}) async-start(s32[32,1,256]{2,1,0:T(1,128)} %copy.98), calls=%async_computation | async-start | bytes 65536 | tf_op jit(solution)/shard_map/all_to_all | solution.py:725
  48.1 1.9 copy.125
  50.0 5.4 %all-to-all-done = s32[32,1,256]{2,1,0:T(1,128)S(1)} async-done(((s32[32,1,256]{2,1,0:T(1,128)}), s32[32,1,256]{2,1,0:T(1,128)S(1)}, u32[]{:S(2)}, u32[]{:S(2)}) %all-to-all-start) | async-done | bytes 32800 | tf_op jit(solution)/shard_map/all_to_all | solution.py:725
  56.0 9.3 %shard_map.357 = bf16[32,64,256]{2,1,0:T(8,128)(2,1)} custom-call(s32[32,256]{1,0:T(8,128)} %bitcast.111, bf16[512,512]{1,0:T(8,128)(2,1)} %bitcast.99), custom_call_target="tpu_custom_call" | custom-call | flops 4294967296 | bytes 1572864 | tf_op jit(solution)/shard_map/pallas_call | solution.py:98
  65.3 2.7 all-to-all-start.1
  68.0 25.0 %all-to-all-done.1.found_ref = bf16[32,64,256]{2,1,0:T(8,128)(2,1)S(1)} async-done(((bf16[32,64,256]{2,1,0:T(8,128)(2,1)}), bf16[32,64,256]{2,1,0:T(8,128)(2,1)S(1)}, u32[]{:S(2)}, u32[]{:S(2)}) %all-to-all-start.1) | async-done | bytes 1048608 | tf_op jit(solution)/shard_map/all_to_all | solution.py:730
  93.0 1.0 copy-done.6
  94.0 6.5 %shard_map.358.flipped_ref = bf16[512,512]{1,0:T(8,128)(2,1)} custom-call(bf16[32,64,256]{2,1,0:T(8,128)(2,1)} %copy-done.6, s32[32,512]{1,0:T(8,128)} %get-tuple-element.26.rank_ref, s32[8,512]{1,0:T(8,128)} %bitcast.116), custom_call_target="tpu_custom_call" | custom-call | flops 536870912 | bytes 1572864 | tf_op jit(solution)/shard_map/pallas_call | solution.py:135
  100.4 1.0 slice.177
  102.0 0.7 reshape.226.middle_back_ref
  108.0 0.8 copy.110
  109.7 0.8 copy.108
  111.9 1.8 fusion.4
  113.7 1.4 copy.104
  115.1 1.2 copy.105
  116.3 1.2 copy.106
  117.5 1.5 slice.173
  119.1 1.6 copy.103
  120.7 25.1 %shard_map.359 = (f32[2,512]{1,0:T(2,128)}, f32[512,512]{1,0:T(8,128)}, bf16[8192,256]{1,0:T(8,128)(2,1)}) custom-call(bf16[512,512]{1,0:T(8,128)(2,1)} %shard_map.358.flipped_ref, bf16[1536,512]{1,0:T(8,128)(2,1)} %bitcast.85, bf16[3072,256]{1,0:T(8,128)(2,1)} %bitcast.76, bf16[1536,256]{1,0:T(8,128)(2,1)} %bitcast.95, bf16[1536,256]{1,0:T(8,128)(2,1)} %bitcast.83, ...), custom_call_target="tpu_custom_call" | custom-call | flops 6241124352 | bytes 25165824 | tf_op jit(solution)/shard_map/pallas_call | solution.py:588
  145.9 51.2 %reduce-scatter.3.cloned.1.call-done = bf16[1024,256]{1,0:T(8,128)(2,1)} async-done(((bf16[8192,256]{1,0:T(8,128)(2,1)}), bf16[1024,256]{1,0:T(8,128)(2,1)}) %reduce-scatter.3.cloned.1.call-update) | async-done | bytes 524304 | tf_op jit(solution)/shard_map/reduce_scatter | solution.py:858
  197.2 24.0 %reduce-scatter.5.cloned.1.call-done = bf16[256,256]{1,0:T(8,128)(2,1)} async-done(((bf16[1024,256]{1,0:T(8,128)(2,1)}), bf16[256,256]{1,0:T(8,128)(2,1)}) %reduce-scatter.5.cloned.1.call-update) | async-done | bytes 131088 | tf_op jit(solution)/shard_map/reduce_scatter | solution.py:859
  221.2 16.8 %all_gather.22 = bf16[1024,256]{1,0:T(8,128)(2,1)} all-gather(bf16[256,256]{1,0:T(8,128)(2,1)} %reduce-scatter.5.cloned.1.call-done), channel_id=1, replica_groups=mesh['dp'=8,'fsdp'=4] {'fsdp'}, dimensions={0}, use_global_device_ids=true | all-gather | bytes 655360 | tf_op jit(solution)/shard_map/all_gather | solution.py:860
  238.0 7.8 %shard_map.360 = bf16[32,64,256]{2,1,0:T(8,128)(2,1)} custom-call(f32[512,512]{1,0:T(8,128)} %get-tuple-element.28.grad_ref, s32[32,512]{1,0:T(8,128)} %get-tuple-element.26.rank_ref, s32[8,512]{1,0:T(8,128)} %bitcast.117), custom_call_target="tpu_custom_call" | custom-call | flops 536870912 | bytes 2097152 | tf_op jit(solution)/shard_map/pallas_call | solution.py:171
  245.8 4.1 %all-to-all-start.2 = ((bf16[32,64,256]{2,1,0:T(8,128)(2,1)}), bf16[32,64,256]{2,1,0:T(8,128)(2,1)S(1)}, u32[]{:S(2)}, u32[]{:S(2)}) async-start(bf16[32,64,256]{2,1,0:T(8,128)(2,1)} %shard_map.360), calls=%async_computation.2 | async-start | bytes 2097152 | tf_op jit(solution)/shard_map/all_to_all | solution.py:854
  250.0 1.3 copy.115
  251.3 23.5 %all-to-all-done.2.came_ref = bf16[32,64,256]{2,1,0:T(8,128)(2,1)S(1)} async-done(((bf16[32,64,256]{2,1,0:T(8,128)(2,1)}), bf16[32,64,256]{2,1,0:T(8,128)(2,1)S(1)}, u32[]{:S(2)}, u32[]{:S(2)}) %all-to-all-start.2) | async-done | bytes 1048608 | tf_op jit(solution)/shard_map/all_to_all | solution.py:854
  274.8 1.0 copy-done.7
  275.8 9.1 %shard_map.361 = f32[4096,64]{1,0:T(8,128)} custom-call(bf16[32,64,256]{2,1,0:T(8,128)(2,1)} %copy-done.7, s32[32,256]{1,0:T(8,128)} %bitcast.112), custom_call_target="tpu_custom_call" | custom-call | flops 4294967296 | bytes 2097152 | tf_op jit(solution)/shard_map/pallas_call | solution.py:219
  284.9 3.1 %copy.116 = f32[4096,64]{0,1:T(8,128)} copy(f32[4096,64]{1,0:T(8,128)} %shard_map.361) | data formatting | bytes 2097152
  288.0 0.7 slice_convert_fusion.6
  289.3 0.8 slice_convert_fusion.5
  290.8 0.7 slice.207
  296.3 0.9 slice_convert_fusion.4
  297.4 0.7 copy.114
  298.8 3.3 %slice_convert_fusion = f32[3072,256]{1,0:T(8,128)} fusion(bf16[8192,256]{1,0:T(8,128)(2,1)} %all-gather.5.cloned.1.call-done), kind=kLoop, calls=%fused_computation | loop fusion | flops 786432 | bytes 4718592 | tf_op jit(solution)/shard_map/convert_element_type | solution.py:658
  302.1 2.3 slice_convert_fusion.1
  (90 shorter events, 16.2 us)
Async XLA Ops:
  7.2 93.3 %all-gather.7.cloned.1.call-start = ((), (), s32[]{:S(2)}) async-start(), calls=%async_computation.8 | async-start | bytes 4718592 | tf_op jit(solution)/shard_map/all_gather | solution.py:755
  41.6 13.8 %all-to-all-start = ((s32[32,1,256]{2,1,0:T(1,128)}), s32[32,1,256]{2,1,0:T(1,128)S(1)}, u32[]{:S(2)}, u32[]{:S(2)}) async-start(s32[32,1,256]{2,1,0:T(1,128)} %copy.98), calls=%async_computation | async-start | bytes 65536 | tf_op jit(solution)/shard_map/all_to_all | solution.py:725
  65.3 27.7 %all-to-all-start.1 = ((bf16[32,64,256]{2,1,0:T(8,128)(2,1)}), bf16[32,64,256]{2,1,0:T(8,128)(2,1)S(1)}, u32[]{:S(2)}, u32[]{:S(2)}) async-start(bf16[32,64,256]{2,1,0:T(8,128)(2,1)} %shard_map.357), calls=%async_computation.1 | async-start | bytes 2097152 | tf_op jit(solution)/shard_map/all_to_all | solution.py:730
  68.0 129.2 %reduce-scatter.3.cloned.1.call-start = ((), (), s32[]{:S(2)}) async-start(), calls=%async_computation.5 | async-start | bytes 4718592 | tf_op jit(solution)/shard_map/reduce_scatter | solution.py:858
  93.0 1.0 copy-start.6
  111.2 3.9 %copy-start.8 = (bf16[512,32]{1,0:T(8,128)(2,1)}, bf16[512,32]{1,0:T(8,128)(2,1)S(1)}, u32[]{:S(2)}) copy-start(bf16[512,32]{1,0:T(8,128)(2,1)S(1)} %fusion.3.gate_one_back_ref) | copy-start | bytes 98308
  113.7 2.6 copy-start.5
  113.7 5.3 %copy-start.3 = (bf16[32,48,256]{2,1,0:T(8,128)(2,1)}, bf16[32,48,256]{2,1,0:T(8,128)(2,1)S(1)}, u32[]{:S(2)}) copy-start(bf16[32,48,256]{2,1,0:T(8,128)(2,1)S(1)} %get-tuple-element.115) | copy-start | bytes 2359300
  113.7 5.3 %copy-start.4 = (bf16[32,48,256]{2,1,0:T(8,128)(2,1)}, bf16[32,48,256]{2,1,0:T(8,128)(2,1)S(1)}, u32[]{:S(2)}) copy-start(bf16[32,48,256]{2,1,0:T(8,128)(2,1)S(1)} %get-tuple-element.116) | copy-start | bytes 2359300
  119.1 1.7 copy-start
  145.9 104.1 %copy-start.1 = (f32[512,512]{1,0:T(8,128)S(1)}, f32[512,512]{1,0:T(8,128)}, u32[]{:S(2)}) copy-start(f32[512,512]{1,0:T(8,128)} %get-tuple-element.28.grad_ref) | copy-start | bytes 3145732
  145.9 75.3 %reduce-scatter.5.cloned.1.call-start = ((), (), s32[]{:S(2)}) async-start(), calls=%async_computation.6 | async-start | bytes 655360 | tf_op jit(solution)/shard_map/reduce_scatter | solution.py:859
  197.2 90.8 %all-gather.5.cloned.1.call-start = ((), (), s32[]{:S(2)}) async-start(), calls=%async_computation.7 | async-start | bytes 4718592 | tf_op jit(solution)/shard_map/all_gather | solution.py:861
  245.8 29.0 %all-to-all-start.2 = ((bf16[32,64,256]{2,1,0:T(8,128)(2,1)}), bf16[32,64,256]{2,1,0:T(8,128)(2,1)S(1)}, u32[]{:S(2)}, u32[]{:S(2)}) async-start(bf16[32,64,256]{2,1,0:T(8,128)(2,1)} %shard_map.360), calls=%async_computation.2 | async-start | bytes 2097152 | tf_op jit(solution)/shard_map/all_to_all | solution.py:854
  274.8 1.0 copy-start.7
  297.4 4.7 %copy-start.2 = (bf16[8192,256]{1,0:T(8,128)(2,1)S(1)}, bf16[8192,256]{1,0:T(8,128)(2,1)}, u32[]{:S(2)}) copy-start(bf16[8192,256]{1,0:T(8,128)(2,1)} %all-gather.5.cloned.1.call-done) | copy-start | bytes 12582916
Sparse Core Ops, SparseCore 0:
  37.9 47.3 all-gather.6
  146.0 51.1 reduce-scatter.2
  199.5 21.6 reduce-scatter.4
  238.1 43.1 all-gather.4
where the time goes:
time: 314 us; the launch traced here: 311 us
  waiting for transfers between devices  129 us (41%)
  Pallas kernels  60.2 us (19%)
  local copies, waits for them, and re-layouts  49.8 us (16%)
  blocking collectives  34.7 us (11%)
  between operations  14.1 us (4%)
  starting transfers between devices  13.4 us (4%)
  other arithmetic  9.46 us (3%)
    reduce_scatter x1, waiting for transfers between devices, on_device(): part = lax.psum_scatter(grads, 'dp', scatter_dimension=0, tiled=True)  51.2 us
    pallas_call x1, Pallas kernels, dense(): pl.pallas_call(dense_body, out_shape=(jax.ShapeDtypeStruct((2, events), j...  25.1 us
    all_to_all x1, waiting for transfers between devices, on_device(): lax.all_to_all(found, ('dp', 'fsdp'), split_axis=0, concat_axis=0, tiled=...  25 us
    reduce_scatter x1, waiting for transfers between devices, on_device(): part = lax.psum_scatter(part, 'fsdp', scatter_dimension=0, tiled=True)  24 us
    all_to_all x1, waiting for transfers between devices, on_device(): lax.all_to_all(outgoing, ('dp', 'fsdp'), split_axis=0, concat_axis=0, til...  23.5 us
    all_gather x1, blocking collectives, on_device(): whole = lax.all_gather(packed, 'fsdp', axis=0, tiled=False)  18 us
    all_gather x1, blocking collectives, on_device(): total = lax.all_gather(part, 'fsdp', axis=0, tiled=True)  16.8 us
    unnamed x37, local copies, waits for them, and re-layouts  14.9 us
  transfers between devices with their start and end apart: 7, of which 5 were waited for; matrix products, arithmetic and copies ran while one was open for 3% of the time, Pallas kernels for 11%

commit v1 on v0

--- a/solution.py
+++ b/solution.py
@@ -1,3 +1,5 @@
+import functools
+
 import jax
 import jax.numpy as jnp
 from jax import lax
@@ -30,7 +32,7 @@
 
 def slot_body(owner_ref, row_ref, request_ref, rank_ref):
     fields, events = owner_ref.shape
-    devices, capacity = request_ref.shape
+    devices, _, capacity = request_ref.shape
     place = iota((devices, events), 0)
     asked = jnp.zeros((devices, events), jnp.float32)
     for field in range(fields):
@@ -54,7 +56,9 @@
             (((1,), (1,)), ((), ())),
             preferred_element_type=jnp.float32,
         )
-    request_ref[...] = (total[:devices] * 64.0 + total[devices:]).astype(jnp.int32)
+    request = (total[:devices] * 64.0 + total[devices:]).astype(jnp.int32)
+    for owner in range(devices):
+        request_ref[owner] = request[owner : owner + 1]
 
 
 def assign_slots(owner_rows, row_rows, devices, capacity):
@@ -62,7 +66,7 @@
     return local_kernel(
         slot_body,
         (
-            jax.ShapeDtypeStruct((devices, capacity), jnp.int32),
+            jax.ShapeDtypeStruct((devices, 1, capacity), jnp.int32),
             jax.ShapeDtypeStruct((devices, events), jnp.int32),
         ),
         2 * devices * events * (events + 2 * fields * capacity),
@@ -70,17 +74,21 @@
     )(owner_rows, row_rows)
 
 
-def find_body(request_ref, table_ref, found_ref):
-    devices, capacity = request_ref.shape
-    depth, span = table_ref.shape
-    width = depth // ROW_BLOCKS
+def find_body(request_ref, table_ref, found_ref, wide_ref):
+    devices, _, capacity = request_ref.shape
+    width = table_ref.shape[0]
+    span = wide_ref.shape[1]
     places = iota((span, capacity), 0)
+    for index in range(ROW_BLOCKS):
+        wide_ref[index * width : (index + 1) * width, :] = table_ref[
+            :, index * span : (index + 1) * span
+        ]
 
     def step(source, carry):
-        rows = request_ref[pl.ds(source, 1), :]
+        rows = request_ref[source]
         block = rows // span
         hits = one_hot(rows - block * span == places)
-        rows_all = jnp.dot(table_ref[...], hits, preferred_element_type=jnp.float32)
+        rows_all = jnp.dot(wide_ref[...], hits, preferred_element_type=jnp.float32)
         picked = jnp.zeros((width, capacity), jnp.float32)
         for index in range(ROW_BLOCKS):
             picked = jnp.where(
@@ -92,15 +100,16 @@
     lax.fori_loop(0, devices, step, 0, unroll=2)
 
 
-def find_rows(request, table_wide):
-    devices, capacity = request.shape
-    depth, span = table_wide.shape
+def find_rows(request, table):
+    devices, _, capacity = request.shape
+    width, rows = table.shape
     return local_kernel(
         find_body,
-        jax.ShapeDtypeStruct((devices, depth // ROW_BLOCKS, capacity), jnp.bfloat16),
-        2 * devices * capacity * depth * span,
-        2 * (depth * span + devices * capacity * depth // ROW_BLOCKS),
-    )(request, table_wide)
+        jax.ShapeDtypeStruct((devices, width, capacity), jnp.bfloat16),
+        2 * devices * capacity * rows * width,
+        2 * (rows * width + devices * capacity * width),
+        [pltpu.VMEM((ROW_BLOCKS * width, rows // ROW_BLOCKS), jnp.bfloat16)],
+    )(request, table)
 
 
 def place_body(found_ref, rank_ref, owner_ref, flipped_ref, total_ref):
@@ -179,7 +188,7 @@
 
 def add_body(came_ref, request_ref, out_ref, total_ref):
     devices, width, capacity = came_ref.shape
-    span = total_ref.shape[0]
+    span = total_ref.shape[1]
     group = 4
     places = iota((span, capacity), 0)
     total_ref[...] = jnp.zeros_like(total_ref)
@@ -189,18 +198,18 @@
         spread = []
         for index in range(group):
             source = start * group + index
-            rows = request_ref[pl.ds(source, 1), :]
+            rows = request_ref[source]
             block = rows // span
             hits.append(one_hot(rows - block * span == places))
             came = came_ref[source].astype(jnp.float32)
             spread.append(
                 jnp.concatenate(
-                    [jnp.where(block == place, came, 0.0) for place in range(ROW_BLOCKS)], axis=0
+                    [jnp.where(block == part, came, 0.0) for part in range(ROW_BLOCKS)], axis=0
                 ).astype(jnp.bfloat16)
             )
         total_ref[...] += lax.dot_general(
+            jnp.concatenate(spread, axis=1),
             jnp.concatenate(hits, axis=1),
-            jnp.concatenate(spread, axis=1),
             (((1,), (1,)), ((), ())),
             preferred_element_type=jnp.float32,
         )
@@ -208,8 +217,8 @@
 
     lax.fori_loop(0, devices // group, step, 0)
     for index in range(ROW_BLOCKS):
-        out_ref[index * span : (index + 1) * span, :] = total_ref[
-            :, index * width : (index + 1) * width
+        out_ref[:, index * span : (index + 1) * span] = total_ref[
+            index * width : (index + 1) * width, :
         ]
 
 
@@ -218,11 +227,133 @@
     span = rows // ROW_BLOCKS
     return local_kernel(
         add_body,
-        jax.ShapeDtypeStruct((rows, width), jnp.float32),
+        jax.ShapeDtypeStruct((width, rows), jnp.float32),
         2 * devices * capacity * rows * width,
         2 * devices * width * capacity + 4 * rows * width,
-        [pltpu.VMEM((span, ROW_BLOCKS * width), jnp.float32)],
+        [pltpu.VMEM((ROW_BLOCKS * width, span), jnp.float32)],
     )(came, request)
+
+
+THIN_ROWS = 48
+
+
+def pack_thin_body(*refs):
+    *biases, tbias, tail, taskgate, sharegate, upgate, inner, middle, thin_ref, hold = refs
+    hold[...] = jnp.zeros_like(hold)
+    for row, piece in enumerate(biases + [tbias, tail]):
+        hold[row : row + 1, : piece.shape[0]] = piece[...].astype(jnp.float32).reshape(1, -1)
+    for row, piece in ((8, taskgate), (16, sharegate), (24, upgate), (32, inner)):
+        hold[row : row + piece.shape[0], : piece.shape[1]] = piece[...].astype(jnp.float32)
+    hold[32 : 32 + middle.shape[0], 128 : 128 + middle.shape[1]] = middle[...].astype(jnp.float32)
+    thin_ref[...] = hold[...].astype(jnp.bfloat16)
+
+
+def pack_thin(biases, tbias, tail, taskgate, sharegate, upgate, inner, middle):
+    return local_kernel(
+        pack_thin_body,
+        jax.ShapeDtypeStruct((THIN_ROWS, 256), jnp.bfloat16),
+        0,
+        THIN_ROWS * 1024,
+        [pltpu.VMEM((THIN_ROWS, 256), jnp.float32)],
+    )(*biases, tbias, tail, taskgate, sharegate, upgate, inner, middle)
+
+
+def prep_thin_body(
+    thin_ref,
+    columns_ref,
+    gate_one_ref,
+    gate_one_back_ref,
+    gate_two_ref,
+    gate_two_back_ref,
+    inner_ref,
+    inner_back_ref,
+    middle_ref,
+    middle_back_ref,
+    rows,
+    task_rows,
+    share_rows,
+    up_rows,
+    inner_rows,
+    middle_rows,
+):
+    devices = thin_ref.shape[0]
+    hidden = columns_ref.shape[0]
+    width = gate_one_ref.shape[1]
+
+    def lay(target, source, index, count):
+        target[:, index * count : (index + 1) * count] = source[:, :count]
+
+    rows[...] = jnp.zeros_like(rows)
+    task_rows[...] = jnp.zeros_like(task_rows)
+    share_rows[...] = jnp.zeros_like(share_rows)
+    up_rows[...] = jnp.zeros_like(up_rows)
+    bias = 6 * hidden // devices
+    flat = hidden // devices
+    for index in range(devices):
+        thin = thin_ref[index].astype(jnp.float32)
+        rows[0:6, index * bias : (index + 1) * bias] = thin[0:6, :bias]
+        rows[6:8, index * flat : (index + 1) * flat] = thin[6:8, :flat]
+        lay(task_rows, thin[8:16], index, 2 * width // devices)
+        lay(share_rows, thin[16:24], index, width // devices)
+        lay(up_rows, thin[24:32], index, 2 * hidden // devices)
+        count = 2 * hidden // devices
+        inner_rows[index * count : (index + 1) * count, :] = thin[32 : 32 + count, :128]
+        count = hidden // devices
+        middle_rows[index * count : (index + 1) * count, :] = thin[32 : 32 + count, 128:192]
+    columns_ref[...] = jnp.zeros_like(columns_ref)
+    for expert in range(6):
+        columns_ref[:, expert * 8 : expert * 8 + 8] = rows[:, expert * hidden : (expert + 1) * hidden].T
+    gates = jnp.concatenate(
+        [
+            task_rows[:, :width],
+            task_rows[:, width:],
+            share_rows[...],
+            jnp.zeros((8, width), jnp.float32),
+        ],
+        axis=0,
+    )
+    gate_one_ref[...] = gates.astype(jnp.bfloat16)
+    gate_one_back_ref[...] = gates.T.astype(jnp.bfloat16)
+    gate_two_ref[...] = jnp.concatenate([up_rows[:, :hidden], up_rows[:, hidden:]], axis=0).astype(
+        jnp.bfloat16
+    )
+    for task in range(2):
+        span = slice(task * hidden, (task + 1) * hidden)
+        wide = jnp.concatenate([up_rows[:, span], jnp.zeros((8, hidden), jnp.float32)], axis=0)
+        gate_two_back_ref[span, :] = wide.T.astype(jnp.bfloat16)
+        inner_ref[task * 128 : (task + 1) * 128, :] = inner_rows[span, :].T.astype(jnp.bfloat16)
+        span = slice(task * 128, (task + 1) * 128)
+        middle_ref[task * 64 : (task + 1) * 64, :] = middle_rows[span, :].T.astype(jnp.bfloat16)
+    inner_back_ref[...] = inner_rows[...].astype(jnp.bfloat16)
+    middle_back_ref[...] = middle_rows[...].astype(jnp.bfloat16)
+
+
+def prep_thin(thin, width, hidden):
+    low = functools.partial(jax.ShapeDtypeStruct, dtype=jnp.bfloat16)
+    return local_kernel(
+        prep_thin_body,
+        (
+            jax.ShapeDtypeStruct((hidden, 64), jnp.float32),
+            low((32, width)),
+            low((width, 32)),
+            low((16, hidden)),
+            low((2 * hidden, 16)),
+            low((hidden, hidden)),
+            low((2 * hidden, 128)),
+            low((128, 128)),
+            low((hidden, 64)),
+        ),
+        0,
+        2 * thin.size,
+        [
+            pltpu.VMEM((8, 6 * hidden), jnp.float32),
+            pltpu.VMEM((8, 2 * width), jnp.float32),
+            pltpu.VMEM((8, width), jnp.float32),
+            pltpu.VMEM((8, 2 * hidden), jnp.float32),
+            pltpu.VMEM((2 * hidden, 128), jnp.float32),
+            pltpu.VMEM((hidden, 64), jnp.float32),
+        ],
+    )(thin)
 
 
 SPAN = 256
@@ -274,48 +405,98 @@
     return probs * (tall - sum_rows(probs * tall))
 
 
-def dense_body(
-    flipped_ref,
-    expand_one_ref,
-    expand_one_back_ref,
-    shrink_one_ref,
-    shrink_one_back_ref,
-    expand_two_ref,
-    expand_two_back_ref,
-    shrink_two_ref,
-    shrink_two_back_ref,
-    gate_one_ref,
-    gate_one_back_ref,
-    gate_two_ref,
-    gate_two_back_ref,
-    inner_ref,
-    inner_back_ref,
-    middle_ref,
-    middle_back_ref,
-    columns_ref,
-    cot_ref,
-    logits_ref,
-    flipped_grad_ref,
-    grads_ref,
-    input_keep,
-    active_one,
-    out_one,
-    pre_one,
-    score_one,
-    carried_keep,
-    active_two,
-    out_two,
-    pre_two,
-    score_two,
-    tower_keep,
-    tower_act_keep,
-    first_keep,
-    top_keep,
-    tail_keep,
-    gain_keep,
-):
+def assemble(bit, own_ref, came_ref, homes, places, blocks):
+    rows = own_ref.shape[0] // blocks
+    sizes = [home.shape[0] // (2 * blocks) for home in homes]
+
+    def lay(pieces):
+        for half, source in enumerate(pieces):
+            for block in range(blocks):
+                start = block * rows
+                for home, size in zip(homes, sizes):
+                    target = places[half][block] * size
+                    home[target : target + size, :] = source[start : start + size, :]
+                    start += size
+
+    @pl.when(bit == 0)
+    def _():
+        lay((own_ref, came_ref))
+
+    @pl.when(bit != 0)
+    def _():
+        lay((came_ref, own_ref))
+
+
+def dense_body(places, *refs):
+    if places is None:
+        *naturals, refs = *refs[:4], refs[4:]
+    else:
+        bit_ref, own_a, own_b, came_a, came_b, *refs = refs
+        naturals, refs = refs[-4:], refs[:-4]
+    expand_one_back_ref, shrink_one_back_ref, expand_two_back_ref, shrink_two_back_ref = naturals
+    (
+        flipped_ref,
+        columns_ref,
+        gate_one_ref,
+        gate_one_back_ref,
+        gate_two_ref,
+        gate_two_back_ref,
+        inner_ref,
+        inner_back_ref,
+        middle_ref,
+        middle_back_ref,
+        cot_ref,
+        logits_ref,
+        flipped_grad_ref,
+        grads_ref,
+        input_keep,
+        active_one,
+        out_one,
+        pre_one,
+        score_one,
+        carried_keep,
+        active_two,
+        out_two,
+        pre_two,
+        score_two,
+        tower_keep,
+        tower_act_keep,
+        first_keep,
+        top_keep,
+        tail_keep,
+        gain_keep,
+        expand_one_ref,
+        shrink_one_ref,
+        expand_two_ref,
+        shrink_two_ref,
+    ) = refs
+    if places is not None:
+        bit = bit_ref[0]
+        blocks = len(places[0][0])
+        assemble(bit, own_a, came_a, [expand_one_back_ref], places[0], blocks)
+        assemble(
+            bit,
+            own_b,
+            came_b,
+            [shrink_one_back_ref, expand_two_back_ref, shrink_two_back_ref],
+            places[1],
+            blocks,
+        )
+    for natural, turned in (
+        (expand_one_back_ref, expand_one_ref),
+        (shrink_one_back_ref, shrink_one_ref),
+        (expand_two_back_ref, expand_two_ref),
+        (shrink_two_back_ref, shrink_two_ref),
+    ):
+        depth = natural.shape[0] // 6
+        across = natural.shape[1]
+        for expert in range(6):
+            turned[expert * across : (expert + 1) * across, :] = natural[
+                expert * depth : (expert + 1) * depth, :
+            ].T
+
     width, events = flipped_ref.shape
-    hidden = shrink_one_ref.shape[1]
+    hidden = shrink_one_back_ref.shape[1]
     inner = inner_ref.shape[0] // 2
     narrow = middle_ref.shape[0] // 2
     tall = hidden + ONES
@@ -349,12 +530,12 @@
                 active, slope, normed, inverse = expert_up(
                     inputs_of(expert),
                     expand_ref[experts_rows(expert), :],
-                    column(level + expert),
+                    column(expert * 8 + level),
                     shrink_ref[experts_rows(expert), :],
-                    column(level + 6 + expert),
+                    column(expert * 8 + level + 1),
                 )
                 active_keep[expert * tall : expert * tall + hidden, lanes] = active
-                kept.append((slope, normed, inverse, normed * column(level + 12 + expert)))
+                kept.append((slope, normed, inverse, normed * column(expert * 8 + level + 2)))
             return kept
 
         kept_one = up(0, lambda expert: inputs, expand_one_ref, shrink_one_ref, active_one)
@@ -370,7 +551,7 @@
             carried_keep[group * tall : group * tall + hidden, lanes] = carried[group]
 
         kept_two = up(
-            18, lambda expert: carried[expert // 2], expand_two_ref, shrink_two_ref, active_two
+            3, lambda expert: carried[expert // 2], expand_two_ref, shrink_two_ref, active_two
         )
         probs_two = []
         tower_grads = []
@@ -386,15 +567,15 @@
             tower_keep[task * tall : task * tall + hidden, lanes] = mixed
             first, first_slope = silu_parts(
                 times(inner_ref[task * inner : (task + 1) * inner, :], mixed)
-                + column(36, inner, task * inner)
+                + column(6, inner, task * inner)
             )
             first = first.astype(jnp.bfloat16)
             tower_act_keep[task * inner : (task + 1) * inner, lanes] = first
             top, top_slope = silu_parts(
                 times(middle_ref[task * narrow : (task + 1) * narrow, :], first)
-                + column(37, narrow, 2 * task * narrow)
+                + column(7, narrow, 2 * task * narrow)
             )
-            weight = column(37, narrow, (2 * task + 1) * narrow)
+            weight = column(7, narrow, (2 * task + 1) * narrow)
             logits_ref[task : task + 1, lanes] = sum_rows(top * weight)
             cot = cot_ref[task : task + 1, lanes]
             top_grad = (cot * weight * top_slope).astype(jnp.bfloat16)
@@ -421,7 +602,7 @@
                 part = part + gained[:, start : start + 128]
             gain_rows = slice((level + expert) * hidden, (level + expert + 1) * hidden)
             gain_keep[gain_rows, :] += part
-            scaled = upstream * column(3 * level + 12 + expert)
+            scaled = upstream * column(expert * 8 + level // 2 + 2)
             scale = 1.0 / hidden
             out_low = (
                 inverse * (scaled - sum_rows(scaled) * scale - normed * (slant * scale))
@@ -580,117 +761,296 @@
     put(rows, jnp.concatenate([biases, jnp.zeros((extra, hidden), jnp.float32)], axis=0))
 
 
-def dense(flipped, weights, columns, cot, grad_rows):
+def dense(flipped, weights, places, thin, cot, grad_rows):
     width, events = flipped.shape
-    hidden = columns.shape[0]
+    hidden = thin[0].shape[0]
     inner, narrow = 128, 64
     tall = hidden + ONES
+    low = functools.partial(pltpu.VMEM, dtype=jnp.bfloat16)
+    kept = (
+        width + ONES,
+        6 * tall,
+        6 * hidden,
+        6 * hidden,
+        32,
+        3 * tall,
+        6 * tall,
+        6 * hidden,
+        6 * hidden,
+        32,
+        2 * tall,
+        2 * inner,
+        2 * inner,
+        2 * narrow,
+        4 * narrow,
+    )
+    scratch = [low((rows, events)) for rows in kept]
+    scratch.append(pltpu.VMEM((12 * hidden, 128), jnp.float32))
+    scratch += [low((6 * hidden, depth)) for depth in (width, hidden, hidden, hidden)]
+    specs = [pl.BlockSpec(memory_space=pltpu.VMEM)] * (len(weights) + len(thin) + 2)
+    if places is not None:
+        scratch += [low((6 * depth, hidden)) for depth in (width, hidden, hidden, hidden)]
+        specs[0] = pl.BlockSpec(memory_space=pltpu.SMEM)
     return pl.pallas_call(
-        dense_body,
+        functools.partial(dense_body, places),
         out_shape=(
             jax.ShapeDtypeStruct((2, events), jnp.float32),
             jax.ShapeDtypeStruct((width, events), jnp.float32),
             jax.ShapeDtypeStruct((grad_rows, hidden), jnp.bfloat16),
         ),
-        scratch_shapes=[
-            pltpu.VMEM((rows, events), jnp.bfloat16)
-            for rows in (
-                width + ONES,
-                6 * tall,
-                6 * hidden,
-                6 * hidden,
-                32,
-                3 * tall,
-                6 * tall,
-                6 * hidden,
-                6 * hidden,
-                32,
-                2 * tall,
-                2 * inner,
-                2 * inner,
-                2 * narrow,
-                4 * narrow,
-            )
-        ]
-        + [pltpu.VMEM((12 * hidden, 128), jnp.float32)],
+        in_specs=specs,
+        scratch_shapes=scratch,
         compiler_params=pltpu.CompilerParams(vmem_limit_bytes=VMEM_LIMIT),
         cost_estimate=pl.CostEstimate(
             flops=6 * events * hidden * (6 * (width + 3 * hidden) + 2 * inner),
             bytes_accessed=24 * 1024 * 1024,
             transcendentals=12 * events * hidden,
         ),
-    )(flipped, *weights, columns, cot)
-
-
-def pack_rows(parts, row_tile):
-    width = 256
-    wide = [part for part in parts if part.ndim == 2 and part.shape[1] == width]
-    thin = [part.reshape(-1) for part in parts if part.ndim != 2 or part.shape[1] != width]
-    rest = jnp.concatenate(thin)
-    rest = jnp.pad(rest, (0, -rest.size % (row_tile * width))).reshape(-1, width)
-    return jnp.concatenate(wide + [rest], axis=0)
-
-
-def unpack_rows(whole, parts):
-    devices, rows, width = whole.shape
-    wide_rows = sum(part.shape[0] for part in parts if part.ndim == 2 and part.shape[1] == width)
-    rest = whole[:, wide_rows:].reshape(devices, -1)
-    out = []
-    row = 0
-    place = 0
-    for part in parts:
-        if part.ndim == 2 and part.shape[1] == width:
-            piece = whole[:, row : row + part.shape[0]]
-            row += part.shape[0]
-        else:
-            piece = rest[:, place : place + part.size]
-            place += part.size
-        out.append(piece.reshape((devices * part.shape[0],) + part.shape[1:]))
-    return out
-
-
-def split_grads(total, width, hidden):
-    place = 0
-
-    def take(rows):
-        nonlocal place
-        place += rows
-        return total[place - rows : place].astype(jnp.float32)
-
-    low_expand = take(6 * width)
-    low_shrink = take(6 * hidden)
-    up_expand = take(6 * hidden)
-    up_shrink = take(6 * hidden)
-    inner = take(hidden).reshape(hidden, 2, -1).transpose(1, 0, 2).reshape(2 * hidden, -1)
-    middle = take(64).reshape(64, 2, -1).transpose(1, 2, 0).reshape(-1, 64)
-    gates = take(32 * (width // hidden)).reshape(-1, 32, hidden).transpose(0, 2, 1).reshape(width, 32)
-    taskgate = jnp.concatenate([gates[:, 0:4], gates[:, 8:12]], axis=0)
-    sharegate = gates[:, 16:22]
-    upper = take(32).reshape(2, 16, hidden)[:, :4].transpose(0, 2, 1).reshape(2 * hidden, 4)
-    rows = take(48)
-    low_inbias, low_outbias, up_inbias, up_outbias = (
-        rows[6 * index : 6 * index + 6].reshape(-1) for index in range(4)
+    )(*weights, flipped, *thin, cot)
+
+
+def grad_layout(width, hidden):
+    sizes = [6 * width, 6 * hidden, 6 * hidden, 6 * hidden]
+    starts = [sum(sizes[:index]) for index in range(5)]
+    return sizes, starts
+
+
+def finish_body(
+    bit_ref,
+    own_a_ref,
+    own_b_ref,
+    came_a_ref,
+    came_b_ref,
+    low_expand_ref,
+    low_inbias_ref,
+    low_shrink_ref,
+    low_outbias_ref,
+    low_gain_ref,
+    low_taskgate_ref,
+    low_sharegate_ref,
+    up_expand_ref,
+    up_inbias_ref,
+    up_shrink_ref,
+    up_outbias_ref,
+    up_gain_ref,
+    up_taskgate_ref,
+    inner_ref,
+    tbias_ref,
+    middle_ref,
+    tail_ref,
+):
+    part = own_a_ref.shape[0]
+    hidden = up_expand_ref.shape[1]
+    width = low_expand_ref.shape[0] // 6
+    inner = inner_ref.shape[1]
+    narrow = middle_ref.shape[0]
+    wide = (low_expand_ref, low_shrink_ref, up_expand_ref, up_shrink_ref)
+    sizes, starts = grad_layout(width, hidden)
+    block = 128
+
+    def move(source, start, target, place, rows):
+        def step(index, carry):
+            target[pl.ds(pl.multiple_of(place + index * block, block), block), :] = source[
+                pl.ds(pl.multiple_of(start + index * block, block), block), :
+            ].astype(jnp.float32)
+            return carry
+
+        lax.fori_loop(0, rows // block, step, 0)
+
+    def rest(source, start):
+        def take(rows):
+            nonlocal start
+            start += rows
+            return source[start - rows : start, :].astype(jnp.float32)
+
+        both = take(hidden)
+        inner_ref[:hidden, :] = both[:, :inner]
+        inner_ref[hidden:, :] = both[:, inner:]
+        both = take(narrow)
+        middle_ref[...] = both
+        for index in range(width // hidden):
+            gates = take(32)
+            span = slice(index * hidden, (index + 1) * hidden)
+            low_taskgate_ref[:, span] = gates[0:4]
+            low_taskgate_ref[:, width + index * hidden : width + (index + 1) * hidden] = gates[8:12]
+            low_sharegate_ref[:, span] = gates[16:22]
+        for task in range(2):
+            up_taskgate_ref[:, task * hidden : (task + 1) * hidden] = take(16)[0:4]
+        rows = take(48)
+        flat = (low_inbias_ref, low_outbias_ref, up_inbias_ref, up_outbias_ref, tbias_ref, tail_ref)
+        place = 0
+        for target in flat + (low_gain_ref, up_gain_ref):
+            for index in range(target.shape[0] // hidden):
+                target[index * hidden : (index + 1) * hidden] = rows[place]
+                place += 1
+
+    def all_parts(pieces):
+        for index, source in enumerate(pieces):
+            first, last = index * part, (index + 1) * part
+            for target, start, size in zip(wide, starts, sizes):
+                low, high = max(first, start), min(last, start + size)
+                if low < high:
+                    move(source, low - first, target, low - start, high - low)
+        rest(pieces[-1], starts[4] - (len(pieces) - 1) * part)
+
+    @pl.when(bit_ref[0] == 0)
+    def _():
+        all_parts((own_a_ref, own_b_ref, came_a_ref, came_b_ref))
+
+    @pl.when(bit_ref[0] != 0)
+    def _():
+        all_parts((came_a_ref, came_b_ref, own_a_ref, own_b_ref))
+
+
+def finish(bit, own, came, width, hidden):
+    shapes = (
+        (6 * width, hidden),
+        (6 * hidden,),
+        (6 * hidden, hidden),
+        (6 * hidden,),
+        (6 * hidden,),
+        (4, 2 * width),
+        (6, width),
+        (6 * hidden, hidden),
+        (6 * hidden,),
+        (6 * hidden, hidden),
+        (6 * hidden,),
+        (6 * hidden,),
+        (4, 2 * hidden),
+        (2 * hidden, 128),
+        (256,),
+        (64, 256),
+        (256,),
     )
-    low_gain, up_gain = (rows[26 + 6 * index : 32 + 6 * index].reshape(-1) for index in range(2))
-    return (
-        low_expand,
-        low_inbias,
-        low_shrink,
-        low_outbias,
-        low_gain,
-        taskgate,
-        sharegate,
-        up_expand,
-        up_inbias,
-        up_shrink,
-        up_outbias,
-        up_gain,
-        upper,
-        inner,
-        rows[24],
-        middle,
-        rows[25],
+    done = pl.pallas_call(
+        finish_body,
+        out_shape=tuple(jax.ShapeDtypeStruct(shape, jnp.float32) for shape in shapes),
+        in_specs=[pl.BlockSpec(memory_space=pltpu.SMEM)] + [pl.BlockSpec(memory_space=pltpu.VMEM)] * 4,
+        compiler_params=pltpu.CompilerParams(vmem_limit_bytes=VMEM_LIMIT),
+        cost_estimate=pl.CostEstimate(
+            flops=0, bytes_accessed=12 * width * hidden * 16, transcendentals=0
+        ),
+    )(bit, *own, *came)
+    return tuple(value.T if value.shape[0] in (4, 6, 64) else value for value in done)
+
+
+def partners(mask, size):
+    return [(index, index ^ mask) for index in range(size)]
+
+
+def swap_with(values, mask, size):
+    return lax.ppermute(values, "dp", partners(mask, size))
+
+
+def halve(values, mask, place, size):
+    rows = values.shape[0] // 2
+    bit = jnp.where((place & mask) != 0, 1, 0)
+    sent = lax.dynamic_slice_in_dim(values, (1 - bit) * rows, rows, 0)
+    kept = lax.dynamic_slice_in_dim(values, bit * rows, rows, 0)
+    came = swap_with(sent, mask, size)
+    return (kept.astype(jnp.float32) + came.astype(jnp.float32)).astype(values.dtype)
+
+
+def double(values, mask, place, size):
+    came = swap_with(values, mask, size)
+    upper = (place & mask) != 0
+    return jnp.concatenate(
+        [jnp.where(upper, came, values), jnp.where(upper, values, came)], axis=0
     )
+
+
+def swap_groups(values, mask):
+    return lax.ppermute(values, "fsdp", partners(mask, lax.axis_size("fsdp")))
+
+
+def share(values):
+    group = lax.axis_size("fsdp")
+    place = lax.axis_index("fsdp")
+    pieces = [values] + [swap_groups(values, mask) for mask in range(1, group)]
+    return jnp.stack([pick(place ^ index, pieces) for index in range(group)])
+
+
+def pick(index, pieces):
+    chosen = pieces[0]
+    for place in range(1, len(pieces)):
+        chosen = jnp.where(index == place, pieces[place], chosen)
+    return chosen
+
+
+def scatter_sum(values):
+    group = lax.axis_size("fsdp")
+    place = lax.axis_index("fsdp")
+    rows = values.shape[0] // group
+    pieces = [
+        lax.dynamic_slice_in_dim(values, (place ^ mask) * rows, rows, 0) for mask in range(group)
+    ]
+    pieces = pieces[:1] + [swap_groups(pieces[mask], mask) for mask in range(1, group)]
+    total = pieces[0].astype(jnp.float32)
+    for piece in pieces[1:]:
+        total = total + piece.astype(jnp.float32)
+    return total.astype(values.dtype)
+
+
+def dp_masks(size):
+    return [1 << index for index in range(size.bit_length() - 1)]
+
+
+def dp_orders():
+    first, *others = dp_masks(lax.axis_size("dp"))
+    return first, [others, others[::-1]]
+
+
+def spread(parts):
+    size = lax.axis_size("dp")
+    place = lax.axis_index("dp")
+    first, orders = dp_orders()
+    for step in reversed(range(len(orders[0]))):
+        parts = [double(part, order[step], place, size) for part, order in zip(parts, orders)]
+    return parts, [swap_with(part, first, size) for part in parts]
+
+
+def arrival(order, first, group):
+    devices = []
+    for half in range(2):
+        places = []
+        for block in range(1 << len(order)):
+            dp = half * first
+            for index, mask in enumerate(order):
+                if block >> (len(order) - 1 - index) & 1:
+                    dp |= mask
+            places += [dp * group + index for index in range(group)]
+        devices.append(places)
+    return devices
+
+
+def in_order(own, came, bit, places, rows):
+    whole = jnp.concatenate([jnp.where(bit == 0, own, came), jnp.where(bit == 0, came, own)], axis=0)
+    whole = whole.reshape((-1, rows) + own.shape[1:])
+    flat = places[0] + places[1]
+    return jnp.stack([whole[flat.index(device)] for device in range(len(flat))])
+
+
+def sum_grads(grads, flipped_grad, send, width, hidden):
+    size = lax.axis_size("dp")
+    place = lax.axis_index("dp")
+    first, orders = dp_orders()
+    mine = halve(grads, first, place, size)
+    rows = mine.shape[0] // 2
+    parts = [mine[:rows], mine[rows:]]
+    parts, flipped_grad = lax.optimization_barrier((parts, flipped_grad))
+    outgoing = send(flipped_grad)
+    for step in range(len(orders[0])):
+        parts = [halve(part, order[step], place, size) for part, order in zip(parts, orders)]
+        if step == 0:
+            parts, outgoing = lax.optimization_barrier((parts, outgoing))
+    rows = parts[0].shape[0]
+    summed = scatter_sum(jnp.concatenate([part.reshape((lax.axis_size("fsdp"), -1) + part.shape[1:]) for part in parts], axis=1).reshape((-1,) + grads.shape[1:]))
+    shared = share(summed)
+    parts = [
+        piece.reshape((-1,) + grads.shape[1:]) for piece in jnp.split(shared, 2, axis=1)
+    ]
+    own, came = spread(parts)
+    return finish((place & first).reshape(1), own, came, width, hidden), outgoing
 
 
 def on_device(
@@ -720,146 +1080,63 @@
     events, fields = owner_ids.shape
     emb_width = embed_table.shape[1]
     capacity = 2 * events * fields // devices
+    hidden = expandone.shape[1]
+    width = fields * emb_width
+    group = lax.axis_size("fsdp")
     owner_rows = owner_ids.T
     request, rank = assign_slots(owner_rows, row_ids.T, devices, capacity)
     asked_rows = lax.all_to_all(request, ("dp", "fsdp"), split_axis=0, concat_axis=0, tiled=True)
-    table_wide = (
-        embed_table.reshape(ROW_BLOCKS, -1, emb_width).transpose(0, 2, 1).reshape(ROW_BLOCKS * emb_width, -1)
+
+    thin = pack_thin(
+        (expbiasone, redbiasone, normgainone, expbiastwo, redbiastwo, normgaintwo),
+        towerbias,
+        towertail,
+        taskgateone.T,
+        sharegateone.T,
+        taskgatetwo.T,
+        towerinner,
+        towermiddle,
     )
-    found = find_rows(asked_rows, table_wide)
+    packed = jnp.concatenate([expandone, reduceone, expandtwo, reducetwo, thin], axis=0)
+    packed = share(packed)
+    shards = (expandone, reduceone, expandtwo, reducetwo)
+    sizes = [shard.shape[0] for shard in shards]
+    wide_rows = sum(sizes)
+    thin = lax.all_gather(packed[:, wide_rows:], "dp", axis=0, tiled=True)
+    thin = prep_thin(thin, width, hidden)
+    first, orders = dp_orders()
+    parts = [packed[:, : sizes[0]], packed[:, sizes[0] : wide_rows]]
+    own, came = spread([part.reshape(-1, hidden) for part in parts])
+    bit = (lax.axis_index("dp") & first).reshape(1)
+    places = [arrival(order, first, group) for order in orders]
+    if all(size % 16 == 0 for size in sizes):
+        weights = (bit, *own, *came)
+    else:
+        whole = [
+            in_order(mine, other, bit[0], place, part.shape[1])
+            for mine, other, place, part in zip(own, came, places, parts)
+        ]
+        whole = jnp.concatenate(whole, axis=1)
+        starts = [sum(sizes[:index]) for index in range(4)]
+        weights = tuple(
+            whole[:, start : start + size].reshape(-1, hidden) for start, size in zip(starts, sizes)
+        )
+        places = None
+
+    found = find_rows(asked_rows, embed_table.T)
     returned = lax.all_to_all(found, ("dp", "fsdp"), split_axis=0, concat_axis=0, tiled=True)
     flipped = place_rows(returned, rank, owner_rows)
-    packed = pack_rows(
-        (
-            expandone,
-            reduceone,
-            expandtwo,
-            reducetwo,
-            expbiasone,
-            redbiasone,
-            normgainone,
-            expbiastwo,
-            redbiastwo,
-            normgaintwo,
-            taskgateone,
-            sharegateone,
-            taskgatetwo,
-            towerinner,
-            towerbias,
-            towermiddle,
-            towertail,
-        ),
-        16,
-    )
-    whole = lax.all_gather(packed, "fsdp", axis=0, tiled=False)
-    whole = lax.all_gather(whole, "dp", axis=0, tiled=False)
-    whole = whole.reshape((devices,) + packed.shape)
-    (
-        one_expand,
-        one_shrink,
-        two_expand,
-        two_shrink,
-        one_inbias,
-        one_outbias,
-        one_gain,
-        two_inbias,
-        two_outbias,
-        two_gain,
-        one_taskgate,
-        one_sharegate,
-        two_taskgate,
-        inner_full,
-        tbias_full,
-        middle_full,
-        tail_full,
-    ) = unpack_rows(
-        whole,
-        (
-            expandone,
-            reduceone,
-            expandtwo,
-            reducetwo,
-            expbiasone,
-            redbiasone,
-            normgainone,
-            expbiastwo,
-            redbiastwo,
-            normgaintwo,
-            taskgateone,
-            sharegateone,
-            taskgatetwo,
-            towerinner,
-            towerbias,
-            towermiddle,
-            towertail,
-        ),
-    )
-    hidden = expandone.shape[1]
-    width = fields * emb_width
-    gates = jnp.concatenate(
-        [
-            jnp.pad(one_taskgate.reshape(2, width, 4), ((0, 0), (0, 0), (0, 4)))[0],
-            jnp.pad(one_taskgate.reshape(2, width, 4), ((0, 0), (0, 0), (0, 4)))[1],
-            jnp.pad(one_sharegate, ((0, 0), (0, 10))),
-        ],
-        axis=1,
-    )
-    upper = jnp.pad(two_taskgate.reshape(2, hidden, 4), ((0, 0), (0, 0), (0, 12)))
-
-    def swap(weight, blocks):
-        return weight.reshape(blocks, -1, weight.shape[1]).transpose(0, 2, 1).reshape(
-            blocks * weight.shape[1], -1
-        )
-
-    weights = (
-        swap(one_expand, 6),
-        one_expand,
-        swap(one_shrink, 6),
-        one_shrink,
-        swap(two_expand, 6),
-        two_expand,
-        swap(two_shrink, 6),
-        two_shrink,
-        gates[:, :24].T,
-        gates,
-        upper[:, :, :8].transpose(0, 2, 1).reshape(16, hidden),
-        upper.reshape(2 * hidden, 16),
-        swap(inner_full, 2),
-        inner_full,
-        swap(middle_full, 2),
-        middle_full,
-    )
-    columns = (
-        jnp.concatenate(
-            [
-                one_inbias,
-                one_outbias,
-                one_gain,
-                two_inbias,
-                two_outbias,
-                two_gain,
-                tbias_full,
-                tail_full,
-            ]
-        )
-        .reshape(-1, hidden)
-        .astype(jnp.float32)
-        .T
-    )
     chunk = 16 * devices
-    grad_rows = -(-(12 * (width + 3 * hidden) // 2 + 2 * hidden) // chunk) * chunk
-    logits, flipped_grad, grads = dense(flipped, weights, columns, logit_cot, grad_rows)
-    x_grad = flipped_grad.T
-    outgoing = send_rows(flipped_grad, rank, owner_rows, capacity)
-    incoming = lax.all_to_all(
-        outgoing, ("dp", "fsdp"), split_axis=0, concat_axis=0, tiled=True
-    )
+    grad_rows = -(-(6 * (width + 3 * hidden) + 2 * hidden) // chunk) * chunk
+    logits, flipped_grad, grads = dense(flipped, weights, places, thin, logit_cot, grad_rows)
+
+    def send(flipped_grad):
+        return send_rows(flipped_grad, rank, owner_rows, capacity)
+
+    done, outgoing = sum_grads(grads, flipped_grad, send, width, hidden)
+    incoming = lax.all_to_all(outgoing, ("dp", "fsdp"), split_axis=0, concat_axis=0, tiled=True)
     table_grad = add_rows(incoming, asked_rows, embed_table.shape[0])
-    part = lax.psum_scatter(grads, "dp", scatter_dimension=0, tiled=True)
-    part = lax.psum_scatter(part, "fsdp", scatter_dimension=0, tiled=True)
-    total = lax.all_gather(part, "fsdp", axis=0, tiled=True)
-    total = lax.all_gather(total, "dp", axis=0, tiled=True)
-    return (logits, x_grad, table_grad, *split_grads(total, width, hidden))
+    return (logits, flipped_grad.T, table_grad.T, *done)
 
 
 def solution(mesh):

time: 314 us -> 237 us (0.75)
  local copies, waits for them, and re-layouts: 49.8 us -> 10.9 us
  waiting for transfers between devices: 129 us -> 93.8 us
  starting transfers between devices: 13.4 us -> 41 us
  blocking collectives: 34.7 us -> 11.9 us
  between operations: 14.1 us -> 1.2 us
  Pallas kernels: 60.2 us -> 70.5 us
    ppermute x0 -> x26, waiting for transfers between devices: none -> 89.6 us  [the longest x17 60.6 us: swap_with(): return lax.ppermute(values, 'dp', partners(mask, size))]
    reduce_scatter x2 -> x0, waiting for transfers between devices: 75.2 us -> none  [the longest x1 51.2 us: on_device(): part = lax.psum_scatter(grads, 'dp', scatter_dimension=0, tiled=True)]
    ppermute x0 -> x26, starting transfers between devices: none -> 29.8 us  [the longest x17 15.2 us: swap_with(): return lax.ppermute(values, 'dp', partners(mask, size))]
    all_to_all x1, waiting for transfers between devices: 25 us -> 0.01 us  [on_device(): lax.all_to_all(found, ('dp', 'fsdp'), split_axis=0, concat_axis=0, tiled=...]
    all_to_all x1, waiting for transfers between devices: 23.5 us -> 0.01 us  [on_device(): lax.all_to_all(outgoing, ('dp', 'fsdp'), split_axis=0, concat_axis=0, til...]
    all_gather x2 -> x1, blocking collectives: 34.7 us -> 11.9 us  [on_device(): thin = lax.all_gather(packed[:, wide_rows:], 'dp', axis=0, tiled=True)]
    pallas_call x4 -> x7, Pallas kernels: 45.9 us -> 56 us  [the longest x1 25.3 us: dense(): pl.pallas_call(functools.partial(dense_body, places), out_shape=(jax.Shap...]
    reshape x27 -> x0, local copies, waits for them, and re-layouts: 9.79 us -> none  [the longest x4 2.4 us: split_grads(): rows[6 * index:6 * index + 6].reshape(-1)]
  transfers between devices with their start and end apart: 7 -> 29, of which waited for: 5 -> 17; matrix products, arithmetic and copies ran while one was open for 3% -> 2% of each run, Pallas kernels for 11% -> 16%
where the time goes in v1:
time: 237 us; the launch traced here: 236 us
  waiting for transfers between devices  93.8 us (40%)
  Pallas kernels  70.5 us (30%)
  starting transfers between devices  41 us (17%)
  blocking collectives  11.9 us (5%)
  local copies, waits for them, and re-layouts  10.9 us (5%)
  other arithmetic  7.02 us (3%)
    ppermute x17, waiting for transfers between devices, swap_with(): return lax.ppermute(values, 'dp', partners(mask, size))  60.6 us
    ppermute x9, waiting for transfers between devices, swap_groups(): return lax.ppermute(values, 'fsdp', partners(mask, lax.axis_size('fsdp')))  29 us
    pallas_call x1, Pallas kernels, dense(): pl.pallas_call(functools.partial(dense_body, places), out_shape=(jax.Shap...  25.3 us
    ppermute x17, starting transfers between devices, swap_with(): return lax.ppermute(values, 'dp', partners(mask, size))  15.2 us
    ppermute x9, starting transfers between devices, swap_groups(): return lax.ppermute(values, 'fsdp', partners(mask, lax.axis_size('fsdp')))  14.6 us
    all_gather x1, blocking collectives, on_device(): thin = lax.all_gather(packed[:, wide_rows:], 'dp', axis=0, tiled=True)  11.9 us
    pallas_call x1, Pallas kernels, find_rows(): local_kernel(find_body, jax.ShapeDtypeStruct((devices, width, capacity),...  9.34 us
    pallas_call x1, Pallas kernels, add_rows(): local_kernel(add_body, jax.ShapeDtypeStruct((width, rows), jnp.float32),...  8.4 us
  transfers between devices with their start and end apart: 29, of which 17 were waited for; matrix products, arithmetic and copies ran while one was open for 2% of the time, Pallas kernels for 16%

profile of v1, /device:TPU:0, one launch (start us, length us, event | category | flops | bytes accessed | tf_op | source)
XLA Modules:
  0.0 236.4 jit_solution(6708542531828810476)
XLA Ops:
  3.7 1.5 shard_map.356
  5.9 3.0 %collective-permute-start.2 = (bf16[288,256]{1,0:T(8,128)(2,1)S(1)}, bf16[288,256]{1,0:T(8,128)(2,1)S(1)}, u32[]{:S(2)}, u32[]{:S(2)}) collective-permute-start(bf16[288,256]{1,0:T(8,128)(2,1)S(1)} %constant_dynamic-update-slice_fusion), channel_id=1, source_target_pairs={{0,1},{1,0},{2,3},{3,2},{4,5},{5,4},{6,7},{7,6},{8,9},{9,8},{10,11... | collective-permute-start | bytes 442376 | tf_op jit(solution)/shard_map/ppermute | solution.py:963
  8.9 2.6 %collective-permute-start.1 = (bf16[288,256]{1,0:T(8,128)(2,1)S(1)}, bf16[288,256]{1,0:T(8,128)(2,1)S(1)}, u32[]{:S(2)}, u32[]{:S(2)}) collective-permute-start(bf16[288,256]{1,0:T(8,128)(2,1)S(1)} %constant_dynamic-update-slice_fusion), channel_id=1, source_target_pairs={{0,2},{1,3},{2,0},{3,1},{4,6},{5,7},{6,4},{7,5},{8,10},{9,11},{10,... | collective-permute-start | bytes 442376 | tf_op jit(solution)/shard_map/ppermute | solution.py:963
  11.5 3.3 %collective-permute-done.2 = bf16[288,256]{1,0:T(8,128)(2,1)S(1)} collective-permute-done((bf16[288,256]{1,0:T(8,128)(2,1)S(1)}, bf16[288,256]{1,0:T(8,128)(2,1)S(1)}, u32[]{:S(2)}, u32[]{:S(2)}) %collective-permute-start.2) | collective-permute-done | bytes 147488 | tf_op jit(solution)/shard_map/ppermute | solution.py:963
  14.7 8.1 %collective-permute-done.1 = bf16[288,256]{1,0:T(8,128)(2,1)S(1)} collective-permute-done((bf16[288,256]{1,0:T(8,128)(2,1)S(1)}, bf16[288,256]{1,0:T(8,128)(2,1)S(1)}, u32[]{:S(2)}, u32[]{:S(2)}) %collective-permute-start.1) | collective-permute-done | bytes 147488 | tf_op jit(solution)/shard_map/ppermute | solution.py:963
  23.1 1.6 collective-permute-start.5
  24.6 2.4 %shard_map.357 = (s32[32,1,256]{2,1,0:T(1,128)}, s32[32,512]{1,0:T(8,128)}) custom-call(s32[8,512]{1,0:T(8,128)} %bitcast.53, s32[8,512]{1,0:T(8,128)} %bitcast.61), custom_call_target="tpu_custom_call" | custom-call | flops 150994944 | bytes 98304 | tf_op jit(solution)/shard_map/pallas_call | solution.py:66
  27.1 4.6 %all-to-all-start = ((s32[32,1,256]{2,1,0:T(1,128)}), s32[32,1,256]{2,1,0:T(1,128)S(1)}, u32[]{:S(2)}, u32[]{:S(2)}) async-start(s32[32,1,256]{2,1,0:T(1,128)} %get-tuple-element.57), calls=%async_computation | async-start | bytes 65536 | tf_op jit(solution)/shard_map/all_to_all | solution.py:1088
  31.7 1.8 collective-permute-start.3
  34.7 4.2 %all-to-all-done.request_ref = s32[32,1,256]{2,1,0:T(1,128)S(1)} async-done(((s32[32,1,256]{2,1,0:T(1,128)}), s32[32,1,256]{2,1,0:T(1,128)S(1)}, u32[]{:S(2)}, u32[]{:S(2)}) %all-to-all-start) | async-done | bytes 32800 | tf_op jit(solution)/shard_map/all_to_all | solution.py:1088
  39.6 9.3 %shard_map.358 = bf16[32,64,256]{2,1,0:T(8,128)(2,1)} custom-call(s32[32,1,256]{2,1,0:T(1,128)} %copy-done.5, bf16[64,4096]{1,0:T(8,128)(2,1)} %bitcast.59), custom_call_target="tpu_custom_call" | custom-call | flops 4294967296 | bytes 1572864 | tf_op jit(solution)/shard_map/pallas_call | solution.py:106
  48.9 2.6 %all-to-all-start.1 = ((bf16[32,64,256]{2,1,0:T(8,128)(2,1)}), bf16[32,64,256]{2,1,0:T(8,128)(2,1)S(1)}, u32[]{:S(2)}, u32[]{:S(2)}) async-start(bf16[32,64,256]{2,1,0:T(8,128)(2,1)} %shard_map.358), calls=%async_computation.1 | async-start | bytes 2097152 | tf_op jit(solution)/shard_map/all_to_all | solution.py:1127
  51.7 1.7 collective-permute-start.4
  53.8 18.5 %collective-permute-done.4 = bf16[768,256]{1,0:T(8,128)(2,1)S(1)} collective-permute-done((bf16[768,256]{1,0:T(8,128)(2,1)S(1)}, bf16[768,256]{1,0:T(8,128)(2,1)S(1)}, u32[]{:S(2)}, u32[]{:S(2)}) %collective-permute-start.4) | collective-permute-done | bytes 393248 | tf_op jit(solution)/shard_map/ppermute | solution.py:942
  73.3 11.9 %all_gather.3.thin_ref = bf16[32,48,256]{2,1,0:T(8,128)(2,1)} all-gather(bf16[4,48,256]{2,1,0:T(8,128)(2,1)S(1)} %pad_maximum_fusion.11), channel_id=1, replica_groups=mesh['dp'=8,'fsdp'=4] {'dp'}, dimensions={0}, use_global_device_ids=true | all-gather | bytes 884736 | tf_op jit(solution)/shard_map/all_gather | solution.py:1105
  85.3 2.7 %shard_map.360 = (f32[256,64]{1,0:T(8,128)}, bf16[32,512]{1,0:T(8,128)(2,1)}, bf16[512,32]{1,0:T(8,128)(2,1)}, bf16[16,256]{1,0:T(8,128)(2,1)}, bf16[512,16]{1,0...) custom-call(bf16[32,48,256]{2,1,0:T(8,128)(2,1)} %all_gather.3.thin_ref), custom_call_target="tpu_custom_call" | custom-call | bytes 786432 | tf_op jit(solution)/shard_map/pallas_call | solution.py:333
  89.0 6.5 %shard_map.359.refs_5_ = bf16[512,512]{1,0:T(8,128)(2,1)} custom-call(bf16[32,64,256]{2,1,0:T(8,128)(2,1)} %copy-done.4, s32[32,512]{1,0:T(8,128)} %get-tuple-element.58.rank_ref, s32[8,512]{1,0:T(8,128)} %bitcast.54), custom_call_target="tpu_custom_call" | custom-call | flops 536870912 | bytes 1572864 | tf_op jit(solution)/shard_map/pallas_call | solution.py:144
  95.5 25.3 %shard_map.361 = (f32[2,512]{1,0:T(2,128)}, f32[512,512]{1,0:T(8,128)}, bf16[8192,256]{1,0:T(8,128)(2,1)}) custom-call(s32[1]{0:T(128)} %bitcast.refs_0_.bit_ref, bf16[1536,256]{1,0:T(8,128)(2,1)} %pad_maximum_fusion.3.refs_1_, bf16[2304,256]{1,0:T(8,128)(2,1)} %copy-done.3, bf16[1536,256]{1,0:T(8,128)(2,1)} %collective-permute-done.7.refs_3_, ...), custom_call_target="tpu_custom_call" | custom-call | flops 6241124352 | bytes 25165824 | tf_op jit(solution)/shard_map/pallas_call | solution.py:794
  120.8 3.0 %constant_dynamic-slice_fusion.7 = bf16[4096,256]{1,0:T(8,128)(2,1)} fusion(bf16[8192,256]{1,0:T(8,128)(2,1)} %get-tuple-element.70, s32[]{:T(128)S(6)} %select_n.332), kind=kLoop, calls=%fused_computation.54 | loop fusion | bytes 4194308 | tf_op jit(solution)/shard_map/dynamic_slice | solution.py:948
  124.2 4.0 %collective-permute-done.9 = bf16[4096,256]{1,0:T(8,128)(2,1)S(1)} collective-permute-done((bf16[4096,256]{1,0:T(8,128)(2,1)}, bf16[4096,256]{1,0:T(8,128)(2,1)S(1)}, u32[]{:S(2)}, u32[]{:S(2)}) %collective-permute-start.9) | collective-permute-done | bytes 2097184 | tf_op jit(solution)/shard_map/ppermute | solution.py:942
  128.2 2.1 add_convert_fusion
  132.2 1.3 collective-permute-start.10
  133.4 8.0 %shard_map.362 = bf16[32,64,256]{2,1,0:T(8,128)(2,1)} custom-call(f32[512,512]{1,0:T(8,128)} %get-tuple-element.73.grad_ref, s32[32,512]{1,0:T(8,128)} %get-tuple-element.58.rank_ref, s32[8,512]{1,0:T(8,128)} %bitcast.55), custom_call_target="tpu_custom_call" | custom-call | flops 536870912 | bytes 2097152 | tf_op jit(solution)/shard_map/pallas_call | solution.py:180
  141.5 3.3 %collective-permute-done.11 = bf16[1024,256]{1,0:T(8,128)(2,1)S(1)} collective-permute-done((bf16[1024,256]{1,0:T(8,128)(2,1)S(1)}, bf16[1024,256]{1,0:T(8,128)(2,1)S(1)}, u32[]{:S(2)}, u32[]{:S(2)}) %collective-permute-start.11) | collective-permute-done | bytes 524320 | tf_op jit(solution)/shard_map/ppermute | solution.py:942
  144.9 1.5 collective-permute-done.10
  146.4 1.2 add_convert_fusion.2
  147.6 1.3 collective-permute-start.13
  149.8 5.3 %collective-permute-done.13 = bf16[512,256]{1,0:T(8,128)(2,1)S(1)} collective-permute-done((bf16[512,256]{1,0:T(8,128)(2,1)S(1)}, bf16[512,256]{1,0:T(8,128)(2,1)S(1)}, u32[]{:S(2)}, u32[]{:S(2)}) %collective-permute-start.13) | collective-permute-done | bytes 262176 | tf_op jit(solution)/shard_map/ppermute | solution.py:942
  155.2 1.0 collective-permute-done.12
  156.3 1.8 collective-permute-start.14
  158.2 2.5 %collective-permute-start.16 = (bf16[256,256]{1,0:T(8,128)(2,1)S(1)}, bf16[256,256]{1,0:T(8,128)(2,1)S(1)}, u32[]{:S(2)}, u32[]{:S(2)}) collective-permute-start(bf16[256,256]{1,0:T(8,128)(2,1)S(1)} %get-tuple-element.161), channel_id=1, source_target_pairs={{0,3},{1,2},{2,1},{3,0},{4,7},{5,6},{6,5},{7,4},{8,11},{9,10},{10,... | collective-permute-start | bytes 393224 | tf_op jit(solution)/shard_map/ppermute | solution.py:963
  160.9 2.0 collective-permute-done.14
  162.8 3.5 %collective-permute-done.16 = bf16[256,256]{1,0:T(8,128)(2,1)S(1)} collective-permute-done((bf16[256,256]{1,0:T(8,128)(2,1)S(1)}, bf16[256,256]{1,0:T(8,128)(2,1)S(1)}, u32[]{:S(2)}, u32[]{:S(2)}) %collective-permute-start.16) | collective-permute-done | bytes 131104 | tf_op jit(solution)/shard_map/ppermute | solution.py:963
  166.3 4.4 %collective-permute-done.15 = bf16[256,256]{1,0:T(8,128)(2,1)S(1)} collective-permute-done((bf16[256,256]{1,0:T(8,128)(2,1)S(1)}, bf16[256,256]{1,0:T(8,128)(2,1)S(1)}, u32[]{:S(2)}, u32[]{:S(2)}) %collective-permute-start.15) | collective-permute-done | bytes 131104 | tf_op jit(solution)/shard_map/ppermute | solution.py:963
  170.8 3.2 %collective-permute-start.18 = (bf16[256,256]{1,0:T(8,128)(2,1)S(1)}, bf16[256,256]{1,0:T(8,128)(2,1)S(1)}, u32[]{:S(2)}, u32[]{:S(2)}) collective-permute-start(bf16[256,256]{1,0:T(8,128)(2,1)S(1)} %add_convert_fusion.5), channel_id=1, source_target_pairs={{0,2},{1,3},{2,0},{3,1},{4,6},{5,7},{6,4},{7,5},{8,10},{9,11},{10,... | collective-permute-start | bytes 393224 | tf_op jit(solution)/shard_map/ppermute | solution.py:963
  174.0 1.2 collective-permute-start.17
  175.2 1.9 collective-permute-done.19
  177.1 5.9 %collective-permute-done.18 = bf16[256,256]{1,0:T(8,128)(2,1)S(1)} collective-permute-done((bf16[256,256]{1,0:T(8,128)(2,1)S(1)}, bf16[256,256]{1,0:T(8,128)(2,1)S(1)}, u32[]{:S(2)}, u32[]{:S(2)}) %collective-permute-start.18) | collective-permute-done | bytes 131104 | tf_op jit(solution)/shard_map/ppermute | solution.py:963
  183.2 1.2 collective-permute-start.22
  185.3 4.3 %collective-permute-done.22 = bf16[512,256]{1,0:T(8,128)(2,1)S(1)} collective-permute-done((bf16[512,256]{1,0:T(8,128)(2,1)S(1)}, bf16[512,256]{1,0:T(8,128)(2,1)S(1)}, u32[]{:S(2)}, u32[]{:S(2)}) %collective-permute-start.22) | collective-permute-done | bytes 262176 | tf_op jit(solution)/shard_map/ppermute | solution.py:942
  189.7 1.2 collective-permute-start.23
  191.0 3.9 %all-to-all-start.2 = ((bf16[32,64,256]{2,1,0:T(8,128)(2,1)}), bf16[32,64,256]{2,1,0:T(8,128)(2,1)}, u32[]{:S(2)}, u32[]{:S(2)}) async-start(bf16[32,64,256]{2,1,0:T(8,128)(2,1)} %shard_map.362), calls=%async_computation.2 | async-start | bytes 2097152 | tf_op jit(solution)/shard_map/all_to_all | solution.py:1137
  195.0 1.8 collective-permute-start.21
  196.8 12.2 %collective-permute-done.23 = bf16[1024,256]{1,0:T(8,128)(2,1)S(1)} collective-permute-done((bf16[1024,256]{1,0:T(8,128)(2,1)S(1)}, bf16[1024,256]{1,0:T(8,128)(2,1)S(1)}, u32[]{:S(2)}, u32[]{:S(2)}) %collective-permute-start.23) | collective-permute-done | bytes 524320 | tf_op jit(solution)/shard_map/ppermute | solution.py:942
  209.3 10.4 %collective-permute-done.21 = bf16[1024,256]{1,0:T(8,128)(2,1)S(1)} collective-permute-done((bf16[1024,256]{1,0:T(8,128)(2,1)S(1)}, bf16[1024,256]{1,0:T(8,128)(2,1)S(1)}, u32[]{:S(2)}, u32[]{:S(2)}) %collective-permute-start.21) | collective-permute-done | bytes 524320 | tf_op jit(solution)/shard_map/ppermute | solution.py:942
  220.1 1.3 copy.42
  221.5 8.4 %shard_map.363 = f32[64,4096]{1,0:T(8,128)} custom-call(bf16[32,64,256]{2,1,0:T(8,128)(2,1)} %all-to-all-done.2.came_ref, s32[32,1,256]{2,1,0:T(1,128)} %copy-done.5), custom_call_target="tpu_custom_call" | custom-call | flops 4294967296 | bytes 2097152 | tf_op jit(solution)/shard_map/pallas_call | solution.py:228
  229.9 6.3 %shard_map.364 = (f32[3072,256]{1,0:T(8,128)}, f32[1536]{0:T(1024)}, f32[1536,256]{1,0:T(8,128)}, f32[1536]{0:T(1024)}, f32[1536]{0:T(1024)}, /*index=5*/f32[4,1...) custom-call(s32[1]{0:T(128)} %bitcast.refs_0_.bit_ref, ...), custom_call_target="tpu_custom_call" | custom-call | bytes 25165824 | tf_op jit(solution)/shard_map/pallas_call | solution.py:925
  (76 shorter events, 14.0 us)
Async XLA Ops:
  5.9 8.9 %collective-permute-start.2 = (bf16[288,256]{1,0:T(8,128)(2,1)S(1)}, bf16[288,256]{1,0:T(8,128)(2,1)S(1)}, u32[]{:S(2)}, u32[]{:S(2)}) collective-permute-start(bf16[288,256]{1,0:T(8,128)(2,1)S(1)} %constant_dynamic-update-slice_fusion), channel_id=1, source_target_pairs={{0,1},{1,0},{2,3},{3,2},{4,5},{5,4},{6,7},{7,6},{8,9},{9,8},{10,11... | collective-permute-start | bytes 442376 | tf_op jit(solution)/shard_map/ppermute | solution.py:963
  8.9 14.0 %collective-permute-start.1 = (bf16[288,256]{1,0:T(8,128)(2,1)S(1)}, bf16[288,256]{1,0:T(8,128)(2,1)S(1)}, u32[]{:S(2)}, u32[]{:S(2)}) collective-permute-start(bf16[288,256]{1,0:T(8,128)(2,1)S(1)} %constant_dynamic-update-slice_fusion), channel_id=1, source_target_pairs={{0,2},{1,3},{2,0},{3,1},{4,6},{5,7},{6,4},{7,5},{8,10},{9,11},{10,... | collective-permute-start | bytes 442376 | tf_op jit(solution)/shard_map/ppermute | solution.py:963
  11.5 11.4 %collective-permute-start = (bf16[288,256]{1,0:T(8,128)(2,1)S(1)}, bf16[288,256]{1,0:T(8,128)(2,1)S(1)}, u32[]{:S(2)}, u32[]{:S(2)}) collective-permute-start(bf16[288,256]{1,0:T(8,128)(2,1)S(1)} %constant_dynamic-update-slice_fusion), channel_id=1, source_target_pairs={{0,3},{1,2},{2,1},{3,0},{4,7},{5,6},{6,5},{7,4},{8,11},{9,10},{10,... | collective-permute-start | bytes 442376 | tf_op jit(solution)/shard_map/ppermute | solution.py:963
  23.1 10.5 %collective-permute-start.5 = (bf16[576,256]{1,0:T(8,128)(2,1)S(1)}, bf16[576,256]{1,0:T(8,128)(2,1)S(1)}, u32[]{:S(2)}, u32[]{:S(2)}) collective-permute-start(bf16[576,256]{1,0:T(8,128)(2,1)S(1)} %bitcast.47), channel_id=1, source_target_pairs={{0,8},{4,12},{8,0},{12,4},{16,24},{20,28},{24,16},{28,20},{1,9},{5... | collective-permute-start | bytes 884744 | tf_op jit(solution)/shard_map/ppermute | solution.py:942
  27.1 11.9 %all-to-all-start = ((s32[32,1,256]{2,1,0:T(1,128)}), s32[32,1,256]{2,1,0:T(1,128)S(1)}, u32[]{:S(2)}, u32[]{:S(2)}) async-start(s32[32,1,256]{2,1,0:T(1,128)} %get-tuple-element.57), calls=%async_computation | async-start | bytes 65536 | tf_op jit(solution)/shard_map/all_to_all | solution.py:1088
  31.7 19.9 %collective-permute-start.3 = (bf16[384,256]{1,0:T(8,128)(2,1)S(1)}, bf16[384,256]{1,0:T(8,128)(2,1)S(1)}, u32[]{:S(2)}, u32[]{:S(2)}) collective-permute-start(bf16[384,256]{1,0:T(8,128)(2,1)S(1)} %bitcast.52), channel_id=1, source_target_pairs={{0,16},{4,20},{8,24},{12,28},{16,0},{20,4},{24,8},{28,12},{1,17},{... | collective-permute-start | bytes 589832 | tf_op jit(solution)/shard_map/ppermute | solution.py:942
  34.5 18.9 %collective-permute-start.6 = (bf16[1152,256]{1,0:T(8,128)(2,1)}, bf16[1152,256]{1,0:T(8,128)(2,1)S(1)}, u32[]{:S(2)}, u32[]{:S(2)}) collective-permute-start(bf16[1152,256]{1,0:T(8,128)(2,1)} %pad_maximum_fusion.5), channel_id=1, source_target_pairs={{0,16},{4,20},{8,24},{12,28},{16,0},{20,4},{24,8},{28,12},{1,17},{... | collective-permute-start | bytes 1769480 | tf_op jit(solution)/shard_map/ppermute | solution.py:942
  39.0 0.6 copy-start.5
  48.9 39.1 %all-to-all-start.1 = ((bf16[32,64,256]{2,1,0:T(8,128)(2,1)}), bf16[32,64,256]{2,1,0:T(8,128)(2,1)S(1)}, u32[]{:S(2)}, u32[]{:S(2)}) async-start(bf16[32,64,256]{2,1,0:T(8,128)(2,1)} %shard_map.358), calls=%async_computation.1 | async-start | bytes 2097152 | tf_op jit(solution)/shard_map/all_to_all | solution.py:1127
  51.7 20.6 %collective-permute-start.4 = (bf16[768,256]{1,0:T(8,128)(2,1)S(1)}, bf16[768,256]{1,0:T(8,128)(2,1)S(1)}, u32[]{:S(2)}, u32[]{:S(2)}) collective-permute-start(bf16[768,256]{1,0:T(8,128)(2,1)S(1)} %pad_maximum_fusion.10), channel_id=1, source_target_pairs={{0,8},{4,12},{8,0},{12,4},{16,24},{20,28},{24,16},{28,20},{1,9},{5... | collective-permute-start | bytes 1179656 | tf_op jit(solution)/shard_map/ppermute | solution.py:942
  53.7 31.6 %copy-start.3 = (bf16[2304,256]{1,0:T(8,128)(2,1)}, bf16[2304,256]{1,0:T(8,128)(2,1)S(1)}, u32[]{:S(2)}) copy-start(bf16[2304,256]{1,0:T(8,128)(2,1)S(1)} %pad_maximum_fusion.refs_2_) | copy-start | bytes 3538948
  53.7 41.7 %collective-permute-start.8 = (bf16[2304,256]{1,0:T(8,128)(2,1)S(1)}, bf16[2304,256]{1,0:T(8,128)(2,1)}, u32[]{:S(2)}, u32[]{:S(2)}) collective-permute-start(bf16[2304,256]{1,0:T(8,128)(2,1)S(1)} %pad_maximum_fusion.refs_2_), channel_id=1, source_target_pairs={{0,4},{4,0},{8,12},{12,8},{16,20},{20,16},{24,28},{28,24},{1,5},{5... | collective-permute-start | bytes 3538952 | tf_op jit(solution)/shard_map/ppermute | solution.py:942
  73.3 22.1 %collective-permute-start.7 = (bf16[1536,256]{1,0:T(8,128)(2,1)}, bf16[1536,256]{1,0:T(8,128)(2,1)}, u32[]{:S(2)}, u32[]{:S(2)}) collective-permute-start(bf16[1536,256]{1,0:T(8,128)(2,1)} %pad_maximum_fusion.3.refs_1_), channel_id=1, source_target_pairs={{0,4},{4,0},{8,12},{12,8},{16,20},{20,16},{24,28},{28,24},{1,5},{5... | collective-permute-start | bytes 2359304 | tf_op jit(solution)/shard_map/ppermute | solution.py:942
  88.0 1.0 copy-start.4
  123.8 4.4 %collective-permute-start.9 = (bf16[4096,256]{1,0:T(8,128)(2,1)}, bf16[4096,256]{1,0:T(8,128)(2,1)S(1)}, u32[]{:S(2)}, u32[]{:S(2)}) collective-permute-start(bf16[4096,256]{1,0:T(8,128)(2,1)} %constant_dynamic-slice_fusion.7), channel_id=1, source_target_pairs={{0,4},{4,0},{8,12},{12,8},{16,20},{20,16},{24,28},{28,24},{1,5},{5... | collective-permute-start | bytes 6291464 | tf_op jit(solution)/shard_map/ppermute | solution.py:942
  130.5 14.2 %collective-permute-start.11 = (bf16[1024,256]{1,0:T(8,128)(2,1)S(1)}, bf16[1024,256]{1,0:T(8,128)(2,1)S(1)}, u32[]{:S(2)}, u32[]{:S(2)}) collective-permute-start(bf16[1024,256]{1,0:T(8,128)(2,1)S(1)} %constant_dynamic-slice_fusion.5), channel_id=1, source_target_pairs={{0,16},{4,20},{8,24},{12,28},{16,0},{20,4},{24,8},{28,12},{1,17},{... | collective-permute-start | bytes 1572872 | tf_op jit(solution)/shard_map/ppermute | solution.py:942
  132.2 14.2 %collective-permute-start.10 = (bf16[1024,256]{1,0:T(8,128)(2,1)}, bf16[1024,256]{1,0:T(8,128)(2,1)}, u32[]{:S(2)}, u32[]{:S(2)}) collective-permute-start(bf16[1024,256]{1,0:T(8,128)(2,1)} %constant_dynamic-slice_fusion.6), channel_id=1, source_target_pairs={{0,8},{4,12},{8,0},{12,4},{16,24},{20,28},{24,16},{28,20},{1,9},{5... | collective-permute-start | bytes 1572872 | tf_op jit(solution)/shard_map/ppermute | solution.py:942
  147.6 7.5 %collective-permute-start.13 = (bf16[512,256]{1,0:T(8,128)(2,1)S(1)}, bf16[512,256]{1,0:T(8,128)(2,1)S(1)}, u32[]{:S(2)}, u32[]{:S(2)}) collective-permute-start(bf16[512,256]{1,0:T(8,128)(2,1)S(1)} %constant_dynamic-slice_fusion.3), channel_id=1, source_target_pairs={{0,8},{4,12},{8,0},{12,4},{16,24},{20,28},{24,16},{28,20},{1,9},{5... | collective-permute-start | bytes 786440 | tf_op jit(solution)/shard_map/ppermute | solution.py:942
  149.0 7.2 %collective-permute-start.12 = (bf16[512,256]{1,0:T(8,128)(2,1)S(1)}, bf16[512,256]{1,0:T(8,128)(2,1)S(1)}, u32[]{:S(2)}, u32[]{:S(2)}) collective-permute-start(bf16[512,256]{1,0:T(8,128)(2,1)S(1)} %constant_dynamic-slice_fusion.4), channel_id=1, source_target_pairs={{0,16},{4,20},{8,24},{12,28},{16,0},{20,4},{24,8},{28,12},{1,17},{... | collective-permute-start | bytes 786440 | tf_op jit(solution)/shard_map/ppermute | solution.py:942
  156.3 6.5 %collective-permute-start.14 = (bf16[256,256]{1,0:T(8,128)(2,1)S(1)}, bf16[256,256]{1,0:T(8,128)(2,1)S(1)}, u32[]{:S(2)}, u32[]{:S(2)}) collective-permute-start(bf16[256,256]{1,0:T(8,128)(2,1)S(1)} %get-tuple-element.160), channel_id=1, source_target_pairs={{0,1},{1,0},{2,3},{3,2},{4,5},{5,4},{6,7},{7,6},{8,9},{9,8},{10,11... | collective-permute-start | bytes 393224 | tf_op jit(solution)/shard_map/ppermute | solution.py:963
  158.2 8.1 %collective-permute-start.16 = (bf16[256,256]{1,0:T(8,128)(2,1)S(1)}, bf16[256,256]{1,0:T(8,128)(2,1)S(1)}, u32[]{:S(2)}, u32[]{:S(2)}) collective-permute-start(bf16[256,256]{1,0:T(8,128)(2,1)S(1)} %get-tuple-element.161), channel_id=1, source_target_pairs={{0,3},{1,2},{2,1},{3,0},{4,7},{5,6},{6,5},{7,4},{8,11},{9,10},{10,... | collective-permute-start | bytes 393224 | tf_op jit(solution)/shard_map/ppermute | solution.py:963
  160.6 10.0 %collective-permute-start.15 = (bf16[256,256]{1,0:T(8,128)(2,1)S(1)}, bf16[256,256]{1,0:T(8,128)(2,1)S(1)}, u32[]{:S(2)}, u32[]{:S(2)}) collective-permute-start(bf16[256,256]{1,0:T(8,128)(2,1)S(1)} %get-tuple-element.162), channel_id=1, source_target_pairs={{0,2},{1,3},{2,0},{3,1},{4,6},{5,7},{6,4},{7,5},{8,10},{9,11},{10,... | collective-permute-start | bytes 393224 | tf_op jit(solution)/shard_map/ppermute | solution.py:963
  170.8 6.4 %collective-permute-start.19 = (bf16[256,256]{1,0:T(8,128)(2,1)S(1)}, bf16[256,256]{1,0:T(8,128)(2,1)S(1)}, u32[]{:S(2)}, u32[]{:S(2)}) collective-permute-start(bf16[256,256]{1,0:T(8,128)(2,1)S(1)} %add_convert_fusion.5), channel_id=1, source_target_pairs={{0,1},{1,0},{2,3},{3,2},{4,5},{5,4},{6,7},{7,6},{8,9},{9,8},{10,11... | collective-permute-start | bytes 393224 | tf_op jit(solution)/shard_map/ppermute | solution.py:963
  170.8 12.2 %collective-permute-start.18 = (bf16[256,256]{1,0:T(8,128)(2,1)S(1)}, bf16[256,256]{1,0:T(8,128)(2,1)S(1)}, u32[]{:S(2)}, u32[]{:S(2)}) collective-permute-start(bf16[256,256]{1,0:T(8,128)(2,1)S(1)} %add_convert_fusion.5), channel_id=1, source_target_pairs={{0,2},{1,3},{2,0},{3,1},{4,6},{5,7},{6,4},{7,5},{8,10},{9,11},{10,... | collective-permute-start | bytes 393224 | tf_op jit(solution)/shard_map/ppermute | solution.py:963
  174.0 9.0 %collective-permute-start.17 = (bf16[256,256]{1,0:T(8,128)(2,1)S(1)}, bf16[256,256]{1,0:T(8,128)(2,1)S(1)}, u32[]{:S(2)}, u32[]{:S(2)}) collective-permute-start(bf16[256,256]{1,0:T(8,128)(2,1)S(1)} %add_convert_fusion.5), channel_id=1, source_target_pairs={{0,3},{1,2},{2,1},{3,0},{4,7},{5,6},{6,5},{7,4},{8,11},{9,10},{10,... | collective-permute-start | bytes 393224 | tf_op jit(solution)/shard_map/ppermute | solution.py:963
  183.2 6.4 %collective-permute-start.22 = (bf16[512,256]{1,0:T(8,128)(2,1)S(1)}, bf16[512,256]{1,0:T(8,128)(2,1)S(1)}, u32[]{:S(2)}, u32[]{:S(2)}) collective-permute-start(bf16[512,256]{1,0:T(8,128)(2,1)S(1)} %bitcast.49), channel_id=1, source_target_pairs={{0,8},{4,12},{8,0},{12,4},{16,24},{20,28},{24,16},{28,20},{1,9},{5... | collective-permute-start | bytes 786440 | tf_op jit(solution)/shard_map/ppermute | solution.py:942
  184.4 10.5 %collective-permute-start.20 = (bf16[512,256]{1,0:T(8,128)(2,1)S(1)}, bf16[512,256]{1,0:T(8,128)(2,1)S(1)}, u32[]{:S(2)}, u32[]{:S(2)}) collective-permute-start(bf16[512,256]{1,0:T(8,128)(2,1)S(1)} %bitcast.48), channel_id=1, source_target_pairs={{0,16},{4,20},{8,24},{12,28},{16,0},{20,4},{24,8},{28,12},{1,17},{... | collective-permute-start | bytes 786440 | tf_op jit(solution)/shard_map/ppermute | solution.py:942
  189.7 19.2 %collective-permute-start.23 = (bf16[1024,256]{1,0:T(8,128)(2,1)S(1)}, bf16[1024,256]{1,0:T(8,128)(2,1)S(1)}, u32[]{:S(2)}, u32[]{:S(2)}) collective-permute-start(bf16[1024,256]{1,0:T(8,128)(2,1)S(1)} %pad_maximum_fusion.9), channel_id=1, source_target_pairs={{0,16},{4,20},{8,24},{12,28},{16,0},{20,4},{24,8},{28,12},{1,17},{... | collective-permute-start | bytes 1572872 | tf_op jit(solution)/shard_map/ppermute | solution.py:942
  191.0 30.5 %all-to-all-start.2 = ((bf16[32,64,256]{2,1,0:T(8,128)(2,1)}), bf16[32,64,256]{2,1,0:T(8,128)(2,1)}, u32[]{:S(2)}, u32[]{:S(2)}) async-start(bf16[32,64,256]{2,1,0:T(8,128)(2,1)} %shard_map.362), calls=%async_computation.2 | async-start | bytes 2097152 | tf_op jit(solution)/shard_map/all_to_all | solution.py:1137
  195.0 24.7 %collective-permute-start.21 = (bf16[1024,256]{1,0:T(8,128)(2,1)S(1)}, bf16[1024,256]{1,0:T(8,128)(2,1)S(1)}, u32[]{:S(2)}, u32[]{:S(2)}) collective-permute-start(bf16[1024,256]{1,0:T(8,128)(2,1)S(1)} %pad_maximum_fusion.8), channel_id=1, source_target_pairs={{0,8},{4,12},{8,0},{12,4},{16,24},{20,28},{24,16},{28,20},{1,9},{5... | collective-permute-start | bytes 1572872 | tf_op jit(solution)/shard_map/ppermute | solution.py:942
  209.2 10.8 %copy-start = (bf16[2048,256]{1,0:T(8,128)(2,1)}, bf16[2048,256]{1,0:T(8,128)(2,1)S(1)}, u32[]{:S(2)}) copy-start(bf16[2048,256]{1,0:T(8,128)(2,1)S(1)} %pad_maximum_fusion.2.own_b_ref) | copy-start | bytes 3145732
  209.2 10.9 %copy-start.2 = (f32[512,512]{1,0:T(8,128)S(1)}, f32[512,512]{1,0:T(8,128)}, u32[]{:S(2)}) copy-start(f32[512,512]{1,0:T(8,128)} %get-tuple-element.73.grad_ref) | copy-start | bytes 3145732
  209.2 20.6 %collective-permute-start.25 = (bf16[2048,256]{1,0:T(8,128)(2,1)S(1)}, bf16[2048,256]{1,0:T(8,128)(2,1)}, u32[]{:S(2)}, u32[]{:S(2)}) collective-permute-start(bf16[2048,256]{1,0:T(8,128)(2,1)S(1)} %pad_maximum_fusion.2.own_b_ref), channel_id=1, source_target_pairs={{0,4},{4,0},{8,12},{12,8},{16,20},{20,16},{24,28},{28,24},{1,5},{5... | collective-permute-start | bytes 3145736 | tf_op jit(solution)/shard_map/ppermute | solution.py:942
  220.0 9.8 %copy-start.1 = (bf16[2048,256]{1,0:T(8,128)(2,1)}, bf16[2048,256]{1,0:T(8,128)(2,1)S(1)}, u32[]{:S(2)}) copy-start(bf16[2048,256]{1,0:T(8,128)(2,1)S(1)} %pad_maximum_fusion.1.own_a_ref) | copy-start | bytes 3145732
  220.1 9.8 %collective-permute-start.24 = (bf16[2048,256]{1,0:T(8,128)(2,1)S(1)}, bf16[2048,256]{1,0:T(8,128)(2,1)}, u32[]{:S(2)}, u32[]{:S(2)}) collective-permute-start(bf16[2048,256]{1,0:T(8,128)(2,1)S(1)} %pad_maximum_fusion.1.own_a_ref), channel_id=1, source_target_pairs={{0,4},{4,0},{8,12},{12,8},{16,20},{20,16},{24,28},{28,24},{1,5},{5... | collective-permute-start | bytes 3145736 | tf_op jit(solution)/shard_map/ppermute | solution.py:942

commit v2 on v1

--- a/solution.py
+++ b/solution.py
@@ -238,28 +238,46 @@
 
 
 def pack_thin_body(*refs):
-    *biases, tbias, tail, taskgate, sharegate, upgate, inner, middle, thin_ref, hold = refs
+    *biases, tbias, tail, taskgate, sharegate, upgate, inner, middle = refs[:13]
+    *wide, out_ref, hold = refs[13:]
     hold[...] = jnp.zeros_like(hold)
     for row, piece in enumerate(biases + [tbias, tail]):
         hold[row : row + 1, : piece.shape[0]] = piece[...].astype(jnp.float32).reshape(1, -1)
     for row, piece in ((8, taskgate), (16, sharegate), (24, upgate), (32, inner)):
         hold[row : row + piece.shape[0], : piece.shape[1]] = piece[...].astype(jnp.float32)
     hold[32 : 32 + middle.shape[0], 128 : 128 + middle.shape[1]] = middle[...].astype(jnp.float32)
-    thin_ref[...] = hold[...].astype(jnp.bfloat16)
-
-
-def pack_thin(biases, tbias, tail, taskgate, sharegate, upgate, inner, middle):
-    return local_kernel(
+    thin = hold[...].astype(jnp.bfloat16)
+    if not wide:
+        out_ref[...] = thin
+    start = 0
+    for index, piece in enumerate(wide):
+        out_ref[start : start + piece.shape[0], :] = piece[...]
+        start += piece.shape[0]
+        if index == 0:
+            out_ref[start : start + THIN_ROWS, :] = thin
+            start += THIN_ROWS
+
+
+def pack(biases, others, wide):
+    aligned = all(piece.shape[0] % 16 == 0 for piece in wide)
+    rows = THIN_ROWS + (sum(piece.shape[0] for piece in wide) if aligned else 0)
+    packed = local_kernel(
         pack_thin_body,
-        jax.ShapeDtypeStruct((THIN_ROWS, 256), jnp.bfloat16),
+        jax.ShapeDtypeStruct((rows, 256), jnp.bfloat16),
         0,
-        THIN_ROWS * 1024,
+        rows * 1024,
         [pltpu.VMEM((THIN_ROWS, 256), jnp.float32)],
-    )(*biases, tbias, tail, taskgate, sharegate, upgate, inner, middle)
+    )(*biases, *others, *(wide if aligned else ()))
+    if aligned:
+        return packed
+    return jnp.concatenate([wide[0], packed, *wide[1:]], axis=0)
 
 
 def prep_thin_body(
-    thin_ref,
+    places,
+    bit_ref,
+    own_ref,
+    came_ref,
     columns_ref,
     gate_one_ref,
     gate_one_back_ref,
@@ -276,7 +294,8 @@
     inner_rows,
     middle_rows,
 ):
-    devices = thin_ref.shape[0]
+    devices = 2 * len(places[0])
+    shard = own_ref.shape[0] // len(places[0])
     hidden = columns_ref.shape[0]
     width = gate_one_ref.shape[1]
 
@@ -289,17 +308,30 @@
     up_rows[...] = jnp.zeros_like(up_rows)
     bias = 6 * hidden // devices
     flat = hidden // devices
-    for index in range(devices):
-        thin = thin_ref[index].astype(jnp.float32)
-        rows[0:6, index * bias : (index + 1) * bias] = thin[0:6, :bias]
-        rows[6:8, index * flat : (index + 1) * flat] = thin[6:8, :flat]
-        lay(task_rows, thin[8:16], index, 2 * width // devices)
-        lay(share_rows, thin[16:24], index, width // devices)
-        lay(up_rows, thin[24:32], index, 2 * hidden // devices)
-        count = 2 * hidden // devices
-        inner_rows[index * count : (index + 1) * count, :] = thin[32 : 32 + count, :128]
-        count = hidden // devices
-        middle_rows[index * count : (index + 1) * count, :] = thin[32 : 32 + count, 128:192]
+
+    def unpack(pieces):
+        for half, source in enumerate(pieces):
+            for block, index in enumerate(places[half]):
+                end = (block + 1) * shard
+                thin = source[end - THIN_ROWS : end, :].astype(jnp.float32)
+                rows[0:6, index * bias : (index + 1) * bias] = thin[0:6, :bias]
+                rows[6:8, index * flat : (index + 1) * flat] = thin[6:8, :flat]
+                lay(task_rows, thin[8:16], index, 2 * width // devices)
+                lay(share_rows, thin[16:24], index, width // devices)
+                lay(up_rows, thin[24:32], index, 2 * hidden // devices)
+                count = 2 * hidden // devices
+                inner_rows[index * count : (index + 1) * count, :] = thin[32 : 32 + count, :128]
+                count = hidden // devices
+                middle_rows[index * count : (index + 1) * count, :] = thin[32 : 32 + count, 128:192]
+
+    @pl.when(bit_ref[0] == 0)
+    def _():
+        unpack((own_ref, came_ref))
+
+    @pl.when(bit_ref[0] != 0)
+    def _():
+        unpack((came_ref, own_ref))
+
     columns_ref[...] = jnp.zeros_like(columns_ref)
     for expert in range(6):
         columns_ref[:, expert * 8 : expert * 8 + 8] = rows[:, expert * hidden : (expert + 1) * hidden].T
@@ -328,11 +360,11 @@
     middle_back_ref[...] = middle_rows[...].astype(jnp.bfloat16)
 
 
-def prep_thin(thin, width, hidden):
+def prep_thin(bit, own, came, places, width, hidden):
     low = functools.partial(jax.ShapeDtypeStruct, dtype=jnp.bfloat16)
-    return local_kernel(
-        prep_thin_body,
-        (
+    return pl.pallas_call(
+        functools.partial(prep_thin_body, places),
+        out_shape=(
             jax.ShapeDtypeStruct((hidden, 64), jnp.float32),
             low((32, width)),
             low((width, 32)),
@@ -343,9 +375,8 @@
             low((128, 128)),
             low((hidden, 64)),
         ),
-        0,
-        2 * thin.size,
-        [
+        in_specs=[pl.BlockSpec(memory_space=pltpu.SMEM)] + [pl.BlockSpec(memory_space=pltpu.VMEM)] * 2,
+        scratch_shapes=[
             pltpu.VMEM((8, 6 * hidden), jnp.float32),
             pltpu.VMEM((8, 2 * width), jnp.float32),
             pltpu.VMEM((8, width), jnp.float32),
@@ -353,7 +384,9 @@
             pltpu.VMEM((2 * hidden, 128), jnp.float32),
             pltpu.VMEM((hidden, 64), jnp.float32),
         ],
-    )(thin)
+        compiler_params=pltpu.CompilerParams(vmem_limit_bytes=VMEM_LIMIT),
+        cost_estimate=pl.CostEstimate(flops=0, bytes_accessed=4 * own.size, transcendentals=0),
+    )(bit, own, came)
 
 
 SPAN = 256
@@ -428,10 +461,11 @@
 
 
 def dense_body(places, *refs):
+    bit_ref, *refs = refs
     if places is None:
         *naturals, refs = *refs[:4], refs[4:]
     else:
-        bit_ref, own_a, own_b, came_a, came_b, *refs = refs
+        own_a, own_b, came_a, came_b, *refs = refs
         naturals, refs = refs[-4:], refs[:-4]
     expand_one_back_ref, shrink_one_back_ref, expand_two_back_ref, shrink_two_back_ref = naturals
     (
@@ -448,6 +482,9 @@
         cot_ref,
         logits_ref,
         flipped_grad_ref,
+        kept_ref,
+        sent_ref,
+        sems,
         grads_ref,
         input_keep,
         active_one,
@@ -470,8 +507,8 @@
         expand_two_ref,
         shrink_two_ref,
     ) = refs
+    bit = jnp.minimum(bit_ref[0], 1)
     if places is not None:
-        bit = bit_ref[0]
         blocks = len(places[0][0])
         assemble(bit, own_a, came_a, [expand_one_back_ref], places[0], blocks)
         assemble(
@@ -678,8 +715,14 @@
 
     lax.fori_loop(0, events // span, span_step, 0)
 
+    half_rows = grads_ref.shape[1]
+
     def put(row, value):
-        grads_ref[row : row + value.shape[0], :] = value.astype(jnp.bfloat16)
+        while value.shape[0]:
+            half, start = row // half_rows, row % half_rows
+            count = min(value.shape[0], half_rows - start)
+            grads_ref[half, start : start + count, :] = value[:count].astype(jnp.bfloat16)
+            row, value = row + count, value[count:]
 
     rows = 0
     biases = []
@@ -757,11 +800,19 @@
     for expert in range(12):
         biases.append(gains[:, experts_rows(expert)])
     biases = jnp.concatenate(biases, axis=0)
-    extra = grads_ref.shape[0] - rows - biases.shape[0]
+    extra = 2 * half_rows - rows - biases.shape[0]
     put(rows, jnp.concatenate([biases, jnp.zeros((extra, hidden), jnp.float32)], axis=0))
-
-
-def dense(flipped, weights, places, thin, cot, grad_rows):
+    copies = [
+        pltpu.make_async_copy(grads_ref.at[1 - bit], sent_ref, sems.at[0]),
+        pltpu.make_async_copy(grads_ref.at[bit], kept_ref, sems.at[1]),
+    ]
+    for copy in copies:
+        copy.start()
+    for copy in copies:
+        copy.wait()
+
+
+def dense(bit, flipped, weights, places, thin, cot, grad_rows):
     width, events = flipped.shape
     hidden = thin[0].shape[0]
     inner, narrow = 128, 64
@@ -784,21 +835,26 @@
         2 * narrow,
         4 * narrow,
     )
-    scratch = [low((rows, events)) for rows in kept]
+    half = (grad_rows // 2, hidden)
+    scratch = [pltpu.SemaphoreType.DMA((2,)), low((2,) + half)]
+    scratch += [low((rows, events)) for rows in kept]
     scratch.append(pltpu.VMEM((12 * hidden, 128), jnp.float32))
     scratch += [low((6 * hidden, depth)) for depth in (width, hidden, hidden, hidden)]
-    specs = [pl.BlockSpec(memory_space=pltpu.VMEM)] * (len(weights) + len(thin) + 2)
+    vmem = pl.BlockSpec(memory_space=pltpu.VMEM)
+    outside = pl.BlockSpec(memory_space=pl.ANY)
+    specs = [pl.BlockSpec(memory_space=pltpu.SMEM)] + [vmem] * (len(weights) + len(thin) + 2)
     if places is not None:
         scratch += [low((6 * depth, hidden)) for depth in (width, hidden, hidden, hidden)]
-        specs[0] = pl.BlockSpec(memory_space=pltpu.SMEM)
     return pl.pallas_call(
         functools.partial(dense_body, places),
         out_shape=(
             jax.ShapeDtypeStruct((2, events), jnp.float32),
             jax.ShapeDtypeStruct((width, events), jnp.float32),
-            jax.ShapeDtypeStruct((grad_rows, hidden), jnp.bfloat16),
+            jax.ShapeDtypeStruct(half, jnp.bfloat16),
+            jax.ShapeDtypeStruct(half, jnp.bfloat16),
         ),
         in_specs=specs,
+        out_specs=(vmem, vmem, outside, outside),
         scratch_shapes=scratch,
         compiler_params=pltpu.CompilerParams(vmem_limit_bytes=VMEM_LIMIT),
         cost_estimate=pl.CostEstimate(
@@ -806,7 +862,7 @@
             bytes_accessed=24 * 1024 * 1024,
             transcendentals=12 * events * hidden,
         ),
-    )(*weights, flipped, *thin, cot)
+    )(bit, *weights, flipped, *thin, cot)
 
 
 def grad_layout(width, hidden):
@@ -942,13 +998,15 @@
     return lax.ppermute(values, "dp", partners(mask, size))
 
 
-def halve(values, mask, place, size):
+def cut(values, mask, place):
     rows = values.shape[0] // 2
     bit = jnp.where((place & mask) != 0, 1, 0)
     sent = lax.dynamic_slice_in_dim(values, (1 - bit) * rows, rows, 0)
-    kept = lax.dynamic_slice_in_dim(values, bit * rows, rows, 0)
-    came = swap_with(sent, mask, size)
-    return (kept.astype(jnp.float32) + came.astype(jnp.float32)).astype(values.dtype)
+    return sent, lax.dynamic_slice_in_dim(values, bit * rows, rows, 0)
+
+
+def add_low(kept, came):
+    return (kept.astype(jnp.float32) + came.astype(jnp.float32)).astype(kept.dtype)
 
 
 def double(values, mask, place, size):
@@ -963,10 +1021,12 @@
     return lax.ppermute(values, "fsdp", partners(mask, lax.axis_size("fsdp")))
 
 
-def share(values):
+def share(values, also=None):
     group = lax.axis_size("fsdp")
     place = lax.axis_index("fsdp")
     pieces = [values] + [swap_groups(values, mask) for mask in range(1, group)]
+    if also is not None:
+        pieces, _ = lax.optimization_barrier((pieces, also))
     return jnp.stack([pick(place ^ index, pieces) for index in range(group)])
 
 
@@ -1000,13 +1060,16 @@
     return first, [others, others[::-1]]
 
 
-def spread(parts):
+def spread(parts, late=None, early=None):
     size = lax.axis_size("dp")
     place = lax.axis_index("dp")
     first, orders = dp_orders()
     for step in reversed(range(len(orders[0]))):
         parts = [double(part, order[step], place, size) for part, order in zip(parts, orders)]
-    return parts, [swap_with(part, first, size) for part in parts]
+        if step == len(orders[0]) - 1 and early is not None:
+            parts, early = lax.optimization_barrier((parts, early))
+    parts, late = lax.optimization_barrier((parts, late))
+    return parts, [swap_with(part, first, size) for part in parts], late, early
 
 
 def arrival(order, first, group):
@@ -1030,27 +1093,34 @@
     return jnp.stack([whole[flat.index(device)] for device in range(len(flat))])
 
 
-def sum_grads(grads, flipped_grad, send, width, hidden):
+def sum_grads(kept, sent, flipped_grad, prepare, finish_rows, width, hidden):
     size = lax.axis_size("dp")
+    group = lax.axis_size("fsdp")
     place = lax.axis_index("dp")
     first, orders = dp_orders()
-    mine = halve(grads, first, place, size)
+    mine = add_low(kept, swap_with(sent, first, size))
     rows = mine.shape[0] // 2
     parts = [mine[:rows], mine[rows:]]
-    parts, flipped_grad = lax.optimization_barrier((parts, flipped_grad))
-    outgoing = send(flipped_grad)
     for step in range(len(orders[0])):
-        parts = [halve(part, order[step], place, size) for part, order in zip(parts, orders)]
+        halves = [cut(part, order[step], place) for part, order in zip(parts, orders)]
+        if step == 0:
+            halves, flipped_grad = lax.optimization_barrier((halves, flipped_grad))
+            outgoing = prepare(flipped_grad)
+        parts = [
+            add_low(kept, swap_with(sent, order[step], size))
+            for (sent, kept), order in zip(halves, orders)
+        ]
         if step == 0:
             parts, outgoing = lax.optimization_barrier((parts, outgoing))
-    rows = parts[0].shape[0]
-    summed = scatter_sum(jnp.concatenate([part.reshape((lax.axis_size("fsdp"), -1) + part.shape[1:]) for part in parts], axis=1).reshape((-1,) + grads.shape[1:]))
+    incoming = lax.all_to_all(outgoing, ("dp", "fsdp"), split_axis=0, concat_axis=0, tiled=True)
+    both = [part.reshape((group, -1) + part.shape[1:]) for part in parts]
+    summed = scatter_sum(jnp.concatenate(both, axis=1).reshape((-1,) + kept.shape[1:]))
+    summed, incoming = lax.optimization_barrier((summed, incoming))
     shared = share(summed)
-    parts = [
-        piece.reshape((-1,) + grads.shape[1:]) for piece in jnp.split(shared, 2, axis=1)
-    ]
-    own, came = spread(parts)
-    return finish((place & first).reshape(1), own, came, width, hidden), outgoing
+    late = (finish_rows(incoming), flipped_grad.T)
+    parts = [piece.reshape((-1,) + kept.shape[1:]) for piece in jnp.split(shared, 2, axis=1)]
+    own, came, late, _ = spread(parts, late)
+    return finish((place & first).reshape(1), own, came, width, hidden), *late
 
 
 def on_device(
@@ -1086,57 +1156,50 @@
     owner_rows = owner_ids.T
     request, rank = assign_slots(owner_rows, row_ids.T, devices, capacity)
     asked_rows = lax.all_to_all(request, ("dp", "fsdp"), split_axis=0, concat_axis=0, tiled=True)
-
-    thin = pack_thin(
+    packed = pack(
         (expbiasone, redbiasone, normgainone, expbiastwo, redbiastwo, normgaintwo),
-        towerbias,
-        towertail,
-        taskgateone.T,
-        sharegateone.T,
-        taskgatetwo.T,
-        towerinner,
-        towermiddle,
+        (towerbias, towertail, taskgateone.T, sharegateone.T, taskgatetwo.T, towerinner, towermiddle),
+        (expandone, reduceone, expandtwo, reducetwo),
     )
-    packed = jnp.concatenate([expandone, reduceone, expandtwo, reducetwo, thin], axis=0)
-    packed = share(packed)
-    shards = (expandone, reduceone, expandtwo, reducetwo)
-    sizes = [shard.shape[0] for shard in shards]
-    wide_rows = sum(sizes)
-    thin = lax.all_gather(packed[:, wide_rows:], "dp", axis=0, tiled=True)
-    thin = prep_thin(thin, width, hidden)
+    found = find_rows(asked_rows, embed_table.T)
+    packed = share(packed, asked_rows)
+    split = expandone.shape[0] + THIN_ROWS
     first, orders = dp_orders()
-    parts = [packed[:, : sizes[0]], packed[:, sizes[0] : wide_rows]]
-    own, came = spread([part.reshape(-1, hidden) for part in parts])
+    parts = [packed[:, :split], packed[:, split:]]
+    own, came, _, found = spread([part.reshape(-1, hidden) for part in parts], early=found)
+    returned = lax.all_to_all(found, ("dp", "fsdp"), split_axis=0, concat_axis=0, tiled=True)
     bit = (lax.axis_index("dp") & first).reshape(1)
     places = [arrival(order, first, group) for order in orders]
+    thin = prep_thin(bit, own[0], came[0], places[0], width, hidden)
+    sizes = [shard.shape[0] for shard in (expandone, reduceone, expandtwo, reducetwo)]
     if all(size % 16 == 0 for size in sizes):
-        weights = (bit, *own, *came)
+        weights = (*own, *came)
     else:
         whole = [
             in_order(mine, other, bit[0], place, part.shape[1])
             for mine, other, place, part in zip(own, came, places, parts)
         ]
-        whole = jnp.concatenate(whole, axis=1)
-        starts = [sum(sizes[:index]) for index in range(4)]
+        starts = [0, 0, sizes[1], sizes[1] + sizes[2]]
         weights = tuple(
-            whole[:, start : start + size].reshape(-1, hidden) for start, size in zip(starts, sizes)
+            whole[min(index, 1)][:, start : start + size].reshape(-1, hidden)
+            for index, (start, size) in enumerate(zip(starts, sizes))
         )
         places = None
 
-    found = find_rows(asked_rows, embed_table.T)
-    returned = lax.all_to_all(found, ("dp", "fsdp"), split_axis=0, concat_axis=0, tiled=True)
+    thin, returned = lax.optimization_barrier((thin, returned))
     flipped = place_rows(returned, rank, owner_rows)
     chunk = 16 * devices
     grad_rows = -(-(6 * (width + 3 * hidden) + 2 * hidden) // chunk) * chunk
-    logits, flipped_grad, grads = dense(flipped, weights, places, thin, logit_cot, grad_rows)
-
-    def send(flipped_grad):
+    logits, flipped_grad, kept, sent = dense(bit, flipped, weights, places, thin, logit_cot, grad_rows)
+
+    def prepare(flipped_grad):
         return send_rows(flipped_grad, rank, owner_rows, capacity)
 
-    done, outgoing = sum_grads(grads, flipped_grad, send, width, hidden)
-    incoming = lax.all_to_all(outgoing, ("dp", "fsdp"), split_axis=0, concat_axis=0, tiled=True)
-    table_grad = add_rows(incoming, asked_rows, embed_table.shape[0])
-    return (logits, flipped_grad.T, table_grad.T, *done)
+    def finish_rows(incoming):
+        return add_rows(incoming, asked_rows, embed_table.shape[0])
+
+    done, table_grad, x_grad = sum_grads(kept, sent, flipped_grad, prepare, finish_rows, width, hidden)
+    return (logits, x_grad, table_grad.T, *done)
 
 
 def solution(mesh):

time: 237 us -> 217 us (0.916)
  blocking collectives: 11.9 us -> 0 us
  local copies, waits for them, and re-layouts: 10.9 us -> 3.64 us
  waiting for transfers between devices: 93.8 us -> 89.8 us
  starting transfers between devices: 41 us -> 44.8 us
    all_gather x1 -> x0, blocking collectives: 11.9 us -> none  [on_device(): thin = lax.all_gather(packed[:, wide_rows:], 'dp', axis=0, tiled=True)]
    ppermute x9, waiting for transfers between devices: 29 us -> 23.6 us  [swap_groups(): return lax.ppermute(values, 'fsdp', partners(mask, lax.axis_size('fsdp')))]
    dynamic_slice x5 -> x4, local copies, waits for them, and re-layouts: 3.96 us -> 0.2 us  [the longest x2 0.16 us: cut(): return (sent, lax.dynamic_slice_in_dim(values, bit * rows, rows, 0))]
    all_to_all x1, waiting for transfers between devices: 4.25 us -> 7.25 us  [on_device(): lax.all_to_all(request, ('dp', 'fsdp'), split_axis=0, concat_axis=0, tile...]
    unnamed x17, local copies, waits for them, and re-layouts: 5.94 us -> 3.19 us
  transfers between devices with their start and end apart: 29 -> 29, of which waited for: 17 -> 18; matrix products, arithmetic and copies ran while one was open for 2% -> 1% of each run, Pallas kernels for 16% -> 17%
where the time goes in v2:
time: 217 us
  waiting for transfers between devices  89.8 us (41%)
  Pallas kernels  72 us (33%)
  starting transfers between devices  44.8 us (21%)
  other arithmetic  5.12 us (2%)
  local copies, waits for them, and re-layouts  3.64 us (2%)
    ppermute x17, waiting for transfers between devices, swap_with(): return lax.ppermute(values, 'dp', partners(mask, size))  59 us
    pallas_call x1, Pallas kernels, dense(): pl.pallas_call(functools.partial(dense_body, places), out_shape=(jax.Shap...  26.5 us
    ppermute x9, waiting for transfers between devices, swap_groups(): return lax.ppermute(values, 'fsdp', partners(mask, lax.axis_size('fsdp')))  23.6 us
    ppermute x17, starting transfers between devices, swap_with(): return lax.ppermute(values, 'dp', partners(mask, size))  15.7 us
    ppermute x9, starting transfers between devices, swap_groups(): return lax.ppermute(values, 'fsdp', partners(mask, lax.axis_size('fsdp')))  15.4 us
    pallas_call x1, Pallas kernels, find_rows(): local_kernel(find_body, jax.ShapeDtypeStruct((devices, width, capacity),...  9.34 us
    pallas_call x1, Pallas kernels, add_rows(): local_kernel(add_body, jax.ShapeDtypeStruct((width, rows), jnp.float32),...  8.4 us
    pallas_call x1, Pallas kernels, send_rows(): local_kernel(send_body, jax.ShapeDtypeStruct((devices, width, capacity),...  7.83 us
  transfers between devices with their start and end apart: 29, of which 18 were waited for; matrix products, arithmetic and copies ran while one was open for 1% of the time, Pallas kernels for 17%

profile of v2, /device:TPU:0, one launch (start us, length us, event | category | flops | bytes accessed | tf_op | source)
XLA Modules:
  0.0 216.7 jit_solution(10448411020444247023)
XLA Ops:
  0.7 1.6 shard_map.356
  2.3 5.0 %collective-permute-start.2 = (bf16[288,256]{1,0:T(8,128)(2,1)}, bf16[288,256]{1,0:T(8,128)(2,1)S(1)}, u32[]{:S(2)}, u32[]{:S(2)}) collective-permute-start(bf16[288,256]{1,0:T(8,128)(2,1)} %shard_map.356), channel_id=1, source_target_pairs={{0,3},{1,2},{2,1},{3,0},{4,7},{5,6},{6,5},{7,4},{8,11},{9,10},{10,... | collective-permute-start | bytes 442376 | tf_op jit(solution)/shard_map/ppermute | solution.py:1021
  7.3 0.6 collective-permute-start
  7.9 2.4 %shard_map.357 = (s32[32,1,256]{2,1,0:T(1,128)}, s32[32,512]{1,0:T(8,128)}) custom-call(s32[8,512]{1,0:T(8,128)} %bitcast.53, s32[8,512]{1,0:T(8,128)} %bitcast.61), custom_call_target="tpu_custom_call" | custom-call | flops 150994944 | bytes 98304 | tf_op jit(solution)/shard_map/pallas_call | solution.py:66
  10.4 6.0 %all-to-all-start = ((s32[32,1,256]{2,1,0:T(1,128)}), s32[32,1,256]{2,1,0:T(1,128)S(1)}, u32[]{:S(2)}, u32[]{:S(2)}) async-start(s32[32,1,256]{2,1,0:T(1,128)} %get-tuple-element.85), calls=%async_computation | async-start | bytes 65536 | tf_op jit(solution)/shard_map/all_to_all | solution.py:1158
  16.4 7.2 %all-to-all-done.request_ref = s32[32,1,256]{2,1,0:T(1,128)S(1)} async-done(((s32[32,1,256]{2,1,0:T(1,128)}), s32[32,1,256]{2,1,0:T(1,128)S(1)}, u32[]{:S(2)}, u32[]{:S(2)}) %all-to-all-start) | async-done | bytes 32800 | tf_op jit(solution)/shard_map/all_to_all | solution.py:1158
  23.7 1.0 select_bitcast_fusion.3
  24.8 0.7 collective-permute-start.3
  26.0 9.3 %shard_map.358 = bf16[32,64,256]{2,1,0:T(8,128)(2,1)} custom-call(s32[32,1,256]{2,1,0:T(1,128)} %copy-done.7, bf16[64,4096]{1,0:T(8,128)(2,1)} %bitcast.59), custom_call_target="tpu_custom_call" | custom-call | flops 4294967296 | bytes 1572864 | tf_op jit(solution)/shard_map/pallas_call | solution.py:106
  35.6 1.6 collective-permute-start.5
  37.2 3.4 %all-to-all-start.1 = ((bf16[32,64,256]{2,1,0:T(8,128)(2,1)}), bf16[32,64,256]{2,1,0:T(8,128)(2,1)}, u32[]{:S(2)}, u32[]{:S(2)}) async-start(bf16[32,64,256]{2,1,0:T(8,128)(2,1)} %shard_map.358), calls=%async_computation.1 | async-start | bytes 2097152 | tf_op jit(solution)/shard_map/all_to_all | solution.py:1170
  40.6 1.6 collective-permute-start.6
  42.2 15.1 %collective-permute-done.5 = bf16[1152,256]{1,0:T(8,128)(2,1)S(1)} collective-permute-done((bf16[1152,256]{1,0:T(8,128)(2,1)S(1)}, bf16[1152,256]{1,0:T(8,128)(2,1)S(1)}, u32[]{:S(2)}, u32[]{:S(2)}) %collective-permute-start.5) | collective-permute-done | bytes 589856 | tf_op jit(solution)/shard_map/ppermute | solution.py:998
  57.5 9.5 %collective-permute-done.6 = bf16[1152,256]{1,0:T(8,128)(2,1)S(1)} collective-permute-done((bf16[1152,256]{1,0:T(8,128)(2,1)S(1)}, bf16[1152,256]{1,0:T(8,128)(2,1)S(1)}, u32[]{:S(2)}, u32[]{:S(2)}) %collective-permute-start.6) | collective-permute-done | bytes 589856 | tf_op jit(solution)/shard_map/ppermute | solution.py:998
  67.9 3.2 %collective-permute-done.7.came_ref.refs_3_ = bf16[2304,256]{1,0:T(8,128)(2,1)S(1)} collective-permute-done((bf16[2304,256]{1,0:T(8,128)(2,1)S(1)}, bf16[2304,256]{1,0:T(8,128)(2,1)S(1)}, u32[]{:S(2)}, u32[]{:S(2)}) %collective-permute-start.7) | collective-permute-done | bytes 1179680 | tf_op jit(solution)/shard_map/ppermute | solution.py:998
  71.1 1.0 copy-done.4
  72.1 3.2 %shard_map.359 = (f32[256,64]{1,0:T(8,128)}, bf16[32,512]{1,0:T(8,128)(2,1)}, bf16[512,32]{1,0:T(8,128)(2,1)}, bf16[16,256]{1,0:T(8,128)(2,1)}, bf16[512,16]{1,0...) custom-call(s32[1]{0:T(128)} %bitcast.bit_ref.refs_0_, ...), custom_call_target="tpu_custom_call" | custom-call | bytes 2359296 | tf_op jit(solution)/shard_map/pallas_call | solution.py:365
  75.3 6.5 %shard_map.360.refs_5_ = bf16[512,512]{1,0:T(8,128)(2,1)} custom-call(bf16[32,64,256]{2,1,0:T(8,128)(2,1)} %all-to-all-done.1.found_ref, s32[32,512]{1,0:T(8,128)} %get-tuple-element.105.rank_ref, s32[8,512]{1,0:T(8,128)} %bitcast.54), custom_call_target="tpu_custom_call" | custom-call | flops 536870912 | bytes 1572864 | tf_op jit(solution)/shard_map/pallas_call | solution.py:144
  81.8 26.5 %shard_map.361 = (f32[2,512]{1,0:T(2,128)}, f32[512,512]{1,0:T(8,128)}, bf16[4096,256]{1,0:T(8,128)(2,1)}, bf16[4096,256]{1,0:T(8,128)(2,1)}) custom-call(s32[1]{0:T(128)} %bitcast.bit_ref.refs_0_, bf16[2304,256]{1,0:T(8,128)(2,1)} %copy-done, bf16[2304,256]{1,0:T(8,128)(2,1)} %copy-done.5, bf16[2304,256]{1,0:T(8,128)(2,1)} %copy-done.4, ...), custom_call_target="tpu_custom_call" | custom-call | flops 6241124352 | bytes 25165824 | tf_op jit(solution)/shard_map/pallas_call | solution.py:848
  108.5 4.2 %collective-permute-done.9 = bf16[4096,256]{1,0:T(8,128)(2,1)S(1)} collective-permute-done((bf16[4096,256]{1,0:T(8,128)(2,1)}, bf16[4096,256]{1,0:T(8,128)(2,1)S(1)}, u32[]{:S(2)}, u32[]{:S(2)}) %collective-permute-start.9) | collective-permute-done | bytes 2097184 | tf_op jit(solution)/shard_map/ppermute | solution.py:998
  112.8 2.1 add_convert_fusion
  115.2 1.3 collective-permute-start.10
  117.0 7.8 %shard_map.362 = bf16[32,64,256]{2,1,0:T(8,128)(2,1)} custom-call(f32[512,512]{1,0:T(8,128)} %get-tuple-element.123.grad_ref, s32[32,512]{1,0:T(8,128)} %get-tuple-element.105.rank_ref, s32[8,512]{1,0:T(8,128)} %bitcast.55), custom_call_target="tpu_custom_call" | custom-call | flops 536870912 | bytes 2097152 | tf_op jit(solution)/shard_map/pallas_call | solution.py:180
  124.8 4.4 %collective-permute-done.10 = bf16[1024,256]{1,0:T(8,128)(2,1)S(1)} collective-permute-done((bf16[1024,256]{1,0:T(8,128)(2,1)S(1)}, bf16[1024,256]{1,0:T(8,128)(2,1)S(1)}, u32[]{:S(2)}, u32[]{:S(2)}) %collective-permute-start.10) | collective-permute-done | bytes 524320 | tf_op jit(solution)/shard_map/ppermute | solution.py:998
  129.4 0.8 collective-permute-done.11
  130.3 4.3 %all-to-all-start.2 = ((bf16[32,64,256]{2,1,0:T(8,128)(2,1)}), bf16[32,64,256]{2,1,0:T(8,128)(2,1)S(1)}, u32[]{:S(2)}, u32[]{:S(2)}) async-start(bf16[32,64,256]{2,1,0:T(8,128)(2,1)} %shard_map.362), calls=%async_computation.2 | async-start | bytes 2097152 | tf_op jit(solution)/shard_map/all_to_all | solution.py:1115
  134.7 1.6 collective-permute-start.13
  136.3 1.5 collective-permute-start.12
  137.8 13.5 %collective-permute-done.13 = bf16[512,256]{1,0:T(8,128)(2,1)S(1)} collective-permute-done((bf16[512,256]{1,0:T(8,128)(2,1)S(1)}, bf16[512,256]{1,0:T(8,128)(2,1)S(1)}, u32[]{:S(2)}, u32[]{:S(2)}) %collective-permute-start.13) | collective-permute-done | bytes 262176 | tf_op jit(solution)/shard_map/ppermute | solution.py:998
  151.6 1.5 collective-permute-start.14
  153.0 3.3 %collective-permute-start.16 = (bf16[256,256]{1,0:T(8,128)(2,1)S(1)}, bf16[256,256]{1,0:T(8,128)(2,1)S(1)}, u32[]{:S(2)}, u32[]{:S(2)}) collective-permute-start(bf16[256,256]{1,0:T(8,128)(2,1)S(1)} %get-tuple-element.205), channel_id=1, source_target_pairs={{0,3},{1,2},{2,1},{3,0},{4,7},{5,6},{6,5},{7,4},{8,11},{9,10},{10,... | collective-permute-start | bytes 393224 | tf_op jit(solution)/shard_map/ppermute | solution.py:1021
  156.9 3.2 %collective-permute-done.14 = bf16[256,256]{1,0:T(8,128)(2,1)S(1)} collective-permute-done((bf16[256,256]{1,0:T(8,128)(2,1)S(1)}, bf16[256,256]{1,0:T(8,128)(2,1)S(1)}, u32[]{:S(2)}, u32[]{:S(2)}) %collective-permute-start.14) | collective-permute-done | bytes 131104 | tf_op jit(solution)/shard_map/ppermute | solution.py:1021
  160.1 3.4 %collective-permute-done.16 = bf16[256,256]{1,0:T(8,128)(2,1)S(1)} collective-permute-done((bf16[256,256]{1,0:T(8,128)(2,1)S(1)}, bf16[256,256]{1,0:T(8,128)(2,1)S(1)}, u32[]{:S(2)}, u32[]{:S(2)}) %collective-permute-start.16) | collective-permute-done | bytes 131104 | tf_op jit(solution)/shard_map/ppermute | solution.py:1021
  163.5 8.4 %collective-permute-done.15 = bf16[256,256]{1,0:T(8,128)(2,1)S(1)} collective-permute-done((bf16[256,256]{1,0:T(8,128)(2,1)S(1)}, bf16[256,256]{1,0:T(8,128)(2,1)S(1)}, u32[]{:S(2)}, u32[]{:S(2)}) %collective-permute-start.15) | collective-permute-done | bytes 131104 | tf_op jit(solution)/shard_map/ppermute | solution.py:1021
  172.1 2.0 collective-permute-start.18
  174.1 2.4 %collective-permute-start.17 = (bf16[256,256]{1,0:T(8,128)(2,1)S(1)}, bf16[256,256]{1,0:T(8,128)(2,1)S(1)}, u32[]{:S(2)}, u32[]{:S(2)}) collective-permute-start(bf16[256,256]{1,0:T(8,128)(2,1)S(1)} %add_convert_fusion.5), channel_id=1, source_target_pairs={{0,3},{1,2},{2,1},{3,0},{4,7},{5,6},{6,5},{7,4},{8,11},{9,10},{10,... | collective-permute-start | bytes 393224 | tf_op jit(solution)/shard_map/ppermute | solution.py:1021
  176.4 2.3 %collective-permute-done.19 = bf16[256,256]{1,0:T(8,128)(2,1)S(1)} collective-permute-done((bf16[256,256]{1,0:T(8,128)(2,1)S(1)}, bf16[256,256]{1,0:T(8,128)(2,1)S(1)}, u32[]{:S(2)}, u32[]{:S(2)}) %collective-permute-start.19) | collective-permute-done | bytes 131104 | tf_op jit(solution)/shard_map/ppermute | solution.py:1021
  178.8 6.2 %collective-permute-done.18 = bf16[256,256]{1,0:T(8,128)(2,1)S(1)} collective-permute-done((bf16[256,256]{1,0:T(8,128)(2,1)S(1)}, bf16[256,256]{1,0:T(8,128)(2,1)S(1)}, u32[]{:S(2)}, u32[]{:S(2)}) %collective-permute-start.18) | collective-permute-done | bytes 131104 | tf_op jit(solution)/shard_map/ppermute | solution.py:1021
  185.2 1.5 collective-permute-start.20
  186.7 1.5 collective-permute-start.22
  188.2 3.8 %collective-permute-done.20 = bf16[512,256]{1,0:T(8,128)(2,1)S(1)} collective-permute-done((bf16[512,256]{1,0:T(8,128)(2,1)S(1)}, bf16[512,256]{1,0:T(8,128)(2,1)S(1)}, u32[]{:S(2)}, u32[]{:S(2)}) %collective-permute-start.20) | collective-permute-done | bytes 262176 | tf_op jit(solution)/shard_map/ppermute | solution.py:998
  192.1 1.7 collective-permute-start.21
  193.8 2.0 collective-permute-done.22
  196.3 8.4 %shard_map.363 = f32[64,4096]{1,0:T(8,128)} custom-call(bf16[32,64,256]{2,1,0:T(8,128)(2,1)} %copy-done.6, s32[32,1,256]{2,1,0:T(1,128)} %copy-done.7), custom_call_target="tpu_custom_call" | custom-call | flops 4294967296 | bytes 2097152 | tf_op jit(solution)/shard_map/pallas_call | solution.py:228
  206.9 1.3 copy.41
  208.2 0.6 collective-permute-done.24.came_a_ref
  208.7 1.5 collective-permute-done.25.came_b_ref
  210.2 6.3 %shard_map.364 = (f32[3072,256]{1,0:T(8,128)}, f32[1536]{0:T(1024)}, f32[1536,256]{1,0:T(8,128)}, f32[1536]{0:T(1024)}, f32[1536]{0:T(1024)}, /*index=5*/f32[4,1...) custom-call(s32[1]{0:T(128)} %bitcast.bit_ref.refs_0_, ...), custom_call_target="tpu_custom_call" | custom-call | bytes 25165824 | tf_op jit(solution)/shard_map/pallas_call | solution.py:981
  (70 shorter events, 6.8 us)
Async XLA Ops:
  2.3 21.4 %collective-permute-start.2 = (bf16[288,256]{1,0:T(8,128)(2,1)}, bf16[288,256]{1,0:T(8,128)(2,1)S(1)}, u32[]{:S(2)}, u32[]{:S(2)}) collective-permute-start(bf16[288,256]{1,0:T(8,128)(2,1)} %shard_map.356), channel_id=1, source_target_pairs={{0,3},{1,2},{2,1},{3,0},{4,7},{5,6},{6,5},{7,4},{8,11},{9,10},{10,... | collective-permute-start | bytes 442376 | tf_op jit(solution)/shard_map/ppermute | solution.py:1021
  7.3 16.4 %collective-permute-start.1 = (bf16[288,256]{1,0:T(8,128)(2,1)}, bf16[288,256]{1,0:T(8,128)(2,1)S(1)}, u32[]{:S(2)}, u32[]{:S(2)}) collective-permute-start(bf16[288,256]{1,0:T(8,128)(2,1)} %shard_map.356), channel_id=1, source_target_pairs={{0,2},{1,3},{2,0},{3,1},{4,6},{5,7},{6,4},{7,5},{8,10},{9,11},{10,... | collective-permute-start | bytes 442376 | tf_op jit(solution)/shard_map/ppermute | solution.py:1021
  7.3 16.4 %collective-permute-start = (bf16[288,256]{1,0:T(8,128)(2,1)}, bf16[288,256]{1,0:T(8,128)(2,1)S(1)}, u32[]{:S(2)}, u32[]{:S(2)}) collective-permute-start(bf16[288,256]{1,0:T(8,128)(2,1)} %shard_map.356), channel_id=1, source_target_pairs={{0,1},{1,0},{2,3},{3,2},{4,5},{5,4},{6,7},{7,6},{8,9},{9,8},{10,11... | collective-permute-start | bytes 442376 | tf_op jit(solution)/shard_map/ppermute | solution.py:1021
  10.4 13.3 %all-to-all-start = ((s32[32,1,256]{2,1,0:T(1,128)}), s32[32,1,256]{2,1,0:T(1,128)S(1)}, u32[]{:S(2)}, u32[]{:S(2)}) async-start(s32[32,1,256]{2,1,0:T(1,128)} %get-tuple-element.85), calls=%async_computation | async-start | bytes 65536 | tf_op jit(solution)/shard_map/all_to_all | solution.py:1158
  23.7 2.4 %copy-start.7 = (s32[32,1,256]{2,1,0:T(1,128)}, s32[32,1,256]{2,1,0:T(1,128)S(1)}, u32[]{:S(2)}) copy-start(s32[32,1,256]{2,1,0:T(1,128)S(1)} %all-to-all-done.request_ref) | copy-start | bytes 98308
  24.8 10.5 %collective-permute-start.3 = (bf16[576,256]{1,0:T(8,128)(2,1)S(1)}, bf16[576,256]{1,0:T(8,128)(2,1)S(1)}, u32[]{:S(2)}, u32[]{:S(2)}) collective-permute-start(bf16[576,256]{1,0:T(8,128)(2,1)S(1)} %bitcast.48), channel_id=1, source_target_pairs={{0,16},{4,20},{8,24},{12,28},{16,0},{20,4},{24,8},{28,12},{1,17},{... | collective-permute-start | bytes 884744 | tf_op jit(solution)/shard_map/ppermute | solution.py:998
  25.5 9.9 %collective-permute-start.4 = (bf16[576,256]{1,0:T(8,128)(2,1)S(1)}, bf16[576,256]{1,0:T(8,128)(2,1)S(1)}, u32[]{:S(2)}, u32[]{:S(2)}) collective-permute-start(bf16[576,256]{1,0:T(8,128)(2,1)S(1)} %bitcast.47), channel_id=1, source_target_pairs={{0,8},{4,12},{8,0},{12,4},{16,24},{20,28},{24,16},{28,20},{1,9},{5... | collective-permute-start | bytes 884744 | tf_op jit(solution)/shard_map/ppermute | solution.py:998
  35.6 21.7 %collective-permute-start.5 = (bf16[1152,256]{1,0:T(8,128)(2,1)S(1)}, bf16[1152,256]{1,0:T(8,128)(2,1)S(1)}, u32[]{:S(2)}, u32[]{:S(2)}) collective-permute-start(bf16[1152,256]{1,0:T(8,128)(2,1)S(1)} %get-tuple-element.90), channel_id=1, source_target_pairs={{0,8},{4,12},{8,0},{12,4},{16,24},{20,28},{24,16},{28,20},{1,9},{5... | collective-permute-start | bytes 1769480 | tf_op jit(solution)/shard_map/ppermute | solution.py:998
  37.2 38.2 %all-to-all-start.1 = ((bf16[32,64,256]{2,1,0:T(8,128)(2,1)}), bf16[32,64,256]{2,1,0:T(8,128)(2,1)}, u32[]{:S(2)}, u32[]{:S(2)}) async-start(bf16[32,64,256]{2,1,0:T(8,128)(2,1)} %shard_map.358), calls=%async_computation.1 | async-start | bytes 2097152 | tf_op jit(solution)/shard_map/all_to_all | solution.py:1170
  40.6 26.5 %collective-permute-start.6 = (bf16[1152,256]{1,0:T(8,128)(2,1)S(1)}, bf16[1152,256]{1,0:T(8,128)(2,1)S(1)}, u32[]{:S(2)}, u32[]{:S(2)}) collective-permute-start(bf16[1152,256]{1,0:T(8,128)(2,1)S(1)} %get-tuple-element.91), channel_id=1, source_target_pairs={{0,16},{4,20},{8,24},{12,28},{16,0},{20,4},{24,8},{28,12},{1,17},{... | collective-permute-start | bytes 1769480 | tf_op jit(solution)/shard_map/ppermute | solution.py:998
  57.5 9.8 %copy-start = (bf16[2304,256]{1,0:T(8,128)(2,1)}, bf16[2304,256]{1,0:T(8,128)(2,1)S(1)}, u32[]{:S(2)}) copy-start(bf16[2304,256]{1,0:T(8,128)(2,1)S(1)} %pad_maximum_fusion.own_ref.refs_1_) | copy-start | bytes 3538948
  67.3 14.5 %copy-start.5 = (bf16[2304,256]{1,0:T(8,128)(2,1)}, bf16[2304,256]{1,0:T(8,128)(2,1)S(1)}, u32[]{:S(2)}) copy-start(bf16[2304,256]{1,0:T(8,128)(2,1)S(1)} %pad_maximum_fusion.1.refs_2_) | copy-start | bytes 3538948
  67.3 3.8 %collective-permute-start.7 = (bf16[2304,256]{1,0:T(8,128)(2,1)S(1)}, bf16[2304,256]{1,0:T(8,128)(2,1)S(1)}, u32[]{:S(2)}, u32[]{:S(2)}) collective-permute-start(bf16[2304,256]{1,0:T(8,128)(2,1)S(1)} %pad_maximum_fusion.own_ref.refs_1_), channel_id=1, source_target_pairs={{0,4},{4,0},{8,12},{12,8},{16,20},{20,16},{24,28},{28,24},{1,5},{5... | collective-permute-start | bytes 3538952 | tf_op jit(solution)/shard_map/ppermute | solution.py:998
  67.4 14.4 %collective-permute-start.8 = (bf16[2304,256]{1,0:T(8,128)(2,1)S(1)}, bf16[2304,256]{1,0:T(8,128)(2,1)}, u32[]{:S(2)}, u32[]{:S(2)}) collective-permute-start(bf16[2304,256]{1,0:T(8,128)(2,1)S(1)} %pad_maximum_fusion.1.refs_2_), channel_id=1, source_target_pairs={{0,4},{4,0},{8,12},{12,8},{16,20},{20,16},{24,28},{28,24},{1,5},{5... | collective-permute-start | bytes 3538952 | tf_op jit(solution)/shard_map/ppermute | solution.py:998
  71.1 1.0 copy-start.4
  108.3 4.4 %collective-permute-start.9 = (bf16[4096,256]{1,0:T(8,128)(2,1)}, bf16[4096,256]{1,0:T(8,128)(2,1)S(1)}, u32[]{:S(2)}, u32[]{:S(2)}) collective-permute-start(bf16[4096,256]{1,0:T(8,128)(2,1)} %get-tuple-element.117), channel_id=1, source_target_pairs={{0,4},{4,0},{8,12},{12,8},{16,20},{20,16},{24,28},{28,24},{1,5},{5... | collective-permute-start | bytes 6291464 | tf_op jit(solution)/shard_map/ppermute | solution.py:998
  115.2 14.0 %collective-permute-start.10 = (bf16[1024,256]{1,0:T(8,128)(2,1)S(1)}, bf16[1024,256]{1,0:T(8,128)(2,1)S(1)}, u32[]{:S(2)}, u32[]{:S(2)}) collective-permute-start(bf16[1024,256]{1,0:T(8,128)(2,1)S(1)} %get-tuple-element.120), channel_id=1, source_target_pairs={{0,8},{4,12},{8,0},{12,4},{16,24},{20,28},{24,16},{28,20},{1,9},{5... | collective-permute-start | bytes 1572872 | tf_op jit(solution)/shard_map/ppermute | solution.py:998
  116.5 13.7 %collective-permute-start.11 = (bf16[1024,256]{1,0:T(8,128)(2,1)S(1)}, bf16[1024,256]{1,0:T(8,128)(2,1)S(1)}, u32[]{:S(2)}, u32[]{:S(2)}) collective-permute-start(bf16[1024,256]{1,0:T(8,128)(2,1)S(1)} %get-tuple-element.122), channel_id=1, source_target_pairs={{0,16},{4,20},{8,24},{12,28},{16,0},{20,4},{24,8},{28,12},{1,17},{... | collective-permute-start | bytes 1572872 | tf_op jit(solution)/shard_map/ppermute | solution.py:998
  130.3 41.7 %all-to-all-start.2 = ((bf16[32,64,256]{2,1,0:T(8,128)(2,1)}), bf16[32,64,256]{2,1,0:T(8,128)(2,1)S(1)}, u32[]{:S(2)}, u32[]{:S(2)}) async-start(bf16[32,64,256]{2,1,0:T(8,128)(2,1)} %shard_map.362), calls=%async_computation.2 | async-start | bytes 2097152 | tf_op jit(solution)/shard_map/all_to_all | solution.py:1115
  134.7 16.6 %collective-permute-start.13 = (bf16[512,256]{1,0:T(8,128)(2,1)S(1)}, bf16[512,256]{1,0:T(8,128)(2,1)S(1)}, u32[]{:S(2)}, u32[]{:S(2)}) collective-permute-start(bf16[512,256]{1,0:T(8,128)(2,1)S(1)} %constant_dynamic-slice_fusion.3), channel_id=1, source_target_pairs={{0,8},{4,12},{8,0},{12,4},{16,24},{20,28},{24,16},{28,20},{1,9},{5... | collective-permute-start | bytes 786440 | tf_op jit(solution)/shard_map/ppermute | solution.py:998
  136.3 15.1 %collective-permute-start.12 = (bf16[512,256]{1,0:T(8,128)(2,1)S(1)}, bf16[512,256]{1,0:T(8,128)(2,1)S(1)}, u32[]{:S(2)}, u32[]{:S(2)}) collective-permute-start(bf16[512,256]{1,0:T(8,128)(2,1)S(1)} %constant_dynamic-slice_fusion.4), channel_id=1, source_target_pairs={{0,16},{4,20},{8,24},{12,28},{16,0},{20,4},{24,8},{28,12},{1,17},{... | collective-permute-start | bytes 786440 | tf_op jit(solution)/shard_map/ppermute | solution.py:998
  151.6 8.5 %collective-permute-start.14 = (bf16[256,256]{1,0:T(8,128)(2,1)S(1)}, bf16[256,256]{1,0:T(8,128)(2,1)S(1)}, u32[]{:S(2)}, u32[]{:S(2)}) collective-permute-start(bf16[256,256]{1,0:T(8,128)(2,1)S(1)} %get-tuple-element.204), channel_id=1, source_target_pairs={{0,1},{1,0},{2,3},{3,2},{4,5},{5,4},{6,7},{7,6},{8,9},{9,8},{10,11... | collective-permute-start | bytes 393224 | tf_op jit(solution)/shard_map/ppermute | solution.py:1021
  153.0 10.5 %collective-permute-start.16 = (bf16[256,256]{1,0:T(8,128)(2,1)S(1)}, bf16[256,256]{1,0:T(8,128)(2,1)S(1)}, u32[]{:S(2)}, u32[]{:S(2)}) collective-permute-start(bf16[256,256]{1,0:T(8,128)(2,1)S(1)} %get-tuple-element.205), channel_id=1, source_target_pairs={{0,3},{1,2},{2,1},{3,0},{4,7},{5,6},{6,5},{7,4},{8,11},{9,10},{10,... | collective-permute-start | bytes 393224 | tf_op jit(solution)/shard_map/ppermute | solution.py:1021
  156.4 15.5 %collective-permute-start.15 = (bf16[256,256]{1,0:T(8,128)(2,1)S(1)}, bf16[256,256]{1,0:T(8,128)(2,1)S(1)}, u32[]{:S(2)}, u32[]{:S(2)}) collective-permute-start(bf16[256,256]{1,0:T(8,128)(2,1)S(1)} %get-tuple-element.206), channel_id=1, source_target_pairs={{0,2},{1,3},{2,0},{3,1},{4,6},{5,7},{6,4},{7,5},{8,10},{9,11},{10,... | collective-permute-start | bytes 393224 | tf_op jit(solution)/shard_map/ppermute | solution.py:1021
  172.0 20.1 %copy-start.6 = (bf16[32,64,256]{2,1,0:T(8,128)(2,1)}, bf16[32,64,256]{2,1,0:T(8,128)(2,1)S(1)}, u32[]{:S(2)}) copy-start(bf16[32,64,256]{2,1,0:T(8,128)(2,1)S(1)} %all-to-all-done.2.came_ref) | copy-start | bytes 3145732
  172.0 6.8 %collective-permute-start.19 = (bf16[256,256]{1,0:T(8,128)(2,1)S(1)}, bf16[256,256]{1,0:T(8,128)(2,1)S(1)}, u32[]{:S(2)}, u32[]{:S(2)}) collective-permute-start(bf16[256,256]{1,0:T(8,128)(2,1)S(1)} %add_convert_fusion.5), channel_id=1, source_target_pairs={{0,1},{1,0},{2,3},{3,2},{4,5},{5,4},{6,7},{7,6},{8,9},{9,8},{10,11... | collective-permute-start | bytes 393224 | tf_op jit(solution)/shard_map/ppermute | solution.py:1021
  172.1 12.9 %collective-permute-start.18 = (bf16[256,256]{1,0:T(8,128)(2,1)S(1)}, bf16[256,256]{1,0:T(8,128)(2,1)S(1)}, u32[]{:S(2)}, u32[]{:S(2)}) collective-permute-start(bf16[256,256]{1,0:T(8,128)(2,1)S(1)} %add_convert_fusion.5), channel_id=1, source_target_pairs={{0,2},{1,3},{2,0},{3,1},{4,6},{5,7},{6,4},{7,5},{8,10},{9,11},{10,... | collective-permute-start | bytes 393224 | tf_op jit(solution)/shard_map/ppermute | solution.py:1021
  174.1 10.9 %collective-permute-start.17 = (bf16[256,256]{1,0:T(8,128)(2,1)S(1)}, bf16[256,256]{1,0:T(8,128)(2,1)S(1)}, u32[]{:S(2)}, u32[]{:S(2)}) collective-permute-start(bf16[256,256]{1,0:T(8,128)(2,1)S(1)} %add_convert_fusion.5), channel_id=1, source_target_pairs={{0,3},{1,2},{2,1},{3,0},{4,7},{5,6},{6,5},{7,4},{8,11},{9,10},{10,... | collective-permute-start | bytes 393224 | tf_op jit(solution)/shard_map/ppermute | solution.py:1021
  185.2 6.8 %collective-permute-start.20 = (bf16[512,256]{1,0:T(8,128)(2,1)S(1)}, bf16[512,256]{1,0:T(8,128)(2,1)S(1)}, u32[]{:S(2)}, u32[]{:S(2)}) collective-permute-start(bf16[512,256]{1,0:T(8,128)(2,1)S(1)} %bitcast.50), channel_id=1, source_target_pairs={{0,16},{4,20},{8,24},{12,28},{16,0},{20,4},{24,8},{28,12},{1,17},{... | collective-permute-start | bytes 786440 | tf_op jit(solution)/shard_map/ppermute | solution.py:998
  186.7 9.2 %collective-permute-start.22 = (bf16[512,256]{1,0:T(8,128)(2,1)S(1)}, bf16[512,256]{1,0:T(8,128)(2,1)S(1)}, u32[]{:S(2)}, u32[]{:S(2)}) collective-permute-start(bf16[512,256]{1,0:T(8,128)(2,1)S(1)} %bitcast.49), channel_id=1, source_target_pairs={{0,8},{4,12},{8,0},{12,4},{16,24},{20,28},{24,16},{28,20},{1,9},{5... | collective-permute-start | bytes 786440 | tf_op jit(solution)/shard_map/ppermute | solution.py:998
  192.1 12.6 %collective-permute-start.21 = (bf16[1024,256]{1,0:T(8,128)(2,1)S(1)}, bf16[1024,256]{1,0:T(8,128)(2,1)S(1)}, u32[]{:S(2)}, u32[]{:S(2)}) collective-permute-start(bf16[1024,256]{1,0:T(8,128)(2,1)S(1)} %pad_maximum_fusion.9), channel_id=1, source_target_pairs={{0,8},{4,12},{8,0},{12,4},{16,24},{20,28},{24,16},{28,20},{1,9},{5... | collective-permute-start | bytes 1572872 | tf_op jit(solution)/shard_map/ppermute | solution.py:998
  196.0 9.2 %collective-permute-start.23 = (bf16[1024,256]{1,0:T(8,128)(2,1)S(1)}, bf16[1024,256]{1,0:T(8,128)(2,1)S(1)}, u32[]{:S(2)}, u32[]{:S(2)}) collective-permute-start(bf16[1024,256]{1,0:T(8,128)(2,1)S(1)} %pad_maximum_fusion.10), channel_id=1, source_target_pairs={{0,16},{4,20},{8,24},{12,28},{16,0},{20,4},{24,8},{28,12},{1,17},{... | collective-permute-start | bytes 1572872 | tf_op jit(solution)/shard_map/ppermute | solution.py:998
  204.9 1.0 copy-start.1
  204.9 1.9 copy-start.3
  205.5 4.7 %copy-start.2 = (bf16[2048,256]{1,0:T(8,128)(2,1)}, bf16[2048,256]{1,0:T(8,128)(2,1)S(1)}, u32[]{:S(2)}) copy-start(bf16[2048,256]{1,0:T(8,128)(2,1)S(1)} %pad_maximum_fusion.3.own_b_ref) | copy-start | bytes 3145732
  206.0 2.8 %collective-permute-start.24 = (bf16[2048,256]{1,0:T(8,128)(2,1)S(1)}, bf16[2048,256]{1,0:T(8,128)(2,1)}, u32[]{:S(2)}, u32[]{:S(2)}) collective-permute-start(bf16[2048,256]{1,0:T(8,128)(2,1)S(1)} %pad_maximum_fusion.2.own_a_ref), channel_id=1, source_target_pairs={{0,4},{4,0},{8,12},{12,8},{16,20},{20,16},{24,28},{28,24},{1,5},{5... | collective-permute-start | bytes 3145736 | tf_op jit(solution)/shard_map/ppermute | solution.py:998
  206.0 4.3 %collective-permute-start.25 = (bf16[2048,256]{1,0:T(8,128)(2,1)S(1)}, bf16[2048,256]{1,0:T(8,128)(2,1)}, u32[]{:S(2)}, u32[]{:S(2)}) collective-permute-start(bf16[2048,256]{1,0:T(8,128)(2,1)S(1)} %pad_maximum_fusion.3.own_b_ref), channel_id=1, source_target_pairs={{0,4},{4,0},{8,12},{12,8},{16,20},{20,16},{24,28},{28,24},{1,5},{5... | collective-permute-start | bytes 3145736 | tf_op jit(solution)/shard_map/ppermute | solution.py:998

commit v3 on v2

--- a/solution.py
+++ b/solution.py
@@ -97,7 +97,7 @@
         found_ref[source] = picked.astype(jnp.bfloat16)
         return carry
 
-    lax.fori_loop(0, devices, step, 0, unroll=2)
+    lax.fori_loop(0, devices, step, 0, unroll=16)
 
 
 def find_rows(request, table):
@@ -170,7 +170,7 @@
         ).astype(jnp.bfloat16)
         return carry
 
-    lax.fori_loop(0, devices, step, 0, unroll=2)
+    lax.fori_loop(0, devices, step, 0, unroll=16)
 
 
 def send_rows(grad, rank, owner_rows, capacity):
@@ -189,7 +189,7 @@
 def add_body(came_ref, request_ref, out_ref, total_ref):
     devices, width, capacity = came_ref.shape
     span = total_ref.shape[1]
-    group = 4
+    group = 8
     places = iota((span, capacity), 0)
     total_ref[...] = jnp.zeros_like(total_ref)
 
@@ -215,7 +215,7 @@
         )
         return carry
 
-    lax.fori_loop(0, devices // group, step, 0)
+    lax.fori_loop(0, devices // group, step, 0, unroll=4)
     for index in range(ROW_BLOCKS):
         out_ref[:, index * span : (index + 1) * span] = total_ref[
             index * width : (index + 1) * width, :
@@ -389,7 +389,7 @@
     )(bit, own, came)
 
 
-SPAN = 256
+SPAN = 512
 ONES = 16
 
 
@@ -438,26 +438,17 @@
     return probs * (tall - sum_rows(probs * tall))
 
 
-def assemble(bit, own_ref, came_ref, homes, places, blocks):
+def assemble(bit, own_ref, came_ref, homes, places):
+    blocks = len(places[0])
     rows = own_ref.shape[0] // blocks
-    sizes = [home.shape[0] // (2 * blocks) for home in homes]
-
-    def lay(pieces):
-        for half, source in enumerate(pieces):
-            for block in range(blocks):
-                start = block * rows
-                for home, size in zip(homes, sizes):
-                    target = places[half][block] * size
-                    home[target : target + size, :] = source[start : start + size, :]
-                    start += size
-
-    @pl.when(bit == 0)
-    def _():
-        lay((own_ref, came_ref))
-
-    @pl.when(bit != 0)
-    def _():
-        lay((came_ref, own_ref))
+    for half, source in ((bit, own_ref), (1 - bit, came_ref)):
+        for block in range(blocks):
+            start = block * rows
+            for home in homes:
+                size = home.shape[0] // (2 * blocks)
+                place = places[0][block] * size + half * ((places[1][0] - places[0][0]) * size)
+                home[pl.ds(pl.multiple_of(place, 16), size), :] = source[start : start + size, :]
+                start += size
 
 
 def dense_body(places, *refs):
@@ -509,15 +500,13 @@
     ) = refs
     bit = jnp.minimum(bit_ref[0], 1)
     if places is not None:
-        blocks = len(places[0][0])
-        assemble(bit, own_a, came_a, [expand_one_back_ref], places[0], blocks)
+        assemble(bit, own_a, came_a, [expand_one_back_ref], places[0])
         assemble(
             bit,
             own_b,
             came_b,
             [shrink_one_back_ref, expand_two_back_ref, shrink_two_back_ref],
             places[1],
-            blocks,
         )
     for natural, turned in (
         (expand_one_back_ref, expand_one_ref),
@@ -1170,6 +1159,8 @@
     returned = lax.all_to_all(found, ("dp", "fsdp"), split_axis=0, concat_axis=0, tiled=True)
     bit = (lax.axis_index("dp") & first).reshape(1)
     places = [arrival(order, first, group) for order in orders]
+    flipped = place_rows(returned, rank, owner_rows)
+    came, flipped = lax.optimization_barrier((came, flipped))
     thin = prep_thin(bit, own[0], came[0], places[0], width, hidden)
     sizes = [shard.shape[0] for shard in (expandone, reduceone, expandtwo, reducetwo)]
     if all(size % 16 == 0 for size in sizes):
@@ -1186,8 +1177,6 @@
         )
         places = None
 
-    thin, returned = lax.optimization_barrier((thin, returned))
-    flipped = place_rows(returned, rank, owner_rows)
     chunk = 16 * devices
     grad_rows = -(-(6 * (width + 3 * hidden) + 2 * hidden) // chunk) * chunk
     logits, flipped_grad, kept, sent = dense(bit, flipped, weights, places, thin, logit_cot, grad_rows)

time: 217 us -> 207 us (0.954)
  Pallas kernels: 72 us -> 62.1 us
    pallas_call x1, Pallas kernels: 26.5 us -> 21.6 us  [dense(): pl.pallas_call(functools.partial(dense_body, places), out_shape=(jax.Shap...]
  transfers between devices with their start and end apart: 29 -> 29, of which waited for: 18 -> 20; matrix products, arithmetic and copies ran while one was open for 1% -> 1% of each run, Pallas kernels for 17% -> 14%
where the time goes in v3:
time: 207 us; the launch traced here: 206 us
  waiting for transfers between devices  90.9 us (44%)
  Pallas kernels  62.1 us (30%)
  starting transfers between devices  44.1 us (21%)
  other arithmetic  5.11 us (2%)
  local copies, waits for them, and re-layouts  2.8 us (1%)
    ppermute x17, waiting for transfers between devices, swap_with(): return lax.ppermute(values, 'dp', partners(mask, size))  60.1 us
    ppermute x9, waiting for transfers between devices, swap_groups(): return lax.ppermute(values, 'fsdp', partners(mask, lax.axis_size('fsdp')))  23.6 us
    pallas_call x1, Pallas kernels, dense(): pl.pallas_call(functools.partial(dense_body, places), out_shape=(jax.Shap...  21.6 us
    ppermute x9, starting transfers between devices, swap_groups(): return lax.ppermute(values, 'fsdp', partners(mask, lax.axis_size('fsdp')))  15.4 us
    ppermute x17, starting transfers between devices, swap_with(): return lax.ppermute(values, 'dp', partners(mask, size))  14.9 us
    pallas_call x1, Pallas kernels, find_rows(): local_kernel(find_body, jax.ShapeDtypeStruct((devices, width, capacity),...  7.27 us
    all_to_all x1, waiting for transfers between devices, on_device(): lax.all_to_all(request, ('dp', 'fsdp'), split_axis=0, concat_axis=0, tile...  7.25 us
    pallas_call x1, Pallas kernels, add_rows(): local_kernel(add_body, jax.ShapeDtypeStruct((width, rows), jnp.float32),...  6.73 us
  transfers between devices with their start and end apart: 29, of which 20 were waited for; matrix products, arithmetic and copies ran while one was open for 1% of the time, Pallas kernels for 14%

profile of v3, /device:TPU:0, one launch (start us, length us, event | category | flops | bytes accessed | tf_op | source)
XLA Modules:
  0.0 206.4 jit_solution(664792725738941846)
XLA Ops:
  0.7 1.6 shard_map.356
  2.3 5.0 %collective-permute-start.2 = (bf16[288,256]{1,0:T(8,128)(2,1)}, bf16[288,256]{1,0:T(8,128)(2,1)S(1)}, u32[]{:S(2)}, u32[]{:S(2)}) collective-permute-start(bf16[288,256]{1,0:T(8,128)(2,1)} %shard_map.356), channel_id=1, source_target_pairs={{0,3},{1,2},{2,1},{3,0},{4,7},{5,6},{6,5},{7,4},{8,11},{9,10},{10,... | collective-permute-start | bytes 442376 | tf_op jit(solution)/shard_map/ppermute | solution.py:1010
  7.9 2.4 %shard_map.357 = (s32[32,1,256]{2,1,0:T(1,128)}, s32[32,512]{1,0:T(8,128)}) custom-call(s32[8,512]{1,0:T(8,128)} %bitcast.53, s32[8,512]{1,0:T(8,128)} %bitcast.61), custom_call_target="tpu_custom_call" | custom-call | flops 150994944 | bytes 98304 | tf_op jit(solution)/shard_map/pallas_call | solution.py:66
  10.4 6.0 %all-to-all-start = ((s32[32,1,256]{2,1,0:T(1,128)}), s32[32,1,256]{2,1,0:T(1,128)S(1)}, u32[]{:S(2)}, u32[]{:S(2)}) async-start(s32[32,1,256]{2,1,0:T(1,128)} %get-tuple-element.78), calls=%async_computation | async-start | bytes 65536 | tf_op jit(solution)/shard_map/all_to_all | solution.py:1147
  16.4 7.2 %all-to-all-done.request_ref = s32[32,1,256]{2,1,0:T(1,128)S(1)} async-done(((s32[32,1,256]{2,1,0:T(1,128)}), s32[32,1,256]{2,1,0:T(1,128)S(1)}, u32[]{:S(2)}, u32[]{:S(2)}) %all-to-all-start) | async-done | bytes 32800 | tf_op jit(solution)/shard_map/all_to_all | solution.py:1147
  23.7 1.0 select_bitcast_fusion.3
  24.8 0.7 collective-permute-start.3
  26.0 7.3 %shard_map.358 = bf16[32,64,256]{2,1,0:T(8,128)(2,1)} custom-call(s32[32,1,256]{2,1,0:T(1,128)} %copy-done.7, bf16[64,4096]{1,0:T(8,128)(2,1)} %bitcast.59), custom_call_target="tpu_custom_call" | custom-call | flops 4294967296 | bytes 1572864 | tf_op jit(solution)/shard_map/pallas_call | solution.py:106
  34.3 0.8 collective-permute-start.5
  35.1 3.4 %all-to-all-start.1 = ((bf16[32,64,256]{2,1,0:T(8,128)(2,1)}), bf16[32,64,256]{2,1,0:T(8,128)(2,1)}, u32[]{:S(2)}, u32[]{:S(2)}) async-start(bf16[32,64,256]{2,1,0:T(8,128)(2,1)} %shard_map.358), calls=%async_computation.1 | async-start | bytes 2097152 | tf_op jit(solution)/shard_map/all_to_all | solution.py:1159
  38.5 1.6 collective-permute-start.6
  40.1 15.3 %collective-permute-done.5 = bf16[1152,256]{1,0:T(8,128)(2,1)S(1)} collective-permute-done((bf16[1152,256]{1,0:T(8,128)(2,1)S(1)}, bf16[1152,256]{1,0:T(8,128)(2,1)S(1)}, u32[]{:S(2)}, u32[]{:S(2)}) %collective-permute-start.5) | collective-permute-done | bytes 589856 | tf_op jit(solution)/shard_map/ppermute | solution.py:987
  55.6 9.4 %collective-permute-done.6 = bf16[1152,256]{1,0:T(8,128)(2,1)S(1)} collective-permute-done((bf16[1152,256]{1,0:T(8,128)(2,1)S(1)}, bf16[1152,256]{1,0:T(8,128)(2,1)S(1)}, u32[]{:S(2)}, u32[]{:S(2)}) %collective-permute-start.6) | collective-permute-done | bytes 589856 | tf_op jit(solution)/shard_map/ppermute | solution.py:987
  65.8 6.5 %shard_map.359.refs_5_ = bf16[512,512]{1,0:T(8,128)(2,1)} custom-call(bf16[32,64,256]{2,1,0:T(8,128)(2,1)} %all-to-all-done.1.found_ref, s32[32,512]{1,0:T(8,128)} %get-tuple-element.88.rank_ref, s32[8,512]{1,0:T(8,128)} %bitcast.54), custom_call_target="tpu_custom_call" | custom-call | flops 536870912 | bytes 1572864 | tf_op jit(solution)/shard_map/pallas_call | solution.py:144
  72.3 1.0 copy-done.4
  73.3 3.4 %shard_map.360 = (f32[256,64]{1,0:T(8,128)}, bf16[32,512]{1,0:T(8,128)(2,1)}, bf16[512,32]{1,0:T(8,128)(2,1)}, bf16[16,256]{1,0:T(8,128)(2,1)}, bf16[512,16]{1,0...) custom-call(s32[1]{0:T(128)} %bitcast.bit_ref.refs_0_, ...), custom_call_target="tpu_custom_call" | custom-call | bytes 2359296 | tf_op jit(solution)/shard_map/pallas_call | solution.py:365
  76.7 21.6 %shard_map.361 = (f32[2,512]{1,0:T(2,128)}, f32[512,512]{1,0:T(8,128)}, bf16[4096,256]{1,0:T(8,128)(2,1)}, bf16[4096,256]{1,0:T(8,128)(2,1)}) custom-call(s32[1]{0:T(128)} %bitcast.bit_ref.refs_0_, bf16[2304,256]{1,0:T(8,128)(2,1)} %copy-done, bf16[2304,256]{1,0:T(8,128)(2,1)} %copy-done.5, bf16[2304,256]{1,0:T(8,128)(2,1)} %copy-done.4, ...), custom_call_target="tpu_custom_call" | custom-call | flops 6241124352 | bytes 25165824 | tf_op jit(solution)/shard_map/pallas_call | solution.py:837
  98.5 4.3 %collective-permute-done.9 = bf16[4096,256]{1,0:T(8,128)(2,1)S(1)} collective-permute-done((bf16[4096,256]{1,0:T(8,128)(2,1)}, bf16[4096,256]{1,0:T(8,128)(2,1)S(1)}, u32[]{:S(2)}, u32[]{:S(2)}) %collective-permute-start.9) | collective-permute-done | bytes 2097184 | tf_op jit(solution)/shard_map/ppermute | solution.py:987
  102.7 2.1 %add_convert_fusion = bf16[4096,256]{1,0:T(8,128)(2,1)S(1)} fusion(bf16[4096,256]{1,0:T(8,128)(2,1)S(1)} %collective-permute-done.9, bf16[4096,256]{1,0:T(8,128)(2,1)} %get-tuple-element.102), kind=kLoop, calls=%fused_computation | loop fusion | flops 4194304 | bytes 6291456 | tf_op jit(solution)/shard_map/convert_element_type | solution.py:998
  105.2 1.3 collective-permute-start.10
  107.0 6.4 %shard_map.362 = bf16[32,64,256]{2,1,0:T(8,128)(2,1)} custom-call(f32[512,512]{1,0:T(8,128)} %get-tuple-element.109.grad_ref, s32[32,512]{1,0:T(8,128)} %get-tuple-element.88.rank_ref, s32[8,512]{1,0:T(8,128)} %bitcast.55), custom_call_target="tpu_custom_call" | custom-call | flops 536870912 | bytes 2097152 | tf_op jit(solution)/shard_map/pallas_call | solution.py:180
  113.4 5.8 %collective-permute-done.10 = bf16[1024,256]{1,0:T(8,128)(2,1)S(1)} collective-permute-done((bf16[1024,256]{1,0:T(8,128)(2,1)S(1)}, bf16[1024,256]{1,0:T(8,128)(2,1)S(1)}, u32[]{:S(2)}, u32[]{:S(2)}) %collective-permute-start.10) | collective-permute-done | bytes 524320 | tf_op jit(solution)/shard_map/ppermute | solution.py:987
  119.4 0.8 collective-permute-done.11
  120.3 4.4 %all-to-all-start.2 = ((bf16[32,64,256]{2,1,0:T(8,128)(2,1)}), bf16[32,64,256]{2,1,0:T(8,128)(2,1)S(1)}, u32[]{:S(2)}, u32[]{:S(2)}) async-start(bf16[32,64,256]{2,1,0:T(8,128)(2,1)} %shard_map.362), calls=%async_computation.2 | async-start | bytes 2097152 | tf_op jit(solution)/shard_map/all_to_all | solution.py:1104
  124.7 1.6 collective-permute-start.13
  126.3 1.5 collective-permute-start.12
  127.8 13.5 %collective-permute-done.13 = bf16[512,256]{1,0:T(8,128)(2,1)S(1)} collective-permute-done((bf16[512,256]{1,0:T(8,128)(2,1)S(1)}, bf16[512,256]{1,0:T(8,128)(2,1)S(1)}, u32[]{:S(2)}, u32[]{:S(2)}) %collective-permute-start.13) | collective-permute-done | bytes 262176 | tf_op jit(solution)/shard_map/ppermute | solution.py:987
  141.6 1.5 collective-permute-start.14
  143.0 3.3 %collective-permute-start.16 = (bf16[256,256]{1,0:T(8,128)(2,1)S(1)}, bf16[256,256]{1,0:T(8,128)(2,1)S(1)}, u32[]{:S(2)}, u32[]{:S(2)}) collective-permute-start(bf16[256,256]{1,0:T(8,128)(2,1)S(1)} %get-tuple-element.191), channel_id=1, source_target_pairs={{0,3},{1,2},{2,1},{3,0},{4,7},{5,6},{6,5},{7,4},{8,11},{9,10},{10,... | collective-permute-start | bytes 393224 | tf_op jit(solution)/shard_map/ppermute | solution.py:1010
  146.9 3.2 %collective-permute-done.14 = bf16[256,256]{1,0:T(8,128)(2,1)S(1)} collective-permute-done((bf16[256,256]{1,0:T(8,128)(2,1)S(1)}, bf16[256,256]{1,0:T(8,128)(2,1)S(1)}, u32[]{:S(2)}, u32[]{:S(2)}) %collective-permute-start.14) | collective-permute-done | bytes 131104 | tf_op jit(solution)/shard_map/ppermute | solution.py:1010
  150.1 3.4 %collective-permute-done.16 = bf16[256,256]{1,0:T(8,128)(2,1)S(1)} collective-permute-done((bf16[256,256]{1,0:T(8,128)(2,1)S(1)}, bf16[256,256]{1,0:T(8,128)(2,1)S(1)}, u32[]{:S(2)}, u32[]{:S(2)}) %collective-permute-start.16) | collective-permute-done | bytes 131104 | tf_op jit(solution)/shard_map/ppermute | solution.py:1010
  153.5 8.4 %collective-permute-done.15 = bf16[256,256]{1,0:T(8,128)(2,1)S(1)} collective-permute-done((bf16[256,256]{1,0:T(8,128)(2,1)S(1)}, bf16[256,256]{1,0:T(8,128)(2,1)S(1)}, u32[]{:S(2)}, u32[]{:S(2)}) %collective-permute-start.15) | collective-permute-done | bytes 131104 | tf_op jit(solution)/shard_map/ppermute | solution.py:1010
  162.0 2.0 collective-permute-start.18
  164.1 2.4 %collective-permute-start.17 = (bf16[256,256]{1,0:T(8,128)(2,1)S(1)}, bf16[256,256]{1,0:T(8,128)(2,1)S(1)}, u32[]{:S(2)}, u32[]{:S(2)}) collective-permute-start(bf16[256,256]{1,0:T(8,128)(2,1)S(1)} %add_convert_fusion.5), channel_id=1, source_target_pairs={{0,3},{1,2},{2,1},{3,0},{4,7},{5,6},{6,5},{7,4},{8,11},{9,10},{10,... | collective-permute-start | bytes 393224 | tf_op jit(solution)/shard_map/ppermute | solution.py:1010
  166.4 2.3 %collective-permute-done.19 = bf16[256,256]{1,0:T(8,128)(2,1)S(1)} collective-permute-done((bf16[256,256]{1,0:T(8,128)(2,1)S(1)}, bf16[256,256]{1,0:T(8,128)(2,1)S(1)}, u32[]{:S(2)}, u32[]{:S(2)}) %collective-permute-start.19) | collective-permute-done | bytes 131104 | tf_op jit(solution)/shard_map/ppermute | solution.py:1010
  168.8 6.2 %collective-permute-done.18 = bf16[256,256]{1,0:T(8,128)(2,1)S(1)} collective-permute-done((bf16[256,256]{1,0:T(8,128)(2,1)S(1)}, bf16[256,256]{1,0:T(8,128)(2,1)S(1)}, u32[]{:S(2)}, u32[]{:S(2)}) %collective-permute-start.18) | collective-permute-done | bytes 131104 | tf_op jit(solution)/shard_map/ppermute | solution.py:1010
  175.2 1.5 collective-permute-start.20
  176.7 1.5 collective-permute-start.22
  178.2 3.8 %collective-permute-done.20 = bf16[512,256]{1,0:T(8,128)(2,1)S(1)} collective-permute-done((bf16[512,256]{1,0:T(8,128)(2,1)S(1)}, bf16[512,256]{1,0:T(8,128)(2,1)S(1)}, u32[]{:S(2)}, u32[]{:S(2)}) %collective-permute-start.20) | collective-permute-done | bytes 262176 | tf_op jit(solution)/shard_map/ppermute | solution.py:987
  182.1 1.7 collective-permute-start.21
  183.8 2.0 collective-permute-done.22
  186.2 6.7 %shard_map.363 = f32[64,4096]{1,0:T(8,128)} custom-call(bf16[32,64,256]{2,1,0:T(8,128)(2,1)} %copy-done.6, s32[32,1,256]{2,1,0:T(1,128)} %copy-done.7), custom_call_target="tpu_custom_call" | custom-call | flops 4294967296 | bytes 2097152 | tf_op jit(solution)/shard_map/pallas_call | solution.py:228
  193.0 1.1 collective-permute-done.21
  194.3 0.9 collective-permute-done.23
  196.1 1.3 copy.41
  197.4 1.0 collective-permute-done.24.came_a_ref
  198.4 1.5 collective-permute-done.25.came_b_ref
  199.9 6.3 %shard_map.364 = (f32[3072,256]{1,0:T(8,128)}, f32[1536]{0:T(1024)}, f32[1536,256]{1,0:T(8,128)}, f32[1536]{0:T(1024)}, f32[1536]{0:T(1024)}, /*index=5*/f32[4,1...) custom-call(s32[1]{0:T(128)} %bitcast.bit_ref.refs_0_, ...), custom_call_target="tpu_custom_call" | custom-call | bytes 25165824 | tf_op jit(solution)/shard_map/pallas_call | solution.py:970
  (70 shorter events, 7.1 us)
Async XLA Ops:
  2.3 21.4 %collective-permute-start.2 = (bf16[288,256]{1,0:T(8,128)(2,1)}, bf16[288,256]{1,0:T(8,128)(2,1)S(1)}, u32[]{:S(2)}, u32[]{:S(2)}) collective-permute-start(bf16[288,256]{1,0:T(8,128)(2,1)} %shard_map.356), channel_id=1, source_target_pairs={{0,3},{1,2},{2,1},{3,0},{4,7},{5,6},{6,5},{7,4},{8,11},{9,10},{10,... | collective-permute-start | bytes 442376 | tf_op jit(solution)/shard_map/ppermute | solution.py:1010
  7.3 16.4 %collective-permute-start.1 = (bf16[288,256]{1,0:T(8,128)(2,1)}, bf16[288,256]{1,0:T(8,128)(2,1)S(1)}, u32[]{:S(2)}, u32[]{:S(2)}) collective-permute-start(bf16[288,256]{1,0:T(8,128)(2,1)} %shard_map.356), channel_id=1, source_target_pairs={{0,2},{1,3},{2,0},{3,1},{4,6},{5,7},{6,4},{7,5},{8,10},{9,11},{10,... | collective-permute-start | bytes 442376 | tf_op jit(solution)/shard_map/ppermute | solution.py:1010
  7.3 16.4 %collective-permute-start = (bf16[288,256]{1,0:T(8,128)(2,1)}, bf16[288,256]{1,0:T(8,128)(2,1)S(1)}, u32[]{:S(2)}, u32[]{:S(2)}) collective-permute-start(bf16[288,256]{1,0:T(8,128)(2,1)} %shard_map.356), channel_id=1, source_target_pairs={{0,1},{1,0},{2,3},{3,2},{4,5},{5,4},{6,7},{7,6},{8,9},{9,8},{10,11... | collective-permute-start | bytes 442376 | tf_op jit(solution)/shard_map/ppermute | solution.py:1010
  10.4 13.3 %all-to-all-start = ((s32[32,1,256]{2,1,0:T(1,128)}), s32[32,1,256]{2,1,0:T(1,128)S(1)}, u32[]{:S(2)}, u32[]{:S(2)}) async-start(s32[32,1,256]{2,1,0:T(1,128)} %get-tuple-element.78), calls=%async_computation | async-start | bytes 65536 | tf_op jit(solution)/shard_map/all_to_all | solution.py:1147
  23.7 2.4 %copy-start.7 = (s32[32,1,256]{2,1,0:T(1,128)}, s32[32,1,256]{2,1,0:T(1,128)S(1)}, u32[]{:S(2)}) copy-start(s32[32,1,256]{2,1,0:T(1,128)S(1)} %all-to-all-done.request_ref) | copy-start | bytes 98308
  24.8 8.7 %collective-permute-start.3 = (bf16[576,256]{1,0:T(8,128)(2,1)S(1)}, bf16[576,256]{1,0:T(8,128)(2,1)S(1)}, u32[]{:S(2)}, u32[]{:S(2)}) collective-permute-start(bf16[576,256]{1,0:T(8,128)(2,1)S(1)} %bitcast.48), channel_id=1, source_target_pairs={{0,16},{4,20},{8,24},{12,28},{16,0},{20,4},{24,8},{28,12},{1,17},{... | collective-permute-start | bytes 884744 | tf_op jit(solution)/shard_map/ppermute | solution.py:987
  25.5 8.6 %collective-permute-start.4 = (bf16[576,256]{1,0:T(8,128)(2,1)S(1)}, bf16[576,256]{1,0:T(8,128)(2,1)S(1)}, u32[]{:S(2)}, u32[]{:S(2)}) collective-permute-start(bf16[576,256]{1,0:T(8,128)(2,1)S(1)} %bitcast.47), channel_id=1, source_target_pairs={{0,8},{4,12},{8,0},{12,4},{16,24},{20,28},{24,16},{28,20},{1,9},{5... | collective-permute-start | bytes 884744 | tf_op jit(solution)/shard_map/ppermute | solution.py:987
  34.3 21.1 %collective-permute-start.5 = (bf16[1152,256]{1,0:T(8,128)(2,1)S(1)}, bf16[1152,256]{1,0:T(8,128)(2,1)S(1)}, u32[]{:S(2)}, u32[]{:S(2)}) collective-permute-start(bf16[1152,256]{1,0:T(8,128)(2,1)S(1)} %get-tuple-element.83), channel_id=1, source_target_pairs={{0,8},{4,12},{8,0},{12,4},{16,24},{20,28},{24,16},{28,20},{1,9},{5... | collective-permute-start | bytes 1769480 | tf_op jit(solution)/shard_map/ppermute | solution.py:987
  35.1 30.7 %all-to-all-start.1 = ((bf16[32,64,256]{2,1,0:T(8,128)(2,1)}), bf16[32,64,256]{2,1,0:T(8,128)(2,1)}, u32[]{:S(2)}, u32[]{:S(2)}) async-start(bf16[32,64,256]{2,1,0:T(8,128)(2,1)} %shard_map.358), calls=%async_computation.1 | async-start | bytes 2097152 | tf_op jit(solution)/shard_map/all_to_all | solution.py:1159
  38.5 26.5 %collective-permute-start.6 = (bf16[1152,256]{1,0:T(8,128)(2,1)S(1)}, bf16[1152,256]{1,0:T(8,128)(2,1)S(1)}, u32[]{:S(2)}, u32[]{:S(2)}) collective-permute-start(bf16[1152,256]{1,0:T(8,128)(2,1)S(1)} %get-tuple-element.84), channel_id=1, source_target_pairs={{0,16},{4,20},{8,24},{12,28},{16,0},{20,4},{24,8},{28,12},{1,17},{... | collective-permute-start | bytes 1769480 | tf_op jit(solution)/shard_map/ppermute | solution.py:987
  55.6 9.7 %copy-start = (bf16[2304,256]{1,0:T(8,128)(2,1)}, bf16[2304,256]{1,0:T(8,128)(2,1)S(1)}, u32[]{:S(2)}) copy-start(bf16[2304,256]{1,0:T(8,128)(2,1)S(1)} %pad_maximum_fusion.own_ref.refs_1_) | copy-start | bytes 3538948
  65.2 11.5 %copy-start.5 = (bf16[2304,256]{1,0:T(8,128)(2,1)}, bf16[2304,256]{1,0:T(8,128)(2,1)S(1)}, u32[]{:S(2)}) copy-start(bf16[2304,256]{1,0:T(8,128)(2,1)S(1)} %pad_maximum_fusion.1.refs_2_) | copy-start | bytes 3538948
  65.2 7.0 %collective-permute-start.8 = (bf16[2304,256]{1,0:T(8,128)(2,1)S(1)}, bf16[2304,256]{1,0:T(8,128)(2,1)}, u32[]{:S(2)}, u32[]{:S(2)}) collective-permute-start(bf16[2304,256]{1,0:T(8,128)(2,1)S(1)} %pad_maximum_fusion.1.refs_2_), channel_id=1, source_target_pairs={{0,4},{4,0},{8,12},{12,8},{16,20},{20,16},{24,28},{28,24},{1,5},{5... | collective-permute-start | bytes 3538952 | tf_op jit(solution)/shard_map/ppermute | solution.py:987
  65.3 7.0 %collective-permute-start.7 = (bf16[2304,256]{1,0:T(8,128)(2,1)S(1)}, bf16[2304,256]{1,0:T(8,128)(2,1)S(1)}, u32[]{:S(2)}, u32[]{:S(2)}) collective-permute-start(bf16[2304,256]{1,0:T(8,128)(2,1)S(1)} %pad_maximum_fusion.own_ref.refs_1_), channel_id=1, source_target_pairs={{0,4},{4,0},{8,12},{12,8},{16,20},{20,16},{24,28},{28,24},{1,5},{5... | collective-permute-start | bytes 3538952 | tf_op jit(solution)/shard_map/ppermute | solution.py:987
  72.3 1.0 copy-start.4
  98.3 4.4 %collective-permute-start.9 = (bf16[4096,256]{1,0:T(8,128)(2,1)}, bf16[4096,256]{1,0:T(8,128)(2,1)S(1)}, u32[]{:S(2)}, u32[]{:S(2)}) collective-permute-start(bf16[4096,256]{1,0:T(8,128)(2,1)} %get-tuple-element.103), channel_id=1, source_target_pairs={{0,4},{4,0},{8,12},{12,8},{16,20},{20,16},{24,28},{28,24},{1,5},{5... | collective-permute-start | bytes 6291464 | tf_op jit(solution)/shard_map/ppermute | solution.py:987
  105.2 14.0 %collective-permute-start.10 = (bf16[1024,256]{1,0:T(8,128)(2,1)S(1)}, bf16[1024,256]{1,0:T(8,128)(2,1)S(1)}, u32[]{:S(2)}, u32[]{:S(2)}) collective-permute-start(bf16[1024,256]{1,0:T(8,128)(2,1)S(1)} %get-tuple-element.106), channel_id=1, source_target_pairs={{0,8},{4,12},{8,0},{12,4},{16,24},{20,28},{24,16},{28,20},{1,9},{5... | collective-permute-start | bytes 1572872 | tf_op jit(solution)/shard_map/ppermute | solution.py:987
  106.5 13.7 %collective-permute-start.11 = (bf16[1024,256]{1,0:T(8,128)(2,1)S(1)}, bf16[1024,256]{1,0:T(8,128)(2,1)S(1)}, u32[]{:S(2)}, u32[]{:S(2)}) collective-permute-start(bf16[1024,256]{1,0:T(8,128)(2,1)S(1)} %get-tuple-element.108), channel_id=1, source_target_pairs={{0,16},{4,20},{8,24},{12,28},{16,0},{20,4},{24,8},{28,12},{1,17},{... | collective-permute-start | bytes 1572872 | tf_op jit(solution)/shard_map/ppermute | solution.py:987
  120.3 41.7 %all-to-all-start.2 = ((bf16[32,64,256]{2,1,0:T(8,128)(2,1)}), bf16[32,64,256]{2,1,0:T(8,128)(2,1)S(1)}, u32[]{:S(2)}, u32[]{:S(2)}) async-start(bf16[32,64,256]{2,1,0:T(8,128)(2,1)} %shard_map.362), calls=%async_computation.2 | async-start | bytes 2097152 | tf_op jit(solution)/shard_map/all_to_all | solution.py:1104
  124.7 16.6 %collective-permute-start.13 = (bf16[512,256]{1,0:T(8,128)(2,1)S(1)}, bf16[512,256]{1,0:T(8,128)(2,1)S(1)}, u32[]{:S(2)}, u32[]{:S(2)}) collective-permute-start(bf16[512,256]{1,0:T(8,128)(2,1)S(1)} %constant_dynamic-slice_fusion.3), channel_id=1, source_target_pairs={{0,8},{4,12},{8,0},{12,4},{16,24},{20,28},{24,16},{28,20},{1,9},{5... | collective-permute-start | bytes 786440 | tf_op jit(solution)/shard_map/ppermute | solution.py:987
  126.3 15.1 %collective-permute-start.12 = (bf16[512,256]{1,0:T(8,128)(2,1)S(1)}, bf16[512,256]{1,0:T(8,128)(2,1)S(1)}, u32[]{:S(2)}, u32[]{:S(2)}) collective-permute-start(bf16[512,256]{1,0:T(8,128)(2,1)S(1)} %constant_dynamic-slice_fusion.4), channel_id=1, source_target_pairs={{0,16},{4,20},{8,24},{12,28},{16,0},{20,4},{24,8},{28,12},{1,17},{... | collective-permute-start | bytes 786440 | tf_op jit(solution)/shard_map/ppermute | solution.py:987
  141.6 8.5 %collective-permute-start.14 = (bf16[256,256]{1,0:T(8,128)(2,1)S(1)}, bf16[256,256]{1,0:T(8,128)(2,1)S(1)}, u32[]{:S(2)}, u32[]{:S(2)}) collective-permute-start(bf16[256,256]{1,0:T(8,128)(2,1)S(1)} %get-tuple-element.190), channel_id=1, source_target_pairs={{0,1},{1,0},{2,3},{3,2},{4,5},{5,4},{6,7},{7,6},{8,9},{9,8},{10,11... | collective-permute-start | bytes 393224 | tf_op jit(solution)/shard_map/ppermute | solution.py:1010
  143.0 10.5 %collective-permute-start.16 = (bf16[256,256]{1,0:T(8,128)(2,1)S(1)}, bf16[256,256]{1,0:T(8,128)(2,1)S(1)}, u32[]{:S(2)}, u32[]{:S(2)}) collective-permute-start(bf16[256,256]{1,0:T(8,128)(2,1)S(1)} %get-tuple-element.191), channel_id=1, source_target_pairs={{0,3},{1,2},{2,1},{3,0},{4,7},{5,6},{6,5},{7,4},{8,11},{9,10},{10,... | collective-permute-start | bytes 393224 | tf_op jit(solution)/shard_map/ppermute | solution.py:1010
  146.4 15.5 %collective-permute-start.15 = (bf16[256,256]{1,0:T(8,128)(2,1)S(1)}, bf16[256,256]{1,0:T(8,128)(2,1)S(1)}, u32[]{:S(2)}, u32[]{:S(2)}) collective-permute-start(bf16[256,256]{1,0:T(8,128)(2,1)S(1)} %get-tuple-element.192), channel_id=1, source_target_pairs={{0,2},{1,3},{2,0},{3,1},{4,6},{5,7},{6,4},{7,5},{8,10},{9,11},{10,... | collective-permute-start | bytes 393224 | tf_op jit(solution)/shard_map/ppermute | solution.py:1010
  162.0 20.1 %copy-start.6 = (bf16[32,64,256]{2,1,0:T(8,128)(2,1)}, bf16[32,64,256]{2,1,0:T(8,128)(2,1)S(1)}, u32[]{:S(2)}) copy-start(bf16[32,64,256]{2,1,0:T(8,128)(2,1)S(1)} %all-to-all-done.2.came_ref) | copy-start | bytes 3145732
  162.0 6.8 %collective-permute-start.19 = (bf16[256,256]{1,0:T(8,128)(2,1)S(1)}, bf16[256,256]{1,0:T(8,128)(2,1)S(1)}, u32[]{:S(2)}, u32[]{:S(2)}) collective-permute-start(bf16[256,256]{1,0:T(8,128)(2,1)S(1)} %add_convert_fusion.5), channel_id=1, source_target_pairs={{0,1},{1,0},{2,3},{3,2},{4,5},{5,4},{6,7},{7,6},{8,9},{9,8},{10,11... | collective-permute-start | bytes 393224 | tf_op jit(solution)/shard_map/ppermute | solution.py:1010
  162.0 12.9 %collective-permute-start.18 = (bf16[256,256]{1,0:T(8,128)(2,1)S(1)}, bf16[256,256]{1,0:T(8,128)(2,1)S(1)}, u32[]{:S(2)}, u32[]{:S(2)}) collective-permute-start(bf16[256,256]{1,0:T(8,128)(2,1)S(1)} %add_convert_fusion.5), channel_id=1, source_target_pairs={{0,2},{1,3},{2,0},{3,1},{4,6},{5,7},{6,4},{7,5},{8,10},{9,11},{10,... | collective-permute-start | bytes 393224 | tf_op jit(solution)/shard_map/ppermute | solution.py:1010
  164.1 10.9 %collective-permute-start.17 = (bf16[256,256]{1,0:T(8,128)(2,1)S(1)}, bf16[256,256]{1,0:T(8,128)(2,1)S(1)}, u32[]{:S(2)}, u32[]{:S(2)}) collective-permute-start(bf16[256,256]{1,0:T(8,128)(2,1)S(1)} %add_convert_fusion.5), channel_id=1, source_target_pairs={{0,3},{1,2},{2,1},{3,0},{4,7},{5,6},{6,5},{7,4},{8,11},{9,10},{10,... | collective-permute-start | bytes 393224 | tf_op jit(solution)/shard_map/ppermute | solution.py:1010
  175.2 6.8 %collective-permute-start.20 = (bf16[512,256]{1,0:T(8,128)(2,1)S(1)}, bf16[512,256]{1,0:T(8,128)(2,1)S(1)}, u32[]{:S(2)}, u32[]{:S(2)}) collective-permute-start(bf16[512,256]{1,0:T(8,128)(2,1)S(1)} %bitcast.50), channel_id=1, source_target_pairs={{0,16},{4,20},{8,24},{12,28},{16,0},{20,4},{24,8},{28,12},{1,17},{... | collective-permute-start | bytes 786440 | tf_op jit(solution)/shard_map/ppermute | solution.py:987
  176.7 9.2 %collective-permute-start.22 = (bf16[512,256]{1,0:T(8,128)(2,1)S(1)}, bf16[512,256]{1,0:T(8,128)(2,1)S(1)}, u32[]{:S(2)}, u32[]{:S(2)}) collective-permute-start(bf16[512,256]{1,0:T(8,128)(2,1)S(1)} %bitcast.49), channel_id=1, source_target_pairs={{0,8},{4,12},{8,0},{12,4},{16,24},{20,28},{24,16},{28,20},{1,9},{5... | collective-permute-start | bytes 786440 | tf_op jit(solution)/shard_map/ppermute | solution.py:987
  182.1 12.0 %collective-permute-start.21 = (bf16[1024,256]{1,0:T(8,128)(2,1)S(1)}, bf16[1024,256]{1,0:T(8,128)(2,1)S(1)}, u32[]{:S(2)}, u32[]{:S(2)}) collective-permute-start(bf16[1024,256]{1,0:T(8,128)(2,1)S(1)} %pad_maximum_fusion.9), channel_id=1, source_target_pairs={{0,8},{4,12},{8,0},{12,4},{16,24},{20,28},{24,16},{28,20},{1,9},{5... | collective-permute-start | bytes 1572872 | tf_op jit(solution)/shard_map/ppermute | solution.py:987
  186.0 9.2 %collective-permute-start.23 = (bf16[1024,256]{1,0:T(8,128)(2,1)S(1)}, bf16[1024,256]{1,0:T(8,128)(2,1)S(1)}, u32[]{:S(2)}, u32[]{:S(2)}) collective-permute-start(bf16[1024,256]{1,0:T(8,128)(2,1)S(1)} %pad_maximum_fusion.10), channel_id=1, source_target_pairs={{0,16},{4,20},{8,24},{12,28},{16,0},{20,4},{24,8},{28,12},{1,17},{... | collective-permute-start | bytes 1572872 | tf_op jit(solution)/shard_map/ppermute | solution.py:987
  194.3 1.2 copy-start.1
  194.3 1.8 copy-start.3
  195.5 4.4 %copy-start.2 = (bf16[2048,256]{1,0:T(8,128)(2,1)}, bf16[2048,256]{1,0:T(8,128)(2,1)S(1)}, u32[]{:S(2)}) copy-start(bf16[2048,256]{1,0:T(8,128)(2,1)S(1)} %pad_maximum_fusion.3.own_b_ref) | copy-start | bytes 3145732
  195.5 2.9 %collective-permute-start.24 = (bf16[2048,256]{1,0:T(8,128)(2,1)S(1)}, bf16[2048,256]{1,0:T(8,128)(2,1)}, u32[]{:S(2)}, u32[]{:S(2)}) collective-permute-start(bf16[2048,256]{1,0:T(8,128)(2,1)S(1)} %pad_maximum_fusion.2.own_a_ref), channel_id=1, source_target_pairs={{0,4},{4,0},{8,12},{12,8},{16,20},{20,16},{24,28},{28,24},{1,5},{5... | collective-permute-start | bytes 3145736 | tf_op jit(solution)/shard_map/ppermute | solution.py:987
  195.6 4.3 %collective-permute-start.25 = (bf16[2048,256]{1,0:T(8,128)(2,1)S(1)}, bf16[2048,256]{1,0:T(8,128)(2,1)}, u32[]{:S(2)}, u32[]{:S(2)}) collective-permute-start(bf16[2048,256]{1,0:T(8,128)(2,1)S(1)} %pad_maximum_fusion.3.own_b_ref), channel_id=1, source_target_pairs={{0,4},{4,0},{8,12},{12,8},{16,20},{20,16},{24,28},{28,24},{1,5},{5... | collective-permute-start | bytes 3145736 | tf_op jit(solution)/shard_map/ppermute | solution.py:987

commit v4 on v3

--- a/solution.py
+++ b/solution.py
@@ -24,6 +24,10 @@
 
 def one_hot(hit):
     return jnp.where(hit, 1.0, 0.0).astype(jnp.bfloat16)
+
+
+def low(value):
+    return value.astype(jnp.float32).astype(jnp.bfloat16)
 
 
 def iota(shape, axis):
@@ -117,6 +121,7 @@
     fields, events = owner_ref.shape
     slots = iota((capacity, events), 0)
     group = 4
+    owners_low = low(owner_ref[...])
     total_ref[...] = jnp.zeros_like(total_ref)
 
     def step(start, carry):
@@ -124,18 +129,22 @@
         for index in range(group):
             owner = start * group + index
             hits = one_hot(rank_ref[pl.ds(owner, 1), :] == slots)
-            pieces.append(jnp.dot(found_ref[owner], hits, preferred_element_type=jnp.float32))
+            pieces.append(
+                jnp.dot(found_ref[owner], hits, preferred_element_type=jnp.float32).astype(
+                    jnp.bfloat16
+                )
+            )
         for field in range(fields):
             rows = slice(field * width, (field + 1) * width)
-            owners = owner_ref[field : field + 1, :]
+            owners = owners_low[field : field + 1, :]
             value = total_ref[rows, :]
             for index in range(group):
-                value = jnp.where(owners == start * group + index, pieces[index], value)
+                value = jnp.where(owners == low(start * group + index), pieces[index], value)
             total_ref[rows, :] = value
         return carry
 
     lax.fori_loop(0, devices // group, step, 0)
-    flipped_ref[...] = total_ref[...].astype(jnp.bfloat16)
+    flipped_ref[...] = total_ref[...]
 
 
 def place_rows(found, rank, owner_rows):
@@ -146,24 +155,29 @@
         jax.ShapeDtypeStruct((fields * width, events), jnp.bfloat16),
         2 * devices * width * capacity * events,
         2 * (devices * width * capacity + fields * width * events),
-        [pltpu.VMEM((fields * width, events), jnp.float32)],
+        [pltpu.VMEM((fields * width, events), jnp.bfloat16)],
     )(found, rank, owner_rows)
 
 
-def send_body(grad_ref, rank_ref, owner_ref, sent_ref, low_ref):
+def send_body(group, grad_ref, rank_ref, owner_ref, sent_ref, turned_ref, low_ref):
     devices, width, capacity = sent_ref.shape
     fields, events = owner_ref.shape
     slots = iota((capacity, events), 0)
-    low_ref[...] = grad_ref[...].astype(jnp.bfloat16).astype(jnp.float32)
+    owners_low = low(owner_ref[...])
+    low_ref[...] = grad_ref[...].astype(jnp.bfloat16)
+    turned_ref[...] = grad_ref[...].T
 
     def step(owner, carry):
-        chosen = jnp.zeros((width, events), jnp.float32)
+        chosen = jnp.zeros((width, events), jnp.bfloat16)
         for field in range(fields):
             rows = slice(field * width, (field + 1) * width)
-            chosen = jnp.where(owner_ref[field : field + 1, :] == owner, low_ref[rows, :], chosen)
+            chosen = jnp.where(
+                owners_low[field : field + 1, :] == low(owner), low_ref[rows, :], chosen
+            )
         hits = one_hot(rank_ref[pl.ds(owner, 1), :] == slots)
-        sent_ref[owner] = lax.dot_general(
-            chosen.astype(jnp.bfloat16),
+        place = lax.rem(owner, group) * (devices // group) + lax.div(owner, group)
+        sent_ref[place] = lax.dot_general(
+            chosen,
             hits,
             (((1,), (1,)), ((), ())),
             preferred_element_type=jnp.float32,
@@ -173,16 +187,19 @@
     lax.fori_loop(0, devices, step, 0, unroll=16)
 
 
-def send_rows(grad, rank, owner_rows, capacity):
+def send_rows(grad, rank, owner_rows, capacity, group):
     devices = rank.shape[0]
     fields, events = owner_rows.shape
     width = grad.shape[0] // fields
     return local_kernel(
-        send_body,
-        jax.ShapeDtypeStruct((devices, width, capacity), jnp.bfloat16),
+        functools.partial(send_body, group),
+        (
+            jax.ShapeDtypeStruct((devices, width, capacity), jnp.bfloat16),
+            jax.ShapeDtypeStruct((events, fields * width), jnp.float32),
+        ),
         2 * devices * width * capacity * events,
         2 * (devices * width * capacity + 2 * fields * width * events),
-        [pltpu.VMEM((fields * width, events), jnp.float32)],
+        [pltpu.VMEM((fields * width, events), jnp.bfloat16)],
     )(grad, rank, owner_rows)
 
 
@@ -293,9 +310,18 @@
     up_rows,
     inner_rows,
     middle_rows,
+    thin_own,
+    thin_came,
+    sems,
 ):
     devices = 2 * len(places[0])
-    shard = own_ref.shape[0] // len(places[0])
+    start = own_ref.shape[1] - THIN_ROWS
+    copies = [
+        pltpu.make_async_copy(ref.at[:, pl.ds(start, THIN_ROWS), :], held, sems.at[index])
+        for index, (ref, held) in enumerate(((own_ref, thin_own), (came_ref, thin_came)))
+    ]
+    for copy in copies:
+        copy.start()
     hidden = columns_ref.shape[0]
     width = gate_one_ref.shape[1]
 
@@ -312,8 +338,7 @@
     def unpack(pieces):
         for half, source in enumerate(pieces):
             for block, index in enumerate(places[half]):
-                end = (block + 1) * shard
-                thin = source[end - THIN_ROWS : end, :].astype(jnp.float32)
+                thin = source[block].astype(jnp.float32)
                 rows[0:6, index * bias : (index + 1) * bias] = thin[0:6, :bias]
                 rows[6:8, index * flat : (index + 1) * flat] = thin[6:8, :flat]
                 lay(task_rows, thin[8:16], index, 2 * width // devices)
@@ -324,13 +349,16 @@
                 count = hidden // devices
                 middle_rows[index * count : (index + 1) * count, :] = thin[32 : 32 + count, 128:192]
 
+    for copy in copies:
+        copy.wait()
+
     @pl.when(bit_ref[0] == 0)
     def _():
-        unpack((own_ref, came_ref))
+        unpack((thin_own, thin_came))
 
     @pl.when(bit_ref[0] != 0)
     def _():
-        unpack((came_ref, own_ref))
+        unpack((thin_came, thin_own))
 
     columns_ref[...] = jnp.zeros_like(columns_ref)
     for expert in range(6):
@@ -361,6 +389,7 @@
 
 
 def prep_thin(bit, own, came, places, width, hidden):
+    blocks = len(places[0])
     low = functools.partial(jax.ShapeDtypeStruct, dtype=jnp.bfloat16)
     return pl.pallas_call(
         functools.partial(prep_thin_body, places),
@@ -375,7 +404,7 @@
             low((128, 128)),
             low((hidden, 64)),
         ),
-        in_specs=[pl.BlockSpec(memory_space=pltpu.SMEM)] + [pl.BlockSpec(memory_space=pltpu.VMEM)] * 2,
+        in_specs=[pl.BlockSpec(memory_space=pltpu.SMEM)] + [pl.BlockSpec(memory_space=pl.ANY)] * 2,
         scratch_shapes=[
             pltpu.VMEM((8, 6 * hidden), jnp.float32),
             pltpu.VMEM((8, 2 * width), jnp.float32),
@@ -383,10 +412,13 @@
             pltpu.VMEM((8, 2 * hidden), jnp.float32),
             pltpu.VMEM((2 * hidden, 128), jnp.float32),
             pltpu.VMEM((hidden, 64), jnp.float32),
+            pltpu.VMEM((blocks, THIN_ROWS, hidden), jnp.bfloat16),
+            pltpu.VMEM((blocks, THIN_ROWS, hidden), jnp.bfloat16),
+            pltpu.SemaphoreType.DMA((2,)),
         ],
         compiler_params=pltpu.CompilerParams(vmem_limit_bytes=VMEM_LIMIT),
         cost_estimate=pl.CostEstimate(flops=0, bytes_accessed=4 * own.size, transcendentals=0),
-    )(bit, own, came)
+    )(bit, own.reshape(blocks, -1, hidden), came.reshape(blocks, -1, hidden))
 
 
 SPAN = 512
@@ -706,12 +738,21 @@
 
     half_rows = grads_ref.shape[1]
 
+    def leave(half):
+        for target, sem, when in ((kept_ref, 0, half), (sent_ref, 1, 1 - half)):
+
+            @pl.when(bit == when)
+            def _():
+                pltpu.make_async_copy(grads_ref.at[half], target, sems.at[sem]).start()
+
     def put(row, value):
         while value.shape[0]:
             half, start = row // half_rows, row % half_rows
             count = min(value.shape[0], half_rows - start)
             grads_ref[half, start : start + count, :] = value[:count].astype(jnp.bfloat16)
             row, value = row + count, value[count:]
+            if row % half_rows == 0:
+                leave(half)
 
     rows = 0
     biases = []
@@ -791,14 +832,8 @@
     biases = jnp.concatenate(biases, axis=0)
     extra = 2 * half_rows - rows - biases.shape[0]
     put(rows, jnp.concatenate([biases, jnp.zeros((extra, hidden), jnp.float32)], axis=0))
-    copies = [
-        pltpu.make_async_copy(grads_ref.at[1 - bit], sent_ref, sems.at[0]),
-        pltpu.make_async_copy(grads_ref.at[bit], kept_ref, sems.at[1]),
-    ]
-    for copy in copies:
-        copy.start()
-    for copy in copies:
-        copy.wait()
+    pltpu.make_async_copy(grads_ref.at[bit], kept_ref, sems.at[0]).wait()
+    pltpu.make_async_copy(grads_ref.at[1 - bit], sent_ref, sems.at[1]).wait()
 
 
 def dense(bit, flipped, weights, places, thin, cot, grad_rows):
@@ -860,105 +895,128 @@
     return sizes, starts
 
 
-def finish_body(
-    bit_ref,
-    own_a_ref,
-    own_b_ref,
-    came_a_ref,
-    came_b_ref,
-    low_expand_ref,
-    low_inbias_ref,
-    low_shrink_ref,
-    low_outbias_ref,
-    low_gain_ref,
-    low_taskgate_ref,
-    low_sharegate_ref,
-    up_expand_ref,
-    up_inbias_ref,
-    up_shrink_ref,
-    up_outbias_ref,
-    up_gain_ref,
-    up_taskgate_ref,
-    inner_ref,
-    tbias_ref,
-    middle_ref,
-    tail_ref,
-):
-    part = own_a_ref.shape[0]
-    hidden = up_expand_ref.shape[1]
-    width = low_expand_ref.shape[0] // 6
-    inner = inner_ref.shape[1]
-    narrow = middle_ref.shape[0]
-    wide = (low_expand_ref, low_shrink_ref, up_expand_ref, up_shrink_ref)
+def grad_moves(part, wide, half, hidden, width):
     sizes, starts = grad_layout(width, hidden)
+    moves = []
+    for index in range(2):
+        first = (2 * half + index) * part
+        for target, (start, size) in enumerate(zip(starts, sizes)):
+            low_row, high_row = max(first, start), min(first + part, start + size)
+            if low_row < high_row:
+                moves.append((index, low_row - first, target, low_row - start, high_row - low_row))
+    return moves
+
+
+def write_wide(half, pieces, wide, hold, sems, width, hidden):
+    part = pieces[0].shape[0]
     block = 128
-
-    def move(source, start, target, place, rows):
-        def step(index, carry):
-            target[pl.ds(pl.multiple_of(place + index * block, block), block), :] = source[
-                pl.ds(pl.multiple_of(start + index * block, block), block), :
+    copies = []
+    for number, (index, start, target, place, rows) in enumerate(
+        grad_moves(part, wide, half, hidden, width)
+    ):
+        source = pieces[index]
+        base = index * part + start
+
+        def step(count, carry):
+            hold[pl.ds(pl.multiple_of(base + count * block, block), block), :] = source[
+                pl.ds(pl.multiple_of(start + count * block, block), block), :
             ].astype(jnp.float32)
             return carry
 
-        lax.fori_loop(0, rows // block, step, 0)
-
-    def rest(source, start):
-        def take(rows):
-            nonlocal start
-            start += rows
-            return source[start - rows : start, :].astype(jnp.float32)
-
-        both = take(hidden)
-        inner_ref[:hidden, :] = both[:, :inner]
-        inner_ref[hidden:, :] = both[:, inner:]
-        both = take(narrow)
-        middle_ref[...] = both
-        for index in range(width // hidden):
-            gates = take(32)
-            span = slice(index * hidden, (index + 1) * hidden)
-            low_taskgate_ref[:, span] = gates[0:4]
-            low_taskgate_ref[:, width + index * hidden : width + (index + 1) * hidden] = gates[8:12]
-            low_sharegate_ref[:, span] = gates[16:22]
-        for task in range(2):
-            up_taskgate_ref[:, task * hidden : (task + 1) * hidden] = take(16)[0:4]
-        rows = take(48)
-        flat = (low_inbias_ref, low_outbias_ref, up_inbias_ref, up_outbias_ref, tbias_ref, tail_ref)
-        place = 0
-        for target in flat + (low_gain_ref, up_gain_ref):
-            for index in range(target.shape[0] // hidden):
-                target[index * hidden : (index + 1) * hidden] = rows[place]
-                place += 1
-
-    def all_parts(pieces):
-        for index, source in enumerate(pieces):
-            first, last = index * part, (index + 1) * part
-            for target, start, size in zip(wide, starts, sizes):
-                low, high = max(first, start), min(last, start + size)
-                if low < high:
-                    move(source, low - first, target, low - start, high - low)
-        rest(pieces[-1], starts[4] - (len(pieces) - 1) * part)
-
-    @pl.when(bit_ref[0] == 0)
-    def _():
-        all_parts((own_a_ref, own_b_ref, came_a_ref, came_b_ref))
-
-    @pl.when(bit_ref[0] != 0)
-    def _():
-        all_parts((came_a_ref, came_b_ref, own_a_ref, own_b_ref))
+        lax.fori_loop(0, rows // block, step, 0, unroll=4)
+        copy = pltpu.make_async_copy(
+            hold.at[pl.ds(base, rows), :], wide[target].at[pl.ds(place, rows), :], sems.at[number]
+        )
+        copy.start()
+        copies.append(copy)
+    return copies
+
+
+def own_body(bit_ref, own_a_ref, own_b_ref, *refs):
+    *wide, hold, sems = refs
+    hidden = wide[0].shape[1]
+    width = wide[0].shape[0] // 6
+
+    for half in range(2):
+
+        @pl.when(jnp.minimum(bit_ref[0], 1) == half)
+        def _():
+            for copy in write_wide(half, (own_a_ref, own_b_ref), wide, hold, sems, width, hidden):
+                copy.wait()
+
+
+def came_body(bit_ref, own_b_ref, came_a_ref, came_b_ref, *refs):
+    wide, outs, (hold, sems) = refs[4:8], refs[8:21], refs[21:]
+    hidden = wide[0].shape[1]
+    width = wide[0].shape[0] // 6
+    part = came_a_ref.shape[0]
+    start = grad_layout(width, hidden)[1][4] - 3 * part
+
+    for half in range(2):
+
+        @pl.when(jnp.minimum(bit_ref[0], 1) != half)
+        def _():
+            copies = write_wide(half, (came_a_ref, came_b_ref), wide, hold, sems, width, hidden)
+            write_rest(came_b_ref if half else own_b_ref, start, outs, width, hidden)
+            for copy in copies:
+                copy.wait()
+
+
+def write_rest(source, start, outs, width, hidden):
+    (
+        low_inbias_ref,
+        low_outbias_ref,
+        low_gain_ref,
+        low_taskgate_ref,
+        low_sharegate_ref,
+        up_inbias_ref,
+        up_outbias_ref,
+        up_gain_ref,
+        up_taskgate_ref,
+        inner_ref,
+        tbias_ref,
+        middle_ref,
+        tail_ref,
+    ) = outs
+    inner = inner_ref.shape[1]
+
+    def take(rows):
+        nonlocal start
+        start += rows
+        return source[start - rows : start, :].astype(jnp.float32)
+
+    both = take(hidden)
+    inner_ref[:hidden, :] = both[:, :inner]
+    inner_ref[hidden:, :] = both[:, inner:]
+    middle_ref[...] = take(middle_ref.shape[0])
+    for index in range(width // hidden):
+        gates = take(32)
+        span = slice(index * hidden, (index + 1) * hidden)
+        low_taskgate_ref[:, span] = gates[0:4]
+        low_taskgate_ref[:, width + index * hidden : width + (index + 1) * hidden] = gates[8:12]
+        low_sharegate_ref[:, span] = gates[16:22]
+    for task in range(2):
+        up_taskgate_ref[:, task * hidden : (task + 1) * hidden] = take(16)[0:4]
+    rows = take(48)
+    flat = (low_inbias_ref, low_outbias_ref, up_inbias_ref, up_outbias_ref, tbias_ref, tail_ref)
+    place = 0
+    for target in flat + (low_gain_ref, up_gain_ref):
+        for index in range(target.shape[0] // hidden):
+            target[index * hidden : (index + 1) * hidden] = rows[place]
+            place += 1
 
 
 def finish(bit, own, came, width, hidden):
-    shapes = (
-        (6 * width, hidden),
+    wide_shapes = tuple(
+        jax.ShapeDtypeStruct((size, hidden), jnp.float32) for size in grad_layout(width, hidden)[0]
+    )
+    rest_shapes = (
         (6 * hidden,),
-        (6 * hidden, hidden),
         (6 * hidden,),
         (6 * hidden,),
         (4, 2 * width),
         (6, width),
-        (6 * hidden, hidden),
         (6 * hidden,),
-        (6 * hidden, hidden),
         (6 * hidden,),
         (6 * hidden,),
         (4, 2 * hidden),
@@ -967,16 +1025,34 @@
         (64, 256),
         (256,),
     )
+    outside, inside = pl.BlockSpec(memory_space=pl.ANY), pl.BlockSpec(memory_space=pltpu.VMEM)
+    small = pl.BlockSpec(memory_space=pltpu.SMEM)
+    params = pltpu.CompilerParams(vmem_limit_bytes=VMEM_LIMIT)
+    moved = 6 * 2 * own[0].size
+    scratch = [pltpu.VMEM((2 * own[0].shape[0], hidden), jnp.float32), pltpu.SemaphoreType.DMA((4,))]
+    wide = pl.pallas_call(
+        own_body,
+        out_shape=wide_shapes,
+        in_specs=[small, inside, inside],
+        out_specs=(outside,) * 4,
+        scratch_shapes=scratch,
+        compiler_params=params,
+        cost_estimate=pl.CostEstimate(flops=0, bytes_accessed=moved, transcendentals=0),
+    )(bit, *own)
     done = pl.pallas_call(
-        finish_body,
-        out_shape=tuple(jax.ShapeDtypeStruct(shape, jnp.float32) for shape in shapes),
-        in_specs=[pl.BlockSpec(memory_space=pltpu.SMEM)] + [pl.BlockSpec(memory_space=pltpu.VMEM)] * 4,
-        compiler_params=pltpu.CompilerParams(vmem_limit_bytes=VMEM_LIMIT),
-        cost_estimate=pl.CostEstimate(
-            flops=0, bytes_accessed=12 * width * hidden * 16, transcendentals=0
-        ),
-    )(bit, *own, *came)
-    return tuple(value.T if value.shape[0] in (4, 6, 64) else value for value in done)
+        came_body,
+        out_shape=wide_shapes
+        + tuple(jax.ShapeDtypeStruct(shape, jnp.float32) for shape in rest_shapes),
+        in_specs=[small] + [inside] * 3 + [outside] * 4,
+        out_specs=(outside,) * 4 + (inside,) * 13,
+        scratch_shapes=scratch,
+        input_output_aliases={4 + index: index for index in range(4)},
+        compiler_params=params,
+        cost_estimate=pl.CostEstimate(flops=0, bytes_accessed=moved, transcendentals=0),
+    )(bit, own[1], *came, *wide)
+    done = [value.T if value.shape[0] in (4, 6, 64) else value for value in done]
+    wide, rest = done[:4], done[4:]
+    return (wide[0], rest[0], wide[1], *rest[1:5], wide[2], rest[5], wide[3], *rest[6:])
 
 
 def partners(mask, size):
@@ -1026,18 +1102,21 @@
     return chosen
 
 
-def scatter_sum(values):
+def z_pieces(values):
     group = lax.axis_size("fsdp")
     place = lax.axis_index("fsdp")
     rows = values.shape[0] // group
-    pieces = [
+    return [
         lax.dynamic_slice_in_dim(values, (place ^ mask) * rows, rows, 0) for mask in range(group)
     ]
-    pieces = pieces[:1] + [swap_groups(pieces[mask], mask) for mask in range(1, group)]
+
+
+def scatter_sum(pieces):
+    came = [swap_groups(piece, mask) for mask, piece in enumerate(pieces) if mask]
     total = pieces[0].astype(jnp.float32)
-    for piece in pieces[1:]:
+    for piece in came:
         total = total + piece.astype(jnp.float32)
-    return total.astype(values.dtype)
+    return total.astype(pieces[0].dtype)
 
 
 def dp_masks(size):
@@ -1087,26 +1166,29 @@
     group = lax.axis_size("fsdp")
     place = lax.axis_index("dp")
     first, orders = dp_orders()
-    mine = add_low(kept, swap_with(sent, first, size))
+    came = swap_with(sent, first, size)
+    outgoing, x_grad = prepare(flipped_grad)
+    came, outgoing = lax.optimization_barrier((came, outgoing))
+    mine = add_low(kept, came)
     rows = mine.shape[0] // 2
     parts = [mine[:rows], mine[rows:]]
     for step in range(len(orders[0])):
         halves = [cut(part, order[step], place) for part, order in zip(parts, orders)]
         if step == 0:
-            halves, flipped_grad = lax.optimization_barrier((halves, flipped_grad))
-            outgoing = prepare(flipped_grad)
+            halves, outgoing = lax.optimization_barrier((halves, outgoing))
+            incoming = lax.all_to_all(
+                outgoing, ("dp", "fsdp"), split_axis=0, concat_axis=0, tiled=True
+            )
         parts = [
             add_low(kept, swap_with(sent, order[step], size))
             for (sent, kept), order in zip(halves, orders)
         ]
-        if step == 0:
-            parts, outgoing = lax.optimization_barrier((parts, outgoing))
-    incoming = lax.all_to_all(outgoing, ("dp", "fsdp"), split_axis=0, concat_axis=0, tiled=True)
     both = [part.reshape((group, -1) + part.shape[1:]) for part in parts]
-    summed = scatter_sum(jnp.concatenate(both, axis=1).reshape((-1,) + kept.shape[1:]))
-    summed, incoming = lax.optimization_barrier((summed, incoming))
-    shared = share(summed)
-    late = (finish_rows(incoming), flipped_grad.T)
+    both = jnp.concatenate(both, axis=1).reshape((-1,) + kept.shape[1:])
+    pieces = z_pieces(both)
+    pieces, incoming = lax.optimization_barrier((pieces, incoming))
+    shared = share(scatter_sum(pieces))
+    late = (finish_rows(incoming), x_grad)
     parts = [piece.reshape((-1,) + kept.shape[1:]) for piece in jnp.split(shared, 2, axis=1)]
     own, came, late, _ = spread(parts, late)
     return finish((place & first).reshape(1), own, came, width, hidden), *late
@@ -1182,7 +1264,7 @@
     logits, flipped_grad, kept, sent = dense(bit, flipped, weights, places, thin, logit_cot, grad_rows)
 
     def prepare(flipped_grad):
-        return send_rows(flipped_grad, rank, owner_rows, capacity)
+        return send_rows(flipped_grad, rank, owner_rows, capacity, 1)
 
     def finish_rows(incoming):
         return add_rows(incoming, asked_rows, embed_table.shape[0])

time: 207 us -> 204 us (0.986)
  waiting for transfers between devices: 90.9 us -> 85.6 us
    ppermute x9, waiting for transfers between devices: 23.6 us -> 17.7 us  [swap_groups(): return lax.ppermute(values, 'fsdp', partners(mask, lax.axis_size('fsdp')))]
    pallas_call x2 -> x3, Pallas kernels: 12.7 us -> 14.7 us  [the longest x1 6.46 us: send_rows(): local_kernel(functools.partial(send_body, group), (jax.ShapeDtypeStruct((...]
  transfers between devices with their start and end apart: 29 -> 29, of which waited for: 20 -> 16; matrix products, arithmetic and copies ran while one was open for 1% -> 2% of each run, Pallas kernels for 14% -> 16%
where the time goes in v4:
time: 204 us; the launch traced here: 203 us
  waiting for transfers between devices  85.6 us (42%)
  Pallas kernels  62.6 us (31%)
  starting transfers between devices  42.7 us (21%)
  other arithmetic  7.09 us (3%)
  local copies, waits for them, and re-layouts  4 us (2%)
    ppermute x17, waiting for transfers between devices, swap_with(): return lax.ppermute(values, 'dp', partners(mask, size))  60.6 us
    pallas_call x1, Pallas kernels, dense(): pl.pallas_call(functools.partial(dense_body, places), out_shape=(jax.Shap...  21.1 us
    ppermute x9, waiting for transfers between devices, swap_groups(): return lax.ppermute(values, 'fsdp', partners(mask, lax.axis_size('fsdp')))  17.7 us
    ppermute x9, starting transfers between devices, swap_groups(): return lax.ppermute(values, 'fsdp', partners(mask, lax.axis_size('fsdp')))  14.8 us
    ppermute x17, starting transfers between devices, swap_with(): return lax.ppermute(values, 'dp', partners(mask, size))  14.2 us
    pallas_call x1, Pallas kernels, find_rows(): local_kernel(find_body, jax.ShapeDtypeStruct((devices, width, capacity),...  7.27 us
    all_to_all x1, waiting for transfers between devices, on_device(): lax.all_to_all(request, ('dp', 'fsdp'), split_axis=0, concat_axis=0, tile...  7.25 us
    pallas_call x1, Pallas kernels, add_rows(): local_kernel(add_body, jax.ShapeDtypeStruct((width, rows), jnp.float32),...  6.73 us
  transfers between devices with their start and end apart: 29, of which 16 were waited for; matrix products, arithmetic and copies ran while one was open for 2% of the time, Pallas kernels for 16%

profile of v4, /device:TPU:0, one launch (start us, length us, event | category | flops | bytes accessed | tf_op | source)
XLA Modules:
  0.0 203.3 jit_solution(5439395784780487635)
XLA Ops:
  0.7 1.6 shard_map.356
  2.3 5.0 %collective-permute-start.2 = (bf16[288,256]{1,0:T(8,128)(2,1)}, bf16[288,256]{1,0:T(8,128)(2,1)S(1)}, u32[]{:S(2)}, u32[]{:S(2)}) collective-permute-start(bf16[288,256]{1,0:T(8,128)(2,1)} %shard_map.356), channel_id=1, source_target_pairs={{0,3},{1,2},{2,1},{3,0},{4,7},{5,6},{6,5},{7,4},{8,11},{9,10},{10,... | collective-permute-start | bytes 442376 | tf_op jit(solution)/shard_map/ppermute | solution.py:1086
  7.9 2.4 %shard_map.357 = (s32[32,1,256]{2,1,0:T(1,128)}, s32[32,512]{1,0:T(8,128)}) custom-call(s32[8,512]{1,0:T(8,128)} %bitcast.60, s32[8,512]{1,0:T(8,128)} %bitcast.59), custom_call_target="tpu_custom_call" | custom-call | flops 150994944 | bytes 98304 | tf_op jit(solution)/shard_map/pallas_call | solution.py:70
  10.4 6.0 %all-to-all-start = ((s32[32,1,256]{2,1,0:T(1,128)}), s32[32,1,256]{2,1,0:T(1,128)S(1)}, u32[]{:S(2)}, u32[]{:S(2)}) async-start(s32[32,1,256]{2,1,0:T(1,128)} %get-tuple-element.86), calls=%async_computation | async-start | bytes 65536 | tf_op jit(solution)/shard_map/all_to_all | solution.py:1229
  16.4 7.3 %all-to-all-done.request_ref = s32[32,1,256]{2,1,0:T(1,128)S(1)} async-done(((s32[32,1,256]{2,1,0:T(1,128)}), s32[32,1,256]{2,1,0:T(1,128)S(1)}, u32[]{:S(2)}, u32[]{:S(2)}) %all-to-all-start) | async-done | bytes 32800 | tf_op jit(solution)/shard_map/all_to_all | solution.py:1229
  23.7 1.0 select_bitcast_fusion.3
  24.8 0.7 collective-permute-start.3
  26.0 7.3 %shard_map.358 = bf16[32,64,256]{2,1,0:T(8,128)(2,1)} custom-call(s32[32,1,256]{2,1,0:T(1,128)} %copy-done.8, bf16[64,4096]{1,0:T(8,128)(2,1)} %bitcast.57), custom_call_target="tpu_custom_call" | custom-call | flops 4294967296 | bytes 1572864 | tf_op jit(solution)/shard_map/pallas_call | solution.py:110
  34.3 0.8 collective-permute-start.5
  35.1 3.4 %all-to-all-start.1 = ((bf16[32,64,256]{2,1,0:T(8,128)(2,1)}), bf16[32,64,256]{2,1,0:T(8,128)(2,1)}, u32[]{:S(2)}, u32[]{:S(2)}) async-start(bf16[32,64,256]{2,1,0:T(8,128)(2,1)} %shard_map.358), calls=%async_computation.1 | async-start | bytes 2097152 | tf_op jit(solution)/shard_map/all_to_all | solution.py:1241
  38.5 1.6 collective-permute-start.6
  40.1 15.3 %collective-permute-done.5 = bf16[1152,256]{1,0:T(8,128)(2,1)S(1)} collective-permute-done((bf16[1152,256]{1,0:T(8,128)(2,1)S(1)}, bf16[1152,256]{1,0:T(8,128)(2,1)S(1)}, u32[]{:S(2)}, u32[]{:S(2)}) %collective-permute-start.5) | collective-permute-done | bytes 589856 | tf_op jit(solution)/shard_map/ppermute | solution.py:1063
  55.6 9.4 %collective-permute-done.6 = bf16[1152,256]{1,0:T(8,128)(2,1)S(1)} collective-permute-done((bf16[1152,256]{1,0:T(8,128)(2,1)S(1)}, bf16[1152,256]{1,0:T(8,128)(2,1)S(1)}, u32[]{:S(2)}, u32[]{:S(2)}) %collective-permute-start.6) | collective-permute-done | bytes 589856 | tf_op jit(solution)/shard_map/ppermute | solution.py:1063
  65.8 6.0 %shard_map.359.refs_5_ = bf16[512,512]{1,0:T(8,128)(2,1)} custom-call(bf16[32,64,256]{2,1,0:T(8,128)(2,1)} %all-to-all-done.1.found_ref, s32[32,512]{1,0:T(8,128)} %get-tuple-element.96.rank_ref, s32[8,512]{1,0:T(8,128)} %bitcast.61), custom_call_target="tpu_custom_call" | custom-call | flops 536870912 | bytes 1572864 | tf_op jit(solution)/shard_map/pallas_call | solution.py:153
  71.8 1.0 copy-done.3
  72.8 2.9 %shard_map.360 = (f32[256,64]{1,0:T(8,128)}, bf16[32,512]{1,0:T(8,128)(2,1)}, bf16[512,32]{1,0:T(8,128)(2,1)}, bf16[16,256]{1,0:T(8,128)(2,1)}, bf16[512,16]{1,0...) custom-call(s32[1]{0:T(128)} %bitcast.bit_ref.refs_0_, ...), custom_call_target="tpu_custom_call" | custom-call | bytes 2359296 | tf_op jit(solution)/shard_map/pallas_call | solution.py:394
  75.7 21.1 %shard_map.361 = (f32[2,512]{1,0:T(2,128)}, f32[512,512]{1,0:T(8,128)}, bf16[4096,256]{1,0:T(8,128)(2,1)}, bf16[4096,256]{1,0:T(8,128)(2,1)}) custom-call(s32[1]{0:T(128)} %bitcast.bit_ref.refs_0_, bf16[2304,256]{1,0:T(8,128)(2,1)} %copy-done.1, bf16[2304,256]{1,0:T(8,128)(2,1)} %copy-done.4, bf16[2304,256]{1,0:T(8,128)(2,1)} %copy-done.3, ...), custom_call_target="tpu_custom_call" | custom-call | flops 6241124352 | bytes 25165824 | tf_op jit(solution)/shard_map/pallas_call | solution.py:872
  96.9 6.5 %shard_map.362 = (bf16[32,64,256]{2,1,0:T(8,128)(2,1)}, f32[512,512]{1,0:T(8,128)}) custom-call(f32[512,512]{1,0:T(8,128)} %get-tuple-element.112.grad_ref, s32[32,512]{1,0:T(8,128)} %get-tuple-element.96.rank_ref, s32[8,512]{1,0:T(8,128)} %bitcast.62), custom_call_target="tpu_custom_call" | custom-call | flops 536870912 | bytes 2097152 | tf_op jit(solution)/shard_map/pallas_call | solution.py:194
  103.3 2.1 %add_convert_fusion = bf16[4096,256]{1,0:T(8,128)(2,1)S(1)} fusion(bf16[4096,256]{1,0:T(8,128)(2,1)S(1)} %collective-permute-done.9, bf16[4096,256]{1,0:T(8,128)(2,1)} %get-tuple-element.110), kind=kLoop, calls=%fused_computation | loop fusion | flops 4194304 | bytes 6291456 | tf_op jit(solution)/shard_map/convert_element_type | solution.py:1074
  105.6 0.9 constant_dynamic-slice_fusion.6
  106.5 1.3 collective-permute-start.10
  107.8 4.4 %all-to-all-start.2 = ((bf16[32,64,256]{2,1,0:T(8,128)(2,1)}), bf16[32,64,256]{2,1,0:T(8,128)(2,1)S(1)}, u32[]{:S(2)}, u32[]{:S(2)}) async-start(bf16[32,64,256]{2,1,0:T(8,128)(2,1)} %get-tuple-element.120), calls=%async_computation.2 | async-start | bytes 2097152 | tf_op jit(solution)/shard_map/all_to_all | solution.py:1179
  112.2 1.6 collective-permute-start.12
  113.8 12.8 %collective-permute-done.10 = bf16[1024,256]{1,0:T(8,128)(2,1)} collective-permute-done((bf16[1024,256]{1,0:T(8,128)(2,1)S(1)}, bf16[1024,256]{1,0:T(8,128)(2,1)}, u32[]{:S(2)}, u32[]{:S(2)}) %collective-permute-start.10) | collective-permute-done | bytes 524320 | tf_op jit(solution)/shard_map/ppermute | solution.py:1063
  126.5 1.2 add_convert_fusion.2
  128.0 9.7 %collective-permute-done.12 = bf16[1024,256]{1,0:T(8,128)(2,1)S(1)} collective-permute-done((bf16[1024,256]{1,0:T(8,128)(2,1)}, bf16[1024,256]{1,0:T(8,128)(2,1)S(1)}, u32[]{:S(2)}, u32[]{:S(2)}) %collective-permute-start.12) | collective-permute-done | bytes 524320 | tf_op jit(solution)/shard_map/ppermute | solution.py:1063
  137.9 1.1 collective-permute-start.13
  139.0 4.0 %collective-permute-done.11 = bf16[512,256]{1,0:T(8,128)(2,1)} collective-permute-done((bf16[512,256]{1,0:T(8,128)(2,1)S(1)}, bf16[512,256]{1,0:T(8,128)(2,1)}, u32[]{:S(2)}, u32[]{:S(2)}) %collective-permute-start.11) | collective-permute-done | bytes 262176 | tf_op jit(solution)/shard_map/ppermute | solution.py:1063
  143.0 1.0 add_convert_fusion.4
  144.0 0.6 collective-permute-done.13
  144.8 2.0 collective-permute-start.14
  146.8 2.7 %collective-permute-start.15 = (bf16[256,256]{1,0:T(8,128)(2,1)S(1)}, bf16[256,256]{1,0:T(8,128)(2,1)S(1)}, u32[]{:S(2)}, u32[]{:S(2)}) collective-permute-start(bf16[256,256]{1,0:T(8,128)(2,1)S(1)} %get-tuple-element.123), channel_id=1, source_target_pairs={{0,2},{1,3},{2,0},{3,1},{4,6},{5,7},{6,4},{7,5},{8,10},{9,11},{10,... | collective-permute-start | bytes 393224 | tf_op jit(solution)/shard_map/ppermute | solution.py:1086
  149.5 1.8 collective-permute-done.14
  151.3 7.2 %collective-permute-done.15 = bf16[256,256]{1,0:T(8,128)(2,1)S(1)} collective-permute-done((bf16[256,256]{1,0:T(8,128)(2,1)S(1)}, bf16[256,256]{1,0:T(8,128)(2,1)S(1)}, u32[]{:S(2)}, u32[]{:S(2)}) %collective-permute-start.15) | collective-permute-done | bytes 131104 | tf_op jit(solution)/shard_map/ppermute | solution.py:1086
  158.5 2.0 collective-permute-start.19
  160.6 0.9 collective-permute-start.18
  161.5 1.5 collective-permute-start.17
  163.0 1.5 collective-permute-done.19
  164.5 7.3 %collective-permute-done.18 = bf16[256,256]{1,0:T(8,128)(2,1)S(1)} collective-permute-done((bf16[256,256]{1,0:T(8,128)(2,1)S(1)}, bf16[256,256]{1,0:T(8,128)(2,1)S(1)}, u32[]{:S(2)}, u32[]{:S(2)}) %collective-permute-start.18) | collective-permute-done | bytes 131104 | tf_op jit(solution)/shard_map/ppermute | solution.py:1086
  172.0 1.7 collective-permute-start.20
  173.7 0.7 collective-permute-start.22
  174.4 5.7 %collective-permute-done.20 = bf16[512,256]{1,0:T(8,128)(2,1)S(1)} collective-permute-done((bf16[512,256]{1,0:T(8,128)(2,1)S(1)}, bf16[512,256]{1,0:T(8,128)(2,1)S(1)}, u32[]{:S(2)}, u32[]{:S(2)}) %collective-permute-start.20) | collective-permute-done | bytes 262176 | tf_op jit(solution)/shard_map/ppermute | solution.py:1063
  180.1 2.3 %collective-permute-start.21 = (bf16[1024,256]{1,0:T(8,128)(2,1)S(1)}, bf16[1024,256]{1,0:T(8,128)(2,1)S(1)}, u32[]{:S(2)}, u32[]{:S(2)}) collective-permute-start(bf16[1024,256]{1,0:T(8,128)(2,1)S(1)} %pad_maximum_fusion.9), channel_id=1, source_target_pairs={{0,8},{4,12},{8,0},{12,4},{16,24},{20,28},{24,16},{28,20},{1,9},{5... | collective-permute-start | bytes 1572872 | tf_op jit(solution)/shard_map/ppermute | solution.py:1063
  183.4 6.7 %shard_map.363 = f32[64,4096]{1,0:T(8,128)} custom-call(bf16[32,64,256]{2,1,0:T(8,128)(2,1)} %copy-done.5, s32[32,1,256]{2,1,0:T(1,128)} %copy-done.8), custom_call_target="tpu_custom_call" | custom-call | flops 4294967296 | bytes 2097152 | tf_op jit(solution)/shard_map/pallas_call | solution.py:245
  190.4 1.9 collective-permute-done.23
  193.5 3.7 %shard_map.364 = (f32[3072,256]{1,0:T(8,128)}, f32[1536,256]{1,0:T(8,128)}, f32[1536,256]{1,0:T(8,128)}, f32[1536,256]{1,0:T(8,128)}) custom-call(s32[1]{0:T(128)} %bitcast.bit_ref.refs_0_, bf16[2048,256]{1,0:T(8,128)(2,1)} %copy-done.2, bf16[2048,256]{1,0:T(8,128)(2,1)} %copy-done), custom_call_target="tpu_custom_call" | custom-call | bytes 6291456 | tf_op jit(solution)/shard_map/pallas_call | solution.py:1033
  197.3 1.0 copy-done.6
  198.6 4.5 %shard_map.365 = (f32[3072,256]{1,0:T(8,128)}, f32[1536,256]{1,0:T(8,128)}, f32[1536,256]{1,0:T(8,128)}, f32[1536,256]{1,0:T(8,128)}, f32[1536]{0:T(1024)}, /*in...) custom-call(s32[1]{0:T(128)} %bitcast.bit_ref.refs_0_, ...), custom_call_target="tpu_custom_call", output_to_operand_aliasing={{0}: (4, {}), {1}: (5, {}), {2}: (6, {}), {3}: (7, {})} | custom-call | bytes 6291456 | tf_op jit(solution)/shard_map/pallas_call | solution.py:1042
  (72 shorter events, 7.2 us)
Async XLA Ops:
  2.3 21.4 %collective-permute-start.2 = (bf16[288,256]{1,0:T(8,128)(2,1)}, bf16[288,256]{1,0:T(8,128)(2,1)S(1)}, u32[]{:S(2)}, u32[]{:S(2)}) collective-permute-start(bf16[288,256]{1,0:T(8,128)(2,1)} %shard_map.356), channel_id=1, source_target_pairs={{0,3},{1,2},{2,1},{3,0},{4,7},{5,6},{6,5},{7,4},{8,11},{9,10},{10,... | collective-permute-start | bytes 442376 | tf_op jit(solution)/shard_map/ppermute | solution.py:1086
  7.3 16.4 %collective-permute-start.1 = (bf16[288,256]{1,0:T(8,128)(2,1)}, bf16[288,256]{1,0:T(8,128)(2,1)S(1)}, u32[]{:S(2)}, u32[]{:S(2)}) collective-permute-start(bf16[288,256]{1,0:T(8,128)(2,1)} %shard_map.356), channel_id=1, source_target_pairs={{0,2},{1,3},{2,0},{3,1},{4,6},{5,7},{6,4},{7,5},{8,10},{9,11},{10,... | collective-permute-start | bytes 442376 | tf_op jit(solution)/shard_map/ppermute | solution.py:1086
  7.3 16.4 %collective-permute-start = (bf16[288,256]{1,0:T(8,128)(2,1)}, bf16[288,256]{1,0:T(8,128)(2,1)S(1)}, u32[]{:S(2)}, u32[]{:S(2)}) collective-permute-start(bf16[288,256]{1,0:T(8,128)(2,1)} %shard_map.356), channel_id=1, source_target_pairs={{0,1},{1,0},{2,3},{3,2},{4,5},{5,4},{6,7},{7,6},{8,9},{9,8},{10,11... | collective-permute-start | bytes 442376 | tf_op jit(solution)/shard_map/ppermute | solution.py:1086
  10.4 13.3 %all-to-all-start = ((s32[32,1,256]{2,1,0:T(1,128)}), s32[32,1,256]{2,1,0:T(1,128)S(1)}, u32[]{:S(2)}, u32[]{:S(2)}) async-start(s32[32,1,256]{2,1,0:T(1,128)} %get-tuple-element.86), calls=%async_computation | async-start | bytes 65536 | tf_op jit(solution)/shard_map/all_to_all | solution.py:1229
  23.7 2.4 %copy-start.8 = (s32[32,1,256]{2,1,0:T(1,128)}, s32[32,1,256]{2,1,0:T(1,128)S(1)}, u32[]{:S(2)}) copy-start(s32[32,1,256]{2,1,0:T(1,128)S(1)} %all-to-all-done.request_ref) | copy-start | bytes 98308
  24.8 8.7 %collective-permute-start.3 = (bf16[576,256]{1,0:T(8,128)(2,1)S(1)}, bf16[576,256]{1,0:T(8,128)(2,1)S(1)}, u32[]{:S(2)}, u32[]{:S(2)}) collective-permute-start(bf16[576,256]{1,0:T(8,128)(2,1)S(1)} %bitcast.49), channel_id=1, source_target_pairs={{0,16},{4,20},{8,24},{12,28},{16,0},{20,4},{24,8},{28,12},{1,17},{... | collective-permute-start | bytes 884744 | tf_op jit(solution)/shard_map/ppermute | solution.py:1063
  25.5 8.6 %collective-permute-start.4 = (bf16[576,256]{1,0:T(8,128)(2,1)S(1)}, bf16[576,256]{1,0:T(8,128)(2,1)S(1)}, u32[]{:S(2)}, u32[]{:S(2)}) collective-permute-start(bf16[576,256]{1,0:T(8,128)(2,1)S(1)} %bitcast.48), channel_id=1, source_target_pairs={{0,8},{4,12},{8,0},{12,4},{16,24},{20,28},{24,16},{28,20},{1,9},{5... | collective-permute-start | bytes 884744 | tf_op jit(solution)/shard_map/ppermute | solution.py:1063
  34.3 21.1 %collective-permute-start.5 = (bf16[1152,256]{1,0:T(8,128)(2,1)S(1)}, bf16[1152,256]{1,0:T(8,128)(2,1)S(1)}, u32[]{:S(2)}, u32[]{:S(2)}) collective-permute-start(bf16[1152,256]{1,0:T(8,128)(2,1)S(1)} %get-tuple-element.91), channel_id=1, source_target_pairs={{0,8},{4,12},{8,0},{12,4},{16,24},{20,28},{24,16},{28,20},{1,9},{5... | collective-permute-start | bytes 1769480 | tf_op jit(solution)/shard_map/ppermute | solution.py:1063
  35.1 30.7 %all-to-all-start.1 = ((bf16[32,64,256]{2,1,0:T(8,128)(2,1)}), bf16[32,64,256]{2,1,0:T(8,128)(2,1)}, u32[]{:S(2)}, u32[]{:S(2)}) async-start(bf16[32,64,256]{2,1,0:T(8,128)(2,1)} %shard_map.358), calls=%async_computation.1 | async-start | bytes 2097152 | tf_op jit(solution)/shard_map/all_to_all | solution.py:1241
  38.5 26.5 %collective-permute-start.6 = (bf16[1152,256]{1,0:T(8,128)(2,1)S(1)}, bf16[1152,256]{1,0:T(8,128)(2,1)S(1)}, u32[]{:S(2)}, u32[]{:S(2)}) collective-permute-start(bf16[1152,256]{1,0:T(8,128)(2,1)S(1)} %get-tuple-element.92), channel_id=1, source_target_pairs={{0,16},{4,20},{8,24},{12,28},{16,0},{20,4},{24,8},{28,12},{1,17},{... | collective-permute-start | bytes 1769480 | tf_op jit(solution)/shard_map/ppermute | solution.py:1063
  55.6 9.7 %copy-start.1 = (bf16[2304,256]{1,0:T(8,128)(2,1)}, bf16[2304,256]{1,0:T(8,128)(2,1)S(1)}, u32[]{:S(2)}) copy-start(bf16[2304,256]{1,0:T(8,128)(2,1)S(1)} %pad_maximum_fusion.refs_1_) | copy-start | bytes 3538948
  65.2 10.5 %copy-start.4 = (bf16[2304,256]{1,0:T(8,128)(2,1)}, bf16[2304,256]{1,0:T(8,128)(2,1)S(1)}, u32[]{:S(2)}) copy-start(bf16[2304,256]{1,0:T(8,128)(2,1)S(1)} %pad_maximum_fusion.1.refs_2_) | copy-start | bytes 3538948
  65.2 6.5 %collective-permute-start.8 = (bf16[2304,256]{1,0:T(8,128)(2,1)S(1)}, bf16[2304,256]{1,0:T(8,128)(2,1)}, u32[]{:S(2)}, u32[]{:S(2)}) collective-permute-start(bf16[2304,256]{1,0:T(8,128)(2,1)S(1)} %pad_maximum_fusion.1.refs_2_), channel_id=1, source_target_pairs={{0,4},{4,0},{8,12},{12,8},{16,20},{20,16},{24,28},{28,24},{1,5},{5... | collective-permute-start | bytes 3538952 | tf_op jit(solution)/shard_map/ppermute | solution.py:1063
  65.3 6.5 %collective-permute-start.7 = (bf16[2304,256]{1,0:T(8,128)(2,1)S(1)}, bf16[2304,256]{1,0:T(8,128)(2,1)S(1)}, u32[]{:S(2)}, u32[]{:S(2)}) collective-permute-start(bf16[2304,256]{1,0:T(8,128)(2,1)S(1)} %pad_maximum_fusion.refs_1_), channel_id=1, source_target_pairs={{0,4},{4,0},{8,12},{12,8},{16,20},{20,16},{24,28},{28,24},{1,5},{5... | collective-permute-start | bytes 3538952 | tf_op jit(solution)/shard_map/ppermute | solution.py:1063
  71.8 1.0 copy-start.3
  96.7 6.6 %collective-permute-start.9 = (bf16[4096,256]{1,0:T(8,128)(2,1)}, bf16[4096,256]{1,0:T(8,128)(2,1)S(1)}, u32[]{:S(2)}, u32[]{:S(2)}) collective-permute-start(bf16[4096,256]{1,0:T(8,128)(2,1)} %get-tuple-element.111), channel_id=1, source_target_pairs={{0,4},{4,0},{8,12},{12,8},{16,20},{20,16},{24,28},{28,24},{1,5},{5... | collective-permute-start | bytes 6291464 | tf_op jit(solution)/shard_map/ppermute | solution.py:1063
  106.5 20.0 %collective-permute-start.10 = (bf16[1024,256]{1,0:T(8,128)(2,1)S(1)}, bf16[1024,256]{1,0:T(8,128)(2,1)}, u32[]{:S(2)}, u32[]{:S(2)}) collective-permute-start(bf16[1024,256]{1,0:T(8,128)(2,1)S(1)} %get-tuple-element.117), channel_id=1, source_target_pairs={{0,8},{4,12},{8,0},{12,4},{16,24},{20,28},{24,16},{28,20},{1,9},{5... | collective-permute-start | bytes 1572872 | tf_op jit(solution)/shard_map/ppermute | solution.py:1063
  107.8 37.0 %all-to-all-start.2 = ((bf16[32,64,256]{2,1,0:T(8,128)(2,1)}), bf16[32,64,256]{2,1,0:T(8,128)(2,1)S(1)}, u32[]{:S(2)}, u32[]{:S(2)}) async-start(bf16[32,64,256]{2,1,0:T(8,128)(2,1)} %get-tuple-element.120), calls=%async_computation.2 | async-start | bytes 2097152 | tf_op jit(solution)/shard_map/all_to_all | solution.py:1179
  112.2 25.6 %collective-permute-start.12 = (bf16[1024,256]{1,0:T(8,128)(2,1)}, bf16[1024,256]{1,0:T(8,128)(2,1)S(1)}, u32[]{:S(2)}, u32[]{:S(2)}) collective-permute-start(bf16[1024,256]{1,0:T(8,128)(2,1)} %get-tuple-element.119), channel_id=1, source_target_pairs={{0,16},{4,20},{8,24},{12,28},{16,0},{20,4},{24,8},{28,12},{1,17},{... | collective-permute-start | bytes 1572872 | tf_op jit(solution)/shard_map/ppermute | solution.py:1063
  127.7 15.2 %collective-permute-start.11 = (bf16[512,256]{1,0:T(8,128)(2,1)S(1)}, bf16[512,256]{1,0:T(8,128)(2,1)}, u32[]{:S(2)}, u32[]{:S(2)}) collective-permute-start(bf16[512,256]{1,0:T(8,128)(2,1)S(1)} %constant_dynamic-slice_fusion.5), channel_id=1, source_target_pairs={{0,16},{4,20},{8,24},{12,28},{16,0},{20,4},{24,8},{28,12},{1,17},{... | collective-permute-start | bytes 786440 | tf_op jit(solution)/shard_map/ppermute | solution.py:1063
  137.9 6.7 %collective-permute-start.13 = (bf16[512,256]{1,0:T(8,128)(2,1)S(1)}, bf16[512,256]{1,0:T(8,128)(2,1)S(1)}, u32[]{:S(2)}, u32[]{:S(2)}) collective-permute-start(bf16[512,256]{1,0:T(8,128)(2,1)S(1)} %constant_dynamic-slice_fusion.4), channel_id=1, source_target_pairs={{0,8},{4,12},{8,0},{12,4},{16,24},{20,28},{24,16},{28,20},{1,9},{5... | collective-permute-start | bytes 786440 | tf_op jit(solution)/shard_map/ppermute | solution.py:1063
  144.8 35.3 %copy-start.5 = (bf16[32,64,256]{2,1,0:T(8,128)(2,1)}, bf16[32,64,256]{2,1,0:T(8,128)(2,1)S(1)}, u32[]{:S(2)}) copy-start(bf16[32,64,256]{2,1,0:T(8,128)(2,1)S(1)} %all-to-all-done.2.came_ref) | copy-start | bytes 3145732
  144.8 6.4 %collective-permute-start.14 = (bf16[256,256]{1,0:T(8,128)(2,1)S(1)}, bf16[256,256]{1,0:T(8,128)(2,1)S(1)}, u32[]{:S(2)}, u32[]{:S(2)}) collective-permute-start(bf16[256,256]{1,0:T(8,128)(2,1)S(1)} %get-tuple-element.122), channel_id=1, source_target_pairs={{0,1},{1,0},{2,3},{3,2},{4,5},{5,4},{6,7},{7,6},{8,9},{9,8},{10,11... | collective-permute-start | bytes 393224 | tf_op jit(solution)/shard_map/ppermute | solution.py:1086
  146.8 11.7 %collective-permute-start.15 = (bf16[256,256]{1,0:T(8,128)(2,1)S(1)}, bf16[256,256]{1,0:T(8,128)(2,1)S(1)}, u32[]{:S(2)}, u32[]{:S(2)}) collective-permute-start(bf16[256,256]{1,0:T(8,128)(2,1)S(1)} %get-tuple-element.123), channel_id=1, source_target_pairs={{0,2},{1,3},{2,0},{3,1},{4,6},{5,7},{6,4},{7,5},{8,10},{9,11},{10,... | collective-permute-start | bytes 393224 | tf_op jit(solution)/shard_map/ppermute | solution.py:1086
  149.5 9.0 %collective-permute-start.16 = (bf16[256,256]{1,0:T(8,128)(2,1)S(1)}, bf16[256,256]{1,0:T(8,128)(2,1)S(1)}, u32[]{:S(2)}, u32[]{:S(2)}) collective-permute-start(bf16[256,256]{1,0:T(8,128)(2,1)S(1)} %get-tuple-element.124), channel_id=1, source_target_pairs={{0,3},{1,2},{2,1},{3,0},{4,7},{5,6},{6,5},{7,4},{8,11},{9,10},{10,... | collective-permute-start | bytes 393224 | tf_op jit(solution)/shard_map/ppermute | solution.py:1086
  158.5 6.0 %collective-permute-start.19 = (bf16[256,256]{1,0:T(8,128)(2,1)S(1)}, bf16[256,256]{1,0:T(8,128)(2,1)S(1)}, u32[]{:S(2)}, u32[]{:S(2)}) collective-permute-start(bf16[256,256]{1,0:T(8,128)(2,1)S(1)} %add_convert_fusion.5), channel_id=1, source_target_pairs={{0,1},{1,0},{2,3},{3,2},{4,5},{5,4},{6,7},{7,6},{8,9},{9,8},{10,11... | collective-permute-start | bytes 393224 | tf_op jit(solution)/shard_map/ppermute | solution.py:1086
  160.6 11.2 %collective-permute-start.18 = (bf16[256,256]{1,0:T(8,128)(2,1)S(1)}, bf16[256,256]{1,0:T(8,128)(2,1)S(1)}, u32[]{:S(2)}, u32[]{:S(2)}) collective-permute-start(bf16[256,256]{1,0:T(8,128)(2,1)S(1)} %add_convert_fusion.5), channel_id=1, source_target_pairs={{0,2},{1,3},{2,0},{3,1},{4,6},{5,7},{6,4},{7,5},{8,10},{9,11},{10,... | collective-permute-start | bytes 393224 | tf_op jit(solution)/shard_map/ppermute | solution.py:1086
  161.5 10.3 %collective-permute-start.17 = (bf16[256,256]{1,0:T(8,128)(2,1)S(1)}, bf16[256,256]{1,0:T(8,128)(2,1)S(1)}, u32[]{:S(2)}, u32[]{:S(2)}) collective-permute-start(bf16[256,256]{1,0:T(8,128)(2,1)S(1)} %add_convert_fusion.5), channel_id=1, source_target_pairs={{0,3},{1,2},{2,1},{3,0},{4,7},{5,6},{6,5},{7,4},{8,11},{9,10},{10,... | collective-permute-start | bytes 393224 | tf_op jit(solution)/shard_map/ppermute | solution.py:1086
  172.0 8.0 %collective-permute-start.20 = (bf16[512,256]{1,0:T(8,128)(2,1)S(1)}, bf16[512,256]{1,0:T(8,128)(2,1)S(1)}, u32[]{:S(2)}, u32[]{:S(2)}) collective-permute-start(bf16[512,256]{1,0:T(8,128)(2,1)S(1)} %bitcast.51), channel_id=1, source_target_pairs={{0,16},{4,20},{8,24},{12,28},{16,0},{20,4},{24,8},{28,12},{1,17},{... | collective-permute-start | bytes 786440 | tf_op jit(solution)/shard_map/ppermute | solution.py:1063
  173.7 9.2 %collective-permute-start.22 = (bf16[512,256]{1,0:T(8,128)(2,1)S(1)}, bf16[512,256]{1,0:T(8,128)(2,1)S(1)}, u32[]{:S(2)}, u32[]{:S(2)}) collective-permute-start(bf16[512,256]{1,0:T(8,128)(2,1)S(1)} %bitcast.50), channel_id=1, source_target_pairs={{0,8},{4,12},{8,0},{12,4},{16,24},{20,28},{24,16},{28,20},{1,9},{5... | collective-permute-start | bytes 786440 | tf_op jit(solution)/shard_map/ppermute | solution.py:1063
  180.1 10.0 %collective-permute-start.21 = (bf16[1024,256]{1,0:T(8,128)(2,1)S(1)}, bf16[1024,256]{1,0:T(8,128)(2,1)S(1)}, u32[]{:S(2)}, u32[]{:S(2)}) collective-permute-start(bf16[1024,256]{1,0:T(8,128)(2,1)S(1)} %pad_maximum_fusion.9), channel_id=1, source_target_pairs={{0,8},{4,12},{8,0},{12,4},{16,24},{20,28},{24,16},{28,20},{1,9},{5... | collective-permute-start | bytes 1572872 | tf_op jit(solution)/shard_map/ppermute | solution.py:1063
  183.0 9.2 %collective-permute-start.23 = (bf16[1024,256]{1,0:T(8,128)(2,1)S(1)}, bf16[1024,256]{1,0:T(8,128)(2,1)S(1)}, u32[]{:S(2)}, u32[]{:S(2)}) collective-permute-start(bf16[1024,256]{1,0:T(8,128)(2,1)S(1)} %pad_maximum_fusion.10), channel_id=1, source_target_pairs={{0,16},{4,20},{8,24},{12,28},{16,0},{20,4},{24,8},{28,12},{1,17},{... | collective-permute-start | bytes 1572872 | tf_op jit(solution)/shard_map/ppermute | solution.py:1063
  190.4 2.2 %copy-start.2 = (bf16[2048,256]{1,0:T(8,128)(2,1)}, bf16[2048,256]{1,0:T(8,128)(2,1)S(1)}, u32[]{:S(2)}) copy-start(bf16[2048,256]{1,0:T(8,128)(2,1)S(1)} %pad_maximum_fusion.2.own_a_ref) | copy-start | bytes 3145732
  192.5 1.0 copy-start
  192.5 4.8 %collective-permute-start.24 = (bf16[2048,256]{1,0:T(8,128)(2,1)S(1)}, bf16[2048,256]{1,0:T(8,128)(2,1)S(1)}, u32[]{:S(2)}, u32[]{:S(2)}) collective-permute-start(bf16[2048,256]{1,0:T(8,128)(2,1)S(1)} %pad_maximum_fusion.2.own_a_ref), channel_id=1, source_target_pairs={{0,4},{4,0},{8,12},{12,8},{16,20},{20,16},{24,28},{28,24},{1,5},{5... | collective-permute-start | bytes 3145736 | tf_op jit(solution)/shard_map/ppermute | solution.py:1063
  192.6 4.7 %collective-permute-start.25 = (bf16[2048,256]{1,0:T(8,128)(2,1)S(1)}, bf16[2048,256]{1,0:T(8,128)(2,1)S(1)}, u32[]{:S(2)}, u32[]{:S(2)}) collective-permute-start(bf16[2048,256]{1,0:T(8,128)(2,1)S(1)} %pad_maximum_fusion.3.own_b_ref), channel_id=1, source_target_pairs={{0,4},{4,0},{8,12},{12,8},{16,20},{20,16},{24,28},{28,24},{1,5},{5... | collective-permute-start | bytes 3145736 | tf_op jit(solution)/shard_map/ppermute | solution.py:1063
  197.3 1.0 copy-start.6
  197.3 1.3 copy-start.7

commit v5 on v4

--- a/solution.py
+++ b/solution.py
@@ -9,15 +9,16 @@
 
 EPS = 1e-05
 VMEM_LIMIT = 56 * 1024 * 1024
+SMALL_LIMIT = 16 * 1024 * 1024
 ROW_BLOCKS = 8
 
 
-def local_kernel(body, out_shape, flops, moved, scratch=()):
+def local_kernel(body, out_shape, flops, moved, scratch=(), limit=SMALL_LIMIT):
     return pl.pallas_call(
         body,
         out_shape=out_shape,
         scratch_shapes=list(scratch),
-        compiler_params=pltpu.CompilerParams(vmem_limit_bytes=VMEM_LIMIT),
+        compiler_params=pltpu.CompilerParams(vmem_limit_bytes=limit),
         cost_estimate=pl.CostEstimate(flops=flops, bytes_accessed=moved, transcendentals=0),
     )
 
@@ -75,6 +76,7 @@
         ),
         2 * devices * events * (events + 2 * fields * capacity),
         4 * events * (2 * fields + devices),
+        limit=VMEM_LIMIT,
     )(owner_rows, row_rows)
 
 
@@ -110,7 +112,7 @@
     return local_kernel(
         find_body,
         jax.ShapeDtypeStruct((devices, width, capacity), jnp.bfloat16),
-        2 * devices * capacity * rows * width,
+        16 * devices * capacity * rows * width,
         2 * (rows * width + devices * capacity * width),
         [pltpu.VMEM((ROW_BLOCKS * width, rows // ROW_BLOCKS), jnp.bfloat16)],
     )(request, table)
@@ -284,61 +286,42 @@
         0,
         rows * 1024,
         [pltpu.VMEM((THIN_ROWS, 256), jnp.float32)],
+        limit=VMEM_LIMIT,
     )(*biases, *others, *(wide if aligned else ()))
     if aligned:
         return packed
     return jnp.concatenate([wide[0], packed, *wide[1:]], axis=0)
 
 
-def prep_thin_body(
-    places,
-    bit_ref,
-    own_ref,
-    came_ref,
-    columns_ref,
-    gate_one_ref,
-    gate_one_back_ref,
-    gate_two_ref,
-    gate_two_back_ref,
-    inner_ref,
-    inner_back_ref,
-    middle_ref,
-    middle_back_ref,
-    rows,
-    task_rows,
-    share_rows,
-    up_rows,
-    inner_rows,
-    middle_rows,
-    thin_own,
-    thin_came,
-    sems,
-):
+def lay_thin(bit, sources, places, outs, holds):
+    (
+        columns_ref,
+        gate_one_ref,
+        gate_one_back_ref,
+        gate_two_ref,
+        gate_two_back_ref,
+        inner_ref,
+        inner_back_ref,
+        middle_ref,
+        middle_back_ref,
+    ) = outs
+    rows, task_rows, share_rows, up_rows, inner_rows, middle_rows = holds
     devices = 2 * len(places[0])
-    start = own_ref.shape[1] - THIN_ROWS
-    copies = [
-        pltpu.make_async_copy(ref.at[:, pl.ds(start, THIN_ROWS), :], held, sems.at[index])
-        for index, (ref, held) in enumerate(((own_ref, thin_own), (came_ref, thin_came)))
-    ]
-    for copy in copies:
-        copy.start()
     hidden = columns_ref.shape[0]
     width = gate_one_ref.shape[1]
 
     def lay(target, source, index, count):
         target[:, index * count : (index + 1) * count] = source[:, :count]
 
-    rows[...] = jnp.zeros_like(rows)
-    task_rows[...] = jnp.zeros_like(task_rows)
-    share_rows[...] = jnp.zeros_like(share_rows)
-    up_rows[...] = jnp.zeros_like(up_rows)
+    for held in (rows, task_rows, share_rows, up_rows):
+        held[...] = jnp.zeros_like(held)
     bias = 6 * hidden // devices
     flat = hidden // devices
 
     def unpack(pieces):
         for half, source in enumerate(pieces):
             for block, index in enumerate(places[half]):
-                thin = source[block].astype(jnp.float32)
+                thin = source(block).astype(jnp.float32)
                 rows[0:6, index * bias : (index + 1) * bias] = thin[0:6, :bias]
                 rows[6:8, index * flat : (index + 1) * flat] = thin[6:8, :flat]
                 lay(task_rows, thin[8:16], index, 2 * width // devices)
@@ -349,16 +332,13 @@
                 count = hidden // devices
                 middle_rows[index * count : (index + 1) * count, :] = thin[32 : 32 + count, 128:192]
 
-    for copy in copies:
-        copy.wait()
-
-    @pl.when(bit_ref[0] == 0)
+    @pl.when(bit == 0)
     def _():
-        unpack((thin_own, thin_came))
-
-    @pl.when(bit_ref[0] != 0)
+        unpack(sources)
+
+    @pl.when(bit != 0)
     def _():
-        unpack((thin_came, thin_own))
+        unpack(sources[::-1])
 
     columns_ref[...] = jnp.zeros_like(columns_ref)
     for expert in range(6):
@@ -388,34 +368,53 @@
     middle_back_ref[...] = middle_rows[...].astype(jnp.bfloat16)
 
 
+def prep_thin_body(places, bit_ref, own_ref, came_ref, *refs):
+    outs, holds, (thin_own, thin_came, sems) = refs[:9], refs[9:15], refs[15:]
+    start = own_ref.shape[1] - THIN_ROWS
+    copies = [
+        pltpu.make_async_copy(ref.at[:, pl.ds(start, THIN_ROWS), :], held, sems.at[index])
+        for index, (ref, held) in enumerate(((own_ref, thin_own), (came_ref, thin_came)))
+    ]
+    for copy in copies:
+        copy.start()
+    for copy in copies:
+        copy.wait()
+    sources = (lambda block: thin_own[block], lambda block: thin_came[block])
+    lay_thin(bit_ref[0], sources, places, outs, holds)
+
+
+def thin_shapes(width, hidden):
+    outs = (
+        ((hidden, 64), jnp.float32),
+        ((32, width), jnp.bfloat16),
+        ((width, 32), jnp.bfloat16),
+        ((16, hidden), jnp.bfloat16),
+        ((2 * hidden, 16), jnp.bfloat16),
+        ((hidden, hidden), jnp.bfloat16),
+        ((2 * hidden, 128), jnp.bfloat16),
+        ((128, 128), jnp.bfloat16),
+        ((hidden, 64), jnp.bfloat16),
+    )
+    holds = (
+        (8, 6 * hidden),
+        (8, 2 * width),
+        (8, width),
+        (8, 2 * hidden),
+        (2 * hidden, 128),
+        (hidden, 64),
+    )
+    return outs, [pltpu.VMEM(shape, jnp.float32) for shape in holds]
+
+
 def prep_thin(bit, own, came, places, width, hidden):
     blocks = len(places[0])
-    low = functools.partial(jax.ShapeDtypeStruct, dtype=jnp.bfloat16)
+    outs, holds = thin_shapes(width, hidden)
+    thin_held = pltpu.VMEM((blocks, THIN_ROWS, hidden), jnp.bfloat16)
     return pl.pallas_call(
         functools.partial(prep_thin_body, places),
-        out_shape=(
-            jax.ShapeDtypeStruct((hidden, 64), jnp.float32),
-            low((32, width)),
-            low((width, 32)),
-            low((16, hidden)),
-            low((2 * hidden, 16)),
-            low((hidden, hidden)),
-            low((2 * hidden, 128)),
-            low((128, 128)),
-            low((hidden, 64)),
-        ),
+        out_shape=tuple(jax.ShapeDtypeStruct(*out) for out in outs),
         in_specs=[pl.BlockSpec(memory_space=pltpu.SMEM)] + [pl.BlockSpec(memory_space=pl.ANY)] * 2,
-        scratch_shapes=[
-            pltpu.VMEM((8, 6 * hidden), jnp.float32),
-            pltpu.VMEM((8, 2 * width), jnp.float32),
-            pltpu.VMEM((8, width), jnp.float32),
-            pltpu.VMEM((8, 2 * hidden), jnp.float32),
-            pltpu.VMEM((2 * hidden, 128), jnp.float32),
-            pltpu.VMEM((hidden, 64), jnp.float32),
-            pltpu.VMEM((blocks, THIN_ROWS, hidden), jnp.bfloat16),
-            pltpu.VMEM((blocks, THIN_ROWS, hidden), jnp.bfloat16),
-            pltpu.SemaphoreType.DMA((2,)),
-        ],
+        scratch_shapes=holds + [thin_held, thin_held, pltpu.SemaphoreType.DMA((2,))],
         compiler_params=pltpu.CompilerParams(vmem_limit_bytes=VMEM_LIMIT),
         cost_estimate=pl.CostEstimate(flops=0, bytes_accessed=4 * own.size, transcendentals=0),
     )(bit, own.reshape(blocks, -1, hidden), came.reshape(blocks, -1, hidden))
@@ -488,8 +487,10 @@
     if places is None:
         *naturals, refs = *refs[:4], refs[4:]
     else:
-        own_a, own_b, came_a, came_b, *refs = refs
-        naturals, refs = refs[-4:], refs[:-4]
+        arrived, refs = refs[:4], refs[4:]
+        refs, naturals, holds, held, loads = refs[:-15], refs[-15:-11], refs[-11:-5], refs[-5:-1], refs[-1]
+        thin, refs = refs[-9:], refs[:-9]
+        refs = [refs[0], *thin, *refs[1:]]
     expand_one_back_ref, shrink_one_back_ref, expand_two_back_ref, shrink_two_back_ref = naturals
     (
         flipped_ref,
@@ -532,6 +533,22 @@
     ) = refs
     bit = jnp.minimum(bit_ref[0], 1)
     if places is not None:
+        copies = [
+            pltpu.make_async_copy(arrived[index], held[index], loads.at[index]) for index in (0, 2, 1, 3)
+        ]
+        for copy in copies:
+            copy.start()
+        own_a, own_b, came_a, came_b = held
+        for copy in copies[:2]:
+            copy.wait()
+        shard = own_a.shape[0] // len(places[0][0])
+
+        def thin_of(ref):
+            return lambda block: ref[(block + 1) * shard - THIN_ROWS : (block + 1) * shard, :]
+
+        lay_thin(bit, (thin_of(own_a), thin_of(came_a)), places[0], thin, holds)
+        for copy in copies[2:]:
+            copy.wait()
         assemble(bit, own_a, came_a, [expand_one_back_ref], places[0])
         assemble(
             bit,
@@ -838,7 +855,7 @@
 
 def dense(bit, flipped, weights, places, thin, cot, grad_rows):
     width, events = flipped.shape
-    hidden = thin[0].shape[0]
+    hidden = weights[0].shape[1]
     inner, narrow = 128, 64
     tall = hidden + ONES
     low = functools.partial(pltpu.VMEM, dtype=jnp.bfloat16)
@@ -866,9 +883,14 @@
     scratch += [low((6 * hidden, depth)) for depth in (width, hidden, hidden, hidden)]
     vmem = pl.BlockSpec(memory_space=pltpu.VMEM)
     outside = pl.BlockSpec(memory_space=pl.ANY)
-    specs = [pl.BlockSpec(memory_space=pltpu.SMEM)] + [vmem] * (len(weights) + len(thin) + 2)
+    specs = [pl.BlockSpec(memory_space=pltpu.SMEM)]
+    specs += [vmem if places is None else outside] * 4 + [vmem] * (len(thin) + 2)
     if places is not None:
+        outs, holds = thin_shapes(width, hidden)
+        scratch += [pltpu.VMEM(*out) for out in outs]
         scratch += [low((6 * depth, hidden)) for depth in (width, hidden, hidden, hidden)]
+        scratch += holds + [low(weight.shape) for weight in weights]
+        scratch.append(pltpu.SemaphoreType.DMA((4,)))
     return pl.pallas_call(
         functools.partial(dense_body, places),
         out_shape=(
@@ -895,25 +917,26 @@
     return sizes, starts
 
 
-def grad_moves(part, wide, half, hidden, width):
+def grad_moves(part, half, hidden, width):
     sizes, starts = grad_layout(width, hidden)
+    most = 512
     moves = []
     for index in range(2):
         first = (2 * half + index) * part
         for target, (start, size) in enumerate(zip(starts, sizes)):
             low_row, high_row = max(first, start), min(first + part, start + size)
-            if low_row < high_row:
-                moves.append((index, low_row - first, target, low_row - start, high_row - low_row))
+            for row in range(low_row, high_row, most):
+                moves.append((index, row - first, target, row - start, min(most, high_row - row)))
     return moves
 
 
-def write_wide(half, pieces, wide, hold, sems, width, hidden):
+def write_wide(half, pieces, ready, wide, hold, sems, width, hidden):
     part = pieces[0].shape[0]
     block = 128
     copies = []
-    for number, (index, start, target, place, rows) in enumerate(
-        grad_moves(part, wide, half, hidden, width)
-    ):
+    for number, (index, start, target, place, rows) in enumerate(grad_moves(part, half, hidden, width)):
+        if ready and start == 0:
+            ready[index].wait()
         source = pieces[index]
         base = index * part + start
 
@@ -941,7 +964,7 @@
 
         @pl.when(jnp.minimum(bit_ref[0], 1) == half)
         def _():
-            for copy in write_wide(half, (own_a_ref, own_b_ref), wide, hold, sems, width, hidden):
+            for copy in write_wide(half, (own_a_ref, own_b_ref), (), wide, hold, sems, width, hidden):
                 copy.wait()
 
 
@@ -951,12 +974,12 @@
     width = wide[0].shape[0] // 6
     part = came_a_ref.shape[0]
     start = grad_layout(width, hidden)[1][4] - 3 * part
-
+    bit = jnp.minimum(bit_ref[0], 1)
     for half in range(2):
 
-        @pl.when(jnp.minimum(bit_ref[0], 1) != half)
+        @pl.when(bit != half)
         def _():
-            copies = write_wide(half, (came_a_ref, came_b_ref), wide, hold, sems, width, hidden)
+            copies = write_wide(half, (came_a_ref, came_b_ref), (), wide, hold, sems, width, hidden)
             write_rest(came_b_ref if half else own_b_ref, start, outs, width, hidden)
             for copy in copies:
                 copy.wait()
@@ -1027,9 +1050,10 @@
     )
     outside, inside = pl.BlockSpec(memory_space=pl.ANY), pl.BlockSpec(memory_space=pltpu.VMEM)
     small = pl.BlockSpec(memory_space=pltpu.SMEM)
-    params = pltpu.CompilerParams(vmem_limit_bytes=VMEM_LIMIT)
+    params = pltpu.CompilerParams(vmem_limit_bytes=SMALL_LIMIT)
     moved = 6 * 2 * own[0].size
-    scratch = [pltpu.VMEM((2 * own[0].shape[0], hidden), jnp.float32), pltpu.SemaphoreType.DMA((4,))]
+    part = own[0].shape[0]
+    scratch = [pltpu.VMEM((2 * part, hidden), jnp.float32), pltpu.SemaphoreType.DMA((16,))]
     wide = pl.pallas_call(
         own_body,
         out_shape=wide_shapes,
@@ -1233,7 +1257,7 @@
         (expandone, reduceone, expandtwo, reducetwo),
     )
     found = find_rows(asked_rows, embed_table.T)
-    packed = share(packed, asked_rows)
+    packed = share(packed, request)
     split = expandone.shape[0] + THIN_ROWS
     first, orders = dp_orders()
     parts = [packed[:, :split], packed[:, split:]]
@@ -1242,12 +1266,11 @@
     bit = (lax.axis_index("dp") & first).reshape(1)
     places = [arrival(order, first, group) for order in orders]
     flipped = place_rows(returned, rank, owner_rows)
-    came, flipped = lax.optimization_barrier((came, flipped))
-    thin = prep_thin(bit, own[0], came[0], places[0], width, hidden)
     sizes = [shard.shape[0] for shard in (expandone, reduceone, expandtwo, reducetwo)]
     if all(size % 16 == 0 for size in sizes):
-        weights = (*own, *came)
+        weights, thin = (*own, *came), ()
     else:
+        thin = prep_thin(bit, own[0], came[0], places[0], width, hidden)
         whole = [
             in_order(mine, other, bit[0], place, part.shape[1])
             for mine, other, place, part in zip(own, came, places, parts)

time: 204 us -> 195 us (0.956)
  Pallas kernels: 62.6 us -> 51.9 us
  starting transfers between devices: 42.7 us -> 45.1 us
    all_to_all x1, waiting for transfers between devices: 7.25 us -> 0.01 us  [on_device(): lax.all_to_all(request, ('dp', 'fsdp'), split_axis=0, concat_axis=0, tile...]
    ppermute x9, waiting for transfers between devices: 17.7 us -> 21.3 us  [swap_groups(): return lax.ppermute(values, 'fsdp', partners(mask, lax.axis_size('fsdp')))]
    pallas_call x1 -> x0, Pallas kernels: 2.87 us -> none  [prep_thin(): pl.pallas_call(functools.partial(prep_thin_body, places), out_shape=(jax....]
    ppermute x17, starting transfers between devices: 14.2 us -> 16.7 us  [swap_with(): return lax.ppermute(values, 'dp', partners(mask, size))]
    ppermute x17, waiting for transfers between devices: 60.6 us -> 62.7 us  [swap_with(): return lax.ppermute(values, 'dp', partners(mask, size))]
    pallas_call x1, Pallas kernels: 5.96 us -> 3.9 us  [place_rows(): local_kernel(place_body, jax.ShapeDtypeStruct((fields * width, events), j...]
  transfers between devices with their start and end apart: 29 -> 29, of which waited for: 16 -> 16; matrix products, arithmetic and copies ran while one was open for 2% -> 3% of each run, Pallas kernels for 16% -> 13%
where the time goes in v5:
time: 195 us; the launch traced here: 194 us
  waiting for transfers between devices  84 us (43%)
  Pallas kernels  51.9 us (27%)
  starting transfers between devices  45.1 us (23%)
  other arithmetic  8.14 us (4%)
  local copies, waits for them, and re-layouts  3.29 us (2%)
    ppermute x17, waiting for transfers between devices, swap_with(): return lax.ppermute(values, 'dp', partners(mask, size))  62.7 us
    pallas_call x1, Pallas kernels, dense(): pl.pallas_call(functools.partial(dense_body, places), out_shape=(jax.Shap...  22 us
    ppermute x9, waiting for transfers between devices, swap_groups(): return lax.ppermute(values, 'fsdp', partners(mask, lax.axis_size('fsdp')))  21.3 us
    ppermute x17, starting transfers between devices, swap_with(): return lax.ppermute(values, 'dp', partners(mask, size))  16.7 us
    ppermute x9, starting transfers between devices, swap_groups(): return lax.ppermute(values, 'fsdp', partners(mask, lax.axis_size('fsdp')))  14.8 us
    pallas_call x1, Pallas kernels, find_rows(): local_kernel(find_body, jax.ShapeDtypeStruct((devices, width, capacity),...  6.2 us
    all_to_all x1, starting transfers between devices, on_device(): lax.all_to_all(request, ('dp', 'fsdp'), split_axis=0, concat_axis=0, tile...  6.01 us
    pallas_call x1, Pallas kernels, add_rows(): local_kernel(add_body, jax.ShapeDtypeStruct((width, rows), jnp.float32),...  5.5 us
  transfers between devices with their start and end apart: 29, of which 16 were waited for; matrix products, arithmetic and copies ran while one was open for 3% of the time, Pallas kernels for 13%

profile of v5, /device:TPU:0, one launch (start us, length us, event | category | flops | bytes accessed | tf_op | source)
XLA Modules:
  0.0 193.7 jit_solution(16728383258871076721)
XLA Ops:
  0.7 1.6 shard_map.356
  2.3 5.0 %collective-permute-start.2 = (bf16[288,256]{1,0:T(8,128)(2,1)}, bf16[288,256]{1,0:T(8,128)(2,1)S(1)}, u32[]{:S(2)}, u32[]{:S(2)}) collective-permute-start(bf16[288,256]{1,0:T(8,128)(2,1)} %shard_map.356), channel_id=1, source_target_pairs={{0,3},{1,2},{2,1},{3,0},{4,7},{5,6},{6,5},{7,4},{8,11},{9,10},{10,... | collective-permute-start | bytes 442376 | tf_op jit(solution)/shard_map/ppermute | solution.py:1110
  7.9 2.5 %shard_map.357 = (s32[32,1,256]{2,1,0:T(1,128)}, s32[32,512]{1,0:T(8,128)}) custom-call(s32[8,512]{1,0:T(8,128)} %bitcast.44, s32[8,512]{1,0:T(8,128)} %bitcast.58), custom_call_target="tpu_custom_call" | custom-call | flops 150994944 | bytes 98304 | tf_op jit(solution)/shard_map/pallas_call | solution.py:71
  10.4 6.0 %all-to-all-start = ((s32[32,1,256]{2,1,0:T(1,128)}), s32[32,1,256]{2,1,0:T(1,128)S(1)}, u32[]{:S(2)}, u32[]{:S(2)}) async-start(s32[32,1,256]{2,1,0:T(1,128)} %get-tuple-element.74), calls=%async_computation | async-start | bytes 65536 | tf_op jit(solution)/shard_map/all_to_all | solution.py:1253
  16.5 3.6 %collective-permute-done.1 = bf16[288,256]{1,0:T(8,128)(2,1)S(1)} collective-permute-done((bf16[288,256]{1,0:T(8,128)(2,1)}, bf16[288,256]{1,0:T(8,128)(2,1)S(1)}, u32[]{:S(2)}, u32[]{:S(2)}) %collective-permute-start.1) | collective-permute-done | bytes 147488 | tf_op jit(solution)/shard_map/ppermute | solution.py:1110
  20.1 1.0 select_bitcast_fusion.3
  21.2 1.6 collective-permute-start.3
  22.8 1.5 collective-permute-start.4
  24.3 6.2 %shard_map.358 = bf16[32,64,256]{2,1,0:T(8,128)(2,1)} custom-call(s32[32,1,256]{2,1,0:T(1,128)S(1)} %all-to-all-done.request_ref, bf16[64,4096]{1,0:T(8,128)(2,1)S(1)} %bitcast.43), custom_call_target="tpu_custom_call" | custom-call | flops 34359738368 | bytes 1572864 | tf_op jit(solution)/shard_map/pallas_call | solution.py:112
  30.7 1.5 collective-permute-start.5
  32.2 3.4 %all-to-all-start.1 = ((bf16[32,64,256]{2,1,0:T(8,128)(2,1)}), bf16[32,64,256]{2,1,0:T(8,128)(2,1)S(1)}, u32[]{:S(2)}, u32[]{:S(2)}) async-start(bf16[32,64,256]{2,1,0:T(8,128)(2,1)} %shard_map.358), calls=%async_computation.1 | async-start | bytes 2097152 | tf_op jit(solution)/shard_map/all_to_all | solution.py:1265
  35.6 1.8 collective-permute-start.6
  37.4 14.6 %collective-permute-done.5 = bf16[1152,256]{1,0:T(8,128)(2,1)S(1)} collective-permute-done((bf16[1152,256]{1,0:T(8,128)(2,1)S(1)}, bf16[1152,256]{1,0:T(8,128)(2,1)S(1)}, u32[]{:S(2)}, u32[]{:S(2)}) %collective-permute-start.5) | collective-permute-done | bytes 589856 | tf_op jit(solution)/shard_map/ppermute | solution.py:1087
  52.3 10.1 %collective-permute-done.6 = bf16[1152,256]{1,0:T(8,128)(2,1)S(1)} collective-permute-done((bf16[1152,256]{1,0:T(8,128)(2,1)S(1)}, bf16[1152,256]{1,0:T(8,128)(2,1)S(1)}, u32[]{:S(2)}, u32[]{:S(2)}) %collective-permute-start.6) | collective-permute-done | bytes 589856 | tf_op jit(solution)/shard_map/ppermute | solution.py:1087
  62.5 1.1 pad_maximum_fusion.1.refs_2_
  64.1 3.9 %shard_map.359.refs_5_ = bf16[512,512]{1,0:T(8,128)(2,1)S(1)} custom-call(bf16[32,64,256]{2,1,0:T(8,128)(2,1)S(1)} %all-to-all-done.1.found_ref, s32[32,512]{1,0:T(8,128)S(1)} %copy-done.4, s32[8,512]{1,0:T(8,128)S(1)} %bitcast.45), custom_call_target="tpu_custom_call" | custom-call | flops 536870912 | bytes 1572864 | tf_op jit(solution)/shard_map/pallas_call | solution.py:155
  68.0 0.8 copy-done.2
  68.8 22.0 %shard_map.360 = (f32[2,512]{1,0:T(2,128)}, f32[512,512]{1,0:T(8,128)}, bf16[4096,256]{1,0:T(8,128)(2,1)}, bf16[4096,256]{1,0:T(8,128)(2,1)}) custom-call(s32[1]{0:T(128)} %bitcast.refs_0_.bit_ref, bf16[2304,256]{1,0:T(8,128)(2,1)} %copy-done.5, bf16[2304,256]{1,0:T(8,128)(2,1)} %pad_maximum_fusion.1.refs_2_, ...), custom_call_target="tpu_custom_call" | custom-call | flops 6241124352 | bytes 25165824 | tf_op jit(solution)/shard_map/pallas_call | solution.py:894
  90.9 1.2 copy-done.3
  92.2 5.3 %shard_map.361 = (bf16[32,64,256]{2,1,0:T(8,128)(2,1)}, f32[512,512]{1,0:T(8,128)}) custom-call(f32[512,512]{1,0:T(8,128)S(1)} %copy-done.3, s32[32,512]{1,0:T(8,128)S(1)} %copy-done.4, s32[8,512]{1,0:T(8,128)S(1)} %bitcast.46), custom_call_target="tpu_custom_call" | custom-call | flops 536870912 | bytes 2097152 | tf_op jit(solution)/shard_map/pallas_call | solution.py:196
  97.5 2.1 %add_convert_fusion = bf16[4096,256]{1,0:T(8,128)(2,1)S(1)} fusion(bf16[4096,256]{1,0:T(8,128)(2,1)S(1)} %collective-permute-done.9, bf16[4096,256]{1,0:T(8,128)(2,1)} %get-tuple-element.86), kind=kLoop, calls=%fused_computation | loop fusion | flops 4194304 | bytes 6291456 | tf_op jit(solution)/shard_map/convert_element_type | solution.py:1098
  99.8 0.9 constant_dynamic-slice_fusion.6
  100.7 1.4 collective-permute-start.10
  102.0 4.2 %all-to-all-start.2 = ((bf16[32,64,256]{2,1,0:T(8,128)(2,1)}), bf16[32,64,256]{2,1,0:T(8,128)(2,1)S(1)}, u32[]{:S(2)}, u32[]{:S(2)}) async-start(bf16[32,64,256]{2,1,0:T(8,128)(2,1)} %get-tuple-element.96), calls=%async_computation.2 | async-start | bytes 2097152 | tf_op jit(solution)/shard_map/all_to_all | solution.py:1203
  106.2 1.6 collective-permute-start.12
  107.8 12.9 %collective-permute-done.10 = bf16[1024,256]{1,0:T(8,128)(2,1)} collective-permute-done((bf16[1024,256]{1,0:T(8,128)(2,1)S(1)}, bf16[1024,256]{1,0:T(8,128)(2,1)}, u32[]{:S(2)}, u32[]{:S(2)}) %collective-permute-start.10) | collective-permute-done | bytes 524320 | tf_op jit(solution)/shard_map/ppermute | solution.py:1087
  120.7 1.2 add_convert_fusion.2
  122.0 9.8 %collective-permute-done.12 = bf16[1024,256]{1,0:T(8,128)(2,1)S(1)} collective-permute-done((bf16[1024,256]{1,0:T(8,128)(2,1)}, bf16[1024,256]{1,0:T(8,128)(2,1)S(1)}, u32[]{:S(2)}, u32[]{:S(2)}) %collective-permute-start.12) | collective-permute-done | bytes 524320 | tf_op jit(solution)/shard_map/ppermute | solution.py:1087
  131.9 1.1 collective-permute-start.13
  133.0 4.0 %collective-permute-done.11 = bf16[512,256]{1,0:T(8,128)(2,1)} collective-permute-done((bf16[512,256]{1,0:T(8,128)(2,1)S(1)}, bf16[512,256]{1,0:T(8,128)(2,1)}, u32[]{:S(2)}, u32[]{:S(2)}) %collective-permute-start.11) | collective-permute-done | bytes 262176 | tf_op jit(solution)/shard_map/ppermute | solution.py:1087
  137.0 1.0 add_convert_fusion.4
  138.9 2.0 %collective-permute-start.14 = (bf16[256,256]{1,0:T(8,128)(2,1)S(1)}, bf16[256,256]{1,0:T(8,128)(2,1)S(1)}, u32[]{:S(2)}, u32[]{:S(2)}) collective-permute-start(bf16[256,256]{1,0:T(8,128)(2,1)S(1)} %get-tuple-element.98), channel_id=1, source_target_pairs={{0,1},{1,0},{2,3},{3,2},{4,5},{5,4},{6,7},{7,6},{8,9},{9,8},{10,11... | collective-permute-start | bytes 393224 | tf_op jit(solution)/shard_map/ppermute | solution.py:1110
  140.8 2.7 %collective-permute-start.15 = (bf16[256,256]{1,0:T(8,128)(2,1)S(1)}, bf16[256,256]{1,0:T(8,128)(2,1)S(1)}, u32[]{:S(2)}, u32[]{:S(2)}) collective-permute-start(bf16[256,256]{1,0:T(8,128)(2,1)S(1)} %get-tuple-element.99), channel_id=1, source_target_pairs={{0,2},{1,3},{2,0},{3,1},{4,6},{5,7},{6,4},{7,5},{8,10},{9,11},{10,... | collective-permute-start | bytes 393224 | tf_op jit(solution)/shard_map/ppermute | solution.py:1110
  143.6 1.8 collective-permute-done.14
  145.3 7.2 %collective-permute-done.15 = bf16[256,256]{1,0:T(8,128)(2,1)S(1)} collective-permute-done((bf16[256,256]{1,0:T(8,128)(2,1)S(1)}, bf16[256,256]{1,0:T(8,128)(2,1)S(1)}, u32[]{:S(2)}, u32[]{:S(2)}) %collective-permute-start.15) | collective-permute-done | bytes 131104 | tf_op jit(solution)/shard_map/ppermute | solution.py:1110
  152.6 2.0 %collective-permute-start.19 = (bf16[256,256]{1,0:T(8,128)(2,1)S(1)}, bf16[256,256]{1,0:T(8,128)(2,1)S(1)}, u32[]{:S(2)}, u32[]{:S(2)}) collective-permute-start(bf16[256,256]{1,0:T(8,128)(2,1)S(1)} %add_convert_fusion.5), channel_id=1, source_target_pairs={{0,1},{1,0},{2,3},{3,2},{4,5},{5,4},{6,7},{7,6},{8,9},{9,8},{10,11... | collective-permute-start | bytes 393224 | tf_op jit(solution)/shard_map/ppermute | solution.py:1110
  154.6 0.9 collective-permute-start.18
  155.6 1.5 collective-permute-start.17
  157.1 1.5 collective-permute-done.19
  158.6 7.3 %collective-permute-done.18 = bf16[256,256]{1,0:T(8,128)(2,1)S(1)} collective-permute-done((bf16[256,256]{1,0:T(8,128)(2,1)S(1)}, bf16[256,256]{1,0:T(8,128)(2,1)S(1)}, u32[]{:S(2)}, u32[]{:S(2)}) %collective-permute-start.18) | collective-permute-done | bytes 131104 | tf_op jit(solution)/shard_map/ppermute | solution.py:1110
  166.0 1.7 collective-permute-start.20
  168.4 5.7 %collective-permute-done.20 = bf16[512,256]{1,0:T(8,128)(2,1)S(1)} collective-permute-done((bf16[512,256]{1,0:T(8,128)(2,1)S(1)}, bf16[512,256]{1,0:T(8,128)(2,1)S(1)}, u32[]{:S(2)}, u32[]{:S(2)}) %collective-permute-start.20) | collective-permute-done | bytes 262176 | tf_op jit(solution)/shard_map/ppermute | solution.py:1087
  174.2 2.3 %collective-permute-start.21 = (bf16[1024,256]{1,0:T(8,128)(2,1)S(1)}, bf16[1024,256]{1,0:T(8,128)(2,1)S(1)}, u32[]{:S(2)}, u32[]{:S(2)}) collective-permute-start(bf16[1024,256]{1,0:T(8,128)(2,1)S(1)} %pad_maximum_fusion.9), channel_id=1, source_target_pairs={{0,8},{4,12},{8,0},{12,4},{16,24},{20,28},{24,16},{28,20},{1,9},{5... | collective-permute-start | bytes 1572872 | tf_op jit(solution)/shard_map/ppermute | solution.py:1087
  177.4 5.5 %shard_map.362 = f32[64,4096]{1,0:T(8,128)} custom-call(bf16[32,64,256]{2,1,0:T(8,128)(2,1)S(1)} %all-to-all-done.2.came_ref, s32[32,1,256]{2,1,0:T(1,128)S(1)} %all-to-all-done.request_ref), custom_call_target="tpu_custom_call" | custom-call | flops 4294967296 | bytes 2097152 | tf_op jit(solution)/shard_map/pallas_call | solution.py:247
  183.9 2.4 %collective-permute-done.23 = bf16[1024,256]{1,0:T(8,128)(2,1)S(1)} collective-permute-done((bf16[1024,256]{1,0:T(8,128)(2,1)S(1)}, bf16[1024,256]{1,0:T(8,128)(2,1)S(1)}, u32[]{:S(2)}, u32[]{:S(2)}) %collective-permute-start.23) | collective-permute-done | bytes 524320 | tf_op jit(solution)/shard_map/ppermute | solution.py:1087
  187.1 2.2 %shard_map.363 = (f32[3072,256]{1,0:T(8,128)}, f32[1536,256]{1,0:T(8,128)}, f32[1536,256]{1,0:T(8,128)}, f32[1536,256]{1,0:T(8,128)}) custom-call(s32[1]{0:T(128)} %bitcast.refs_0_.bit_ref, bf16[2048,256]{1,0:T(8,128)(2,1)S(1)} %pad_maximum_fusion.2.own_a_ref, bf16[2048,256]{1,0:T(8,128)(2,1)S(1)} %pad_maximum_fusion.3.own_b_ref), custom_call_target="tpu_custom_call" | custom-call | bytes 6291456 | tf_op jit(solution)/shard_map/pallas_call | solution.py:1057
  189.3 1.5 collective-permute-done.25.came_b_ref
  190.8 2.8 %shard_map.364 = (f32[3072,256]{1,0:T(8,128)}, f32[1536,256]{1,0:T(8,128)}, f32[1536,256]{1,0:T(8,128)}, f32[1536,256]{1,0:T(8,128)}, f32[1536]{0:T(1024)}, /*in...) custom-call(s32[1]{0:T(128)} %bitcast.refs_0_.bit_ref, ...), custom_call_target="tpu_custom_call", output_to_operand_aliasing={{0}: (4, {}), {1}: (5, {}), {2}: (6, {}), {3}: (7, {})} | custom-call | bytes 6291456 | tf_op jit(solution)/shard_map/pallas_call | solution.py:1066
  (65 shorter events, 7.0 us)
Async XLA Ops:
  2.3 14.2 %collective-permute-start.2 = (bf16[288,256]{1,0:T(8,128)(2,1)}, bf16[288,256]{1,0:T(8,128)(2,1)S(1)}, u32[]{:S(2)}, u32[]{:S(2)}) collective-permute-start(bf16[288,256]{1,0:T(8,128)(2,1)} %shard_map.356), channel_id=1, source_target_pairs={{0,3},{1,2},{2,1},{3,0},{4,7},{5,6},{6,5},{7,4},{8,11},{9,10},{10,... | collective-permute-start | bytes 442376 | tf_op jit(solution)/shard_map/ppermute | solution.py:1110
  7.3 12.8 %collective-permute-start.1 = (bf16[288,256]{1,0:T(8,128)(2,1)}, bf16[288,256]{1,0:T(8,128)(2,1)S(1)}, u32[]{:S(2)}, u32[]{:S(2)}) collective-permute-start(bf16[288,256]{1,0:T(8,128)(2,1)} %shard_map.356), channel_id=1, source_target_pairs={{0,2},{1,3},{2,0},{3,1},{4,6},{5,7},{6,4},{7,5},{8,10},{9,11},{10,... | collective-permute-start | bytes 442376 | tf_op jit(solution)/shard_map/ppermute | solution.py:1110
  7.3 12.8 %collective-permute-start = (bf16[288,256]{1,0:T(8,128)(2,1)}, bf16[288,256]{1,0:T(8,128)(2,1)S(1)}, u32[]{:S(2)}, u32[]{:S(2)}) collective-permute-start(bf16[288,256]{1,0:T(8,128)(2,1)} %shard_map.356), channel_id=1, source_target_pairs={{0,1},{1,0},{2,3},{3,2},{4,5},{5,4},{6,7},{7,6},{8,9},{9,8},{10,11... | collective-permute-start | bytes 442376 | tf_op jit(solution)/shard_map/ppermute | solution.py:1110
  7.9 16.4 %copy-start = (bf16[4096,64]{0,1:T(8,128)(2,1)S(1)}, bf16[4096,64]{0,1:T(8,128)(2,1)}, u32[]{:S(2)}) copy-start(bf16[4096,64]{0,1:T(8,128)(2,1)} %param.23) | copy-start | bytes 1572868
  10.4 13.9 %all-to-all-start = ((s32[32,1,256]{2,1,0:T(1,128)}), s32[32,1,256]{2,1,0:T(1,128)S(1)}, u32[]{:S(2)}, u32[]{:S(2)}) async-start(s32[32,1,256]{2,1,0:T(1,128)} %get-tuple-element.74), calls=%async_computation | async-start | bytes 65536 | tf_op jit(solution)/shard_map/all_to_all | solution.py:1253
  21.2 9.3 %collective-permute-start.3 = (bf16[576,256]{1,0:T(8,128)(2,1)S(1)}, bf16[576,256]{1,0:T(8,128)(2,1)S(1)}, u32[]{:S(2)}, u32[]{:S(2)}) collective-permute-start(bf16[576,256]{1,0:T(8,128)(2,1)S(1)} %bitcast.49), channel_id=1, source_target_pairs={{0,16},{4,20},{8,24},{12,28},{16,0},{20,4},{24,8},{28,12},{1,17},{... | collective-permute-start | bytes 884744 | tf_op jit(solution)/shard_map/ppermute | solution.py:1087
  22.8 7.8 %collective-permute-start.4 = (bf16[576,256]{1,0:T(8,128)(2,1)S(1)}, bf16[576,256]{1,0:T(8,128)(2,1)S(1)}, u32[]{:S(2)}, u32[]{:S(2)}) collective-permute-start(bf16[576,256]{1,0:T(8,128)(2,1)S(1)} %bitcast.48), channel_id=1, source_target_pairs={{0,8},{4,12},{8,0},{12,4},{16,24},{20,28},{24,16},{28,20},{1,9},{5... | collective-permute-start | bytes 884744 | tf_op jit(solution)/shard_map/ppermute | solution.py:1087
  30.7 21.3 %collective-permute-start.5 = (bf16[1152,256]{1,0:T(8,128)(2,1)S(1)}, bf16[1152,256]{1,0:T(8,128)(2,1)S(1)}, u32[]{:S(2)}, u32[]{:S(2)}) collective-permute-start(bf16[1152,256]{1,0:T(8,128)(2,1)S(1)} %get-tuple-element.79), channel_id=1, source_target_pairs={{0,8},{4,12},{8,0},{12,4},{16,24},{20,28},{24,16},{28,20},{1,9},{5... | collective-permute-start | bytes 1769480 | tf_op jit(solution)/shard_map/ppermute | solution.py:1087
  32.2 31.9 %all-to-all-start.1 = ((bf16[32,64,256]{2,1,0:T(8,128)(2,1)}), bf16[32,64,256]{2,1,0:T(8,128)(2,1)S(1)}, u32[]{:S(2)}, u32[]{:S(2)}) async-start(bf16[32,64,256]{2,1,0:T(8,128)(2,1)} %shard_map.358), calls=%async_computation.1 | async-start | bytes 2097152 | tf_op jit(solution)/shard_map/all_to_all | solution.py:1265
  35.6 26.7 %collective-permute-start.6 = (bf16[1152,256]{1,0:T(8,128)(2,1)S(1)}, bf16[1152,256]{1,0:T(8,128)(2,1)S(1)}, u32[]{:S(2)}, u32[]{:S(2)}) collective-permute-start(bf16[1152,256]{1,0:T(8,128)(2,1)S(1)} %get-tuple-element.80), channel_id=1, source_target_pairs={{0,16},{4,20},{8,24},{12,28},{16,0},{20,4},{24,8},{28,12},{1,17},{... | collective-permute-start | bytes 1769480 | tf_op jit(solution)/shard_map/ppermute | solution.py:1087
  52.2 11.3 %copy-start.5 = (bf16[2304,256]{1,0:T(8,128)(2,1)}, bf16[2304,256]{1,0:T(8,128)(2,1)S(1)}, u32[]{:S(2)}) copy-start(bf16[2304,256]{1,0:T(8,128)(2,1)S(1)} %pad_maximum_fusion.refs_1_) | copy-start | bytes 3538948
  52.2 11.9 %copy-start.1 = (s32[512,8]{0,1:T(8,128)S(1)}, s32[512,8]{0,1:T(8,128)}, u32[]{:S(2)}) copy-start(s32[512,8]{0,1:T(8,128)} %param.21) | copy-start | bytes 49156
  52.2 11.8 %copy-start.4 = (s32[32,512]{1,0:T(8,128)S(1)}, s32[32,512]{1,0:T(8,128)}, u32[]{:S(2)}) copy-start(s32[32,512]{1,0:T(8,128)} %get-tuple-element.84.rank_ref) | copy-start | bytes 196612
  63.6 5.2 %collective-permute-start.7 = (bf16[2304,256]{1,0:T(8,128)(2,1)S(1)}, bf16[2304,256]{1,0:T(8,128)(2,1)}, u32[]{:S(2)}, u32[]{:S(2)}) collective-permute-start(bf16[2304,256]{1,0:T(8,128)(2,1)S(1)} %pad_maximum_fusion.refs_1_), channel_id=1, source_target_pairs={{0,4},{4,0},{8,12},{12,8},{16,20},{20,16},{24,28},{28,24},{1,5},{5... | collective-permute-start | bytes 3538952 | tf_op jit(solution)/shard_map/ppermute | solution.py:1087
  63.6 5.2 %collective-permute-start.8 = (bf16[2304,256]{1,0:T(8,128)(2,1)}, bf16[2304,256]{1,0:T(8,128)(2,1)}, u32[]{:S(2)}, u32[]{:S(2)}) collective-permute-start(bf16[2304,256]{1,0:T(8,128)(2,1)} %pad_maximum_fusion.1.refs_2_), channel_id=1, source_target_pairs={{0,4},{4,0},{8,12},{12,8},{16,20},{20,16},{24,28},{28,24},{1,5},{5... | collective-permute-start | bytes 3538952 | tf_op jit(solution)/shard_map/ppermute | solution.py:1087
  68.0 0.8 copy-start.2
  90.8 6.6 %collective-permute-start.9 = (bf16[4096,256]{1,0:T(8,128)(2,1)}, bf16[4096,256]{1,0:T(8,128)(2,1)S(1)}, u32[]{:S(2)}, u32[]{:S(2)}) collective-permute-start(bf16[4096,256]{1,0:T(8,128)(2,1)} %get-tuple-element.87), channel_id=1, source_target_pairs={{0,4},{4,0},{8,12},{12,8},{16,20},{20,16},{24,28},{28,24},{1,5},{5... | collective-permute-start | bytes 6291464 | tf_op jit(solution)/shard_map/ppermute | solution.py:1087
  90.9 1.2 copy-start.3
  100.7 20.0 %collective-permute-start.10 = (bf16[1024,256]{1,0:T(8,128)(2,1)S(1)}, bf16[1024,256]{1,0:T(8,128)(2,1)}, u32[]{:S(2)}, u32[]{:S(2)}) collective-permute-start(bf16[1024,256]{1,0:T(8,128)(2,1)S(1)} %get-tuple-element.93), channel_id=1, source_target_pairs={{0,8},{4,12},{8,0},{12,4},{16,24},{20,28},{24,16},{28,20},{1,9},{5... | collective-permute-start | bytes 1572872 | tf_op jit(solution)/shard_map/ppermute | solution.py:1087
  102.0 36.8 %all-to-all-start.2 = ((bf16[32,64,256]{2,1,0:T(8,128)(2,1)}), bf16[32,64,256]{2,1,0:T(8,128)(2,1)S(1)}, u32[]{:S(2)}, u32[]{:S(2)}) async-start(bf16[32,64,256]{2,1,0:T(8,128)(2,1)} %get-tuple-element.96), calls=%async_computation.2 | async-start | bytes 2097152 | tf_op jit(solution)/shard_map/all_to_all | solution.py:1203
  106.2 25.6 %collective-permute-start.12 = (bf16[1024,256]{1,0:T(8,128)(2,1)}, bf16[1024,256]{1,0:T(8,128)(2,1)S(1)}, u32[]{:S(2)}, u32[]{:S(2)}) collective-permute-start(bf16[1024,256]{1,0:T(8,128)(2,1)} %get-tuple-element.95), channel_id=1, source_target_pairs={{0,16},{4,20},{8,24},{12,28},{16,0},{20,4},{24,8},{28,12},{1,17},{... | collective-permute-start | bytes 1572872 | tf_op jit(solution)/shard_map/ppermute | solution.py:1087
  121.9 15.1 %collective-permute-start.11 = (bf16[512,256]{1,0:T(8,128)(2,1)S(1)}, bf16[512,256]{1,0:T(8,128)(2,1)}, u32[]{:S(2)}, u32[]{:S(2)}) collective-permute-start(bf16[512,256]{1,0:T(8,128)(2,1)S(1)} %constant_dynamic-slice_fusion.5), channel_id=1, source_target_pairs={{0,16},{4,20},{8,24},{12,28},{16,0},{20,4},{24,8},{28,12},{1,17},{... | collective-permute-start | bytes 786440 | tf_op jit(solution)/shard_map/ppermute | solution.py:1087
  131.9 6.7 %collective-permute-start.13 = (bf16[512,256]{1,0:T(8,128)(2,1)S(1)}, bf16[512,256]{1,0:T(8,128)(2,1)S(1)}, u32[]{:S(2)}, u32[]{:S(2)}) collective-permute-start(bf16[512,256]{1,0:T(8,128)(2,1)S(1)} %constant_dynamic-slice_fusion.4), channel_id=1, source_target_pairs={{0,8},{4,12},{8,0},{12,4},{16,24},{20,28},{24,16},{28,20},{1,9},{5... | collective-permute-start | bytes 786440 | tf_op jit(solution)/shard_map/ppermute | solution.py:1087
  138.9 6.4 %collective-permute-start.14 = (bf16[256,256]{1,0:T(8,128)(2,1)S(1)}, bf16[256,256]{1,0:T(8,128)(2,1)S(1)}, u32[]{:S(2)}, u32[]{:S(2)}) collective-permute-start(bf16[256,256]{1,0:T(8,128)(2,1)S(1)} %get-tuple-element.98), channel_id=1, source_target_pairs={{0,1},{1,0},{2,3},{3,2},{4,5},{5,4},{6,7},{7,6},{8,9},{9,8},{10,11... | collective-permute-start | bytes 393224 | tf_op jit(solution)/shard_map/ppermute | solution.py:1110
  140.8 11.7 %collective-permute-start.15 = (bf16[256,256]{1,0:T(8,128)(2,1)S(1)}, bf16[256,256]{1,0:T(8,128)(2,1)S(1)}, u32[]{:S(2)}, u32[]{:S(2)}) collective-permute-start(bf16[256,256]{1,0:T(8,128)(2,1)S(1)} %get-tuple-element.99), channel_id=1, source_target_pairs={{0,2},{1,3},{2,0},{3,1},{4,6},{5,7},{6,4},{7,5},{8,10},{9,11},{10,... | collective-permute-start | bytes 393224 | tf_op jit(solution)/shard_map/ppermute | solution.py:1110
  143.5 9.0 %collective-permute-start.16 = (bf16[256,256]{1,0:T(8,128)(2,1)S(1)}, bf16[256,256]{1,0:T(8,128)(2,1)S(1)}, u32[]{:S(2)}, u32[]{:S(2)}) collective-permute-start(bf16[256,256]{1,0:T(8,128)(2,1)S(1)} %get-tuple-element.100), channel_id=1, source_target_pairs={{0,3},{1,2},{2,1},{3,0},{4,7},{5,6},{6,5},{7,4},{8,11},{9,10},{10,... | collective-permute-start | bytes 393224 | tf_op jit(solution)/shard_map/ppermute | solution.py:1110
  152.6 6.0 %collective-permute-start.19 = (bf16[256,256]{1,0:T(8,128)(2,1)S(1)}, bf16[256,256]{1,0:T(8,128)(2,1)S(1)}, u32[]{:S(2)}, u32[]{:S(2)}) collective-permute-start(bf16[256,256]{1,0:T(8,128)(2,1)S(1)} %add_convert_fusion.5), channel_id=1, source_target_pairs={{0,1},{1,0},{2,3},{3,2},{4,5},{5,4},{6,7},{7,6},{8,9},{9,8},{10,11... | collective-permute-start | bytes 393224 | tf_op jit(solution)/shard_map/ppermute | solution.py:1110
  154.6 11.2 %collective-permute-start.18 = (bf16[256,256]{1,0:T(8,128)(2,1)S(1)}, bf16[256,256]{1,0:T(8,128)(2,1)S(1)}, u32[]{:S(2)}, u32[]{:S(2)}) collective-permute-start(bf16[256,256]{1,0:T(8,128)(2,1)S(1)} %add_convert_fusion.5), channel_id=1, source_target_pairs={{0,2},{1,3},{2,0},{3,1},{4,6},{5,7},{6,4},{7,5},{8,10},{9,11},{10,... | collective-permute-start | bytes 393224 | tf_op jit(solution)/shard_map/ppermute | solution.py:1110
  155.6 10.3 %collective-permute-start.17 = (bf16[256,256]{1,0:T(8,128)(2,1)S(1)}, bf16[256,256]{1,0:T(8,128)(2,1)S(1)}, u32[]{:S(2)}, u32[]{:S(2)}) collective-permute-start(bf16[256,256]{1,0:T(8,128)(2,1)S(1)} %add_convert_fusion.5), channel_id=1, source_target_pairs={{0,3},{1,2},{2,1},{3,0},{4,7},{5,6},{6,5},{7,4},{8,11},{9,10},{10,... | collective-permute-start | bytes 393224 | tf_op jit(solution)/shard_map/ppermute | solution.py:1110
  166.0 8.0 %collective-permute-start.20 = (bf16[512,256]{1,0:T(8,128)(2,1)S(1)}, bf16[512,256]{1,0:T(8,128)(2,1)S(1)}, u32[]{:S(2)}, u32[]{:S(2)}) collective-permute-start(bf16[512,256]{1,0:T(8,128)(2,1)S(1)} %bitcast.51), channel_id=1, source_target_pairs={{0,16},{4,20},{8,24},{12,28},{16,0},{20,4},{24,8},{28,12},{1,17},{... | collective-permute-start | bytes 786440 | tf_op jit(solution)/shard_map/ppermute | solution.py:1087
  167.7 9.2 %collective-permute-start.22 = (bf16[512,256]{1,0:T(8,128)(2,1)S(1)}, bf16[512,256]{1,0:T(8,128)(2,1)S(1)}, u32[]{:S(2)}, u32[]{:S(2)}) collective-permute-start(bf16[512,256]{1,0:T(8,128)(2,1)S(1)} %bitcast.50), channel_id=1, source_target_pairs={{0,8},{4,12},{8,0},{12,4},{16,24},{20,28},{24,16},{28,20},{1,9},{5... | collective-permute-start | bytes 786440 | tf_op jit(solution)/shard_map/ppermute | solution.py:1087
  174.2 9.5 %collective-permute-start.21 = (bf16[1024,256]{1,0:T(8,128)(2,1)S(1)}, bf16[1024,256]{1,0:T(8,128)(2,1)S(1)}, u32[]{:S(2)}, u32[]{:S(2)}) collective-permute-start(bf16[1024,256]{1,0:T(8,128)(2,1)S(1)} %pad_maximum_fusion.9), channel_id=1, source_target_pairs={{0,8},{4,12},{8,0},{12,4},{16,24},{20,28},{24,16},{28,20},{1,9},{5... | collective-permute-start | bytes 1572872 | tf_op jit(solution)/shard_map/ppermute | solution.py:1087
  177.0 9.2 %collective-permute-start.23 = (bf16[1024,256]{1,0:T(8,128)(2,1)S(1)}, bf16[1024,256]{1,0:T(8,128)(2,1)S(1)}, u32[]{:S(2)}, u32[]{:S(2)}) collective-permute-start(bf16[1024,256]{1,0:T(8,128)(2,1)S(1)} %pad_maximum_fusion.10), channel_id=1, source_target_pairs={{0,16},{4,20},{8,24},{12,28},{16,0},{20,4},{24,8},{28,12},{1,17},{... | collective-permute-start | bytes 1572872 | tf_op jit(solution)/shard_map/ppermute | solution.py:1087
  186.6 2.8 %collective-permute-start.24 = (bf16[2048,256]{1,0:T(8,128)(2,1)S(1)}, bf16[2048,256]{1,0:T(8,128)(2,1)S(1)}, u32[]{:S(2)}, u32[]{:S(2)}) collective-permute-start(bf16[2048,256]{1,0:T(8,128)(2,1)S(1)} %pad_maximum_fusion.2.own_a_ref), channel_id=1, source_target_pairs={{0,4},{4,0},{8,12},{12,8},{16,20},{20,16},{24,28},{28,24},{1,5},{5... | collective-permute-start | bytes 3145736 | tf_op jit(solution)/shard_map/ppermute | solution.py:1087
  186.6 4.1 %collective-permute-start.25 = (bf16[2048,256]{1,0:T(8,128)(2,1)S(1)}, bf16[2048,256]{1,0:T(8,128)(2,1)S(1)}, u32[]{:S(2)}, u32[]{:S(2)}) collective-permute-start(bf16[2048,256]{1,0:T(8,128)(2,1)S(1)} %pad_maximum_fusion.3.own_b_ref), channel_id=1, source_target_pairs={{0,4},{4,0},{8,12},{12,8},{16,20},{20,16},{24,28},{28,24},{1,5},{5... | collective-permute-start | bytes 3145736 | tf_op jit(solution)/shard_map/ppermute | solution.py:1087

commit v6 on v5

--- a/solution.py
+++ b/solution.py
@@ -902,7 +902,7 @@
         in_specs=specs,
         out_specs=(vmem, vmem, outside, outside),
         scratch_shapes=scratch,
-        compiler_params=pltpu.CompilerParams(vmem_limit_bytes=VMEM_LIMIT),
+        compiler_params=pltpu.CompilerParams(vmem_limit_bytes=51 * 1024 * 1024),
         cost_estimate=pl.CostEstimate(
             flops=6 * events * hidden * (6 * (width + 3 * hidden) + 2 * inner),
             bytes_accessed=24 * 1024 * 1024,

time: 195 us -> 191 us (0.979)
    unnamed x12 -> x10, local copies, waits for them, and re-layouts: 2.03 us -> 0.03 us
  transfers between devices with their start and end apart: 29 -> 29, of which waited for: 16 -> 17; matrix products, arithmetic and copies ran while one was open for 3% -> 3% of each run, Pallas kernels for 13% -> 13%
where the time goes in v6:
time: 191 us; the launch traced here: 190 us
  waiting for transfers between devices  83.6 us (44%)
  Pallas kernels  50.4 us (26%)
  starting transfers between devices  45.2 us (24%)
  other arithmetic  7.67 us (4%)
  local copies, waits for them, and re-layouts  1.99 us (1%)
    ppermute x17, waiting for transfers between devices, swap_with(): return lax.ppermute(values, 'dp', partners(mask, size))  62.3 us
    ppermute x9, waiting for transfers between devices, swap_groups(): return lax.ppermute(values, 'fsdp', partners(mask, lax.axis_size('fsdp')))  21.3 us
    pallas_call x1, Pallas kernels, dense(): pl.pallas_call(functools.partial(dense_body, places), out_shape=(jax.Shap...  20.4 us
    ppermute x17, starting transfers between devices, swap_with(): return lax.ppermute(values, 'dp', partners(mask, size))  16.9 us
    ppermute x9, starting transfers between devices, swap_groups(): return lax.ppermute(values, 'fsdp', partners(mask, lax.axis_size('fsdp')))  14.8 us
    pallas_call x1, Pallas kernels, find_rows(): local_kernel(find_body, jax.ShapeDtypeStruct((devices, width, capacity),...  6.2 us
    all_to_all x1, starting transfers between devices, on_device(): lax.all_to_all(request, ('dp', 'fsdp'), split_axis=0, concat_axis=0, tile...  6.01 us
    pallas_call x1, Pallas kernels, add_rows(): local_kernel(add_body, jax.ShapeDtypeStruct((width, rows), jnp.float32),...  5.5 us
  transfers between devices with their start and end apart: 29, of which 17 were waited for; matrix products, arithmetic and copies ran while one was open for 3% of the time, Pallas kernels for 13%

profile of v6, /device:TPU:0, one launch (start us, length us, event | category | flops | bytes accessed | tf_op | source)
XLA Modules:
  0.0 190.1 jit_solution(11043199158000510293)
XLA Ops:
  0.7 1.6 shard_map.356
  2.3 5.0 %collective-permute-start.2 = (bf16[288,256]{1,0:T(8,128)(2,1)}, bf16[288,256]{1,0:T(8,128)(2,1)S(1)}, u32[]{:S(2)}, u32[]{:S(2)}) collective-permute-start(bf16[288,256]{1,0:T(8,128)(2,1)} %shard_map.356), channel_id=1, source_target_pairs={{0,3},{1,2},{2,1},{3,0},{4,7},{5,6},{6,5},{7,4},{8,11},{9,10},{10,... | collective-permute-start | bytes 442376 | tf_op jit(solution)/shard_map/ppermute | solution.py:1110
  7.9 2.5 %shard_map.357 = (s32[32,1,256]{2,1,0:T(1,128)}, s32[32,512]{1,0:T(8,128)}) custom-call(s32[8,512]{1,0:T(8,128)} %bitcast.44, s32[8,512]{1,0:T(8,128)} %bitcast.58), custom_call_target="tpu_custom_call" | custom-call | flops 150994944 | bytes 98304 | tf_op jit(solution)/shard_map/pallas_call | solution.py:71
  10.4 6.0 %all-to-all-start = ((s32[32,1,256]{2,1,0:T(1,128)}), s32[32,1,256]{2,1,0:T(1,128)S(1)}, u32[]{:S(2)}, u32[]{:S(2)}) async-start(s32[32,1,256]{2,1,0:T(1,128)} %get-tuple-element.74), calls=%async_computation | async-start | bytes 65536 | tf_op jit(solution)/shard_map/all_to_all | solution.py:1253
  16.5 3.6 %collective-permute-done.1 = bf16[288,256]{1,0:T(8,128)(2,1)S(1)} collective-permute-done((bf16[288,256]{1,0:T(8,128)(2,1)}, bf16[288,256]{1,0:T(8,128)(2,1)S(1)}, u32[]{:S(2)}, u32[]{:S(2)}) %collective-permute-start.1) | collective-permute-done | bytes 147488 | tf_op jit(solution)/shard_map/ppermute | solution.py:1110
  20.1 1.0 select_bitcast_fusion.3
  21.2 1.6 collective-permute-start.3
  22.8 1.5 collective-permute-start.4
  24.3 6.2 %shard_map.358 = bf16[32,64,256]{2,1,0:T(8,128)(2,1)} custom-call(s32[32,1,256]{2,1,0:T(1,128)S(1)} %all-to-all-done.request_ref, bf16[64,4096]{1,0:T(8,128)(2,1)S(1)} %bitcast.43), custom_call_target="tpu_custom_call" | custom-call | flops 34359738368 | bytes 1572864 | tf_op jit(solution)/shard_map/pallas_call | solution.py:112
  30.7 1.5 collective-permute-start.5
  32.2 3.4 %all-to-all-start.1 = ((bf16[32,64,256]{2,1,0:T(8,128)(2,1)}), bf16[32,64,256]{2,1,0:T(8,128)(2,1)S(1)}, u32[]{:S(2)}, u32[]{:S(2)}) async-start(bf16[32,64,256]{2,1,0:T(8,128)(2,1)} %shard_map.358), calls=%async_computation.1 | async-start | bytes 2097152 | tf_op jit(solution)/shard_map/all_to_all | solution.py:1265
  35.6 1.8 collective-permute-start.6
  37.4 14.6 %collective-permute-done.5 = bf16[1152,256]{1,0:T(8,128)(2,1)S(1)} collective-permute-done((bf16[1152,256]{1,0:T(8,128)(2,1)S(1)}, bf16[1152,256]{1,0:T(8,128)(2,1)S(1)}, u32[]{:S(2)}, u32[]{:S(2)}) %collective-permute-start.5) | collective-permute-done | bytes 589856 | tf_op jit(solution)/shard_map/ppermute | solution.py:1087
  52.2 10.1 %collective-permute-done.6 = bf16[1152,256]{1,0:T(8,128)(2,1)S(1)} collective-permute-done((bf16[1152,256]{1,0:T(8,128)(2,1)S(1)}, bf16[1152,256]{1,0:T(8,128)(2,1)S(1)}, u32[]{:S(2)}, u32[]{:S(2)}) %collective-permute-start.6) | collective-permute-done | bytes 589856 | tf_op jit(solution)/shard_map/ppermute | solution.py:1087
  63.1 3.9 %shard_map.359.refs_5_ = bf16[512,512]{1,0:T(8,128)(2,1)S(1)} custom-call(bf16[32,64,256]{2,1,0:T(8,128)(2,1)S(1)} %all-to-all-done.1.found_ref, s32[32,512]{1,0:T(8,128)S(1)} %copy-done.3, s32[8,512]{1,0:T(8,128)S(1)} %bitcast.45), custom_call_target="tpu_custom_call" | custom-call | flops 536870912 | bytes 1572864 | tf_op jit(solution)/shard_map/pallas_call | solution.py:155
  67.3 20.4 %shard_map.360 = (f32[2,512]{1,0:T(2,128)}, f32[512,512]{1,0:T(8,128)S(1)}, bf16[4096,256]{1,0:T(8,128)(2,1)}, bf16[4096,256]{1,0:T(8,128)(2,1)}) custom-call(s32[1]{0:T(128)} %bitcast.refs_0_.bit_ref, bf16[2304,256]{1,0:T(8,128)(2,1)S(1)} %pad_maximum_fusion.refs_1_, bf16[2304,256]{1,0:T(8,128)(2,1)} %copy-done.4, ...), custom_call_target="tpu_custom_call" | custom-call | flops 6241124352 | bytes 25165824 | tf_op jit(solution)/shard_map/pallas_call | solution.py:894
  87.9 5.3 %shard_map.361 = (bf16[32,64,256]{2,1,0:T(8,128)(2,1)}, f32[512,512]{1,0:T(8,128)}) custom-call(f32[512,512]{1,0:T(8,128)S(1)} %get-tuple-element.88.grad_ref, s32[32,512]{1,0:T(8,128)S(1)} %copy-done.3, s32[8,512]{1,0:T(8,128)S(1)} %bitcast.46), custom_call_target="tpu_custom_call" | custom-call | flops 536870912 | bytes 2097152 | tf_op jit(solution)/shard_map/pallas_call | solution.py:196
  93.2 2.8 %add_convert_fusion = bf16[4096,256]{1,0:T(8,128)(2,1)S(1)} fusion(bf16[4096,256]{1,0:T(8,128)(2,1)} %collective-permute-done.9, bf16[4096,256]{1,0:T(8,128)(2,1)} %get-tuple-element.86), kind=kLoop, calls=%fused_computation | loop fusion | flops 4194304 | bytes 6291456 | tf_op jit(solution)/shard_map/convert_element_type | solution.py:1098
  96.1 0.9 constant_dynamic-slice_fusion.6
  97.1 1.4 collective-permute-start.10
  98.4 4.2 %all-to-all-start.2 = ((bf16[32,64,256]{2,1,0:T(8,128)(2,1)}), bf16[32,64,256]{2,1,0:T(8,128)(2,1)S(1)}, u32[]{:S(2)}, u32[]{:S(2)}) async-start(bf16[32,64,256]{2,1,0:T(8,128)(2,1)} %get-tuple-element.96), calls=%async_computation.2 | async-start | bytes 2097152 | tf_op jit(solution)/shard_map/all_to_all | solution.py:1203
  102.6 1.6 collective-permute-start.12
  104.2 12.9 %collective-permute-done.10 = bf16[1024,256]{1,0:T(8,128)(2,1)} collective-permute-done((bf16[1024,256]{1,0:T(8,128)(2,1)S(1)}, bf16[1024,256]{1,0:T(8,128)(2,1)}, u32[]{:S(2)}, u32[]{:S(2)}) %collective-permute-start.10) | collective-permute-done | bytes 524320 | tf_op jit(solution)/shard_map/ppermute | solution.py:1087
  117.1 1.2 add_convert_fusion.2
  118.3 0.7 constant_dynamic-slice_fusion.5
  119.0 9.1 %collective-permute-done.12 = bf16[1024,256]{1,0:T(8,128)(2,1)S(1)} collective-permute-done((bf16[1024,256]{1,0:T(8,128)(2,1)}, bf16[1024,256]{1,0:T(8,128)(2,1)S(1)}, u32[]{:S(2)}, u32[]{:S(2)}) %collective-permute-start.12) | collective-permute-done | bytes 524320 | tf_op jit(solution)/shard_map/ppermute | solution.py:1087
  128.3 1.1 collective-permute-start.13
  129.4 4.0 %collective-permute-done.11 = bf16[512,256]{1,0:T(8,128)(2,1)} collective-permute-done((bf16[512,256]{1,0:T(8,128)(2,1)}, bf16[512,256]{1,0:T(8,128)(2,1)}, u32[]{:S(2)}, u32[]{:S(2)}) %collective-permute-start.11) | collective-permute-done | bytes 262176 | tf_op jit(solution)/shard_map/ppermute | solution.py:1087
  133.4 1.0 add_convert_fusion.4
  135.3 2.0 %collective-permute-start.14 = (bf16[256,256]{1,0:T(8,128)(2,1)S(1)}, bf16[256,256]{1,0:T(8,128)(2,1)S(1)}, u32[]{:S(2)}, u32[]{:S(2)}) collective-permute-start(bf16[256,256]{1,0:T(8,128)(2,1)S(1)} %get-tuple-element.98), channel_id=1, source_target_pairs={{0,1},{1,0},{2,3},{3,2},{4,5},{5,4},{6,7},{7,6},{8,9},{9,8},{10,11... | collective-permute-start | bytes 393224 | tf_op jit(solution)/shard_map/ppermute | solution.py:1110
  137.2 2.7 %collective-permute-start.15 = (bf16[256,256]{1,0:T(8,128)(2,1)S(1)}, bf16[256,256]{1,0:T(8,128)(2,1)S(1)}, u32[]{:S(2)}, u32[]{:S(2)}) collective-permute-start(bf16[256,256]{1,0:T(8,128)(2,1)S(1)} %get-tuple-element.99), channel_id=1, source_target_pairs={{0,2},{1,3},{2,0},{3,1},{4,6},{5,7},{6,4},{7,5},{8,10},{9,11},{10,... | collective-permute-start | bytes 393224 | tf_op jit(solution)/shard_map/ppermute | solution.py:1110
  139.9 1.8 collective-permute-done.14
  141.7 7.2 %collective-permute-done.15 = bf16[256,256]{1,0:T(8,128)(2,1)S(1)} collective-permute-done((bf16[256,256]{1,0:T(8,128)(2,1)S(1)}, bf16[256,256]{1,0:T(8,128)(2,1)S(1)}, u32[]{:S(2)}, u32[]{:S(2)}) %collective-permute-start.15) | collective-permute-done | bytes 131104 | tf_op jit(solution)/shard_map/ppermute | solution.py:1110
  149.0 2.0 %collective-permute-start.19 = (bf16[256,256]{1,0:T(8,128)(2,1)S(1)}, bf16[256,256]{1,0:T(8,128)(2,1)S(1)}, u32[]{:S(2)}, u32[]{:S(2)}) collective-permute-start(bf16[256,256]{1,0:T(8,128)(2,1)S(1)} %add_convert_fusion.5), channel_id=1, source_target_pairs={{0,1},{1,0},{2,3},{3,2},{4,5},{5,4},{6,7},{7,6},{8,9},{9,8},{10,11... | collective-permute-start | bytes 393224 | tf_op jit(solution)/shard_map/ppermute | solution.py:1110
  151.0 0.9 collective-permute-start.18
  151.9 1.5 collective-permute-start.17
  153.4 1.5 collective-permute-done.19
  155.0 7.3 %collective-permute-done.18 = bf16[256,256]{1,0:T(8,128)(2,1)S(1)} collective-permute-done((bf16[256,256]{1,0:T(8,128)(2,1)S(1)}, bf16[256,256]{1,0:T(8,128)(2,1)S(1)}, u32[]{:S(2)}, u32[]{:S(2)}) %collective-permute-start.18) | collective-permute-done | bytes 131104 | tf_op jit(solution)/shard_map/ppermute | solution.py:1110
  162.4 1.7 collective-permute-start.20
  164.1 0.7 collective-permute-start.22
  164.8 5.7 %collective-permute-done.20 = bf16[512,256]{1,0:T(8,128)(2,1)S(1)} collective-permute-done((bf16[512,256]{1,0:T(8,128)(2,1)S(1)}, bf16[512,256]{1,0:T(8,128)(2,1)S(1)}, u32[]{:S(2)}, u32[]{:S(2)}) %collective-permute-start.20) | collective-permute-done | bytes 262176 | tf_op jit(solution)/shard_map/ppermute | solution.py:1087
  170.6 2.3 %collective-permute-start.21 = (bf16[1024,256]{1,0:T(8,128)(2,1)S(1)}, bf16[1024,256]{1,0:T(8,128)(2,1)S(1)}, u32[]{:S(2)}, u32[]{:S(2)}) collective-permute-start(bf16[1024,256]{1,0:T(8,128)(2,1)S(1)} %pad_maximum_fusion.9), channel_id=1, source_target_pairs={{0,8},{4,12},{8,0},{12,4},{16,24},{20,28},{24,16},{28,20},{1,9},{5... | collective-permute-start | bytes 1572872 | tf_op jit(solution)/shard_map/ppermute | solution.py:1087
  173.8 5.5 %shard_map.362 = f32[64,4096]{1,0:T(8,128)} custom-call(bf16[32,64,256]{2,1,0:T(8,128)(2,1)S(1)} %all-to-all-done.2.came_ref, s32[32,1,256]{2,1,0:T(1,128)S(1)} %all-to-all-done.request_ref), custom_call_target="tpu_custom_call" | custom-call | flops 4294967296 | bytes 2097152 | tf_op jit(solution)/shard_map/pallas_call | solution.py:247
  179.3 0.7 collective-permute-done.21
  180.3 2.4 %collective-permute-done.23 = bf16[1024,256]{1,0:T(8,128)(2,1)S(1)} collective-permute-done((bf16[1024,256]{1,0:T(8,128)(2,1)S(1)}, bf16[1024,256]{1,0:T(8,128)(2,1)S(1)}, u32[]{:S(2)}, u32[]{:S(2)}) %collective-permute-start.23) | collective-permute-done | bytes 524320 | tf_op jit(solution)/shard_map/ppermute | solution.py:1087
  183.5 2.2 %shard_map.363 = (f32[3072,256]{1,0:T(8,128)}, f32[1536,256]{1,0:T(8,128)}, f32[1536,256]{1,0:T(8,128)}, f32[1536,256]{1,0:T(8,128)}) custom-call(s32[1]{0:T(128)} %bitcast.refs_0_.bit_ref, bf16[2048,256]{1,0:T(8,128)(2,1)S(1)} %pad_maximum_fusion.2.own_a_ref, bf16[2048,256]{1,0:T(8,128)(2,1)S(1)} %pad_maximum_fusion.3.own_b_ref), custom_call_target="tpu_custom_call" | custom-call | bytes 6291456 | tf_op jit(solution)/shard_map/pallas_call | solution.py:1057
  185.7 1.5 collective-permute-done.25.came_b_ref
  187.2 2.8 %shard_map.364 = (f32[3072,256]{1,0:T(8,128)}, f32[1536,256]{1,0:T(8,128)}, f32[1536,256]{1,0:T(8,128)}, f32[1536,256]{1,0:T(8,128)}, f32[1536]{0:T(1024)}, /*in...) custom-call(s32[1]{0:T(128)} %bitcast.refs_0_.bit_ref, ...), custom_call_target="tpu_custom_call", output_to_operand_aliasing={{0}: (4, {}), {1}: (5, {}), {2}: (6, {}), {3}: (7, {})} | custom-call | bytes 6291456 | tf_op jit(solution)/shard_map/pallas_call | solution.py:1066
  (63 shorter events, 5.8 us)
Async XLA Ops:
  2.3 14.2 %collective-permute-start.2 = (bf16[288,256]{1,0:T(8,128)(2,1)}, bf16[288,256]{1,0:T(8,128)(2,1)S(1)}, u32[]{:S(2)}, u32[]{:S(2)}) collective-permute-start(bf16[288,256]{1,0:T(8,128)(2,1)} %shard_map.356), channel_id=1, source_target_pairs={{0,3},{1,2},{2,1},{3,0},{4,7},{5,6},{6,5},{7,4},{8,11},{9,10},{10,... | collective-permute-start | bytes 442376 | tf_op jit(solution)/shard_map/ppermute | solution.py:1110
  7.3 12.8 %collective-permute-start.1 = (bf16[288,256]{1,0:T(8,128)(2,1)}, bf16[288,256]{1,0:T(8,128)(2,1)S(1)}, u32[]{:S(2)}, u32[]{:S(2)}) collective-permute-start(bf16[288,256]{1,0:T(8,128)(2,1)} %shard_map.356), channel_id=1, source_target_pairs={{0,2},{1,3},{2,0},{3,1},{4,6},{5,7},{6,4},{7,5},{8,10},{9,11},{10,... | collective-permute-start | bytes 442376 | tf_op jit(solution)/shard_map/ppermute | solution.py:1110
  7.3 12.8 %collective-permute-start = (bf16[288,256]{1,0:T(8,128)(2,1)}, bf16[288,256]{1,0:T(8,128)(2,1)S(1)}, u32[]{:S(2)}, u32[]{:S(2)}) collective-permute-start(bf16[288,256]{1,0:T(8,128)(2,1)} %shard_map.356), channel_id=1, source_target_pairs={{0,1},{1,0},{2,3},{3,2},{4,5},{5,4},{6,7},{7,6},{8,9},{9,8},{10,11... | collective-permute-start | bytes 442376 | tf_op jit(solution)/shard_map/ppermute | solution.py:1110
  7.9 16.4 %copy-start = (bf16[4096,64]{0,1:T(8,128)(2,1)S(1)}, bf16[4096,64]{0,1:T(8,128)(2,1)}, u32[]{:S(2)}) copy-start(bf16[4096,64]{0,1:T(8,128)(2,1)} %param.23) | copy-start | bytes 1572868
  10.4 13.9 %all-to-all-start = ((s32[32,1,256]{2,1,0:T(1,128)}), s32[32,1,256]{2,1,0:T(1,128)S(1)}, u32[]{:S(2)}, u32[]{:S(2)}) async-start(s32[32,1,256]{2,1,0:T(1,128)} %get-tuple-element.74), calls=%async_computation | async-start | bytes 65536 | tf_op jit(solution)/shard_map/all_to_all | solution.py:1253
  21.2 9.3 %collective-permute-start.3 = (bf16[576,256]{1,0:T(8,128)(2,1)S(1)}, bf16[576,256]{1,0:T(8,128)(2,1)S(1)}, u32[]{:S(2)}, u32[]{:S(2)}) collective-permute-start(bf16[576,256]{1,0:T(8,128)(2,1)S(1)} %bitcast.49), channel_id=1, source_target_pairs={{0,16},{4,20},{8,24},{12,28},{16,0},{20,4},{24,8},{28,12},{1,17},{... | collective-permute-start | bytes 884744 | tf_op jit(solution)/shard_map/ppermute | solution.py:1087
  22.8 7.8 %collective-permute-start.4 = (bf16[576,256]{1,0:T(8,128)(2,1)S(1)}, bf16[576,256]{1,0:T(8,128)(2,1)S(1)}, u32[]{:S(2)}, u32[]{:S(2)}) collective-permute-start(bf16[576,256]{1,0:T(8,128)(2,1)S(1)} %bitcast.48), channel_id=1, source_target_pairs={{0,8},{4,12},{8,0},{12,4},{16,24},{20,28},{24,16},{28,20},{1,9},{5... | collective-permute-start | bytes 884744 | tf_op jit(solution)/shard_map/ppermute | solution.py:1087
  30.7 21.3 %collective-permute-start.5 = (bf16[1152,256]{1,0:T(8,128)(2,1)S(1)}, bf16[1152,256]{1,0:T(8,128)(2,1)S(1)}, u32[]{:S(2)}, u32[]{:S(2)}) collective-permute-start(bf16[1152,256]{1,0:T(8,128)(2,1)S(1)} %get-tuple-element.79), channel_id=1, source_target_pairs={{0,8},{4,12},{8,0},{12,4},{16,24},{20,28},{24,16},{28,20},{1,9},{5... | collective-permute-start | bytes 1769480 | tf_op jit(solution)/shard_map/ppermute | solution.py:1087
  32.2 30.9 %all-to-all-start.1 = ((bf16[32,64,256]{2,1,0:T(8,128)(2,1)}), bf16[32,64,256]{2,1,0:T(8,128)(2,1)S(1)}, u32[]{:S(2)}, u32[]{:S(2)}) async-start(bf16[32,64,256]{2,1,0:T(8,128)(2,1)} %shard_map.358), calls=%async_computation.1 | async-start | bytes 2097152 | tf_op jit(solution)/shard_map/all_to_all | solution.py:1265
  35.6 26.7 %collective-permute-start.6 = (bf16[1152,256]{1,0:T(8,128)(2,1)S(1)}, bf16[1152,256]{1,0:T(8,128)(2,1)S(1)}, u32[]{:S(2)}, u32[]{:S(2)}) collective-permute-start(bf16[1152,256]{1,0:T(8,128)(2,1)S(1)} %get-tuple-element.80), channel_id=1, source_target_pairs={{0,16},{4,20},{8,24},{12,28},{16,0},{20,4},{24,8},{28,12},{1,17},{... | collective-permute-start | bytes 1769480 | tf_op jit(solution)/shard_map/ppermute | solution.py:1087
  52.2 10.9 %copy-start.1 = (s32[512,8]{0,1:T(8,128)S(1)}, s32[512,8]{0,1:T(8,128)}, u32[]{:S(2)}) copy-start(s32[512,8]{0,1:T(8,128)} %param.21) | copy-start | bytes 49156
  52.2 10.9 %copy-start.3 = (s32[32,512]{1,0:T(8,128)S(1)}, s32[32,512]{1,0:T(8,128)}, u32[]{:S(2)}) copy-start(s32[32,512]{1,0:T(8,128)} %get-tuple-element.84.rank_ref) | copy-start | bytes 196612
  62.4 4.8 %copy-start.2 = (f32[2,512]{1,0:T(2,128)S(1)}, f32[2,512]{1,0:T(2,128)}, u32[]{:S(2)}) copy-start(f32[2,512]{1,0:T(2,128)} %refs_6_.3) | copy-start | bytes 12292
  62.5 4.7 %copy-start.4 = (bf16[2304,256]{1,0:T(8,128)(2,1)}, bf16[2304,256]{1,0:T(8,128)(2,1)S(1)}, u32[]{:S(2)}) copy-start(bf16[2304,256]{1,0:T(8,128)(2,1)S(1)} %pad_maximum_fusion.1.refs_2_) | copy-start | bytes 3538948
  62.5 4.5 %collective-permute-start.7 = (bf16[2304,256]{1,0:T(8,128)(2,1)S(1)}, bf16[2304,256]{1,0:T(8,128)(2,1)}, u32[]{:S(2)}, u32[]{:S(2)}) collective-permute-start(bf16[2304,256]{1,0:T(8,128)(2,1)S(1)} %pad_maximum_fusion.refs_1_), channel_id=1, source_target_pairs={{0,4},{4,0},{8,12},{12,8},{16,20},{20,16},{24,28},{28,24},{1,5},{5... | collective-permute-start | bytes 3538952 | tf_op jit(solution)/shard_map/ppermute | solution.py:1087
  62.6 4.7 %collective-permute-start.8 = (bf16[2304,256]{1,0:T(8,128)(2,1)S(1)}, bf16[2304,256]{1,0:T(8,128)(2,1)}, u32[]{:S(2)}, u32[]{:S(2)}) collective-permute-start(bf16[2304,256]{1,0:T(8,128)(2,1)S(1)} %pad_maximum_fusion.1.refs_2_), channel_id=1, source_target_pairs={{0,4},{4,0},{8,12},{12,8},{16,20},{20,16},{24,28},{28,24},{1,5},{5... | collective-permute-start | bytes 3538952 | tf_op jit(solution)/shard_map/ppermute | solution.py:1087
  87.7 5.5 %collective-permute-start.9 = (bf16[4096,256]{1,0:T(8,128)(2,1)}, bf16[4096,256]{1,0:T(8,128)(2,1)}, u32[]{:S(2)}, u32[]{:S(2)}) collective-permute-start(bf16[4096,256]{1,0:T(8,128)(2,1)} %get-tuple-element.87), channel_id=1, source_target_pairs={{0,4},{4,0},{8,12},{12,8},{16,20},{20,16},{24,28},{28,24},{1,5},{5... | collective-permute-start | bytes 6291464 | tf_op jit(solution)/shard_map/ppermute | solution.py:1087
  97.1 20.1 %collective-permute-start.10 = (bf16[1024,256]{1,0:T(8,128)(2,1)S(1)}, bf16[1024,256]{1,0:T(8,128)(2,1)}, u32[]{:S(2)}, u32[]{:S(2)}) collective-permute-start(bf16[1024,256]{1,0:T(8,128)(2,1)S(1)} %get-tuple-element.93), channel_id=1, source_target_pairs={{0,8},{4,12},{8,0},{12,4},{16,24},{20,28},{24,16},{28,20},{1,9},{5... | collective-permute-start | bytes 1572872 | tf_op jit(solution)/shard_map/ppermute | solution.py:1087
  98.4 36.8 %all-to-all-start.2 = ((bf16[32,64,256]{2,1,0:T(8,128)(2,1)}), bf16[32,64,256]{2,1,0:T(8,128)(2,1)S(1)}, u32[]{:S(2)}, u32[]{:S(2)}) async-start(bf16[32,64,256]{2,1,0:T(8,128)(2,1)} %get-tuple-element.96), calls=%async_computation.2 | async-start | bytes 2097152 | tf_op jit(solution)/shard_map/all_to_all | solution.py:1203
  102.6 25.6 %collective-permute-start.12 = (bf16[1024,256]{1,0:T(8,128)(2,1)}, bf16[1024,256]{1,0:T(8,128)(2,1)S(1)}, u32[]{:S(2)}, u32[]{:S(2)}) collective-permute-start(bf16[1024,256]{1,0:T(8,128)(2,1)} %get-tuple-element.95), channel_id=1, source_target_pairs={{0,16},{4,20},{8,24},{12,28},{16,0},{20,4},{24,8},{28,12},{1,17},{... | collective-permute-start | bytes 1572872 | tf_op jit(solution)/shard_map/ppermute | solution.py:1087
  119.0 14.4 %collective-permute-start.11 = (bf16[512,256]{1,0:T(8,128)(2,1)}, bf16[512,256]{1,0:T(8,128)(2,1)}, u32[]{:S(2)}, u32[]{:S(2)}) collective-permute-start(bf16[512,256]{1,0:T(8,128)(2,1)} %constant_dynamic-slice_fusion.5), channel_id=1, source_target_pairs={{0,16},{4,20},{8,24},{12,28},{16,0},{20,4},{24,8},{28,12},{1,17},{... | collective-permute-start | bytes 786440 | tf_op jit(solution)/shard_map/ppermute | solution.py:1087
  128.3 6.7 %collective-permute-start.13 = (bf16[512,256]{1,0:T(8,128)(2,1)S(1)}, bf16[512,256]{1,0:T(8,128)(2,1)S(1)}, u32[]{:S(2)}, u32[]{:S(2)}) collective-permute-start(bf16[512,256]{1,0:T(8,128)(2,1)S(1)} %constant_dynamic-slice_fusion.4), channel_id=1, source_target_pairs={{0,8},{4,12},{8,0},{12,4},{16,24},{20,28},{24,16},{28,20},{1,9},{5... | collective-permute-start | bytes 786440 | tf_op jit(solution)/shard_map/ppermute | solution.py:1087
  135.3 6.4 %collective-permute-start.14 = (bf16[256,256]{1,0:T(8,128)(2,1)S(1)}, bf16[256,256]{1,0:T(8,128)(2,1)S(1)}, u32[]{:S(2)}, u32[]{:S(2)}) collective-permute-start(bf16[256,256]{1,0:T(8,128)(2,1)S(1)} %get-tuple-element.98), channel_id=1, source_target_pairs={{0,1},{1,0},{2,3},{3,2},{4,5},{5,4},{6,7},{7,6},{8,9},{9,8},{10,11... | collective-permute-start | bytes 393224 | tf_op jit(solution)/shard_map/ppermute | solution.py:1110
  137.2 11.7 %collective-permute-start.15 = (bf16[256,256]{1,0:T(8,128)(2,1)S(1)}, bf16[256,256]{1,0:T(8,128)(2,1)S(1)}, u32[]{:S(2)}, u32[]{:S(2)}) collective-permute-start(bf16[256,256]{1,0:T(8,128)(2,1)S(1)} %get-tuple-element.99), channel_id=1, source_target_pairs={{0,2},{1,3},{2,0},{3,1},{4,6},{5,7},{6,4},{7,5},{8,10},{9,11},{10,... | collective-permute-start | bytes 393224 | tf_op jit(solution)/shard_map/ppermute | solution.py:1110
  139.9 9.0 %collective-permute-start.16 = (bf16[256,256]{1,0:T(8,128)(2,1)S(1)}, bf16[256,256]{1,0:T(8,128)(2,1)S(1)}, u32[]{:S(2)}, u32[]{:S(2)}) collective-permute-start(bf16[256,256]{1,0:T(8,128)(2,1)S(1)} %get-tuple-element.100), channel_id=1, source_target_pairs={{0,3},{1,2},{2,1},{3,0},{4,7},{5,6},{6,5},{7,4},{8,11},{9,10},{10,... | collective-permute-start | bytes 393224 | tf_op jit(solution)/shard_map/ppermute | solution.py:1110
  149.0 6.0 %collective-permute-start.19 = (bf16[256,256]{1,0:T(8,128)(2,1)S(1)}, bf16[256,256]{1,0:T(8,128)(2,1)S(1)}, u32[]{:S(2)}, u32[]{:S(2)}) collective-permute-start(bf16[256,256]{1,0:T(8,128)(2,1)S(1)} %add_convert_fusion.5), channel_id=1, source_target_pairs={{0,1},{1,0},{2,3},{3,2},{4,5},{5,4},{6,7},{7,6},{8,9},{9,8},{10,11... | collective-permute-start | bytes 393224 | tf_op jit(solution)/shard_map/ppermute | solution.py:1110
  151.0 11.2 %collective-permute-start.18 = (bf16[256,256]{1,0:T(8,128)(2,1)S(1)}, bf16[256,256]{1,0:T(8,128)(2,1)S(1)}, u32[]{:S(2)}, u32[]{:S(2)}) collective-permute-start(bf16[256,256]{1,0:T(8,128)(2,1)S(1)} %add_convert_fusion.5), channel_id=1, source_target_pairs={{0,2},{1,3},{2,0},{3,1},{4,6},{5,7},{6,4},{7,5},{8,10},{9,11},{10,... | collective-permute-start | bytes 393224 | tf_op jit(solution)/shard_map/ppermute | solution.py:1110
  151.9 10.3 %collective-permute-start.17 = (bf16[256,256]{1,0:T(8,128)(2,1)S(1)}, bf16[256,256]{1,0:T(8,128)(2,1)S(1)}, u32[]{:S(2)}, u32[]{:S(2)}) collective-permute-start(bf16[256,256]{1,0:T(8,128)(2,1)S(1)} %add_convert_fusion.5), channel_id=1, source_target_pairs={{0,3},{1,2},{2,1},{3,0},{4,7},{5,6},{6,5},{7,4},{8,11},{9,10},{10,... | collective-permute-start | bytes 393224 | tf_op jit(solution)/shard_map/ppermute | solution.py:1110
  162.4 8.0 %collective-permute-start.20 = (bf16[512,256]{1,0:T(8,128)(2,1)S(1)}, bf16[512,256]{1,0:T(8,128)(2,1)S(1)}, u32[]{:S(2)}, u32[]{:S(2)}) collective-permute-start(bf16[512,256]{1,0:T(8,128)(2,1)S(1)} %bitcast.51), channel_id=1, source_target_pairs={{0,16},{4,20},{8,24},{12,28},{16,0},{20,4},{24,8},{28,12},{1,17},{... | collective-permute-start | bytes 786440 | tf_op jit(solution)/shard_map/ppermute | solution.py:1087
  164.1 9.2 %collective-permute-start.22 = (bf16[512,256]{1,0:T(8,128)(2,1)S(1)}, bf16[512,256]{1,0:T(8,128)(2,1)S(1)}, u32[]{:S(2)}, u32[]{:S(2)}) collective-permute-start(bf16[512,256]{1,0:T(8,128)(2,1)S(1)} %bitcast.50), channel_id=1, source_target_pairs={{0,8},{4,12},{8,0},{12,4},{16,24},{20,28},{24,16},{28,20},{1,9},{5... | collective-permute-start | bytes 786440 | tf_op jit(solution)/shard_map/ppermute | solution.py:1087
  170.6 9.5 %collective-permute-start.21 = (bf16[1024,256]{1,0:T(8,128)(2,1)S(1)}, bf16[1024,256]{1,0:T(8,128)(2,1)S(1)}, u32[]{:S(2)}, u32[]{:S(2)}) collective-permute-start(bf16[1024,256]{1,0:T(8,128)(2,1)S(1)} %pad_maximum_fusion.9), channel_id=1, source_target_pairs={{0,8},{4,12},{8,0},{12,4},{16,24},{20,28},{24,16},{28,20},{1,9},{5... | collective-permute-start | bytes 1572872 | tf_op jit(solution)/shard_map/ppermute | solution.py:1087
  173.4 9.2 %collective-permute-start.23 = (bf16[1024,256]{1,0:T(8,128)(2,1)S(1)}, bf16[1024,256]{1,0:T(8,128)(2,1)S(1)}, u32[]{:S(2)}, u32[]{:S(2)}) collective-permute-start(bf16[1024,256]{1,0:T(8,128)(2,1)S(1)} %pad_maximum_fusion.10), channel_id=1, source_target_pairs={{0,16},{4,20},{8,24},{12,28},{16,0},{20,4},{24,8},{28,12},{1,17},{... | collective-permute-start | bytes 1572872 | tf_op jit(solution)/shard_map/ppermute | solution.py:1087
  182.9 2.8 %collective-permute-start.24 = (bf16[2048,256]{1,0:T(8,128)(2,1)S(1)}, bf16[2048,256]{1,0:T(8,128)(2,1)S(1)}, u32[]{:S(2)}, u32[]{:S(2)}) collective-permute-start(bf16[2048,256]{1,0:T(8,128)(2,1)S(1)} %pad_maximum_fusion.2.own_a_ref), channel_id=1, source_target_pairs={{0,4},{4,0},{8,12},{12,8},{16,20},{20,16},{24,28},{28,24},{1,5},{5... | collective-permute-start | bytes 3145736 | tf_op jit(solution)/shard_map/ppermute | solution.py:1087
  183.0 4.1 %collective-permute-start.25 = (bf16[2048,256]{1,0:T(8,128)(2,1)S(1)}, bf16[2048,256]{1,0:T(8,128)(2,1)S(1)}, u32[]{:S(2)}, u32[]{:S(2)}) collective-permute-start(bf16[2048,256]{1,0:T(8,128)(2,1)S(1)} %pad_maximum_fusion.3.own_b_ref), channel_id=1, source_target_pairs={{0,4},{4,0},{8,12},{12,8},{16,20},{20,16},{24,28},{28,24},{1,5},{5... | collective-permute-start | bytes 3145736 | tf_op jit(solution)/shard_map/ppermute | solution.py:1087

commit v7 on v6

--- a/solution.py
+++ b/solution.py
@@ -9,7 +9,7 @@
 
 EPS = 1e-05
 VMEM_LIMIT = 56 * 1024 * 1024
-SMALL_LIMIT = 16 * 1024 * 1024
+SMALL_LIMIT = 24 * 1024 * 1024
 ROW_BLOCKS = 8
 
 
@@ -199,7 +199,7 @@
             jax.ShapeDtypeStruct((devices, width, capacity), jnp.bfloat16),
             jax.ShapeDtypeStruct((events, fields * width), jnp.float32),
         ),
-        2 * devices * width * capacity * events,
+        32 * devices * width * capacity * events,
         2 * (devices * width * capacity + 2 * fields * width * events),
         [pltpu.VMEM((fields * width, events), jnp.bfloat16)],
     )(grad, rank, owner_rows)

time: 191 us -> 190 us (level)
  no operation moved by 1% of the time
where the time goes in v7:
time: 190 us; the launch traced here: 189 us
  waiting for transfers between devices  83.6 us (44%)
  Pallas kernels  50.4 us (27%)
  starting transfers between devices  45.2 us (24%)
  other arithmetic  7.02 us (4%)
  local copies, waits for them, and re-layouts  1.99 us (1%)
    ppermute x17, waiting for transfers between devices, swap_with(): return lax.ppermute(values, 'dp', partners(mask, size))  62.3 us
    ppermute x9, waiting for transfers between devices, swap_groups(): return lax.ppermute(values, 'fsdp', partners(mask, lax.axis_size('fsdp')))  21.3 us
    pallas_call x1, Pallas kernels, dense(): pl.pallas_call(functools.partial(dense_body, places), out_shape=(jax.Shap...  20.5 us
    ppermute x17, starting transfers between devices, swap_with(): return lax.ppermute(values, 'dp', partners(mask, size))  16.8 us
    ppermute x9, starting transfers between devices, swap_groups(): return lax.ppermute(values, 'fsdp', partners(mask, lax.axis_size('fsdp')))  14.8 us
    pallas_call x1, Pallas kernels, find_rows(): local_kernel(find_body, jax.ShapeDtypeStruct((devices, width, capacity),...  6.2 us
    all_to_all x1, starting transfers between devices, on_device(): lax.all_to_all(request, ('dp', 'fsdp'), split_axis=0, concat_axis=0, tile...  6.01 us
    pallas_call x1, Pallas kernels, add_rows(): local_kernel(add_body, jax.ShapeDtypeStruct((width, rows), jnp.float32),...  5.5 us
  transfers between devices with their start and end apart: 29, of which 17 were waited for; matrix products, arithmetic and copies ran while one was open for 3% of the time, Pallas kernels for 13%

profile of v7, /device:TPU:0, one launch (start us, length us, event | category | flops | bytes accessed | tf_op | source)
XLA Modules:
  0.0 189.5 jit_solution(11454190579269915853)
XLA Ops:
  0.7 1.6 shard_map.356
  2.3 5.0 %collective-permute-start.2 = (bf16[288,256]{1,0:T(8,128)(2,1)}, bf16[288,256]{1,0:T(8,128)(2,1)S(1)}, u32[]{:S(2)}, u32[]{:S(2)}) collective-permute-start(bf16[288,256]{1,0:T(8,128)(2,1)} %shard_map.356), channel_id=1, source_target_pairs={{0,3},{1,2},{2,1},{3,0},{4,7},{5,6},{6,5},{7,4},{8,11},{9,10},{10,... | collective-permute-start | bytes 442376 | tf_op jit(solution)/shard_map/ppermute | solution.py:1110
  7.9 2.5 %shard_map.357 = (s32[32,1,256]{2,1,0:T(1,128)}, s32[32,512]{1,0:T(8,128)}) custom-call(s32[8,512]{1,0:T(8,128)} %bitcast.44, s32[8,512]{1,0:T(8,128)} %bitcast.58), custom_call_target="tpu_custom_call" | custom-call | flops 150994944 | bytes 98304 | tf_op jit(solution)/shard_map/pallas_call | solution.py:71
  10.4 6.0 %all-to-all-start = ((s32[32,1,256]{2,1,0:T(1,128)}), s32[32,1,256]{2,1,0:T(1,128)S(1)}, u32[]{:S(2)}, u32[]{:S(2)}) async-start(s32[32,1,256]{2,1,0:T(1,128)} %get-tuple-element.74), calls=%async_computation | async-start | bytes 65536 | tf_op jit(solution)/shard_map/all_to_all | solution.py:1253
  16.5 3.6 %collective-permute-done.1 = bf16[288,256]{1,0:T(8,128)(2,1)S(1)} collective-permute-done((bf16[288,256]{1,0:T(8,128)(2,1)}, bf16[288,256]{1,0:T(8,128)(2,1)S(1)}, u32[]{:S(2)}, u32[]{:S(2)}) %collective-permute-start.1) | collective-permute-done | bytes 147488 | tf_op jit(solution)/shard_map/ppermute | solution.py:1110
  20.1 1.0 select_bitcast_fusion.3
  21.2 1.6 collective-permute-start.3
  22.8 1.5 collective-permute-start.4
  24.3 6.2 %shard_map.358 = bf16[32,64,256]{2,1,0:T(8,128)(2,1)} custom-call(s32[32,1,256]{2,1,0:T(1,128)S(1)} %all-to-all-done.request_ref, bf16[64,4096]{1,0:T(8,128)(2,1)S(1)} %bitcast.43), custom_call_target="tpu_custom_call" | custom-call | flops 34359738368 | bytes 1572864 | tf_op jit(solution)/shard_map/pallas_call | solution.py:112
  30.7 1.5 collective-permute-start.5
  32.2 3.4 %all-to-all-start.1 = ((bf16[32,64,256]{2,1,0:T(8,128)(2,1)}), bf16[32,64,256]{2,1,0:T(8,128)(2,1)S(1)}, u32[]{:S(2)}, u32[]{:S(2)}) async-start(bf16[32,64,256]{2,1,0:T(8,128)(2,1)} %shard_map.358), calls=%async_computation.1 | async-start | bytes 2097152 | tf_op jit(solution)/shard_map/all_to_all | solution.py:1265
  35.6 1.8 collective-permute-start.6
  37.4 14.6 %collective-permute-done.5 = bf16[1152,256]{1,0:T(8,128)(2,1)S(1)} collective-permute-done((bf16[1152,256]{1,0:T(8,128)(2,1)S(1)}, bf16[1152,256]{1,0:T(8,128)(2,1)S(1)}, u32[]{:S(2)}, u32[]{:S(2)}) %collective-permute-start.5) | collective-permute-done | bytes 589856 | tf_op jit(solution)/shard_map/ppermute | solution.py:1087
  52.2 10.1 %collective-permute-done.6 = bf16[1152,256]{1,0:T(8,128)(2,1)S(1)} collective-permute-done((bf16[1152,256]{1,0:T(8,128)(2,1)S(1)}, bf16[1152,256]{1,0:T(8,128)(2,1)S(1)}, u32[]{:S(2)}, u32[]{:S(2)}) %collective-permute-start.6) | collective-permute-done | bytes 589856 | tf_op jit(solution)/shard_map/ppermute | solution.py:1087
  63.1 3.9 %shard_map.359.refs_5_ = bf16[512,512]{1,0:T(8,128)(2,1)S(1)} custom-call(bf16[32,64,256]{2,1,0:T(8,128)(2,1)S(1)} %all-to-all-done.1.found_ref, s32[32,512]{1,0:T(8,128)S(1)} %copy-done.3, s32[8,512]{1,0:T(8,128)S(1)} %bitcast.45), custom_call_target="tpu_custom_call" | custom-call | flops 536870912 | bytes 1572864 | tf_op jit(solution)/shard_map/pallas_call | solution.py:155
  67.3 20.5 %shard_map.360 = (f32[2,512]{1,0:T(2,128)}, f32[512,512]{1,0:T(8,128)S(1)}, bf16[4096,256]{1,0:T(8,128)(2,1)}, bf16[4096,256]{1,0:T(8,128)(2,1)}) custom-call(s32[1]{0:T(128)} %bitcast.refs_0_.bit_ref, bf16[2304,256]{1,0:T(8,128)(2,1)S(1)} %pad_maximum_fusion.refs_1_, bf16[2304,256]{1,0:T(8,128)(2,1)} %copy-done.5, ...), custom_call_target="tpu_custom_call" | custom-call | flops 6241124352 | bytes 25165824 | tf_op jit(solution)/shard_map/pallas_call | solution.py:894
  87.9 5.3 %shard_map.361 = (bf16[32,64,256]{2,1,0:T(8,128)(2,1)}, f32[512,512]{1,0:T(8,128)}) custom-call(f32[512,512]{1,0:T(8,128)S(1)} %get-tuple-element.88.grad_ref, s32[32,512]{1,0:T(8,128)S(1)} %copy-done.3, s32[8,512]{1,0:T(8,128)S(1)} %bitcast.46), custom_call_target="tpu_custom_call" | custom-call | flops 8589934592 | bytes 2097152 | tf_op jit(solution)/shard_map/pallas_call | solution.py:196
  93.2 2.1 %add_convert_fusion = bf16[4096,256]{1,0:T(8,128)(2,1)S(1)} fusion(bf16[4096,256]{1,0:T(8,128)(2,1)} %collective-permute-done.9, bf16[4096,256]{1,0:T(8,128)(2,1)S(1)} %copy-done.4), kind=kLoop, calls=%fused_computation | loop fusion | flops 4194304 | bytes 6291456 | tf_op jit(solution)/shard_map/convert_element_type | solution.py:1098
  95.5 0.9 constant_dynamic-slice_fusion.6
  96.4 1.4 collective-permute-start.10
  97.8 4.2 %all-to-all-start.2 = ((bf16[32,64,256]{2,1,0:T(8,128)(2,1)}), bf16[32,64,256]{2,1,0:T(8,128)(2,1)S(1)}, u32[]{:S(2)}, u32[]{:S(2)}) async-start(bf16[32,64,256]{2,1,0:T(8,128)(2,1)} %get-tuple-element.96), calls=%async_computation.2 | async-start | bytes 2097152 | tf_op jit(solution)/shard_map/all_to_all | solution.py:1203
  102.0 1.6 collective-permute-start.12
  103.5 12.9 %collective-permute-done.10 = bf16[1024,256]{1,0:T(8,128)(2,1)} collective-permute-done((bf16[1024,256]{1,0:T(8,128)(2,1)S(1)}, bf16[1024,256]{1,0:T(8,128)(2,1)}, u32[]{:S(2)}, u32[]{:S(2)}) %collective-permute-start.10) | collective-permute-done | bytes 524320 | tf_op jit(solution)/shard_map/ppermute | solution.py:1087
  116.5 1.2 add_convert_fusion.2
  117.7 0.7 constant_dynamic-slice_fusion.5
  118.4 9.1 %collective-permute-done.12 = bf16[1024,256]{1,0:T(8,128)(2,1)S(1)} collective-permute-done((bf16[1024,256]{1,0:T(8,128)(2,1)}, bf16[1024,256]{1,0:T(8,128)(2,1)S(1)}, u32[]{:S(2)}, u32[]{:S(2)}) %collective-permute-start.12) | collective-permute-done | bytes 524320 | tf_op jit(solution)/shard_map/ppermute | solution.py:1087
  127.7 1.1 collective-permute-start.13
  128.8 4.0 %collective-permute-done.11 = bf16[512,256]{1,0:T(8,128)(2,1)} collective-permute-done((bf16[512,256]{1,0:T(8,128)(2,1)}, bf16[512,256]{1,0:T(8,128)(2,1)}, u32[]{:S(2)}, u32[]{:S(2)}) %collective-permute-start.11) | collective-permute-done | bytes 262176 | tf_op jit(solution)/shard_map/ppermute | solution.py:1087
  132.8 1.0 add_convert_fusion.4
  134.6 2.0 %collective-permute-start.14 = (bf16[256,256]{1,0:T(8,128)(2,1)S(1)}, bf16[256,256]{1,0:T(8,128)(2,1)S(1)}, u32[]{:S(2)}, u32[]{:S(2)}) collective-permute-start(bf16[256,256]{1,0:T(8,128)(2,1)S(1)} %get-tuple-element.98), channel_id=1, source_target_pairs={{0,1},{1,0},{2,3},{3,2},{4,5},{5,4},{6,7},{7,6},{8,9},{9,8},{10,11... | collective-permute-start | bytes 393224 | tf_op jit(solution)/shard_map/ppermute | solution.py:1110
  136.6 2.7 %collective-permute-start.15 = (bf16[256,256]{1,0:T(8,128)(2,1)S(1)}, bf16[256,256]{1,0:T(8,128)(2,1)S(1)}, u32[]{:S(2)}, u32[]{:S(2)}) collective-permute-start(bf16[256,256]{1,0:T(8,128)(2,1)S(1)} %get-tuple-element.99), channel_id=1, source_target_pairs={{0,2},{1,3},{2,0},{3,1},{4,6},{5,7},{6,4},{7,5},{8,10},{9,11},{10,... | collective-permute-start | bytes 393224 | tf_op jit(solution)/shard_map/ppermute | solution.py:1110
  139.3 1.8 collective-permute-done.14
  141.0 7.2 %collective-permute-done.15 = bf16[256,256]{1,0:T(8,128)(2,1)S(1)} collective-permute-done((bf16[256,256]{1,0:T(8,128)(2,1)S(1)}, bf16[256,256]{1,0:T(8,128)(2,1)S(1)}, u32[]{:S(2)}, u32[]{:S(2)}) %collective-permute-start.15) | collective-permute-done | bytes 131104 | tf_op jit(solution)/shard_map/ppermute | solution.py:1110
  148.3 2.0 %collective-permute-start.19 = (bf16[256,256]{1,0:T(8,128)(2,1)S(1)}, bf16[256,256]{1,0:T(8,128)(2,1)S(1)}, u32[]{:S(2)}, u32[]{:S(2)}) collective-permute-start(bf16[256,256]{1,0:T(8,128)(2,1)S(1)} %add_convert_fusion.5), channel_id=1, source_target_pairs={{0,1},{1,0},{2,3},{3,2},{4,5},{5,4},{6,7},{7,6},{8,9},{9,8},{10,11... | collective-permute-start | bytes 393224 | tf_op jit(solution)/shard_map/ppermute | solution.py:1110
  150.3 0.9 collective-permute-start.18
  151.3 1.5 collective-permute-start.17
  152.8 1.5 collective-permute-done.19
  154.3 7.3 %collective-permute-done.18 = bf16[256,256]{1,0:T(8,128)(2,1)S(1)} collective-permute-done((bf16[256,256]{1,0:T(8,128)(2,1)S(1)}, bf16[256,256]{1,0:T(8,128)(2,1)S(1)}, u32[]{:S(2)}, u32[]{:S(2)}) %collective-permute-start.18) | collective-permute-done | bytes 131104 | tf_op jit(solution)/shard_map/ppermute | solution.py:1110
  161.8 1.7 collective-permute-start.20
  163.4 0.7 collective-permute-start.22
  164.1 5.7 %collective-permute-done.20 = bf16[512,256]{1,0:T(8,128)(2,1)S(1)} collective-permute-done((bf16[512,256]{1,0:T(8,128)(2,1)S(1)}, bf16[512,256]{1,0:T(8,128)(2,1)S(1)}, u32[]{:S(2)}, u32[]{:S(2)}) %collective-permute-start.20) | collective-permute-done | bytes 262176 | tf_op jit(solution)/shard_map/ppermute | solution.py:1087
  169.9 2.3 %collective-permute-start.21 = (bf16[1024,256]{1,0:T(8,128)(2,1)S(1)}, bf16[1024,256]{1,0:T(8,128)(2,1)S(1)}, u32[]{:S(2)}, u32[]{:S(2)}) collective-permute-start(bf16[1024,256]{1,0:T(8,128)(2,1)S(1)} %pad_maximum_fusion.9), channel_id=1, source_target_pairs={{0,8},{4,12},{8,0},{12,4},{16,24},{20,28},{24,16},{28,20},{1,9},{5... | collective-permute-start | bytes 1572872 | tf_op jit(solution)/shard_map/ppermute | solution.py:1087
  173.2 5.5 %shard_map.362 = f32[64,4096]{1,0:T(8,128)} custom-call(bf16[32,64,256]{2,1,0:T(8,128)(2,1)S(1)} %all-to-all-done.2.came_ref, s32[32,1,256]{2,1,0:T(1,128)S(1)} %all-to-all-done.request_ref), custom_call_target="tpu_custom_call" | custom-call | flops 4294967296 | bytes 2097152 | tf_op jit(solution)/shard_map/pallas_call | solution.py:247
  178.7 0.7 collective-permute-done.21
  179.6 2.4 %collective-permute-done.23 = bf16[1024,256]{1,0:T(8,128)(2,1)S(1)} collective-permute-done((bf16[1024,256]{1,0:T(8,128)(2,1)S(1)}, bf16[1024,256]{1,0:T(8,128)(2,1)S(1)}, u32[]{:S(2)}, u32[]{:S(2)}) %collective-permute-start.23) | collective-permute-done | bytes 524320 | tf_op jit(solution)/shard_map/ppermute | solution.py:1087
  182.9 2.2 %shard_map.363 = (f32[3072,256]{1,0:T(8,128)}, f32[1536,256]{1,0:T(8,128)}, f32[1536,256]{1,0:T(8,128)}, f32[1536,256]{1,0:T(8,128)}) custom-call(s32[1]{0:T(128)} %bitcast.refs_0_.bit_ref, bf16[2048,256]{1,0:T(8,128)(2,1)S(1)} %pad_maximum_fusion.2.own_a_ref, bf16[2048,256]{1,0:T(8,128)(2,1)S(1)} %pad_maximum_fusion.3.own_b_ref), custom_call_target="tpu_custom_call" | custom-call | bytes 6291456 | tf_op jit(solution)/shard_map/pallas_call | solution.py:1057
  185.0 1.5 collective-permute-done.25.came_b_ref
  186.5 2.8 %shard_map.364 = (f32[3072,256]{1,0:T(8,128)}, f32[1536,256]{1,0:T(8,128)}, f32[1536,256]{1,0:T(8,128)}, f32[1536,256]{1,0:T(8,128)}, f32[1536]{0:T(1024)}, /*in...) custom-call(s32[1]{0:T(128)} %bitcast.refs_0_.bit_ref, ...), custom_call_target="tpu_custom_call", output_to_operand_aliasing={{0}: (4, {}), {1}: (5, {}), {2}: (6, {}), {3}: (7, {})} | custom-call | bytes 6291456 | tf_op jit(solution)/shard_map/pallas_call | solution.py:1066
  (65 shorter events, 5.8 us)
Async XLA Ops:
  2.3 14.2 %collective-permute-start.2 = (bf16[288,256]{1,0:T(8,128)(2,1)}, bf16[288,256]{1,0:T(8,128)(2,1)S(1)}, u32[]{:S(2)}, u32[]{:S(2)}) collective-permute-start(bf16[288,256]{1,0:T(8,128)(2,1)} %shard_map.356), channel_id=1, source_target_pairs={{0,3},{1,2},{2,1},{3,0},{4,7},{5,6},{6,5},{7,4},{8,11},{9,10},{10,... | collective-permute-start | bytes 442376 | tf_op jit(solution)/shard_map/ppermute | solution.py:1110
  7.3 12.8 %collective-permute-start.1 = (bf16[288,256]{1,0:T(8,128)(2,1)}, bf16[288,256]{1,0:T(8,128)(2,1)S(1)}, u32[]{:S(2)}, u32[]{:S(2)}) collective-permute-start(bf16[288,256]{1,0:T(8,128)(2,1)} %shard_map.356), channel_id=1, source_target_pairs={{0,2},{1,3},{2,0},{3,1},{4,6},{5,7},{6,4},{7,5},{8,10},{9,11},{10,... | collective-permute-start | bytes 442376 | tf_op jit(solution)/shard_map/ppermute | solution.py:1110
  7.3 12.8 %collective-permute-start = (bf16[288,256]{1,0:T(8,128)(2,1)}, bf16[288,256]{1,0:T(8,128)(2,1)S(1)}, u32[]{:S(2)}, u32[]{:S(2)}) collective-permute-start(bf16[288,256]{1,0:T(8,128)(2,1)} %shard_map.356), channel_id=1, source_target_pairs={{0,1},{1,0},{2,3},{3,2},{4,5},{5,4},{6,7},{7,6},{8,9},{9,8},{10,11... | collective-permute-start | bytes 442376 | tf_op jit(solution)/shard_map/ppermute | solution.py:1110
  7.9 16.4 %copy-start = (bf16[4096,64]{0,1:T(8,128)(2,1)S(1)}, bf16[4096,64]{0,1:T(8,128)(2,1)}, u32[]{:S(2)}) copy-start(bf16[4096,64]{0,1:T(8,128)(2,1)} %param.23) | copy-start | bytes 1572868
  10.4 13.9 %all-to-all-start = ((s32[32,1,256]{2,1,0:T(1,128)}), s32[32,1,256]{2,1,0:T(1,128)S(1)}, u32[]{:S(2)}, u32[]{:S(2)}) async-start(s32[32,1,256]{2,1,0:T(1,128)} %get-tuple-element.74), calls=%async_computation | async-start | bytes 65536 | tf_op jit(solution)/shard_map/all_to_all | solution.py:1253
  21.2 9.3 %collective-permute-start.3 = (bf16[576,256]{1,0:T(8,128)(2,1)S(1)}, bf16[576,256]{1,0:T(8,128)(2,1)S(1)}, u32[]{:S(2)}, u32[]{:S(2)}) collective-permute-start(bf16[576,256]{1,0:T(8,128)(2,1)S(1)} %bitcast.49), channel_id=1, source_target_pairs={{0,16},{4,20},{8,24},{12,28},{16,0},{20,4},{24,8},{28,12},{1,17},{... | collective-permute-start | bytes 884744 | tf_op jit(solution)/shard_map/ppermute | solution.py:1087
  22.8 7.8 %collective-permute-start.4 = (bf16[576,256]{1,0:T(8,128)(2,1)S(1)}, bf16[576,256]{1,0:T(8,128)(2,1)S(1)}, u32[]{:S(2)}, u32[]{:S(2)}) collective-permute-start(bf16[576,256]{1,0:T(8,128)(2,1)S(1)} %bitcast.48), channel_id=1, source_target_pairs={{0,8},{4,12},{8,0},{12,4},{16,24},{20,28},{24,16},{28,20},{1,9},{5... | collective-permute-start | bytes 884744 | tf_op jit(solution)/shard_map/ppermute | solution.py:1087
  30.7 21.3 %collective-permute-start.5 = (bf16[1152,256]{1,0:T(8,128)(2,1)S(1)}, bf16[1152,256]{1,0:T(8,128)(2,1)S(1)}, u32[]{:S(2)}, u32[]{:S(2)}) collective-permute-start(bf16[1152,256]{1,0:T(8,128)(2,1)S(1)} %get-tuple-element.79), channel_id=1, source_target_pairs={{0,8},{4,12},{8,0},{12,4},{16,24},{20,28},{24,16},{28,20},{1,9},{5... | collective-permute-start | bytes 1769480 | tf_op jit(solution)/shard_map/ppermute | solution.py:1087
  32.2 30.9 %all-to-all-start.1 = ((bf16[32,64,256]{2,1,0:T(8,128)(2,1)}), bf16[32,64,256]{2,1,0:T(8,128)(2,1)S(1)}, u32[]{:S(2)}, u32[]{:S(2)}) async-start(bf16[32,64,256]{2,1,0:T(8,128)(2,1)} %shard_map.358), calls=%async_computation.1 | async-start | bytes 2097152 | tf_op jit(solution)/shard_map/all_to_all | solution.py:1265
  35.6 26.7 %collective-permute-start.6 = (bf16[1152,256]{1,0:T(8,128)(2,1)S(1)}, bf16[1152,256]{1,0:T(8,128)(2,1)S(1)}, u32[]{:S(2)}, u32[]{:S(2)}) collective-permute-start(bf16[1152,256]{1,0:T(8,128)(2,1)S(1)} %get-tuple-element.80), channel_id=1, source_target_pairs={{0,16},{4,20},{8,24},{12,28},{16,0},{20,4},{24,8},{28,12},{1,17},{... | collective-permute-start | bytes 1769480 | tf_op jit(solution)/shard_map/ppermute | solution.py:1087
  52.2 10.9 %copy-start.1 = (s32[512,8]{0,1:T(8,128)S(1)}, s32[512,8]{0,1:T(8,128)}, u32[]{:S(2)}) copy-start(s32[512,8]{0,1:T(8,128)} %param.21) | copy-start | bytes 49156
  52.2 10.9 %copy-start.3 = (s32[32,512]{1,0:T(8,128)S(1)}, s32[32,512]{1,0:T(8,128)}, u32[]{:S(2)}) copy-start(s32[32,512]{1,0:T(8,128)} %get-tuple-element.84.rank_ref) | copy-start | bytes 196612
  62.4 4.8 %copy-start.2 = (f32[2,512]{1,0:T(2,128)S(1)}, f32[2,512]{1,0:T(2,128)}, u32[]{:S(2)}) copy-start(f32[2,512]{1,0:T(2,128)} %refs_6_.3) | copy-start | bytes 12292
  62.5 4.7 %copy-start.5 = (bf16[2304,256]{1,0:T(8,128)(2,1)}, bf16[2304,256]{1,0:T(8,128)(2,1)S(1)}, u32[]{:S(2)}) copy-start(bf16[2304,256]{1,0:T(8,128)(2,1)S(1)} %pad_maximum_fusion.1.refs_2_) | copy-start | bytes 3538948
  62.5 4.5 %collective-permute-start.7 = (bf16[2304,256]{1,0:T(8,128)(2,1)S(1)}, bf16[2304,256]{1,0:T(8,128)(2,1)}, u32[]{:S(2)}, u32[]{:S(2)}) collective-permute-start(bf16[2304,256]{1,0:T(8,128)(2,1)S(1)} %pad_maximum_fusion.refs_1_), channel_id=1, source_target_pairs={{0,4},{4,0},{8,12},{12,8},{16,20},{20,16},{24,28},{28,24},{1,5},{5... | collective-permute-start | bytes 3538952 | tf_op jit(solution)/shard_map/ppermute | solution.py:1087
  62.6 4.7 %collective-permute-start.8 = (bf16[2304,256]{1,0:T(8,128)(2,1)S(1)}, bf16[2304,256]{1,0:T(8,128)(2,1)}, u32[]{:S(2)}, u32[]{:S(2)}) collective-permute-start(bf16[2304,256]{1,0:T(8,128)(2,1)S(1)} %pad_maximum_fusion.1.refs_2_), channel_id=1, source_target_pairs={{0,4},{4,0},{8,12},{12,8},{16,20},{20,16},{24,28},{28,24},{1,5},{5... | collective-permute-start | bytes 3538952 | tf_op jit(solution)/shard_map/ppermute | solution.py:1087
  87.7 5.5 %collective-permute-start.9 = (bf16[4096,256]{1,0:T(8,128)(2,1)}, bf16[4096,256]{1,0:T(8,128)(2,1)}, u32[]{:S(2)}, u32[]{:S(2)}) collective-permute-start(bf16[4096,256]{1,0:T(8,128)(2,1)} %get-tuple-element.87), channel_id=1, source_target_pairs={{0,4},{4,0},{8,12},{12,8},{16,20},{20,16},{24,28},{28,24},{1,5},{5... | collective-permute-start | bytes 6291464 | tf_op jit(solution)/shard_map/ppermute | solution.py:1087
  87.9 5.3 %copy-start.4 = (bf16[4096,256]{1,0:T(8,128)(2,1)S(1)}, bf16[4096,256]{1,0:T(8,128)(2,1)}, u32[]{:S(2)}) copy-start(bf16[4096,256]{1,0:T(8,128)(2,1)} %get-tuple-element.86) | copy-start | bytes 6291460
  96.4 20.0 %collective-permute-start.10 = (bf16[1024,256]{1,0:T(8,128)(2,1)S(1)}, bf16[1024,256]{1,0:T(8,128)(2,1)}, u32[]{:S(2)}, u32[]{:S(2)}) collective-permute-start(bf16[1024,256]{1,0:T(8,128)(2,1)S(1)} %get-tuple-element.93), channel_id=1, source_target_pairs={{0,8},{4,12},{8,0},{12,4},{16,24},{20,28},{24,16},{28,20},{1,9},{5... | collective-permute-start | bytes 1572872 | tf_op jit(solution)/shard_map/ppermute | solution.py:1087
  97.8 36.8 %all-to-all-start.2 = ((bf16[32,64,256]{2,1,0:T(8,128)(2,1)}), bf16[32,64,256]{2,1,0:T(8,128)(2,1)S(1)}, u32[]{:S(2)}, u32[]{:S(2)}) async-start(bf16[32,64,256]{2,1,0:T(8,128)(2,1)} %get-tuple-element.96), calls=%async_computation.2 | async-start | bytes 2097152 | tf_op jit(solution)/shard_map/all_to_all | solution.py:1203
  102.0 25.6 %collective-permute-start.12 = (bf16[1024,256]{1,0:T(8,128)(2,1)}, bf16[1024,256]{1,0:T(8,128)(2,1)S(1)}, u32[]{:S(2)}, u32[]{:S(2)}) collective-permute-start(bf16[1024,256]{1,0:T(8,128)(2,1)} %get-tuple-element.95), channel_id=1, source_target_pairs={{0,16},{4,20},{8,24},{12,28},{16,0},{20,4},{24,8},{28,12},{1,17},{... | collective-permute-start | bytes 1572872 | tf_op jit(solution)/shard_map/ppermute | solution.py:1087
  118.4 14.4 %collective-permute-start.11 = (bf16[512,256]{1,0:T(8,128)(2,1)}, bf16[512,256]{1,0:T(8,128)(2,1)}, u32[]{:S(2)}, u32[]{:S(2)}) collective-permute-start(bf16[512,256]{1,0:T(8,128)(2,1)} %constant_dynamic-slice_fusion.5), channel_id=1, source_target_pairs={{0,16},{4,20},{8,24},{12,28},{16,0},{20,4},{24,8},{28,12},{1,17},{... | collective-permute-start | bytes 786440 | tf_op jit(solution)/shard_map/ppermute | solution.py:1087
  127.7 6.7 %collective-permute-start.13 = (bf16[512,256]{1,0:T(8,128)(2,1)S(1)}, bf16[512,256]{1,0:T(8,128)(2,1)S(1)}, u32[]{:S(2)}, u32[]{:S(2)}) collective-permute-start(bf16[512,256]{1,0:T(8,128)(2,1)S(1)} %constant_dynamic-slice_fusion.4), channel_id=1, source_target_pairs={{0,8},{4,12},{8,0},{12,4},{16,24},{20,28},{24,16},{28,20},{1,9},{5... | collective-permute-start | bytes 786440 | tf_op jit(solution)/shard_map/ppermute | solution.py:1087
  134.6 6.4 %collective-permute-start.14 = (bf16[256,256]{1,0:T(8,128)(2,1)S(1)}, bf16[256,256]{1,0:T(8,128)(2,1)S(1)}, u32[]{:S(2)}, u32[]{:S(2)}) collective-permute-start(bf16[256,256]{1,0:T(8,128)(2,1)S(1)} %get-tuple-element.98), channel_id=1, source_target_pairs={{0,1},{1,0},{2,3},{3,2},{4,5},{5,4},{6,7},{7,6},{8,9},{9,8},{10,11... | collective-permute-start | bytes 393224 | tf_op jit(solution)/shard_map/ppermute | solution.py:1110
  136.6 11.7 %collective-permute-start.15 = (bf16[256,256]{1,0:T(8,128)(2,1)S(1)}, bf16[256,256]{1,0:T(8,128)(2,1)S(1)}, u32[]{:S(2)}, u32[]{:S(2)}) collective-permute-start(bf16[256,256]{1,0:T(8,128)(2,1)S(1)} %get-tuple-element.99), channel_id=1, source_target_pairs={{0,2},{1,3},{2,0},{3,1},{4,6},{5,7},{6,4},{7,5},{8,10},{9,11},{10,... | collective-permute-start | bytes 393224 | tf_op jit(solution)/shard_map/ppermute | solution.py:1110
  139.3 9.0 %collective-permute-start.16 = (bf16[256,256]{1,0:T(8,128)(2,1)S(1)}, bf16[256,256]{1,0:T(8,128)(2,1)S(1)}, u32[]{:S(2)}, u32[]{:S(2)}) collective-permute-start(bf16[256,256]{1,0:T(8,128)(2,1)S(1)} %get-tuple-element.100), channel_id=1, source_target_pairs={{0,3},{1,2},{2,1},{3,0},{4,7},{5,6},{6,5},{7,4},{8,11},{9,10},{10,... | collective-permute-start | bytes 393224 | tf_op jit(solution)/shard_map/ppermute | solution.py:1110
  148.3 6.0 %collective-permute-start.19 = (bf16[256,256]{1,0:T(8,128)(2,1)S(1)}, bf16[256,256]{1,0:T(8,128)(2,1)S(1)}, u32[]{:S(2)}, u32[]{:S(2)}) collective-permute-start(bf16[256,256]{1,0:T(8,128)(2,1)S(1)} %add_convert_fusion.5), channel_id=1, source_target_pairs={{0,1},{1,0},{2,3},{3,2},{4,5},{5,4},{6,7},{7,6},{8,9},{9,8},{10,11... | collective-permute-start | bytes 393224 | tf_op jit(solution)/shard_map/ppermute | solution.py:1110
  150.3 11.2 %collective-permute-start.18 = (bf16[256,256]{1,0:T(8,128)(2,1)S(1)}, bf16[256,256]{1,0:T(8,128)(2,1)S(1)}, u32[]{:S(2)}, u32[]{:S(2)}) collective-permute-start(bf16[256,256]{1,0:T(8,128)(2,1)S(1)} %add_convert_fusion.5), channel_id=1, source_target_pairs={{0,2},{1,3},{2,0},{3,1},{4,6},{5,7},{6,4},{7,5},{8,10},{9,11},{10,... | collective-permute-start | bytes 393224 | tf_op jit(solution)/shard_map/ppermute | solution.py:1110
  151.3 10.3 %collective-permute-start.17 = (bf16[256,256]{1,0:T(8,128)(2,1)S(1)}, bf16[256,256]{1,0:T(8,128)(2,1)S(1)}, u32[]{:S(2)}, u32[]{:S(2)}) collective-permute-start(bf16[256,256]{1,0:T(8,128)(2,1)S(1)} %add_convert_fusion.5), channel_id=1, source_target_pairs={{0,3},{1,2},{2,1},{3,0},{4,7},{5,6},{6,5},{7,4},{8,11},{9,10},{10,... | collective-permute-start | bytes 393224 | tf_op jit(solution)/shard_map/ppermute | solution.py:1110
  161.8 8.0 %collective-permute-start.20 = (bf16[512,256]{1,0:T(8,128)(2,1)S(1)}, bf16[512,256]{1,0:T(8,128)(2,1)S(1)}, u32[]{:S(2)}, u32[]{:S(2)}) collective-permute-start(bf16[512,256]{1,0:T(8,128)(2,1)S(1)} %bitcast.51), channel_id=1, source_target_pairs={{0,16},{4,20},{8,24},{12,28},{16,0},{20,4},{24,8},{28,12},{1,17},{... | collective-permute-start | bytes 786440 | tf_op jit(solution)/shard_map/ppermute | solution.py:1087
  163.4 9.2 %collective-permute-start.22 = (bf16[512,256]{1,0:T(8,128)(2,1)S(1)}, bf16[512,256]{1,0:T(8,128)(2,1)S(1)}, u32[]{:S(2)}, u32[]{:S(2)}) collective-permute-start(bf16[512,256]{1,0:T(8,128)(2,1)S(1)} %bitcast.50), channel_id=1, source_target_pairs={{0,8},{4,12},{8,0},{12,4},{16,24},{20,28},{24,16},{28,20},{1,9},{5... | collective-permute-start | bytes 786440 | tf_op jit(solution)/shard_map/ppermute | solution.py:1087
  169.9 9.5 %collective-permute-start.21 = (bf16[1024,256]{1,0:T(8,128)(2,1)S(1)}, bf16[1024,256]{1,0:T(8,128)(2,1)S(1)}, u32[]{:S(2)}, u32[]{:S(2)}) collective-permute-start(bf16[1024,256]{1,0:T(8,128)(2,1)S(1)} %pad_maximum_fusion.9), channel_id=1, source_target_pairs={{0,8},{4,12},{8,0},{12,4},{16,24},{20,28},{24,16},{28,20},{1,9},{5... | collective-permute-start | bytes 1572872 | tf_op jit(solution)/shard_map/ppermute | solution.py:1087
  172.8 9.2 %collective-permute-start.23 = (bf16[1024,256]{1,0:T(8,128)(2,1)S(1)}, bf16[1024,256]{1,0:T(8,128)(2,1)S(1)}, u32[]{:S(2)}, u32[]{:S(2)}) collective-permute-start(bf16[1024,256]{1,0:T(8,128)(2,1)S(1)} %pad_maximum_fusion.10), channel_id=1, source_target_pairs={{0,16},{4,20},{8,24},{12,28},{16,0},{20,4},{24,8},{28,12},{1,17},{... | collective-permute-start | bytes 1572872 | tf_op jit(solution)/shard_map/ppermute | solution.py:1087
  182.3 2.8 %collective-permute-start.24 = (bf16[2048,256]{1,0:T(8,128)(2,1)S(1)}, bf16[2048,256]{1,0:T(8,128)(2,1)S(1)}, u32[]{:S(2)}, u32[]{:S(2)}) collective-permute-start(bf16[2048,256]{1,0:T(8,128)(2,1)S(1)} %pad_maximum_fusion.2.own_a_ref), channel_id=1, source_target_pairs={{0,4},{4,0},{8,12},{12,8},{16,20},{20,16},{24,28},{28,24},{1,5},{5... | collective-permute-start | bytes 3145736 | tf_op jit(solution)/shard_map/ppermute | solution.py:1087
  182.4 4.1 %collective-permute-start.25 = (bf16[2048,256]{1,0:T(8,128)(2,1)S(1)}, bf16[2048,256]{1,0:T(8,128)(2,1)S(1)}, u32[]{:S(2)}, u32[]{:S(2)}) collective-permute-start(bf16[2048,256]{1,0:T(8,128)(2,1)S(1)} %pad_maximum_fusion.3.own_b_ref), channel_id=1, source_target_pairs={{0,4},{4,0},{8,12},{12,8},{16,20},{20,16},{24,28},{28,24},{1,5},{5... | collective-permute-start | bytes 3145736 | tf_op jit(solution)/shard_map/ppermute | solution.py:1087
